TPU v7x, 32 devices: a whole 2x2x4 slice. The times are simulated.
32 devices in a mesh: grp: 8 (over y, x, core), ep: 4 (over z).
Axes of the slice: x: 2, y: 2, z: 4, core: 2. Of those that a mesh axis runs over, the one named last changes fastest.
Arguments:
- tokens: bfloat16 [128, 197, 512], P(('grp', 'ep')), may hold values from -6 to 6
- routes: int32 [128, 197, 2], P(('grp', 'ep')), may hold values from 0 to 7, all different within a row; in each aligned block of 788 rows (0 to 787, 788 to 1575, ..., all dimensions but the last counted through in order) at most 247 rows name the same one
- gates: float32 [128, 197, 2], P(('grp', 'ep')), may hold values from 0 to 1, as said below
- ln1_gain: float32 [512], replicated, may hold values from 0.5 to 1.5
- ln1_bias: float32 [512], replicated, may hold values from -0.6 to 0.6
- w_qkv: bfloat16 [512, 1536], replicated, may hold values from -0.25 to 0.25
- w_out: bfloat16 [512, 512], replicated, may hold values from -1 to 1
- out_bias: float32 [512], replicated, may hold values from -0.6 to 0.6
- ln2_gain: float32 [512], replicated, may hold values from 0.5 to 1.5
- ln2_bias: float32 [512], replicated, may hold values from -0.6 to 0.6
- w_in: bfloat16 [8, 512, 2048], P('ep'), may hold values from -0.25 to 0.25
- in_bias: float32 [8, 2048], P('ep'), may hold values from -0.6 to 0.6
- w_back: bfloat16 [8, 2048, 512], P('ep'), may hold values from -0.125 to 0.125
- back_bias: float32 [8, 512], P('ep'), may hold values from -0.6 to 0.6
- cotangent: bfloat16 [128, 197, 512], P(('grp', 'ep')), may hold values from -6 to 6
Outputs:
- output: bfloat16 [128, 197, 512], P(('grp', 'ep'))
- grad_tokens: bfloat16 [128, 197, 512], P(('grp', 'ep'))
- grad_ln1_gain: float32 [512], P('ep')
- grad_ln1_bias: float32 [512], P('ep')
- grad_w_qkv: float32 [512, 1536], P('ep')
- grad_w_out: float32 [512, 512], P('ep')
- grad_out_bias: float32 [512], P('ep')
- grad_ln2_gain: float32 [512], P('ep')
- grad_ln2_bias: float32 [512], P('ep')
- grad_w_in: float32 [8, 512, 2048], P('ep')
- grad_in_bias: float32 [8, 2048], P('ep')
- grad_w_back: float32 [8, 2048, 512], P('ep')
- grad_back_bias: float32 [8, 512], P('ep')
Inputs may be any that keep to these rules, and one draw needn't show every extreme that they name: `routes`: the two experts of a token differ; no block of 788 tokens names one expert more than 247 times, and some block names some expert exactly 247 times. A token's two gates are positive and sum to one.
All inputs are finite; a program needn't handle non-finite values.
Results may differ from a plain program's by a relative error of at most 0.02.
Values may be sent and summed in bfloat16 or wider, within the bound.
No kernel may reach another device: no remote copies, remote signals or barrier semaphores. Data moves between devices by JAX's collectives and lax.ppermute only.
A program may use at most 192 MiB of HBM per device.

v0:
```python
import jax
import jax.numpy as jnp
from jax import lax
from jax.sharding import PartitionSpec as P

HD = 64


NORM_EPS = 1e-06


def slot_of(route_rows, expert_count):
    flat = route_rows.reshape(-1)
    onehot = (flat[:, None] == jnp.arange(expert_count, dtype=jnp.int32)[None, :]).astype(jnp.int32)
    before = jnp.cumsum(onehot, axis=0) - onehot
    return jnp.sum(before * onehot, axis=1).reshape(route_rows.shape)


def norm_parts(values):
    average = jnp.mean(values, axis=-1, keepdims=True)
    centred = values - average
    inv_std = lax.rsqrt(jnp.mean(centred * centred, axis=-1, keepdims=True) + NORM_EPS)
    return (centred * inv_std, inv_std)


def norm_back(grad_norm, normed, inv_std, gain):
    scaled = grad_norm * gain
    return inv_std * (
        scaled
        - jnp.mean(scaled, axis=-1, keepdims=True)
        - normed * jnp.mean(scaled * normed, axis=-1, keepdims=True)
    )


def gelu_tanh(pre_act):
    return jax.nn.gelu(pre_act, approximate=True)


def local(
    tokens,
    routes,
    gates,
    ln1_gain,
    ln1_bias,
    w_qkv,
    w_out,
    out_bias,
    ln2_gain,
    ln2_bias,
    w_in,
    in_bias,
    w_back,
    back_bias,
    cotangent,
):
    images, seq_len, model_width = tokens.shape
    tok_rows = images * seq_len
    head_count = model_width // HD
    ep_size = lax.axis_size("ep")
    exp_dev = w_in.shape[0]
    experts = exp_dev * ep_size
    capacity = (tok_rows * 10 + 4 * experts - 1) // (4 * experts)
    score_scale = HD ** (-0.5)
    inputs = tokens.reshape(tok_rows, model_width).astype(jnp.float32)
    norm_first, inv_first = norm_parts(inputs)
    first = (norm_first * ln1_gain + ln1_bias).astype(jnp.bfloat16)
    qkv = jnp.dot(first, w_qkv, preferred_element_type=jnp.float32).astype(jnp.bfloat16)
    qkv = qkv.reshape(images, seq_len, 3, head_count, HD)
    query, key_rows, value_rows = (qkv[:, :, 0], qkv[:, :, 1], qkv[:, :, 2])
    scores = (
        jnp.einsum("ishd,ithd->ihst", query, key_rows, preferred_element_type=jnp.float32)
        * score_scale
    )
    row_max = jnp.max(scores, axis=-1, keepdims=True)
    log_total = row_max + jnp.log(jnp.sum(jnp.exp(scores - row_max), axis=-1, keepdims=True))
    attn_prob = jnp.exp(scores - log_total).astype(jnp.bfloat16)
    attended = jnp.einsum(
        "ihst,ithd->ishd", attn_prob, value_rows, preferred_element_type=jnp.float32
    )
    attended = attended.astype(jnp.bfloat16).reshape(tok_rows, model_width)
    resid = inputs + jnp.dot(attended, w_out, preferred_element_type=jnp.float32) + out_bias
    norm_second, inv_second = norm_parts(resid)
    second = (norm_second * ln2_gain + ln2_bias).astype(jnp.bfloat16)
    route_rows = routes.reshape(tok_rows, 2)
    slots = slot_of(route_rows, experts)
    target = (route_rows * capacity + slots).reshape(-1)
    spread = jnp.repeat(second, 2, axis=0)
    buffer = jnp.zeros((experts * capacity, model_width), jnp.bfloat16).at[target].set(spread)
    inbox = lax.all_to_all(
        buffer.reshape(ep_size, exp_dev * capacity, model_width),
        "ep",
        split_axis=0,
        concat_axis=0,
        tiled=True,
    )
    inbox = inbox.reshape(ep_size, exp_dev, capacity, model_width)
    pre_act = (
        jnp.einsum("secd,edf->secf", inbox, w_in, preferred_element_type=jnp.float32)
        + in_bias[None, :, None, :]
    )
    active = gelu_tanh(pre_act).astype(jnp.bfloat16)
    expert_out = (
        jnp.einsum("secf,efd->secd", active, w_back, preferred_element_type=jnp.float32)
        + back_bias[None, :, None, :]
    )
    expert_out = expert_out.astype(jnp.bfloat16)
    returned = lax.all_to_all(
        expert_out.reshape(ep_size, exp_dev * capacity, model_width),
        "ep",
        split_axis=0,
        concat_axis=0,
        tiled=True,
    )
    picked = returned.reshape(experts * capacity, model_width)[target].reshape(
        tok_rows, 2, model_width
    )
    gate_rows = gates.reshape(tok_rows, 2)
    mixed = jnp.sum(picked.astype(jnp.float32) * gate_rows[:, :, None], axis=1)
    output = (resid + mixed).astype(jnp.bfloat16).reshape(images, seq_len, model_width)
    grad_top = cotangent.reshape(tok_rows, model_width).astype(jnp.float32)
    grad_pick = (
        (grad_top[:, None, :] * gate_rows[:, :, None])
        .astype(jnp.bfloat16)
        .reshape(tok_rows * 2, model_width)
    )
    grad_buffer = (
        jnp.zeros((experts * capacity, model_width), jnp.bfloat16).at[target].set(grad_pick)
    )
    grad_inbox_out = lax.all_to_all(
        grad_buffer.reshape(ep_size, exp_dev * capacity, model_width),
        "ep",
        split_axis=0,
        concat_axis=0,
        tiled=True,
    )
    grad_inbox_out = grad_inbox_out.reshape(ep_size, exp_dev, capacity, model_width)
    grad_back_bias = jnp.sum(grad_inbox_out, axis=(0, 2), dtype=jnp.float32)
    grad_w_back = jnp.einsum(
        "secf,secd->efd", active, grad_inbox_out, preferred_element_type=jnp.float32
    )
    grad_active = jnp.einsum(
        "secd,efd->secf", grad_inbox_out, w_back, preferred_element_type=jnp.float32
    )
    unused, gelu_pull = jax.vjp(gelu_tanh, pre_act)
    grad_pre = gelu_pull(grad_active)[0].astype(jnp.bfloat16)
    grad_in_bias = jnp.sum(grad_pre, axis=(0, 2), dtype=jnp.float32)
    grad_w_in = jnp.einsum("secd,secf->edf", inbox, grad_pre, preferred_element_type=jnp.float32)
    grad_inbox = jnp.einsum(
        "secf,edf->secd", grad_pre, w_in, preferred_element_type=jnp.float32
    ).astype(jnp.bfloat16)
    grad_rows = lax.all_to_all(
        grad_inbox.reshape(ep_size, exp_dev * capacity, model_width),
        "ep",
        split_axis=0,
        concat_axis=0,
        tiled=True,
    )
    grad_w_in, grad_in_bias, grad_w_back, grad_back_bias = (
        lax.psum(grad_w_in.astype(jnp.bfloat16), "grp").astype(jnp.float32),
        lax.psum(grad_in_bias.astype(jnp.bfloat16), "grp").astype(jnp.float32),
        lax.psum(grad_w_back.astype(jnp.bfloat16), "grp").astype(jnp.float32),
        lax.psum(grad_back_bias.astype(jnp.bfloat16), "grp").astype(jnp.float32),
    )
    grad_second = grad_rows.reshape(experts * capacity, model_width)[target].reshape(
        tok_rows, 2, model_width
    )
    grad_second = jnp.sum(grad_second.astype(jnp.float32), axis=1)
    grad_ln2_gain = jnp.sum(grad_second * norm_second, axis=0)
    grad_ln2_bias = jnp.sum(grad_second, axis=0)
    grad_resid = grad_top + norm_back(grad_second, norm_second, inv_second, ln2_gain)
    grad_branch = grad_resid.astype(jnp.bfloat16)
    grad_w_out = jnp.einsum("td,te->de", attended, grad_branch, preferred_element_type=jnp.float32)
    grad_out_bias = jnp.sum(grad_branch, axis=0, dtype=jnp.float32)
    grad_attended = jnp.einsum("te,de->td", grad_branch, w_out, preferred_element_type=jnp.float32)
    grad_attended = grad_attended.astype(jnp.bfloat16).reshape(images, seq_len, head_count, HD)
    again = (
        jnp.einsum("ishd,ithd->ihst", query, key_rows, preferred_element_type=jnp.float32)
        * score_scale
    )
    prob_full = jnp.exp(again - log_total)
    grad_prob = jnp.einsum(
        "ishd,ithd->ihst", grad_attended, value_rows, preferred_element_type=jnp.float32
    )
    grad_value = jnp.einsum(
        "ihst,ishd->ithd",
        prob_full.astype(jnp.bfloat16),
        grad_attended,
        preferred_element_type=jnp.float32,
    )
    grad_scores = (
        prob_full * (grad_prob - jnp.sum(grad_prob * prob_full, axis=-1, keepdims=True))
    ).astype(jnp.bfloat16)
    grad_query = (
        jnp.einsum("ihst,ithd->ishd", grad_scores, key_rows, preferred_element_type=jnp.float32)
        * score_scale
    )
    grad_key = (
        jnp.einsum("ihst,ishd->ithd", grad_scores, query, preferred_element_type=jnp.float32)
        * score_scale
    )
    grad_qkv = (
        jnp.stack([grad_query, grad_key, grad_value], axis=2)
        .astype(jnp.bfloat16)
        .reshape(tok_rows, 3 * model_width)
    )
    grad_w_qkv = jnp.einsum("td,te->de", first, grad_qkv, preferred_element_type=jnp.float32)
    grad_first = jnp.einsum("te,de->td", grad_qkv, w_qkv, preferred_element_type=jnp.float32)
    grad_ln1_gain = jnp.sum(grad_first * norm_first, axis=0)
    grad_ln1_bias = jnp.sum(grad_first, axis=0)
    grad_inputs = grad_resid + norm_back(grad_first, norm_first, inv_first, ln1_gain)
    grad_tokens = grad_inputs.astype(jnp.bfloat16).reshape(images, seq_len, model_width)
    shares = (
        lax.psum_scatter(
            grad_ln1_gain.astype(jnp.bfloat16), "ep", scatter_dimension=0, tiled=True
        ).astype(jnp.float32),
        lax.psum_scatter(
            grad_ln1_bias.astype(jnp.bfloat16), "ep", scatter_dimension=0, tiled=True
        ).astype(jnp.float32),
        lax.psum_scatter(
            grad_w_qkv.astype(jnp.bfloat16), "ep", scatter_dimension=0, tiled=True
        ).astype(jnp.float32),
        lax.psum_scatter(
            grad_w_out.astype(jnp.bfloat16), "ep", scatter_dimension=0, tiled=True
        ).astype(jnp.float32),
        lax.psum_scatter(
            grad_out_bias.astype(jnp.bfloat16), "ep", scatter_dimension=0, tiled=True
        ).astype(jnp.float32),
        lax.psum_scatter(
            grad_ln2_gain.astype(jnp.bfloat16), "ep", scatter_dimension=0, tiled=True
        ).astype(jnp.float32),
        lax.psum_scatter(
            grad_ln2_bias.astype(jnp.bfloat16), "ep", scatter_dimension=0, tiled=True
        ).astype(jnp.float32),
    )
    shares = (
        lax.psum(shares[0].astype(jnp.bfloat16), "grp").astype(jnp.float32),
        lax.psum(shares[1].astype(jnp.bfloat16), "grp").astype(jnp.float32),
        lax.psum(shares[2].astype(jnp.bfloat16), "grp").astype(jnp.float32),
        lax.psum(shares[3].astype(jnp.bfloat16), "grp").astype(jnp.float32),
        lax.psum(shares[4].astype(jnp.bfloat16), "grp").astype(jnp.float32),
        lax.psum(shares[5].astype(jnp.bfloat16), "grp").astype(jnp.float32),
        lax.psum(shares[6].astype(jnp.bfloat16), "grp").astype(jnp.float32),
    )
    return (
        output,
        grad_tokens,
        shares[0],
        shares[1],
        shares[2],
        shares[3],
        shares[4],
        shares[5],
        shares[6],
        grad_w_in,
        grad_in_bias,
        grad_w_back,
        grad_back_bias,
    )


def solution(mesh):
    return jax.shard_map(
        local,
        mesh=mesh,
        in_specs=(
            P(("grp", "ep"), None, None),
            P(("grp", "ep"), None, None),
            P(("grp", "ep"), None, None),
            P(),
            P(),
            P(),
            P(),
            P(),
            P(),
            P(),
            P("ep", None, None),
            P("ep", None),
            P("ep", None, None),
            P("ep", None),
            P(("grp", "ep"), None, None),
        ),
        out_specs=(
            P(("grp", "ep"), None, None),
            P(("grp", "ep"), None, None),
            P("ep"),
            P("ep"),
            P("ep", None),
            P("ep", None),
            P("ep"),
            P("ep"),
            P("ep"),
            P("ep", None, None),
            P("ep", None),
            P("ep", None, None),
            P("ep", None),
        ),
        check_vma=False,
    )
```

profile of v0, /device:TPU:0, one launch (start us, length us, event | category | flops | bytes accessed | tf_op | source)
XLA Modules:
  0.0 600.6 jit_solution(16275421576518819410)
XLA Ops:
  18.4 3.0 convolution_convert_fusion
  21.4 7.2 %reshape.303 = bf16[4,197,3,8,64]{4,3,2,1,0:T(8,128)(2,1)} reshape(bf16[788,1536]{1,0:T(8,128)(2,1)} %convolution_convert_fusion) | data formatting | bytes 4841472 | tf_op jit(solution)/shard_map/reshape | solution.py:68
  28.5 4.4 fusion.58
  54.5 5.0 reshape.282
  59.5 12.4 %scatter_custom_fusion = bf16[1976,512]{1,0:T(8,128)(2,1)} fusion(s32[1576]{0:T(1024)S(1)} %fusion.53, bf16[1576,512]{1,0:T(8,128)(2,1)} %reshape.282, bf16[]{:T(256)} %constant.39.clone.1), kind=kCustom, calls=%fused_computation.84 | custom fusion | bytes 2023936 | tf_op jit(solution)/shard_map/scatter | solution.py:88
  71.9 3.4 reshape.246
  75.3 6.4 %all-to-all-start = ((bf16[4,494,512]{2,1,0:T(8,128)(2,1)}), bf16[4,494,512]{2,1,0:T(8,128)(2,1)}, u32[]{:S(2)}, u32[]{:S(2)}) async-start(bf16[4,494,512]{2,1,0:T(8,128)(2,1)} %reshape.246), calls=%async_computation | async-start | bytes 4063232 | tf_op jit(solution)/shard_map/all_to_all | solution.py:89
  89.2 4.2 mul.240
  93.4 5.3 mul.241
  98.7 17.8 %scatter_custom_fusion.1 = bf16[1976,512]{1,0:T(8,128)(2,1)} fusion(s32[1576]{0:T(1024)S(1)} %fusion.53, f32[1576,512]{1,0:T(8,128)} %mul.241, f32[1576]{0:T(1024)S(1)} %mul.242, bf16[]{:T(256)} %constant.39.clone.1), kind=kCustom, calls=%fused_computation.63 | custom fusion | flops 1613824 | bytes 5259266 | tf_op jit(solution)/shard_map/scatter | solution.py:127
  116.5 3.4 reshape.251
  119.9 8.8 %all-to-all-done = bf16[4,494,512]{2,1,0:T(8,128)(2,1)} async-done(((bf16[4,494,512]{2,1,0:T(8,128)(2,1)}), bf16[4,494,512]{2,1,0:T(8,128)(2,1)}, u32[]{:S(2)}, u32[]{:S(2)}) %all-to-all-start) | async-done | bytes 2023456 | tf_op jit(solution)/shard_map/all_to_all | solution.py:89
  128.6 4.4 all-to-all-start.2
  135.9 15.1 %fusion.10 = (bf16[4,2,247,2048]{3,2,0,1:T(8,128)(2,1)}, f32[2,4,247,2048]{3,2,1,0:T(8,128)}) fusion(f32[2,2048]{1,0:T(2,128)S(1)} %copy-done.34, bf16[2,512,2048]{2,1,0:T(8,128)(2,1)} %param.25, bf16[4,2,247,512]{3,2,1,0:T(8,128)(2,1)} %reshape.247), kind=kOutput, calls=%fused_computation.19 | convolution fusion | flops 4184440832 | bytes 30515200 | tf_op jit(solution)/shard_map/secd,edf->secf/dot_general | solution.py:98
  151.0 28.4 %all-to-all-done.2 = bf16[4,494,512]{2,1,0:T(8,128)(2,1)} async-done(((bf16[4,494,512]{2,1,0:T(8,128)(2,1)}), bf16[4,494,512]{2,1,0:T(8,128)(2,1)}, u32[]{:S(2)}, u32[]{:S(2)}) %all-to-all-start.2) | async-done | bytes 2023456 | tf_op jit(solution)/shard_map/all_to_all | solution.py:129
  182.1 20.5 %fusion.60 = (bf16[2,2048]{1,0:T(2,128)(2,1)S(1)}, bf16[4,2,247,2048]{3,2,0,1:T(8,128)(2,1)}) fusion(f32[2,4,247,2048]{3,2,1,0:T(8,128)} %get-tuple-element.99, f32[2,2048]{1,0:T(2,128)S(1)} %copy-done.34, bf16[2,2048,512]{2,1,0:T(8,128)(2,1)} %param.27, bf16[4,2,247,512]{3,2,1,0:T(8,128)(2,1)} %reshape.252), kind=kOutput, calls=%fused_computation.119 | convolution fusion | flops 4232998912 | bytes 30523392 | tf_op jit(solution)/shard_map/secd,efd->secf/dot_general | solution.py:141
  202.7 8.6 %convert_bitcast_fusion = bf16[4,2,247,512]{3,2,0,1:T(8,128)(2,1)S(1)} fusion(bf16[4,2,247,2048]{3,2,0,1:T(8,128)(2,1)} %get-tuple-element.104, bf16[2,512,2048]{2,1,0:T(8,128)(2,1)S(1)} %copy-done.33), kind=kOutput, calls=%fused_computation.47 | convolution fusion | flops 4144984064 | bytes 14311424 | tf_op jit(solution)/shard_map/secf,edf->secd/dot_general | solution.py:148
  215.5 4.6 all-to-all-start.3
  220.1 8.9 %fusion.23 = bf16[4,2,247,512]{3,2,0,1:T(8,128)(2,1)S(1)} fusion(f32[2,512]{1,0:T(2,128)S(1)} %copy-done.35, bf16[4,2,247,2048]{3,2,0,1:T(8,128)(2,1)} %get-tuple-element.98, bf16[2,2048,512]{2,1,0:T(8,128)(2,1)} %param.27), kind=kOutput, calls=%fused_computation.45 | convolution fusion | flops 4145995776 | bytes 14315520 | tf_op jit(solution)/shard_map/secf,efd->secd/dot_general | solution.py:103
  233.3 33.2 %all-to-all-done.3 = bf16[4,494,512]{2,1,0:T(8,128)(2,1)} async-done(((bf16[4,494,512]{2,1,0:T(8,128)(2,1)}), bf16[4,494,512]{2,1,0:T(8,128)(2,1)}, u32[]{:S(2)}, u32[]{:S(2)}) %all-to-all-start.3) | async-done | bytes 2023456 | tf_op jit(solution)/shard_map/all_to_all | solution.py:151
  266.4 4.4 all-to-all-start.1
  277.2 3.5 reshape.254
  280.6 8.3 %gather_fusion.1 = bf16[1576,512]{1,0:T(8,128)(2,1)} fusion(bf16[1976,512]{1,0:T(8,128)(2,1)} %reshape.254, s32[2048]{0:T(1024)S(1)} %pad_clamp_fusion), kind=kCustom, calls=%fused_computation.1 | custom fusion | bytes 3233952 | tf_op jit(solution)/shard_map/gather | solution.py:164
  289.0 4.9 reshape.261
  293.9 23.3 %all-to-all-done.1 = bf16[4,494,512]{2,1,0:T(8,128)(2,1)} async-done(((bf16[4,494,512]{2,1,0:T(8,128)(2,1)}), bf16[4,494,512]{2,1,0:T(8,128)(2,1)}, u32[]{:S(2)}, u32[]{:S(2)}) %all-to-all-start.1) | async-done | bytes 2023456 | tf_op jit(solution)/shard_map/all_to_all | solution.py:107
  317.2 3.4 reshape.249
  320.7 7.9 %gather_fusion = bf16[1576,512]{1,0:T(8,128)(2,1)} fusion(bf16[1976,512]{1,0:T(8,128)(2,1)} %reshape.249, s32[2048]{0:T(1024)S(1)} %pad_clamp_fusion), kind=kCustom, calls=%fused_computation | custom fusion | bytes 3233952 | tf_op jit(solution)/shard_map/gather | solution.py:114
  328.6 4.9 reshape.259
  333.6 6.9 %reduce_sum.209 = f32[788,512]{1,0:T(8,128)} reduce(f32[788,2,512]{2,1,0:T(2,128)} %reshape.261, f32[]{:T(128)} %constant.34.clone.1), dimensions={1}, to_apply=%region_12.13 | reduce | flops 403456 | bytes 4841476 | tf_op jit(solution)/shard_map/reduce_sum | solution.py:167
  340.5 18.1 %multiply_reduce_fusion.2 = f32[788,512]{1,0:T(8,128)S(1)} fusion(f32[788,2,512]{2,1,0:T(2,128)} %reshape.259, f32[788,2]{1,0:T(8,128)} %copy.121), kind=kLoop, calls=%fused_computation.41 | loop fusion | flops 1210368 | bytes 4847776 | tf_op jit(solution)/shard_map/reduce_sum | solution.py:118
  367.5 3.0 copy.127
  370.5 5.1 multiply_reduce_fusion
  375.6 4.7 multiply_convert_fusion
  384.4 4.3 convolution_bitcast_fusion
  389.4 4.5 copy.132
  393.9 7.0 %convert_element_type.215 = bf16[788,1536]{0,1:T(8,128)(2,1)} reshape(bf16[4,197,3,8,64]{1,0,4,3,2:T(4,128)(2,1)} %copy.132) | data formatting | bytes 4841472 | tf_op jit(solution)/shard_map/convert_element_type | solution.py:203
  400.9 4.8 convolution_convert_fusion.1
  405.8 10.7 %bitcast_convert_fusion = bf16[2,2048,512]{2,1,0:T(8,128)(2,1)} fusion(bf16[4,2,247,2048]{3,2,0,1:T(8,128)(2,1)} %get-tuple-element.98, bf16[4,2,247,512]{3,2,1,0:T(8,128)(2,1)} %reshape.252), kind=kOutput, calls=%fused_computation.20 | convolution fusion | flops 4146069504 | bytes 14311424 | tf_op jit(solution)/shard_map/secf,secd->efd/dot_general | solution.py:138
  416.5 9.8 %bitcast_convert_fusion.1 = bf16[2,512,2048]{2,1,0:T(8,128)(2,1)} fusion(bf16[4,2,247,512]{3,2,1,0:T(8,128)(2,1)S(1)} %copy-done.20, bf16[4,2,247,2048]{3,2,0,1:T(8,128)(2,1)} %get-tuple-element.104), kind=kOutput, calls=%fused_computation.21 | convolution fusion | flops 4146069504 | bytes 14311424 | tf_op jit(solution)/shard_map/secd,secf->edf/dot_general | solution.py:147
  426.3 14.8 %reduce-scatter.3.cloned.1.call-done = bf16[128,1536]{1,0:T(8,128)(2,1)} async-done(((bf16[512,1536]{1,0:T(8,128)(2,1)}), bf16[128,1536]{1,0:T(8,128)(2,1)}) %reduce-scatter.3.cloned.1.call-update) | async-done | bytes 393232 | tf_op jit(solution)/shard_map/reduce_scatter | solution.py:219
  443.0 2.9 reduce_sum.221
  452.1 5.5 multiply_reduce_fusion.4
  457.6 10.3 %all-reduce.8 = (bf16[512]{0:T(512)(128)(2,1)S(1)}, bf16[512]{0:T(512)(128)(2,1)S(1)}, bf16[512]{0:T(512)(128)(2,1)S(1)}, bf16[512]{0:T(512)(128)(2,1)S(1)}, bf16[512]{0:T(512)(128)(2,1)S(1)}) all-reduce(bf16[512]{0:T(512)(128)(2,1)S(1)} %get-tuple-element.67, ...), channel_id=2, replica_groups=mesh['grp'=8,'ep'=4] {'ep'}, use_global_device_ids=true, to_apply=%region_19.20.clone | all-reduce | flops 2560 | bytes 10240
  468.2 23.6 %all-reduce.6 = (bf16[128]{0:T(256)(128)(2,1)S(1)}, bf16[128]{0:T(256)(128)(2,1)S(1)}, bf16[128]{0:T(256)(128)(2,1)S(1)}, bf16[128]{0:T(256)(128)(2,1)S(1)}, bf1...) all-reduce(bf16[128]{0:T(256)(128)(2,1)S(1)} %dynamic-slice.1, ...), channel_id=1, replica_groups=mesh['grp'=8,'ep'=4] {'grp'}, use_global_device_ids=true, to_apply=%region_20.21 | all-reduce | flops 5760 | bytes 23040 | tf_op jit(solution)/shard_map/psum | solution.py:236
  495.0 3.9 add_convert_fusion.1
  502.2 76.4 %all-reduce.11.cloned.1.call-done = (bf16[128,1536]{1,0:T(8,128)(2,1)}, bf16[128,512]{1,0:T(8,128)(2,1)}, bf16[2,512,2048]{2,1,0:T(8,128)(2,1)}, bf16[2,2048,512]{2,1,0:T(8,128)(2,1)}) async-done(((bf16[128,1536]{1,0:T(8,128)(2,1)}, bf16[128,512]{1,0:T(8,128)(2,1)}, bf16[2,512,2048]{2,1,0:T(8,128)(2,1)}, bf16[2,2048,512]{2,1,0:T(8,128)(2,1)}), (bf16[128,1536]{1,0:T(8,128)(2,1)}, bf16[128,512]{1,0:T(8,128)(2,1)}, ...) | async-done | bytes 8912912 | tf_op jit(solution)/shard_map/psum | solution.py:238
  582.2 6.8 %convert_element_type.232 = f32[2,512,2048]{2,1,0:T(8,128)} convert(bf16[2,512,2048]{2,1,0:T(8,128)(2,1)} %get-tuple-element.81) | non-fusion elementwise | flops 2097152 | bytes 12582912 | tf_op jit(solution)/shard_map/convert_element_type | solution.py:159
  589.0 4.6 convert_element_type.235
  (171 shorter events, 91.6 us)
Async XLA Ops:
  7.2 11.2 %copy-start = (bf16[512,1536]{1,0:T(8,128)(2,1)S(1)}, bf16[512,1536]{1,0:T(8,128)(2,1)}, u32[]{:S(2)}) copy-start(bf16[512,1536]{1,0:T(8,128)(2,1)} %param.20) | copy-start | bytes 4718596
  7.2 4.0 copy-start.8
  7.2 3.8 copy-start.22
  12.7 5.7 copy-start.25
  12.9 5.5 copy-start.27
  13.5 4.8 copy-start.29
  13.5 4.8 copy-start.32
  18.4 3.0 copy-start.6
  39.7 2.7 copy-start.9
  42.4 2.7 copy-start.1
  42.4 2.7 copy-start.12
  46.5 2.7 copy-start.30
  49.1 3.0 copy-start.24
  49.2 3.0 copy-start.31
  75.3 6.5 %copy-start.23 = (f32[4,197,2]{1,2,0:T(2,128)S(1)}, f32[4,197,2]{1,2,0:T(2,128)}, u32[]{:S(2)}) copy-start(f32[4,197,2]{1,2,0:T(2,128)} %param.17) | copy-start | bytes 18916
  75.3 53.3 %all-to-all-start = ((bf16[4,494,512]{2,1,0:T(8,128)(2,1)}), bf16[4,494,512]{2,1,0:T(8,128)(2,1)}, u32[]{:S(2)}, u32[]{:S(2)}) async-start(bf16[4,494,512]{2,1,0:T(8,128)(2,1)} %reshape.246), calls=%async_computation | async-start | bytes 4063232 | tf_op jit(solution)/shard_map/all_to_all | solution.py:89
  128.6 50.8 %all-to-all-start.2 = ((bf16[4,494,512]{2,1,0:T(8,128)(2,1)}), bf16[4,494,512]{2,1,0:T(8,128)(2,1)}, u32[]{:S(2)}, u32[]{:S(2)}) async-start(bf16[4,494,512]{2,1,0:T(8,128)(2,1)} %reshape.251), calls=%async_computation.2 | async-start | bytes 4063232 | tf_op jit(solution)/shard_map/all_to_all | solution.py:129
  133.1 2.8 copy-start.34
  182.1 20.5 %copy-start.33 = (bf16[2,512,2048]{2,1,0:T(8,128)(2,1)S(1)}, bf16[2,512,2048]{2,1,0:T(8,128)(2,1)}, u32[]{:S(2)}) copy-start(bf16[2,512,2048]{2,1,0:T(8,128)(2,1)} %param.25) | copy-start | bytes 12582916
  215.5 4.6 copy-start.35
  215.5 50.9 %all-to-all-start.3 = ((bf16[4,494,512]{2,1,0:T(8,128)(2,1)}), bf16[4,494,512]{2,1,0:T(8,128)(2,1)}, u32[]{:S(2)}, u32[]{:S(2)}) async-start(bf16[4,494,512]{2,1,0:T(8,128)(2,1)} %reshape.253), calls=%async_computation.3 | async-start | bytes 4063232 | tf_op jit(solution)/shard_map/all_to_all | solution.py:151
  266.4 50.8 %all-to-all-start.1 = ((bf16[4,494,512]{2,1,0:T(8,128)(2,1)}), bf16[4,494,512]{2,1,0:T(8,128)(2,1)}, u32[]{:S(2)}, u32[]{:S(2)}) async-start(bf16[4,494,512]{2,1,0:T(8,128)(2,1)} %reshape.248), calls=%async_computation.1 | async-start | bytes 4063232 | tf_op jit(solution)/shard_map/all_to_all | solution.py:107
  270.9 155.4 %reduce-scatter.5.cloned.1.call-start = ((), (), s32[]{:S(2)}) async-start(), calls=%async_computation.7 | async-start | bytes 655360 | tf_op jit(solution)/shard_map/reduce_scatter | solution.py:222
  340.5 18.2 %copy-start.5 = (f32[788,512]{1,0:T(8,128)S(1)}, f32[788,512]{1,0:T(8,128)}, u32[]{:S(2)}) copy-start(f32[788,512]{1,0:T(8,128)} %reduce_sum.209) | copy-start | bytes 4841476
  358.6 1.5 copy-start.4
  360.1 1.8 copy-start.15
  360.7 1.2 copy-start.2
  360.7 2.7 copy-start.19
  365.5 5.0 copy-start.13
  375.6 4.7 copy-start.11
  380.4 2.2 copy-start.10
  382.5 1.8 copy-start.14
  384.3 56.8 %reduce-scatter.3.cloned.1.call-start = ((), (), s32[]{:S(2)}) async-start(), calls=%async_computation.6 | async-start | bytes 1966080 | tf_op jit(solution)/shard_map/reduce_scatter | solution.py:219
  384.4 4.3 copy-start.17
  384.4 4.3 copy-start.18
  393.9 7.0 %copy-start.21 = (bf16[788,512]{1,0:T(8,128)(2,1)S(1)}, bf16[788,512]{1,0:T(8,128)(2,1)}, u32[]{:S(2)}) copy-start(bf16[788,512]{1,0:T(8,128)(2,1)} %convert_element_type.222) | copy-start | bytes 2420740
  405.7 172.8 %all-reduce.11.cloned.1.call-start = ((), (), s32[]{:S(2)}) async-start(), calls=%async_computation.8 | async-start | bytes 17825792 | tf_op jit(solution)/shard_map/psum | solution.py:238
  405.8 10.7 %copy-start.20 = (bf16[4,2,247,512]{3,2,1,0:T(8,128)(2,1)S(1)}, bf16[4,2,247,512]{3,2,1,0:T(8,128)(2,1)}, u32[]{:S(2)}) copy-start(bf16[4,2,247,512]{3,2,1,0:T(8,128)(2,1)} %reshape.247) | copy-start | bytes 6070276
  441.1 0.7 copy-start.36
  442.9 6.0 copy-start.7
  449.2 2.9 copy-start.26
  449.2 2.9 copy-start.28
  452.1 42.9 %copy-start.3 = (f32[788,512]{1,0:T(8,128)S(1)}, f32[788,512]{1,0:T(8,128)}, u32[]{:S(2)}) copy-start(f32[788,512]{1,0:T(8,128)} %copy-done.2) | copy-start | bytes 4841476
  582.2 6.8 %copy-start.16 = (bf16[2,2048,512]{2,1,0:T(8,128)(2,1)S(1)}, bf16[2,2048,512]{2,1,0:T(8,128)(2,1)}, u32[]{:S(2)}) copy-start(bf16[2,2048,512]{2,1,0:T(8,128)(2,1)} %get-tuple-element.82) | copy-start | bytes 12582916
Sparse Core Ops, SparseCore 0:
  384.4 20.6 reduce-scatter.4
  407.4 33.6 reduce-scatter.2
  445.8 132.7 all-reduce.10
where the time goes:
time: 605 us; the launch traced here: 601 us
  waiting for transfers between devices  185 us (31%)
  local copies, waits for them, and re-layouts  148 us (24%)
  matrix products  110 us (18%)
  other arithmetic  87.6 us (14%)
  blocking collectives  33.9 us (6%)
  starting transfers between devices  20 us (3%)
  between operations  15.6 us (3%)
    psum x1, waiting for transfers between devices, local(): lax.psum(shares[2].astype(jnp.bfloat16), 'grp').astype(jnp.float32)  76.4 us
    all_to_all x1, waiting for transfers between devices, local(): lax.all_to_all(grad_inbox.reshape(ep_size, exp_dev * capacity, model_widt...  33.2 us
    all_to_all x1, waiting for transfers between devices, local(): lax.all_to_all(grad_buffer.reshape(ep_size, exp_dev * capacity, model_wid...  28.4 us
    psum x1, blocking collectives, local(): lax.psum(shares[0].astype(jnp.bfloat16), 'grp').astype(jnp.float32)  23.6 us
    all_to_all x1, waiting for transfers between devices, local(): lax.all_to_all(expert_out.reshape(ep_size, exp_dev * capacity, model_widt...  23.3 us
    dot_general x1, matrix products, local(): jnp.einsum('secd,efd->secf', grad_inbox_out, w_back, preferred_element_ty...  20.5 us
    reduce_sum x1, other arithmetic, local(): mixed = jnp.sum(picked.astype(jnp.float32) * gate_rows[:, :, None], axis=1)  18.1 us
    scatter x1, other arithmetic, local(): jnp.zeros((experts * capacity, model_width), jnp.bfloat16).at[target]  17.8 us
  transfers between devices with their start and end apart: 7, of which 6 were waited for; matrix products, arithmetic and copies ran while one was open for 27% of the time, Pallas kernels for 0%

commit v1 on v0

v1 whole, which is shorter than its diff:
```python
import functools

import jax
import jax.numpy as jnp
from jax import lax
from jax.experimental import pallas as pl
from jax.experimental.pallas import tpu as pltpu
from jax.sharding import PartitionSpec as P

HD = 64
NORM_EPS = 1e-06
BF16 = jnp.bfloat16
F32 = jnp.float32
VMEM_LIMIT = 60 * 1024 * 1024
GELU_C = 0.7978845608028654


def dot_nn(a, b):
    return jnp.dot(a, b, preferred_element_type=F32)


def dot_nt(a, b):
    return lax.dot_general(a, b, (((1,), (1,)), ((), ())), preferred_element_type=F32)


def dot_tn(a, b):
    return lax.dot_general(a, b, (((0,), (0,)), ((), ())), preferred_element_type=F32)


def norm_parts(values):
    average = jnp.mean(values, axis=-1, keepdims=True)
    centred = values - average
    inv_std = lax.rsqrt(jnp.mean(centred * centred, axis=-1, keepdims=True) + NORM_EPS)
    return centred * inv_std, inv_std


def norm_back(grad_norm, normed, inv_std, gain):
    scaled = grad_norm * gain
    return inv_std * (
        scaled
        - jnp.mean(scaled, axis=-1, keepdims=True)
        - normed * jnp.mean(scaled * normed, axis=-1, keepdims=True)
    )


def whole(shape):
    zeros = (0,) * len(shape)
    return pl.BlockSpec(tuple(shape), lambda *_: zeros)


def params(*semantics):
    return pltpu.CompilerParams(
        dimension_semantics=semantics or None, vmem_limit_bytes=VMEM_LIMIT
    )


def route_kernel(exp_dev, me_ref, routes_ref, gates_ref, cot_ref, slot_row_ref, slot_col_ref, gate_col_ref, *rest):
    out_refs, scratch = rest[:-1], rest[-1]
    n_img, seq, _ = routes_ref.shape
    experts = slot_row_ref.shape[1]
    capp = out_refs[0].shape[1]
    me = me_ref[0]
    lane = lax.broadcasted_iota(jnp.int32, (seq, 128), 1)
    later = lax.broadcasted_iota(jnp.int32, (seq, seq), 0)
    earlier = lax.broadcasted_iota(jnp.int32, (seq, seq), 1)
    tri = jnp.where(earlier < later, 1.0, 0.0).astype(BF16)
    carry = jnp.zeros((1, 128), F32)
    gate_rows = []
    for i in range(n_img):
        routes = routes_ref[i]
        rel = ((routes // exp_dev) ^ me) * exp_dev + routes % exp_dev
        gates = gates_ref[i]
        hit0 = lane == rel[:, 0:1]
        hit1 = lane == rel[:, 1:2]
        member = jnp.where(hit0 | hit1, 1.0, 0.0)
        slot = jnp.where(member > 0.5, dot_nn(tri, member.astype(BF16)) + carry, -1.0)
        gate = jnp.where(hit0, gates[:, 0:1], 0.0) + jnp.where(hit1, gates[:, 1:2], 0.0)
        carry = carry + jnp.sum(member, axis=0, keepdims=True)
        slot_col_ref[i] = slot[:, :experts]
        gate_col_ref[i] = gate[:, :experts]
        scratch[0, 0:seq, :] = slot
        scratch[1, 0:seq, :] = gate
        slot_row_ref[i] = jnp.transpose(scratch[0])[:experts, :seq]
        gate_rows.append(jnp.transpose(scratch[1])[:experts, :seq])
    place = lax.broadcasted_iota(jnp.int32, (capp, seq), 0).astype(F32)
    for e in range(experts):
        total = jnp.zeros((capp, cot_ref.shape[2]), F32)
        for i in range(n_img):
            pick = jnp.where(place == slot_row_ref[i, e : e + 1, :], gate_rows[i][e : e + 1, :], 0.0)
            total = total + dot_nn(pick.astype(BF16), cot_ref[i])
        out_refs[e // exp_dev][e % exp_dev] = total.astype(BF16)


def route_call(me, routes, gates, cotangent, ep_size, exp_dev, capp):
    n_img, seq, width = cotangent.shape
    experts = ep_size * exp_dev
    seq_pad = -(-seq // 128) * 128
    chunk = jax.ShapeDtypeStruct((exp_dev, capp, width), BF16)
    return pl.pallas_call(
        functools.partial(route_kernel, exp_dev),
        in_specs=[pl.BlockSpec(memory_space=pltpu.SMEM)] + [pl.BlockSpec(memory_space=pltpu.VMEM)] * 3,
        out_specs=[pl.BlockSpec(memory_space=pltpu.VMEM)] * (3 + ep_size),
        out_shape=[
            jax.ShapeDtypeStruct((n_img, experts, seq), F32),
            jax.ShapeDtypeStruct((n_img, seq, experts), F32),
            jax.ShapeDtypeStruct((n_img, seq, experts), F32),
        ]
        + [chunk] * ep_size,
        scratch_shapes=[pltpu.VMEM((2, seq_pad, 128), F32)],
        compiler_params=params(),
        cost_estimate=pl.CostEstimate(
            flops=2 * experts * capp * n_img * seq * width, bytes_accessed=4 * n_img * seq * width * 2, transcendentals=0
        ),
        name="route_and_dispatch_cotangent",
    )(me, routes, gates, cotangent)


def attention_kernel(
    heads, tok_ref, w_qkv_ref, w_out_ref, vec_ref, slot_row_ref, qkv_ref, att_ref, lse_ref, resid_ref, *rest
):
    out_refs, second_ref = rest[:-1], rest[-1]
    img = pl.program_id(0)
    seq, width = tok_ref.shape[1:]
    exp_dev, capp = out_refs[0].shape[:2]
    inputs = tok_ref[0].astype(F32)
    norm_first, _ = norm_parts(inputs)
    first = (norm_first * vec_ref[0:1, :] + vec_ref[1:2, :]).astype(BF16)
    qkv = dot_nn(first, w_qkv_ref[...]).astype(BF16)
    qkv_ref[0] = qkv
    low = lax.broadcasted_iota(jnp.int32, (seq, 2 * HD), 1) < HD
    nothing = jnp.zeros((seq, 2 * HD), BF16)
    lane = lax.broadcasted_iota(jnp.int32, (seq, 128), 1)
    lse_all = jnp.zeros((seq, 128), F32)
    pieces = []
    for pair in range(heads // 2):
        at = pair * 2 * HD
        query = qkv[:, at : at + 2 * HD] * jnp.asarray(HD ** (-0.5), BF16)
        key = qkv[:, width + at : width + at + 2 * HD]
        value = qkv[:, 2 * width + at : 2 * width + at + 2 * HD]
        halves = []
        for half in range(2):
            mine = low if half == 0 else jnp.logical_not(low)
            scores = dot_nt(jnp.where(mine, query, nothing), key)
            top = jnp.max(scores, axis=-1, keepdims=True)
            weight = jnp.exp(scores - top)
            total = jnp.sum(weight, axis=-1, keepdims=True)
            prob = (weight * (1.0 / total)).astype(BF16)
            halves.append(dot_nn(prob, value))
            lse_all = jnp.where(lane == 2 * pair + half, top + jnp.log(total), lse_all)
        pieces.append(jnp.where(low, halves[0], halves[1]).astype(BF16))
    lse_ref[0] = lse_all
    attended = jnp.concatenate(pieces, axis=1)
    att_ref[0] = attended
    resid = inputs + dot_nn(attended, w_out_ref[...]) + vec_ref[2:3, :]
    resid_ref[0] = resid
    norm_second, _ = norm_parts(resid)
    second_ref[img] = (norm_second * vec_ref[3:4, :] + vec_ref[4:5, :]).astype(BF16)

    @pl.when(img == pl.num_programs(0) - 1)
    def _():
        n_img = second_ref.shape[0]
        place = lax.broadcasted_iota(jnp.int32, (capp, seq), 0).astype(F32)
        for e in range(len(out_refs) * exp_dev):
            total = jnp.zeros((capp, width), F32)
            for i in range(n_img):
                pick = jnp.where(place == slot_row_ref[i, e : e + 1, :], 1.0, 0.0)
                total = total + dot_nn(pick.astype(BF16), second_ref[i])
            out_refs[e // exp_dev][e % exp_dev] = total.astype(BF16)


def attention_call(tokens, w_qkv, w_out, vecs, slot_row, ep_size, exp_dev, capp):
    n_img, seq, width = tokens.shape
    chunk = jax.ShapeDtypeStruct((exp_dev, capp, width), BF16)
    image = lambda *tail: pl.BlockSpec((1,) + tail, lambda i: (i, 0, 0))
    return pl.pallas_call(
        functools.partial(attention_kernel, width // HD),
        grid=(n_img,),
        in_specs=[image(seq, width), whole(w_qkv.shape), whole(w_out.shape), whole(vecs.shape), whole(slot_row.shape)],
        out_specs=[image(seq, 3 * width), image(seq, width), image(seq, 128), image(seq, width)]
        + [whole(chunk.shape)] * ep_size,
        out_shape=[
            jax.ShapeDtypeStruct((n_img, seq, 3 * width), BF16),
            jax.ShapeDtypeStruct((n_img, seq, width), BF16),
            jax.ShapeDtypeStruct((n_img, seq, 128), F32),
            jax.ShapeDtypeStruct((n_img, seq, width), F32),
        ]
        + [chunk] * ep_size,
        scratch_shapes=[pltpu.VMEM((n_img, seq, width), BF16)],
        compiler_params=params("arbitrary"),
        cost_estimate=pl.CostEstimate(flops=6 * 10**9, bytes_accessed=10 * 2**20, transcendentals=10**6),
        name="attention_forward_and_dispatch",
    )(tokens, w_qkv, w_out, vecs, slot_row)


def expert_kernel(count, *refs):
    x_refs, g_refs = refs[:count], refs[count : 2 * count]
    w_in_ref, w_back_ref, b_in_ref, b_back_ref = refs[2 * count : 2 * count + 4]
    outs = refs[2 * count + 4 :]
    act_refs, gpre_refs, out_refs, gdis_refs = (outs[k * count : (k + 1) * count] for k in range(4))
    acc_out, acc_dis = outs[4 * count :]
    step = pl.program_id(1)
    w_in = w_in_ref[0]
    w_back = w_back_ref[0]
    for n in range(count):
        pre = dot_nn(x_refs[n][0], w_in) + b_in_ref[0]
        square = pre * pre
        bent = jnp.tanh(pre * (GELU_C + (GELU_C * 0.044715) * square))
        half = 0.5 + 0.5 * bent
        act = (pre * half).astype(BF16)
        slope = half + (pre * (0.5 - 0.5 * bent * bent)) * (GELU_C + (3 * GELU_C * 0.044715) * square)
        gpre = (dot_nt(g_refs[n][0], w_back) * slope).astype(BF16)
        act_refs[n][0] = act
        gpre_refs[n][0] = gpre
        part_dis = dot_nt(gpre, w_in)
        part_out = dot_nn(act, w_back)

        @pl.when(step == 0)
        def _():
            acc_dis[n] = part_dis
            acc_out[n] = part_out + b_back_ref[0]

        @pl.when(step > 0)
        def _():
            acc_dis[n] += part_dis
            acc_out[n] += part_out

        @pl.when(step == pl.num_programs(1) - 1)
        def _():
            gdis_refs[n][0] = acc_dis[n].astype(BF16)
            out_refs[n][0] = acc_out[n].astype(BF16)


def expert_call(xs, gs, w_in, w_back, b_in, b_back, tile):
    count = len(xs)
    exp_dev, capp, width = xs[0].shape
    hidden = w_in.shape[2]
    rows = pl.BlockSpec((1, capp, width), lambda e, f: (e, 0, 0))
    wide = pl.BlockSpec((1, capp, tile), lambda e, f: (e, 0, f))
    narrow = jax.ShapeDtypeStruct((exp_dev, capp, width), BF16)
    broad = jax.ShapeDtypeStruct((exp_dev, capp, hidden), BF16)
    res = pl.pallas_call(
        functools.partial(expert_kernel, count),
        grid=(exp_dev, hidden // tile),
        in_specs=[rows] * (2 * count)
        + [
            pl.BlockSpec((1, width, tile), lambda e, f: (e, 0, f)),
            pl.BlockSpec((1, tile, width), lambda e, f: (e, f, 0)),
            pl.BlockSpec((1, 1, tile), lambda e, f: (e, 0, f)),
            pl.BlockSpec((1, 1, width), lambda e, f: (e, 0, 0)),
        ],
        out_specs=[wide] * (2 * count) + [rows] * (2 * count),
        out_shape=[broad] * (2 * count) + [narrow] * (2 * count),
        scratch_shapes=[pltpu.VMEM((count, capp, width), F32)] * 2,
        compiler_params=params("arbitrary", "arbitrary"),
        cost_estimate=pl.CostEstimate(
            flops=8 * count * exp_dev * capp * width * hidden,
            bytes_accessed=4 * exp_dev * width * hidden + 4 * count * exp_dev * capp * hidden,
            transcendentals=count * exp_dev * capp * hidden,
        ),
        name="experts",
    )(*xs, *gs, w_in, w_back, b_in, b_back)
    return [res[k * count : (k + 1) * count] for k in range(4)]


def weight_kernel(count, left_first, sel_ref, *refs):
    a_refs, b_refs = refs[:count], refs[count : 2 * count]
    out_ref, bias_ref = refs[2 * count :]
    total = dot_tn(a_refs[0][0], b_refs[0][0])
    for n in range(1, count):
        total = total + dot_tn(a_refs[n][0], b_refs[n][0])
    out_ref[0] = total.astype(BF16)
    if left_first:
        @pl.when(pl.program_id(0) == 0)
        def _():
            bias = jnp.sum(b_refs[0][0].astype(F32), axis=0, keepdims=True)
            for n in range(1, count):
                bias = bias + jnp.sum(b_refs[n][0].astype(F32), axis=0, keepdims=True)
            bias_ref[0] = bias
    else:
        bias = jnp.sum(b_refs[0][0].astype(F32), axis=0, keepdims=True)
        for n in range(1, count):
            bias = bias + jnp.sum(b_refs[n][0].astype(F32), axis=0, keepdims=True)
        bias_ref[0] = bias


def weight_call(lefts, rights, which, rel, blocks, left_first):
    count = len(lefts)
    _, capp, m = lefts[0].shape
    n = rights[0].shape[2]
    if left_first:
        m = m // blocks
    else:
        n = n // blocks
    left_at = (lambda r, s: (s[0], 0, r ^ s[1])) if left_first else (lambda r, s: (s[0], 0, 0))
    right_at = (lambda r, s: (s[0], 0, 0)) if left_first else (lambda r, s: (s[0], 0, r ^ s[1]))
    bias_at = (lambda r, s: (0, 0, 0)) if left_first else (lambda r, s: (0, 0, r ^ s[1]))
    return pl.pallas_call(
        functools.partial(weight_kernel, count, left_first),
        grid_spec=pltpu.PrefetchScalarGridSpec(
            num_scalar_prefetch=1,
            grid=(blocks,),
            in_specs=[pl.BlockSpec((1, capp, m), left_at)] * count + [pl.BlockSpec((1, capp, n), right_at)] * count,
            out_specs=[pl.BlockSpec((1, m, n), lambda r, s: (r, 0, 0)), pl.BlockSpec((1, 1, n), bias_at)],
        ),
        out_shape=[
            jax.ShapeDtypeStruct((blocks, m, n), BF16),
            jax.ShapeDtypeStruct((1, 1, rights[0].shape[2]), F32),
        ],
        compiler_params=params("arbitrary"),
        cost_estimate=pl.CostEstimate(
            flops=2 * count * capp * blocks * m * n, bytes_accessed=2 * blocks * m * n, transcendentals=0
        ),
        name="expert_weight_gradient",
    )(which, *lefts, *rights)


def gather_rows(slot_col, value_col, chunk_refs, capp):
    seq = slot_col.shape[0]
    exp_dev = chunk_refs[0].shape[0]
    place = lax.broadcasted_iota(jnp.int32, (seq, capp), 1).astype(F32)
    total = None
    for e in range(len(chunk_refs) * exp_dev):
        value = 1.0 if value_col is None else value_col[:, e : e + 1]
        pick = jnp.where(place == slot_col[:, e : e + 1], value, 0.0).astype(BF16)
        part = dot_nn(pick, chunk_refs[e // exp_dev][e % exp_dev])
        total = part if total is None else total + part
    return total


def backward_kernel(
    heads, ep_size, tok_ref, cot_ref, resid_ref, qkv_ref, att_ref, lse_ref, slot_col_ref, w_qkv_ref, w_out_ref, vec_ref, *rest
):
    chunk_refs = rest[:ep_size]
    gtok_ref, gw_qkv_ref, gw_out_ref, gvec_ref, gqkv_ref = rest[ep_size:]
    img = pl.program_id(0)
    seq, width = tok_ref.shape[1:]
    capp = chunk_refs[0].shape[1]
    grad_second = gather_rows(slot_col_ref[0], None, chunk_refs, capp)
    norm_second, inv_second = norm_parts(resid_ref[0])
    grad_resid = cot_ref[0].astype(F32) + norm_back(grad_second, norm_second, inv_second, vec_ref[3:4, :])
    grad_branch = grad_resid.astype(BF16)
    grad_att = dot_nt(grad_branch, w_out_ref[...]).astype(BF16)
    gw_out = dot_tn(att_ref[0], grad_branch)
    low = lax.broadcasted_iota(jnp.int32, (seq, 2 * HD), 1) < HD
    nothing = jnp.zeros((seq, 2 * HD), BF16)
    scale = jnp.asarray(HD ** (-0.5), BF16)
    for pair in range(heads // 2):
        at = pair * 2 * HD
        query = qkv_ref[0, :, at : at + 2 * HD] * scale
        key = qkv_ref[0, :, width + at : width + at + 2 * HD]
        value = qkv_ref[0, :, 2 * width + at : 2 * width + at + 2 * HD]
        gatt = grad_att[:, at : at + 2 * HD]
        grad_q = grad_k = grad_v = None
        for half in range(2):
            mine = low if half == 0 else jnp.logical_not(low)
            head = 2 * pair + half
            query_h = jnp.where(mine, query, nothing)
            gatt_h = jnp.where(mine, gatt, nothing)
            key_h = jnp.where(mine, key, nothing) * scale
            prob = jnp.exp(dot_nt(query_h, key) - lse_ref[0, :, head : head + 1])
            grad_prob = dot_nt(gatt_h, value)
            mean = jnp.sum(grad_prob * prob, axis=-1, keepdims=True)
            grad_scores = (prob * (grad_prob - mean)).astype(BF16)
            part_v = dot_tn(prob.astype(BF16), gatt_h)
            part_q = dot_nn(grad_scores, key_h)
            part_k = dot_tn(grad_scores, query_h)
            grad_q = part_q if grad_q is None else grad_q + part_q
            grad_k = part_k if grad_k is None else grad_k + part_k
            grad_v = part_v if grad_v is None else grad_v + part_v
        gqkv_ref[:, at : at + 2 * HD] = grad_q.astype(BF16)
        gqkv_ref[:, width + at : width + at + 2 * HD] = grad_k.astype(BF16)
        gqkv_ref[:, 2 * width + at : 2 * width + at + 2 * HD] = grad_v.astype(BF16)
    grad_qkv = gqkv_ref[...]
    norm_first, inv_first = norm_parts(tok_ref[0].astype(F32))
    first = (norm_first * vec_ref[0:1, :] + vec_ref[1:2, :]).astype(BF16)
    gw_qkv = dot_tn(first, grad_qkv)
    grad_first = dot_nt(grad_qkv, w_qkv_ref[...])
    gtok_ref[0] = (grad_resid + norm_back(grad_first, norm_first, inv_first, vec_ref[0:1, :])).astype(BF16)
    sums = [
        grad_first * norm_first,
        grad_first,
        grad_branch.astype(F32),
        grad_second * norm_second,
        grad_second,
    ]
    gvec = jnp.concatenate([jnp.sum(v, axis=0, keepdims=True) for v in sums] + [jnp.zeros((3, width), F32)], axis=0)

    @pl.when(img == 0)
    def _():
        gw_out_ref[...] = gw_out
        gw_qkv_ref[...] = gw_qkv
        gvec_ref[...] = gvec

    @pl.when(img > 0)
    def _():
        gw_out_ref[...] += gw_out
        gw_qkv_ref[...] += gw_qkv
        gvec_ref[...] += gvec


def backward_call(tokens, cotangent, resid, qkv, attended, lse, slot_col, w_qkv, w_out, vecs, chunks):
    n_img, seq, width = tokens.shape
    image = lambda arr: pl.BlockSpec((1,) + arr.shape[1:], lambda i: (i, 0, 0))
    return pl.pallas_call(
        functools.partial(backward_kernel, width // HD, len(chunks)),
        grid=(n_img,),
        in_specs=[image(a) for a in (tokens, cotangent, resid, qkv, attended, lse, slot_col)]
        + [whole(a.shape) for a in (w_qkv, w_out, vecs, *chunks)],
        out_specs=[image(tokens), whole(w_qkv.shape), whole(w_out.shape), whole((8, width))],
        out_shape=[
            jax.ShapeDtypeStruct(tokens.shape, BF16),
            jax.ShapeDtypeStruct(w_qkv.shape, F32),
            jax.ShapeDtypeStruct(w_out.shape, F32),
            jax.ShapeDtypeStruct((8, width), F32),
        ],
        scratch_shapes=[pltpu.VMEM((seq, 3 * width), BF16)],
        compiler_params=params("arbitrary"),
        cost_estimate=pl.CostEstimate(flops=10 * 10**9, bytes_accessed=16 * 2**20, transcendentals=10**6),
        name="attention_backward",
    )(tokens, cotangent, resid, qkv, attended, lse, slot_col, w_qkv, w_out, vecs, *chunks)


def combine_kernel(ep_size, resid_ref, slot_col_ref, gate_col_ref, *rest):
    chunk_refs, out_ref = rest[:ep_size], rest[ep_size]
    mixed = gather_rows(slot_col_ref[0], gate_col_ref[0], chunk_refs, chunk_refs[0].shape[1])
    out_ref[0] = (resid_ref[0] + mixed).astype(BF16)


def combine_call(resid, slot_col, gate_col, chunks):
    n_img, seq, width = resid.shape
    image = lambda arr: pl.BlockSpec((1,) + arr.shape[1:], lambda i: (i, 0, 0))
    return pl.pallas_call(
        functools.partial(combine_kernel, len(chunks)),
        grid=(n_img,),
        in_specs=[image(a) for a in (resid, slot_col, gate_col)] + [whole(c.shape) for c in chunks],
        out_specs=image(resid),
        out_shape=jax.ShapeDtypeStruct(resid.shape, BF16),
        compiler_params=params("arbitrary"),
        cost_estimate=pl.CostEstimate(flops=2 * 10**9, bytes_accessed=5 * 2**20, transcendentals=0),
        name="combine_output",
    )(resid, slot_col, gate_col, *chunks)


def swap(array, axis, size, distance):
    return lax.ppermute(array, axis, [(i, i ^ distance) for i in range(size)])


def local(
    tokens,
    routes,
    gates,
    ln1_gain,
    ln1_bias,
    w_qkv,
    w_out,
    out_bias,
    ln2_gain,
    ln2_bias,
    w_in,
    in_bias,
    w_back,
    back_bias,
    cotangent,
):
    images, seq_len, width = tokens.shape
    ep_size = lax.axis_size("ep")
    exp_dev = w_in.shape[0]
    experts = exp_dev * ep_size
    capacity = (images * seq_len * 10 + 4 * experts - 1) // (4 * experts)
    capp = -(-capacity // 8) * 8
    me = lax.axis_index("ep").astype(jnp.int32).reshape(1)
    vecs = jnp.stack([ln1_gain, ln1_bias, out_bias, ln2_gain, ln2_bias] + [jnp.zeros_like(ln1_gain)] * 3)

    def exchange(chunks):
        return [chunks[0]] + [swap(chunks[d], "ep", ep_size, d) for d in range(1, ep_size)]

    slot_row, slot_col, gate_col, *g_send = route_call(me, routes, gates, cotangent, ep_size, exp_dev, capp)
    g_all = exchange(g_send)
    qkv, attended, lse, resid, *x_send = attention_call(tokens, w_qkv, w_out, vecs, slot_row, ep_size, exp_dev, capp)
    x_all = exchange(x_send)
    b_in, b_back = in_bias[:, None, :], back_bias[:, None, :]
    acts, gpres, outs, gdis = [], [], [], []
    for d in range(ep_size):
        a, p, o, g = expert_call(x_all[d : d + 1], g_all[d : d + 1], w_in, w_back, b_in, b_back, 512)
        acts += a
        gpres += p
        outs += o
        gdis += g
    gdis_back = exchange(gdis)
    outs_back = exchange(outs)
    gw_back, gb_back, gw_in, gb_in = [], [], [], []
    for e in range(exp_dev):
        which = jnp.array([e, 0], jnp.int32)
        w, b = weight_call(acts, g_all, which, None, 4, True)
        gw_back.append(w.reshape(w_back.shape[1:]))
        gb_back.append(b[0, 0])
        w, b = weight_call(x_all, gpres, which, None, 4, False)
        gw_in.append(w.transpose(1, 0, 2).reshape(w_in.shape[1:]))
        gb_in.append(b[0, 0])
    gw_back, gb_back, gw_in, gb_in = (jnp.stack(v) for v in (gw_back, gb_back, gw_in, gb_in))
    grad_tokens, gw_qkv, gw_out, gvec = backward_call(
        tokens, cotangent, resid, qkv, attended, lse, slot_col, w_qkv, w_out, vecs, gdis_back
    )
    output = combine_call(resid, slot_col, gate_col, outs_back)

    def over_grp(v):
        return lax.psum(v.astype(BF16), "grp").astype(F32)

    def over_all(v):
        return over_grp(lax.psum_scatter(v.astype(BF16), "ep", scatter_dimension=0, tiled=True))

    return (
        output,
        grad_tokens,
        over_all(gvec[0]),
        over_all(gvec[1]),
        over_all(gw_qkv),
        over_all(gw_out),
        over_all(gvec[2]),
        over_all(gvec[3]),
        over_all(gvec[4]),
        over_grp(gw_in),
        over_grp(gb_in),
        over_grp(gw_back),
        over_grp(gb_back),
    )


def solution(mesh):
    rows = P(("grp", "ep"), None, None)
    return jax.shard_map(
        local,
        mesh=mesh,
        in_specs=(rows, rows, rows)
        + (P(),) * 7
        + (P("ep", None, None), P("ep", None), P("ep", None, None), P("ep", None), rows),
        out_specs=(rows, rows)
        + (P("ep"), P("ep"), P("ep", None), P("ep", None), P("ep"), P("ep"), P("ep"))
        + (P("ep", None, None), P("ep", None), P("ep", None, None), P("ep", None)),
        check_vma=False,
    )
```

time: 605 us -> 427 us (0.71)
  Pallas kernels: 0 us -> 128 us
  local copies, waits for them, and re-layouts: 148 us -> 33.5 us
  matrix products: 110 us -> 0 us
  other arithmetic: 87.6 us -> 26 us
  waiting for transfers between devices: 185 us -> 160 us
  blocking collectives: 33.9 us -> 40.9 us
    pallas_call x0 -> x12, Pallas kernels: none -> 128 us  [the longest x4 48.3 us: expert_call(): pl.pallas_call(functools.partial(expert_kernel, count), grid=(exp_dev, hi...]
    dot_general x18 -> x0, matrix products: 110 us -> none  [the longest x1 20.5 us: local(): jnp.einsum('secd,efd->secf', grad_inbox_out, w_back, preferred_element_ty...]
    all_to_all x4 -> x0, waiting for transfers between devices: 93.7 us -> none  [the longest x1 33.2 us: local(): lax.all_to_all(grad_inbox.reshape(ep_size, exp_dev * capacity, model_widt...]
    ppermute x0 -> x12, waiting for transfers between devices: none -> 90.1 us  [swap(): return lax.ppermute(array, axis, [(i, i ^ distance) for i in range(size)])]
    reshape x15 -> x0, local copies, waits for them, and re-layouts: 46.6 us -> none  [the longest x1 7.17 us: local(): qkv = qkv.reshape(images, seq_len, 3, head_count, HD)]
    convert_element_type x13 -> x0, local copies, waits for them, and re-layouts: 36.9 us -> none  [the longest x2 11.5 us: local(): grad_qkv = jnp.stack([grad_query, grad_key, grad_value], axis=2).astype(j...]
    reduce_sum x12 -> x0, other arithmetic: 36.8 us -> none  [the longest x1 18.1 us: local(): mixed = jnp.sum(picked.astype(jnp.float32) * gate_rows[:, :, None], axis=1)]
    psum x1, waiting for transfers between devices: 76.4 us -> 41.7 us  [over_grp(): return lax.psum(v.astype(BF16), 'grp').astype(F32)]
  transfers between devices with their start and end apart: 7 -> 15, of which waited for: 6 -> 8; matrix products, arithmetic and copies ran while one was open for 27% -> 6% of each run, Pallas kernels for 0% -> 20%
where the time goes in v1:
time: 427 us; the launch traced here: 425 us
  waiting for transfers between devices  160 us (37%)
  Pallas kernels  128 us (30%)
  blocking collectives  40.9 us (10%)
  local copies, waits for them, and re-layouts  33.5 us (8%)
  other arithmetic  26 us (6%)
  starting transfers between devices  21 us (5%)
  between operations  14.7 us (3%)
    ppermute x12, waiting for transfers between devices, swap(): return lax.ppermute(array, axis, [(i, i ^ distance) for i in range(size)])  90.1 us
    pallas_call x4, Pallas kernels, expert_call(): pl.pallas_call(functools.partial(expert_kernel, count), grid=(exp_dev, hi...  48.3 us
    psum x1, waiting for transfers between devices, over_grp(): return lax.psum(v.astype(BF16), 'grp').astype(F32)  41.7 us
    pallas_call x4, Pallas kernels, weight_call(): pl.pallas_call(functools.partial(weight_kernel, count, left_first), grid_...  28.8 us
    reduce_scatter x2, waiting for transfers between devices, over_all(): lax.psum_scatter(v.astype(BF16), 'ep', scatter_dimension=0, tiled=True)  28.6 us
    pallas_call x1, Pallas kernels, backward_call(): pl.pallas_call(functools.partial(backward_kernel, width // HD, len(chunks...  25.7 us
    unnamed x79, local copies, waits for them, and re-layouts  24.1 us
    psum x1, blocking collectives, over_grp(): return lax.psum(v.astype(BF16), 'grp').astype(F32)  22.9 us
  transfers between devices with their start and end apart: 15, of which 8 were waited for; matrix products, arithmetic and copies ran while one was open for 6% of the time, Pallas kernels for 20%

profile of v1, /device:TPU:0, one launch (start us, length us, event | category | flops | bytes accessed | tf_op | source)
XLA Modules:
  0.0 424.9 jit_solution(7944489804770098544)
XLA Ops:
  7.2 2.3 copy.52.tok_ref
  9.5 1.6 copy.49.routes_ref
  11.1 1.6 copy.50.gates_ref
  12.8 1.1 copy.51.cot_ref
  13.9 5.4 %route_and_dispatch_cotangent.1 = (f32[4,8,197]{2,1,0:T(8,128)}, f32[4,197,8]{2,1,0:T(8,128)}, f32[4,197,8]{2,1,0:T(8,128)}, bf16[2,248,512]{2,1,0:T(8,128)(2,1)...) custom-call(s32[1]{0:T(128)} %bitcast.5.me_ref, ...), custom_call_target="tpu_custom_call" | custom-call | flops 1600913408 | bytes 3227648 | tf_op jit(solution)/shard_map/route_and_dispatch_cotangent/pallas_call | solution.py:99
  20.0 14.2 %attention_forward_and_dispatch.1 = (bf16[4,197,1536]{2,1,0:T(8,128)(2,1)}, bf16[4,197,512]{2,1,0:T(8,128)(2,1)}, f32[4,197,128]{2,1,0:T(8,128)}, f32[4,197,512]...) custom-call(bf16[4,197,512]{2,1,0:T(8,128)(2,1)} %copy.52.tok_ref, ...), custom_call_target="tpu_custom_call" | custom-call | flops 6000000000 | bytes 10485760 | tf_op jit(solution)/shard_map/attention_forward_and_dispatch/pallas_call | solution.py:175
  34.2 3.1 collective-permute-start
  37.3 2.9 collective-permute-start.3
  40.3 3.9 collective-permute-start.6
  45.4 25.4 %collective-permute-done.refs_0_.refs_1_ = bf16[2,248,512]{2,1,0:T(8,128)(2,1)S(1)} collective-permute-done((bf16[2,248,512]{2,1,0:T(8,128)(2,1)}, bf16[2,248,512]{2,1,0:T(8,128)(2,1)S(1)}, u32[]{:S(2)}, u32[]{:S(2)}) %collective-permute-start) | collective-permute-done | bytes 507936 | tf_op jit(solution)/shard_map/ppermute | solution.py:445
  70.8 2.4 collective-permute-start.7
  73.2 7.7 %collective-permute-done.1.refs_1_.refs_5_ = bf16[2,248,512]{2,1,0:T(8,128)(2,1)S(1)} collective-permute-done((bf16[2,248,512]{2,1,0:T(8,128)(2,1)}, bf16[2,248,512]{2,1,0:T(8,128)(2,1)S(1)}, u32[]{:S(2)}, u32[]{:S(2)}) %collective-permute-start.1) | collective-permute-done | bytes 507936 | tf_op jit(solution)/shard_map/ppermute | solution.py:445
  81.6 12.0 %experts.5 = (bf16[2,248,2048]{2,1,0:T(8,128)(2,1)}, bf16[2,248,2048]{2,1,0:T(8,128)(2,1)}, bf16[2,248,512]{2,1,0:T(8,128)(2,1)}, bf16[2,248,512]{2,1,0:T(8,128)(2,1)}) custom-call(bf16[2,248,512]{2,1,0:T(8,128)(2,1)} %copy-done.4, bf16[2,248,512]{2,1,0:T(8,128)(2,1)} %copy-done.2, bf16[2,512,2048]{2,1,0:T(8,128)(2,1)} %refs_2_.7, ...), custom_call_target="tpu_custom_call" | custom-call | flops 4160749568 | bytes 12451840 | tf_op jit(solution)/shard_map/experts/pallas_call | solution.py:241
  93.8 13.7 %collective-permute-done.4.refs_1_.refs_6_ = bf16[2,248,512]{2,1,0:T(8,128)(2,1)S(1)} collective-permute-done((bf16[2,248,512]{2,1,0:T(8,128)(2,1)}, bf16[2,248,512]{2,1,0:T(8,128)(2,1)S(1)}, u32[]{:S(2)}, u32[]{:S(2)}) %collective-permute-start.4) | collective-permute-done | bytes 507936 | tf_op jit(solution)/shard_map/ppermute | solution.py:445
  107.4 0.8 copy-done.3
  108.3 12.1 %experts.6 = (bf16[2,248,2048]{2,1,0:T(8,128)(2,1)}, bf16[2,248,2048]{2,1,0:T(8,128)(2,1)}, bf16[2,248,512]{2,1,0:T(8,128)(2,1)}, bf16[2,248,512]{2,1,0:T(8,128)(2,1)}) custom-call(bf16[2,248,512]{2,1,0:T(8,128)(2,1)} %copy-done.5, bf16[2,248,512]{2,1,0:T(8,128)(2,1)} %copy-done.3, bf16[2,512,2048]{2,1,0:T(8,128)(2,1)} %refs_2_.7, ...), custom_call_target="tpu_custom_call" | custom-call | flops 4160749568 | bytes 12451840 | tf_op jit(solution)/shard_map/experts/pallas_call | solution.py:241
  120.4 0.8 copy-done.7
  121.2 0.8 copy-done.6
  122.0 12.1 %experts.7 = (bf16[2,248,2048]{2,1,0:T(8,128)(2,1)}, bf16[2,248,2048]{2,1,0:T(8,128)(2,1)}, bf16[2,248,512]{2,1,0:T(8,128)(2,1)}, bf16[2,248,512]{2,1,0:T(8,128)(2,1)}) custom-call(bf16[2,248,512]{2,1,0:T(8,128)(2,1)} %copy-done.7, bf16[2,248,512]{2,1,0:T(8,128)(2,1)} %copy-done.6, bf16[2,512,2048]{2,1,0:T(8,128)(2,1)} %refs_2_.7, ...), custom_call_target="tpu_custom_call" | custom-call | flops 4160749568 | bytes 12451840 | tf_op jit(solution)/shard_map/experts/pallas_call | solution.py:241
  134.2 4.0 collective-permute-start.11
  138.1 12.0 %experts.4 = (bf16[2,248,2048]{2,1,0:T(8,128)(2,1)}, bf16[2,248,2048]{2,1,0:T(8,128)(2,1)}, bf16[2,248,512]{2,1,0:T(8,128)(2,1)}, bf16[2,248,512]{2,1,0:T(8,128)(2,1)}) custom-call(bf16[2,248,512]{2,1,0:T(8,128)(2,1)} %get-tuple-element.60.refs_0_, bf16[2,248,512]{2,1,0:T(8,128)(2,1)} %get-tuple-element.61.refs_1_.refs_4_, bf16[2,512,2048]{2,1,0:T(8,128)(2,1)} %refs_2_.7, ...), custom_call_target="tpu_custom_call" | custom-call | flops 4160749568 | bytes 12451840 | tf_op jit(solution)/shard_map/experts/pallas_call | solution.py:241
  150.2 10.2 %collective-permute-done.10.rest_2_ = bf16[2,248,512]{2,1,0:T(8,128)(2,1)S(1)} collective-permute-done((bf16[2,248,512]{2,1,0:T(8,128)(2,1)}, bf16[2,248,512]{2,1,0:T(8,128)(2,1)S(1)}, u32[]{:S(2)}, u32[]{:S(2)}) %collective-permute-start.10) | collective-permute-done | bytes 507936 | tf_op jit(solution)/shard_map/ppermute | solution.py:445
  161.4 25.7 %attention_backward.1 = (bf16[4,197,512]{2,1,0:T(8,128)(2,1)}, f32[512,1536]{1,0:T(8,128)}, f32[512,512]{1,0:T(8,128)}, f32[8,512]{1,0:T(8,128)}) custom-call(bf16[4,197,512]{2,1,0:T(8,128)(2,1)} %copy.52.tok_ref, bf16[4,197,512]{2,1,0:T(8,128)(2,1)} %copy.51.cot_ref, f32[4,197,512]{2,1,0:T(8,128)} %get-tuple-element.57.resid_ref, ...), custom_call_target="tpu_custom_call" | custom-call | flops 10000000000 | bytes 16777216 | tf_op jit(solution)/shard_map/attention_backward/pallas_call | solution.py:404
  187.1 2.1 convert_element_type.67
  189.3 3.2 convert_element_type.65
  192.6 7.2 %expert_weight_gradient.5 = (bf16[4,512,512]{2,1,0:T(8,128)(2,1)}, f32[1,1,2048]{2,1,0:T(1,128)}) custom-call(s32[2]{0:T(128)} %constant.12.clone.sel_ref, bf16[2,248,512]{2,1,0:T(8,128)(2,1)} %get-tuple-element.60.refs_0_, bf16[2,248,512]{2,1,0:T(8,128)(2,1)} %copy-done.4, bf16[2,248,512]{2,1,0:T(8,128)(2,1)} %copy-done.5, bf16[2,248,512]{2,1,0:T(8,128)(2,1)} %copy-done.7, ...), custom_call_target="tpu_custom_call" | custom-call | flops 2080374784 | bytes 2097152 | tf_op jit(solution)/shard_map/expert_weight_gradient/pallas_call | solution.py:297
  199.8 2.8 copy.56
  203.1 7.2 %expert_weight_gradient.4 = (bf16[4,512,512]{2,1,0:T(8,128)(2,1)}, f32[1,1,2048]{2,1,0:T(1,128)}) custom-call(s32[2]{0:T(128)} %call_exported.0.sel_ref, bf16[2,248,512]{2,1,0:T(8,128)(2,1)} %get-tuple-element.60.refs_0_, bf16[2,248,512]{2,1,0:T(8,128)(2,1)} %copy-done.4, bf16[2,248,512]{2,1,0:T(8,128)(2,1)} %copy-done.5, bf16[2,248,512]{2,1,0:T(8,128)(2,1)} %copy-done.7, ...), custom_call_target="tpu_custom_call" | custom-call | flops 2080374784 | bytes 2097152 | tf_op jit(solution)/shard_map/expert_weight_gradient/pallas_call | solution.py:297
  210.2 4.1 copy.55
  214.4 7.2 %expert_weight_gradient.7 = (bf16[4,512,512]{2,1,0:T(8,128)(2,1)}, f32[1,1,512]{2,1,0:T(1,128)}) custom-call(s32[2]{0:T(128)} %constant.12.clone.sel_ref, bf16[2,248,2048]{2,1,0:T(8,128)(2,1)} %get-tuple-element.91.refs_0_, bf16[2,248,2048]{2,1,0:T(8,128)(2,1)} %get-tuple-element.92.refs_1_, bf16[2,248,2048]{2,1,0:T(8,128)(2,1)} %get-tuple-element.93.refs_2_, ...), custom_call_target="tpu_custom_call" | custom-call | flops 2080374784 | bytes 2097152 | tf_op jit(solution)/shard_map/expert_weight_gradient/pallas_call | solution.py:297
  221.6 7.2 %expert_weight_gradient.6 = (bf16[4,512,512]{2,1,0:T(8,128)(2,1)}, f32[1,1,512]{2,1,0:T(1,128)}) custom-call(s32[2]{0:T(128)} %call_exported.0.sel_ref, bf16[2,248,2048]{2,1,0:T(8,128)(2,1)} %get-tuple-element.91.refs_0_, bf16[2,248,2048]{2,1,0:T(8,128)(2,1)} %get-tuple-element.92.refs_1_, bf16[2,248,2048]{2,1,0:T(8,128)(2,1)} %get-tuple-element.93.refs_2_, ...), custom_call_target="tpu_custom_call" | custom-call | flops 2080374784 | bytes 2097152 | tf_op jit(solution)/shard_map/expert_weight_gradient/pallas_call | solution.py:297
  228.8 4.1 pad_maximum_fusion
  233.0 2.4 pad_maximum_fusion.1
  235.3 28.6 %reduce-scatter.3.cloned.1.call-done = bf16[128,1536]{1,0:T(8,128)(2,1)} async-done(((bf16[512,1536]{1,0:T(8,128)(2,1)}), bf16[128,1536]{1,0:T(8,128)(2,1)}) %reduce-scatter.3.cloned.1.call-update) | async-done | bytes 393232 | tf_op jit(solution)/shard_map/reduce_scatter | solution.py:510
  266.3 1.6 collective-permute-start.5
  267.9 2.4 collective-permute-start.8
  270.4 18.8 %collective-permute-done.2.rest_1_ = bf16[2,248,512]{2,1,0:T(8,128)(2,1)S(1)} collective-permute-done((bf16[2,248,512]{2,1,0:T(8,128)(2,1)S(1)}, bf16[2,248,512]{2,1,0:T(8,128)(2,1)S(1)}, u32[]{:S(2)}, u32[]{:S(2)}) %collective-permute-start.2) | collective-permute-done | bytes 507936 | tf_op jit(solution)/shard_map/ppermute | solution.py:445
  289.2 14.3 %collective-permute-done.5.rest_2_ = bf16[2,248,512]{2,1,0:T(8,128)(2,1)S(1)} collective-permute-done((bf16[2,248,512]{2,1,0:T(8,128)(2,1)S(1)}, bf16[2,248,512]{2,1,0:T(8,128)(2,1)S(1)}, u32[]{:S(2)}, u32[]{:S(2)}) %collective-permute-start.5) | collective-permute-done | bytes 507936 | tf_op jit(solution)/shard_map/ppermute | solution.py:445
  304.5 6.0 %combine_output.1 = bf16[4,197,512]{2,1,0:T(8,128)(2,1)} custom-call(f32[4,197,512]{2,1,0:T(8,128)} %get-tuple-element.57.resid_ref, f32[4,197,8]{2,1,0:T(8,128)} %get-tuple-element.58.slot_col_ref, f32[4,197,8]{2,1,0:T(8,128)} %get-tuple-element.59.gate_col_ref, bf16[2,248,512]{2,1,0:T(8,128)(2,1)} %get-tuple-element.62.rest_0_, ...), custom_call_target="tpu_custom_call" | custom-call | flops 2000000000 | bytes 5242880 | tf_op jit(solution)/shard_map/combine_output/pallas_call | solution.py:432
  310.4 2.6 copy.57
  313.0 1.3 copy.58
  314.4 18.0 %all-reduce.7 = (bf16[512]{0:T(512)(128)(2,1)S(1)}, bf16[512]{0:T(512)(128)(2,1)S(1)}, bf16[512]{0:T(512)(128)(2,1)S(1)}, bf16[512]{0:T(512)(128)(2,1)S(1)}, bf16[512]{0:T(512)(128)(2,1)S(1)}) all-reduce(bf16[512]{0:T(512)(128)(2,1)S(1)} %get-tuple-element.142, ...), channel_id=2, replica_groups=mesh['grp'=8,'ep'=4] {'ep'}, use_global_device_ids=true, to_apply=%region_0.0.clone | all-reduce | flops 2560 | bytes 10240
  332.8 22.9 %all-reduce.5 = (bf16[128]{0:T(256)(128)(2,1)S(1)}, bf16[128]{0:T(256)(128)(2,1)S(1)}, bf16[128]{0:T(256)(128)(2,1)S(1)}, bf16[128]{0:T(256)(128)(2,1)S(1)}, bf1...) all-reduce(bf16[128]{0:T(256)(128)(2,1)S(1)} %dynamic-slice.1, ...), channel_id=1, replica_groups=mesh['grp'=8,'ep'=4] {'grp'}, use_global_device_ids=true, to_apply=%region_1.0 | all-reduce | flops 5760 | bytes 23040 | tf_op jit(solution)/shard_map/psum | solution.py:507
  359.4 41.7 %all-reduce.10.cloned.1.call-done = (bf16[2,512,2048]{1,2,0:T(8,128)(2,1)}, bf16[128,1536]{1,0:T(8,128)(2,1)}, bf16[128,512]{1,0:T(8,128)(2,1)}, bf16[2,2048,512]{2,1,0:T(8,128)(2,1)}) async-done(((bf16[2,512,2048]{1,2,0:T(8,128)(2,1)}, bf16[128,1536]{1,0:T(8,128)(2,1)}, bf16[128,512]{1,0:T(8,128)(2,1)}, bf16[2,2048,512]{2,1,0:T(8,128)(2,1)}), (bf16[2,512,2048]{1,2,0:T(8,128)(2,1)}, ...) | async-done | bytes 8912912 | tf_op jit(solution)/shard_map/psum | solution.py:507
  401.1 2.0 convert_element_type.66
  403.1 1.6 convert_element_type.68
  404.7 6.8 %copy.59 = f32[2,512,2048]{2,1,0:T(8,128)} copy(bf16[2,512,2048]{1,2,0:T(8,128)(2,1)} %get-tuple-element.150) | data formatting | bytes 12582912
  411.6 6.8 %convert_element_type.77 = f32[2,2048,512]{2,1,0:T(8,128)} convert(bf16[2,2048,512]{2,1,0:T(8,128)(2,1)} %get-tuple-element.153) | non-fusion elementwise | flops 2097152 | bytes 12582912 | tf_op jit(solution)/shard_map/convert_element_type | solution.py:507
  (106 shorter events, 11.5 us)
Async XLA Ops:
  7.2 5.6 %copy-start.9 = (bf16[4,197,512]{2,0,1:T(4,128)(2,1)S(1)}, bf16[4,197,512]{2,0,1:T(4,128)(2,1)}, u32[]{:S(2)}) copy-start(bf16[4,197,512]{2,0,1:T(4,128)(2,1)} %param.31) | copy-start | bytes 2420740
  7.2 228.2 %reduce-scatter.5.cloned.1.call-start = ((), (), s32[]{:S(2)}) async-start(), calls=%async_computation.3 | async-start | bytes 655360 | tf_op jit(solution)/shard_map/reduce_scatter | solution.py:510
  13.8 5.4 %copy-start.15 = (f32[512]{0:T(512)S(1)}, f32[512]{0:T(512)}, u32[]{:S(2)}) copy-start(f32[512]{0:T(512)} %param.20) | copy-start | bytes 6148
  13.8 5.4 %copy-start.16 = (f32[512]{0:T(512)S(1)}, f32[512]{0:T(512)}, u32[]{:S(2)}) copy-start(f32[512]{0:T(512)} %param.21) | copy-start | bytes 6148
  13.9 5.4 %copy-start.17 = (f32[512]{0:T(512)S(1)}, f32[512]{0:T(512)}, u32[]{:S(2)}) copy-start(f32[512]{0:T(512)} %param.24) | copy-start | bytes 6148
  13.9 5.5 %copy-start.18 = (f32[512]{0:T(512)S(1)}, f32[512]{0:T(512)}, u32[]{:S(2)}) copy-start(f32[512]{0:T(512)} %param.25) | copy-start | bytes 6148
  13.9 5.5 %copy-start.19 = (f32[512]{0:T(512)S(1)}, f32[512]{0:T(512)}, u32[]{:S(2)}) copy-start(f32[512]{0:T(512)} %param.26) | copy-start | bytes 6148
  20.0 24.3 %copy-start.11 = (f32[2,2048]{1,0:T(2,128)S(1)}, f32[2,2048]{1,0:T(2,128)}, u32[]{:S(2)}) copy-start(f32[2,2048]{1,0:T(2,128)} %param.28) | copy-start | bytes 49156
  20.0 24.9 %copy-start.14 = (f32[2,512]{1,0:T(2,128)S(1)}, f32[2,512]{1,0:T(2,128)}, u32[]{:S(2)}) copy-start(f32[2,512]{1,0:T(2,128)} %param.30) | copy-start | bytes 12292
  20.0 50.8 %copy-start.25 = (bf16[2,248,512]{2,1,0:T(8,128)(2,1)S(1)}, bf16[2,248,512]{2,1,0:T(8,128)(2,1)}, u32[]{:S(2)}) copy-start(bf16[2,248,512]{2,1,0:T(8,128)(2,1)} %get-tuple-element.70) | copy-start | bytes 1523716
  34.2 36.6 %collective-permute-start = (bf16[2,248,512]{2,1,0:T(8,128)(2,1)}, bf16[2,248,512]{2,1,0:T(8,128)(2,1)S(1)}, u32[]{:S(2)}, u32[]{:S(2)}) collective-permute-start(bf16[2,248,512]{2,1,0:T(8,128)(2,1)} %get-tuple-element.63), channel_id=1, source_target_pairs={{0,1},{1,0},{2,3},{3,2},{4,5},{5,4},{6,7},{7,6},{8,9},{9,8},{10,11... | collective-permute-start | bytes 1523720 | tf_op jit(solution)/shard_map/ppermute | solution.py:445
  37.3 43.6 %collective-permute-start.1 = (bf16[2,248,512]{2,1,0:T(8,128)(2,1)}, bf16[2,248,512]{2,1,0:T(8,128)(2,1)S(1)}, u32[]{:S(2)}, u32[]{:S(2)}) collective-permute-start(bf16[2,248,512]{2,1,0:T(8,128)(2,1)} %get-tuple-element.64), channel_id=1, source_target_pairs={{0,1},{1,0},{2,3},{3,2},{4,5},{5,4},{6,7},{7,6},{8,9},{9,8},{10,11... | collective-permute-start | bytes 1523720 | tf_op jit(solution)/shard_map/ppermute | solution.py:445
  37.3 56.4 %collective-permute-start.3 = (bf16[2,248,512]{2,1,0:T(8,128)(2,1)}, bf16[2,248,512]{2,1,0:T(8,128)(2,1)S(1)}, u32[]{:S(2)}, u32[]{:S(2)}) collective-permute-start(bf16[2,248,512]{2,1,0:T(8,128)(2,1)} %get-tuple-element.66), channel_id=1, source_target_pairs={{0,2},{1,3},{2,0},{3,1},{4,6},{5,7},{6,4},{7,5},{8,10},{9,11},{10,... | collective-permute-start | bytes 1523720 | tf_op jit(solution)/shard_map/ppermute | solution.py:445
  40.3 67.2 %collective-permute-start.4 = (bf16[2,248,512]{2,1,0:T(8,128)(2,1)}, bf16[2,248,512]{2,1,0:T(8,128)(2,1)S(1)}, u32[]{:S(2)}, u32[]{:S(2)}) collective-permute-start(bf16[2,248,512]{2,1,0:T(8,128)(2,1)} %get-tuple-element.67), channel_id=1, source_target_pairs={{0,2},{1,3},{2,0},{3,1},{4,6},{5,7},{6,4},{7,5},{8,10},{9,11},{10,... | collective-permute-start | bytes 1523720 | tf_op jit(solution)/shard_map/ppermute | solution.py:445
  40.3 80.1 %collective-permute-start.6 = (bf16[2,248,512]{2,1,0:T(8,128)(2,1)}, bf16[2,248,512]{2,1,0:T(8,128)(2,1)S(1)}, u32[]{:S(2)}, u32[]{:S(2)}) collective-permute-start(bf16[2,248,512]{2,1,0:T(8,128)(2,1)} %get-tuple-element.69), channel_id=1, source_target_pairs={{0,3},{1,2},{2,1},{3,0},{4,7},{5,6},{6,5},{7,4},{8,11},{9,10},{10,... | collective-permute-start | bytes 1523720 | tf_op jit(solution)/shard_map/ppermute | solution.py:445
  70.8 10.0 %copy-start.4 = (bf16[2,248,512]{2,1,0:T(8,128)(2,1)}, bf16[2,248,512]{2,1,0:T(8,128)(2,1)S(1)}, u32[]{:S(2)}) copy-start(bf16[2,248,512]{2,1,0:T(8,128)(2,1)S(1)} %collective-permute-done.refs_0_.refs_1_) | copy-start | bytes 1523716
  70.8 49.6 %collective-permute-start.7 = (bf16[2,248,512]{2,1,0:T(8,128)(2,1)S(1)}, bf16[2,248,512]{2,1,0:T(8,128)(2,1)S(1)}, u32[]{:S(2)}, u32[]{:S(2)}) collective-permute-start(bf16[2,248,512]{2,1,0:T(8,128)(2,1)S(1)} %copy-done.25), channel_id=1, source_target_pairs={{0,3},{1,2},{2,1},{3,0},{4,7},{5,6},{6,5},{7,4},{8,11},{9,10},{10,... | collective-permute-start | bytes 1523720 | tf_op jit(solution)/shard_map/ppermute | solution.py:445
  80.8 0.8 copy-start.2
  93.7 56.5 %collective-permute-start.9 = (bf16[2,248,512]{2,1,0:T(8,128)(2,1)}, bf16[2,248,512]{2,1,0:T(8,128)(2,1)S(1)}, u32[]{:S(2)}, u32[]{:S(2)}) collective-permute-start(bf16[2,248,512]{2,1,0:T(8,128)(2,1)} %get-tuple-element.76), channel_id=1, source_target_pairs={{0,1},{1,0},{2,3},{3,2},{4,5},{5,4},{6,7},{7,6},{8,9},{9,8},{10,11... | collective-permute-start | bytes 1523720 | tf_op jit(solution)/shard_map/ppermute | solution.py:445
  93.8 13.7 %copy-start.5 = (bf16[2,248,512]{2,1,0:T(8,128)(2,1)}, bf16[2,248,512]{2,1,0:T(8,128)(2,1)S(1)}, u32[]{:S(2)}) copy-start(bf16[2,248,512]{2,1,0:T(8,128)(2,1)S(1)} %collective-permute-done.3.refs_0_.refs_2_) | copy-start | bytes 1523716
  107.4 0.8 copy-start.3
  120.4 40.1 %collective-permute-start.10 = (bf16[2,248,512]{2,1,0:T(8,128)(2,1)}, bf16[2,248,512]{2,1,0:T(8,128)(2,1)S(1)}, u32[]{:S(2)}, u32[]{:S(2)}) collective-permute-start(bf16[2,248,512]{2,1,0:T(8,128)(2,1)} %get-tuple-element.77), channel_id=1, source_target_pairs={{0,2},{1,3},{2,0},{3,1},{4,6},{5,7},{6,4},{7,5},{8,10},{9,11},{10,... | collective-permute-start | bytes 1523720 | tf_op jit(solution)/shard_map/ppermute | solution.py:445
  120.4 0.8 copy-start.7
  121.2 0.8 copy-start.6
  134.2 26.3 %collective-permute-start.11 = (bf16[2,248,512]{2,1,0:T(8,128)(2,1)}, bf16[2,248,512]{2,1,0:T(8,128)(2,1)S(1)}, u32[]{:S(2)}, u32[]{:S(2)}) collective-permute-start(bf16[2,248,512]{2,1,0:T(8,128)(2,1)} %get-tuple-element.78), channel_id=1, source_target_pairs={{0,3},{1,2},{2,1},{3,0},{4,7},{5,6},{6,5},{7,4},{8,11},{9,10},{10,... | collective-permute-start | bytes 1523720 | tf_op jit(solution)/shard_map/ppermute | solution.py:445
  150.2 10.3 %copy-start.26 = (bf16[2,248,512]{2,1,0:T(8,128)(2,1)}, bf16[2,248,512]{2,1,0:T(8,128)(2,1)S(1)}, u32[]{:S(2)}) copy-start(bf16[2,248,512]{2,1,0:T(8,128)(2,1)S(1)} %collective-permute-done.9.rest_1_) | copy-start | bytes 1523716
  160.4 0.8 copy-start.28
  160.4 1.0 copy-start.31
  189.2 74.7 %reduce-scatter.3.cloned.1.call-start = ((), (), s32[]{:S(2)}) async-start(), calls=%async_computation.2 | async-start | bytes 1966080 | tf_op jit(solution)/shard_map/reduce_scatter | solution.py:510
  192.6 208.6 %all-reduce.10.cloned.1.call-start = ((), (), s32[]{:S(2)}) async-start(), calls=%async_computation.4 | async-start | bytes 17825792 | tf_op jit(solution)/shard_map/psum | solution.py:507
  228.8 4.1 copy-start
  228.8 4.1 copy-start.1
  263.9 0.7 copy-start.32
  263.9 1.9 copy-start.22
  263.9 2.4 copy-start.23
  263.9 3.9 copy-start.24
  263.9 6.4 %copy-start.20 = (f32[1,1,512]{2,1,0:T(1,128)S(1)}, f32[1,1,512]{2,1,0:T(1,128)}, u32[]{:S(2)}) copy-start(f32[1,1,512]{2,1,0:T(1,128)} %get-tuple-element.98) | copy-start | bytes 6148
  263.9 6.3 %copy-start.21 = (f32[1,1,512]{2,1,0:T(1,128)S(1)}, f32[1,1,512]{2,1,0:T(1,128)}, u32[]{:S(2)}) copy-start(f32[1,1,512]{2,1,0:T(1,128)} %get-tuple-element.97) | copy-start | bytes 6148
  264.0 6.4 %copy-start.12 = (f32[1,1,2048]{2,1,0:T(1,128)S(1)}, f32[1,1,2048]{2,1,0:T(1,128)}, u32[]{:S(2)}) copy-start(f32[1,1,2048]{2,1,0:T(1,128)} %get-tuple-element.90) | copy-start | bytes 24580
  264.0 6.4 %copy-start.13 = (f32[1,1,2048]{2,1,0:T(1,128)S(1)}, f32[1,1,2048]{2,1,0:T(1,128)}, u32[]{:S(2)}) copy-start(f32[1,1,2048]{2,1,0:T(1,128)} %get-tuple-element.89) | copy-start | bytes 24580
  265.8 23.3 %collective-permute-start.2 = (bf16[2,248,512]{2,1,0:T(8,128)(2,1)S(1)}, bf16[2,248,512]{2,1,0:T(8,128)(2,1)S(1)}, u32[]{:S(2)}, u32[]{:S(2)}) collective-permute-start(bf16[2,248,512]{2,1,0:T(8,128)(2,1)S(1)} %copy-done.22), channel_id=1, source_target_pairs={{0,1},{1,0},{2,3},{3,2},{4,5},{5,4},{6,7},{7,6},{8,9},{9,8},{10,11... | collective-permute-start | bytes 1523720 | tf_op jit(solution)/shard_map/ppermute | solution.py:445
  266.3 37.2 %collective-permute-start.5 = (bf16[2,248,512]{2,1,0:T(8,128)(2,1)S(1)}, bf16[2,248,512]{2,1,0:T(8,128)(2,1)S(1)}, u32[]{:S(2)}, u32[]{:S(2)}) collective-permute-start(bf16[2,248,512]{2,1,0:T(8,128)(2,1)S(1)} %copy-done.23), channel_id=1, source_target_pairs={{0,2},{1,3},{2,0},{3,1},{4,6},{5,7},{6,4},{7,5},{8,10},{9,11},{10,... | collective-permute-start | bytes 1523720 | tf_op jit(solution)/shard_map/ppermute | solution.py:445
  267.9 35.6 %collective-permute-start.8 = (bf16[2,248,512]{2,1,0:T(8,128)(2,1)S(1)}, bf16[2,248,512]{2,1,0:T(8,128)(2,1)S(1)}, u32[]{:S(2)}, u32[]{:S(2)}) collective-permute-start(bf16[2,248,512]{2,1,0:T(8,128)(2,1)S(1)} %copy-done.24), channel_id=1, source_target_pairs={{0,3},{1,2},{2,1},{3,0},{4,7},{5,6},{6,5},{7,4},{8,11},{9,10},{10,... | collective-permute-start | bytes 1523720 | tf_op jit(solution)/shard_map/ppermute | solution.py:445
  289.2 14.3 %copy-start.27 = (bf16[2,248,512]{2,1,0:T(8,128)(2,1)}, bf16[2,248,512]{2,1,0:T(8,128)(2,1)S(1)}, u32[]{:S(2)}) copy-start(bf16[2,248,512]{2,1,0:T(8,128)(2,1)S(1)} %collective-permute-done.2.rest_1_) | copy-start | bytes 1523716
  303.5 0.8 copy-start.29
  303.5 1.0 copy-start.30
  310.4 2.6 copy-start.8
  310.4 3.9 copy-start.10
Sparse Core Ops, SparseCore 0:
  189.4 38.5 reduce-scatter.4
  230.3 33.5 reduce-scatter.2
  268.6 132.5 all-reduce.9

commit v2 on v1

--- a/solution.py
+++ b/solution.py
@@ -13,6 +13,7 @@
 F32 = jnp.float32
 VMEM_LIMIT = 60 * 1024 * 1024
 GELU_C = 0.7978845608028654
+COST = pl.CostEstimate(flops=10**6, bytes_accessed=2**12, transcendentals=0)
 
 
 def dot_nn(a, b):
@@ -56,37 +57,36 @@
 
 def route_kernel(exp_dev, me_ref, routes_ref, gates_ref, cot_ref, slot_row_ref, slot_col_ref, gate_col_ref, *rest):
     out_refs, scratch = rest[:-1], rest[-1]
-    n_img, seq, _ = routes_ref.shape
+    n_img, seq, width = cot_ref.shape
     experts = slot_row_ref.shape[1]
     capp = out_refs[0].shape[1]
     me = me_ref[0]
-    lane = lax.broadcasted_iota(jnp.int32, (seq, 128), 1)
-    later = lax.broadcasted_iota(jnp.int32, (seq, seq), 0)
-    earlier = lax.broadcasted_iota(jnp.int32, (seq, seq), 1)
+    expert = lax.broadcasted_iota(jnp.int32, (experts, seq), 0)
+    expert = ((expert // exp_dev) ^ me) * exp_dev + expert % exp_dev
+    earlier = lax.broadcasted_iota(jnp.int32, (seq, seq), 0)
+    later = lax.broadcasted_iota(jnp.int32, (seq, seq), 1)
     tri = jnp.where(earlier < later, 1.0, 0.0).astype(BF16)
-    carry = jnp.zeros((1, 128), F32)
-    gate_rows = []
+    carry = jnp.zeros((experts, 1), F32)
+    slots, gate_rows = [], []
     for i in range(n_img):
-        routes = routes_ref[i]
-        rel = ((routes // exp_dev) ^ me) * exp_dev + routes % exp_dev
-        gates = gates_ref[i]
-        hit0 = lane == rel[:, 0:1]
-        hit1 = lane == rel[:, 1:2]
+        hit0 = expert == routes_ref[0, i : i + 1, :]
+        hit1 = expert == routes_ref[1, i : i + 1, :]
         member = jnp.where(hit0 | hit1, 1.0, 0.0)
-        slot = jnp.where(member > 0.5, dot_nn(tri, member.astype(BF16)) + carry, -1.0)
-        gate = jnp.where(hit0, gates[:, 0:1], 0.0) + jnp.where(hit1, gates[:, 1:2], 0.0)
-        carry = carry + jnp.sum(member, axis=0, keepdims=True)
-        slot_col_ref[i] = slot[:, :experts]
-        gate_col_ref[i] = gate[:, :experts]
-        scratch[0, 0:seq, :] = slot
-        scratch[1, 0:seq, :] = gate
-        slot_row_ref[i] = jnp.transpose(scratch[0])[:experts, :seq]
-        gate_rows.append(jnp.transpose(scratch[1])[:experts, :seq])
+        slot = jnp.where(member > 0.5, dot_nn(member.astype(BF16), tri) + carry, -1.0)
+        gate = jnp.where(hit0, gates_ref[0, i : i + 1, :], jnp.where(hit1, gates_ref[1, i : i + 1, :], 0.0))
+        carry = carry + jnp.sum(member, axis=1, keepdims=True)
+        slots.append(slot)
+        gate_rows.append(gate)
+        slot_row_ref[i] = slot
+        scratch[0, 0:experts, 0:seq] = slot
+        scratch[1, 0:experts, 0:seq] = gate
+        slot_col_ref[i] = jnp.transpose(scratch[0])[:seq, :experts]
+        gate_col_ref[i] = jnp.transpose(scratch[1])[:seq, :experts]
     place = lax.broadcasted_iota(jnp.int32, (capp, seq), 0).astype(F32)
     for e in range(experts):
-        total = jnp.zeros((capp, cot_ref.shape[2]), F32)
+        total = jnp.zeros((capp, width), F32)
         for i in range(n_img):
-            pick = jnp.where(place == slot_row_ref[i, e : e + 1, :], gate_rows[i][e : e + 1, :], 0.0)
+            pick = jnp.where(place == slots[i][e : e + 1, :], gate_rows[i][e : e + 1, :], 0.0)
             total = total + dot_nn(pick.astype(BF16), cot_ref[i])
         out_refs[e // exp_dev][e % exp_dev] = total.astype(BF16)
 
@@ -106,13 +106,11 @@
             jax.ShapeDtypeStruct((n_img, seq, experts), F32),
         ]
         + [chunk] * ep_size,
-        scratch_shapes=[pltpu.VMEM((2, seq_pad, 128), F32)],
+        scratch_shapes=[pltpu.VMEM((2, 128, seq_pad), F32)],
         compiler_params=params(),
-        cost_estimate=pl.CostEstimate(
-            flops=2 * experts * capp * n_img * seq * width, bytes_accessed=4 * n_img * seq * width * 2, transcendentals=0
-        ),
+        cost_estimate=COST,
         name="route_and_dispatch_cotangent",
-    )(me, routes, gates, cotangent)
+    )(me, routes.transpose(2, 0, 1), gates.transpose(2, 0, 1), cotangent)
 
 
 def attention_kernel(
@@ -187,7 +185,7 @@
         + [chunk] * ep_size,
         scratch_shapes=[pltpu.VMEM((n_img, seq, width), BF16)],
         compiler_params=params("arbitrary"),
-        cost_estimate=pl.CostEstimate(flops=6 * 10**9, bytes_accessed=10 * 2**20, transcendentals=10**6),
+        cost_estimate=COST,
         name="attention_forward_and_dispatch",
     )(tokens, w_qkv, w_out, vecs, slot_row)
 
@@ -252,11 +250,7 @@
         out_shape=[broad] * (2 * count) + [narrow] * (2 * count),
         scratch_shapes=[pltpu.VMEM((count, capp, width), F32)] * 2,
         compiler_params=params("arbitrary", "arbitrary"),
-        cost_estimate=pl.CostEstimate(
-            flops=8 * count * exp_dev * capp * width * hidden,
-            bytes_accessed=4 * exp_dev * width * hidden + 4 * count * exp_dev * capp * hidden,
-            transcendentals=count * exp_dev * capp * hidden,
-        ),
+        cost_estimate=COST,
         name="experts",
     )(*xs, *gs, w_in, w_back, b_in, b_back)
     return [res[k * count : (k + 1) * count] for k in range(4)]
@@ -283,7 +277,7 @@
         bias_ref[0] = bias
 
 
-def weight_call(lefts, rights, which, rel, blocks, left_first):
+def weight_call(lefts, rights, which, blocks, left_first):
     count = len(lefts)
     _, capp, m = lefts[0].shape
     n = rights[0].shape[2]
@@ -307,9 +301,7 @@
             jax.ShapeDtypeStruct((1, 1, rights[0].shape[2]), F32),
         ],
         compiler_params=params("arbitrary"),
-        cost_estimate=pl.CostEstimate(
-            flops=2 * count * capp * blocks * m * n, bytes_accessed=2 * blocks * m * n, transcendentals=0
-        ),
+        cost_estimate=COST,
         name="expert_weight_gradient",
     )(which, *lefts, *rights)
 
@@ -328,10 +320,13 @@
 
 
 def backward_kernel(
-    heads, ep_size, tok_ref, cot_ref, resid_ref, qkv_ref, att_ref, lse_ref, slot_col_ref, w_qkv_ref, w_out_ref, vec_ref, *rest
+    heads, ep_size, pack_blocks, place_ref, bias_ref, tok_ref, cot_ref, resid_ref, qkv_ref, att_ref, lse_ref, slot_col_ref, w_qkv_ref, w_out_ref, vec_ref, *rest
 ):
     chunk_refs = rest[:ep_size]
-    gtok_ref, gw_qkv_ref, gw_out_ref, gvec_ref, gqkv_ref = rest[ep_size:]
+    packed = len(pack_blocks)
+    gtok_ref = rest[ep_size]
+    pack_refs = rest[ep_size + 1 : ep_size + 1 + packed]
+    gw_qkv_ref, gw_out_ref, gvec_ref, gqkv_ref = rest[ep_size + 1 + packed : ep_size + 5 + packed]
     img = pl.program_id(0)
     seq, width = tok_ref.shape[1:]
     capp = chunk_refs[0].shape[1]
@@ -397,27 +392,62 @@
         gw_qkv_ref[...] += gw_qkv
         gvec_ref[...] += gvec
 
-
-def backward_call(tokens, cotangent, resid, qkv, attended, lse, slot_col, w_qkv, w_out, vecs, chunks):
+    if not packed:
+        return
+
+    @pl.when(img == pl.num_programs(0) - 1)
+    def _():
+        small_ref = rest[-1]
+        blocks, per_pack, rows = pack_refs[0].shape[:3]
+        per_ep = width // ep_size
+        biases = bias_ref.shape[0]
+        small_ref[...] = jnp.zeros(small_ref.shape, F32)
+        for j in range(ep_size):
+            owner = place_ref[0] ^ j
+            small_ref[0:8, :] = gvec_ref[:, pl.ds(pl.multiple_of(owner * per_ep, per_ep), per_ep)]
+            small_ref[8 : 8 + biases, :] = bias_ref[...] if j == 0 else jnp.zeros(bias_ref.shape, F32)
+            for r in range(blocks):
+                block = pack_blocks[j // per_pack][r] ^ place_ref[1]
+                start = pl.multiple_of(owner * per_ep + block * rows, rows)
+                into = pack_refs[j // per_pack]
+                into[r, j % per_pack, :, 0 : 3 * width] = gw_qkv_ref[pl.ds(start, rows), :].astype(BF16)
+                into[r, j % per_pack, :, 3 * width : 4 * width] = gw_out_ref[pl.ds(start, rows), :].astype(BF16)
+                small = small_ref[pl.ds(pl.multiple_of(block * rows, rows), rows), :]
+                into[r, j % per_pack, :, 4 * width :] = small.astype(BF16)
+
+
+def backward_call(tokens, cotangent, resid, qkv, attended, lse, slot_col, w_qkv, w_out, vecs, chunks, place, biases, pack_blocks):
     n_img, seq, width = tokens.shape
+    ep_size = len(chunks)
+    packed = len(pack_blocks)
     image = lambda arr: pl.BlockSpec((1,) + arr.shape[1:], lambda i: (i, 0, 0))
+    sums = [
+        jax.ShapeDtypeStruct(w_qkv.shape, F32),
+        jax.ShapeDtypeStruct(w_out.shape, F32),
+        jax.ShapeDtypeStruct((8, width), F32),
+    ]
+    scratch = [pltpu.VMEM((seq, 3 * width), BF16)]
+    if packed:
+        grp_size = len(pack_blocks[0])
+        pack = (grp_size, ep_size // 2, width // (ep_size * grp_size), 4 * width + 128)
+        outs = [jax.ShapeDtypeStruct(pack, BF16)] * 2
+        scratch = [pltpu.VMEM(v.shape, F32) for v in sums] + scratch + [pltpu.VMEM((width // ep_size, 128), F32)]
+    else:
+        outs = sums
+        place, biases = jnp.zeros((2,), jnp.int32), jnp.zeros((8, 128), F32)
     return pl.pallas_call(
-        functools.partial(backward_kernel, width // HD, len(chunks)),
+        functools.partial(backward_kernel, width // HD, ep_size, pack_blocks),
         grid=(n_img,),
-        in_specs=[image(a) for a in (tokens, cotangent, resid, qkv, attended, lse, slot_col)]
+        in_specs=[pl.BlockSpec(memory_space=pltpu.SMEM), whole(biases.shape)]
+        + [image(a) for a in (tokens, cotangent, resid, qkv, attended, lse, slot_col)]
         + [whole(a.shape) for a in (w_qkv, w_out, vecs, *chunks)],
-        out_specs=[image(tokens), whole(w_qkv.shape), whole(w_out.shape), whole((8, width))],
-        out_shape=[
-            jax.ShapeDtypeStruct(tokens.shape, BF16),
-            jax.ShapeDtypeStruct(w_qkv.shape, F32),
-            jax.ShapeDtypeStruct(w_out.shape, F32),
-            jax.ShapeDtypeStruct((8, width), F32),
-        ],
-        scratch_shapes=[pltpu.VMEM((seq, 3 * width), BF16)],
+        out_specs=[image(tokens)] + [whole(v.shape) for v in outs],
+        out_shape=[jax.ShapeDtypeStruct(tokens.shape, BF16)] + outs,
+        scratch_shapes=scratch,
         compiler_params=params("arbitrary"),
-        cost_estimate=pl.CostEstimate(flops=10 * 10**9, bytes_accessed=16 * 2**20, transcendentals=10**6),
+        cost_estimate=COST,
         name="attention_backward",
-    )(tokens, cotangent, resid, qkv, attended, lse, slot_col, w_qkv, w_out, vecs, *chunks)
+    )(place, biases, tokens, cotangent, resid, qkv, attended, lse, slot_col, w_qkv, w_out, vecs, *chunks)
 
 
 def combine_kernel(ep_size, resid_ref, slot_col_ref, gate_col_ref, *rest):
@@ -436,13 +466,100 @@
         out_specs=image(resid),
         out_shape=jax.ShapeDtypeStruct(resid.shape, BF16),
         compiler_params=params("arbitrary"),
-        cost_estimate=pl.CostEstimate(flops=2 * 10**9, bytes_accessed=5 * 2**20, transcendentals=0),
+        cost_estimate=COST,
         name="combine_output",
     )(resid, slot_col, gate_col, *chunks)
 
 
 def swap(array, axis, size, distance):
     return lax.ppermute(array, axis, [(i, i ^ distance) for i in range(size)])
+
+
+def digits(index, bits):
+    number = jnp.zeros((), jnp.int32)
+    for bit in bits:
+        number = number * 2 + (index >> bit) % 2
+    return number
+
+
+def scatter_sums(arrays, orders, size):
+    for step in range(len(orders[0])):
+        halves = [a.shape[0] // 2 for a in arrays]
+        came = [swap(a[h:], "grp", size, 1 << o[step]) for a, h, o in zip(arrays, halves, orders)]
+        arrays = [a[:h] + c for a, h, c in zip(arrays, halves, came)]
+    return arrays
+
+
+def gather_sums(block, order, size):
+    pieces = [block]
+    for bit in reversed(order):
+        pieces = pieces + [swap(p, "grp", size, 1 << bit) for p in pieces]
+    return pieces
+
+
+def widen_kernel(exp_dev, count, place_ref, *refs):
+    piece_refs, out_ref = refs[: exp_dev * count], refs[-1]
+    for e in range(exp_dev):
+        for r in range(count):
+            @pl.when((pl.program_id(0) == e) & (pl.program_id(1) == r))
+            def _():
+                out_ref[0] = piece_refs[e * count + r][0].astype(F32)
+
+
+def widen_call(own, other, place, axis, shape):
+    count = len(own)
+    _, m, n = own[0].shape
+    at = (lambda l, r, s: (l ^ s[0], r ^ s[1], 0)) if axis == 0 else (lambda l, r, s: (l ^ s[0], 0, r ^ s[1]))
+    return pl.pallas_call(
+        functools.partial(widen_kernel, 2, count),
+        grid_spec=pltpu.PrefetchScalarGridSpec(
+            num_scalar_prefetch=1,
+            grid=(2, count),
+            in_specs=[pl.BlockSpec((1, m, n), lambda l, r, s: (0, 0, 0))] * (2 * count),
+            out_specs=pl.BlockSpec((1, m, n), at),
+        ),
+        out_shape=jax.ShapeDtypeStruct(shape, F32),
+        compiler_params=params("arbitrary", "arbitrary"),
+        cost_estimate=COST,
+        name="expert_gradient_result",
+    )(place, *own, *other)
+
+
+def unpack_kernel(width, exp_dev, hidden, offsets, place_ref, *refs):
+    piece_refs = refs[: len(offsets)]
+    gw_qkv_ref, gw_out_ref, vec_ref, b_in_ref, b_back_ref, small_ref = refs[len(offsets) :]
+    rows = piece_refs[0].shape[0]
+    for piece_ref, offset in zip(piece_refs, offsets):
+        at = pl.ds(pl.multiple_of((place_ref[0] ^ offset) * rows, rows), rows)
+        gw_qkv_ref[at, :] = piece_ref[:, 0 : 3 * width].astype(F32)
+        gw_out_ref[at, :] = piece_ref[:, 3 * width : 4 * width].astype(F32)
+        small_ref[at, :] = piece_ref[:, 4 * width :].astype(F32)
+    vec_ref[...] = small_ref[0:8, :]
+    row = 8
+    for ref, length in ((b_in_ref, hidden), (b_back_ref, width)):
+        for e in range(exp_dev):
+            for at in range(0, length, 128):
+                ref[e : e + 1, at : at + 128] = small_ref[row : row + 1, :]
+                row += 1
+
+
+def unpack_call(pieces, offsets, place, width, exp_dev, hidden):
+    rows = pieces[0].shape[0] * len(pieces)
+    shapes = [(rows, 3 * width), (rows, width), (8, 128), (exp_dev, hidden), (exp_dev, width)]
+    return pl.pallas_call(
+        functools.partial(unpack_kernel, width, exp_dev, hidden, offsets),
+        in_specs=[pl.BlockSpec(memory_space=pltpu.SMEM)] + [pl.BlockSpec(memory_space=pltpu.VMEM)] * len(pieces),
+        out_specs=[pl.BlockSpec(memory_space=pltpu.VMEM)] * len(shapes),
+        out_shape=[jax.ShapeDtypeStruct(v, F32) for v in shapes],
+        scratch_shapes=[pltpu.VMEM((rows, 128), F32)],
+        compiler_params=params(),
+        cost_estimate=COST,
+        name="parameter_gradient_results",
+    )(place, *pieces)
+
+
+def after(arrays, *others):
+    return lax.optimization_barrier((list(arrays), others))[0]
 
 
 def local(
@@ -488,42 +605,71 @@
         gdis += g
     gdis_back = exchange(gdis)
     outs_back = exchange(outs)
-    gw_back, gb_back, gw_in, gb_in = [], [], [], []
-    for e in range(exp_dev):
-        which = jnp.array([e, 0], jnp.int32)
-        w, b = weight_call(acts, g_all, which, None, 4, True)
-        gw_back.append(w.reshape(w_back.shape[1:]))
-        gb_back.append(b[0, 0])
-        w, b = weight_call(x_all, gpres, which, None, 4, False)
-        gw_in.append(w.transpose(1, 0, 2).reshape(w_in.shape[1:]))
-        gb_in.append(b[0, 0])
-    gw_back, gb_back, gw_in, gb_in = (jnp.stack(v) for v in (gw_back, gb_back, gw_in, gb_in))
-    grad_tokens, gw_qkv, gw_out, gvec = backward_call(
-        tokens, cotangent, resid, qkv, attended, lse, slot_col, w_qkv, w_out, vecs, gdis_back
+    grp_size = lax.axis_size("grp")
+    grp = lax.axis_index("grp").astype(jnp.int32)
+    bits = list(range(grp_size.bit_length() - 1))
+    order_a, order_b = bits[1:], bits[:0:-1]
+    blocks = grp_size // 2
+    core = grp % 2
+    place_a = jnp.stack([core, digits(grp, order_a)])
+    place_b = jnp.stack([core, digits(grp, order_b)])
+    flip = jnp.array([1, 0], jnp.int32)
+    gwb_far, gbb_far = weight_call(acts, g_all, place_a ^ flip, blocks, True)
+    gwi_far, gbi_far = weight_call(x_all, gpres, place_b ^ flip, blocks, False)
+    gwb_far = swap(gwb_far, "grp", grp_size, 1)
+    gwi_far = swap(gwi_far, "grp", grp_size, 1)
+    gwb, gbb = weight_call(acts, g_all, place_a, blocks, True)
+    gwi, gbi = weight_call(x_all, gpres, place_b, blocks, False)
+    sum_b, sum_i = scatter_sums([gwb + gwb_far, gwi + gwi_far], [order_a, order_b], grp_size)
+    all_b, all_i = gather_sums(sum_b, order_a, grp_size), gather_sums(sum_i, order_b, grp_size)
+    oth_b = [swap(p, "grp", grp_size, 1) for p in all_b]
+    oth_i = [swap(p, "grp", grp_size, 1) for p in all_i]
+    gw_back = widen_call(all_b, oth_b, place_a, 0, w_back.shape)
+    gw_in = widen_call(all_i, oth_i, place_b, 1, w_in.shape)
+
+    def by_expert(near, far):
+        return jnp.where(core == 0, jnp.concatenate([near, far]), jnp.concatenate([far, near]))[:, 0]
+
+    gb_in, gb_back = by_expert(gbi, gbi_far), by_expert(gbb, gbb_far)
+    hidden = w_in.shape[2]
+    packed = width // ep_size == 128 and 128 % (16 * grp_size) == 0
+    place, biases, pack_blocks = None, None, ()
+    if packed:
+        order_p, order_q = [0] + order_a, [0] + order_b
+        pack_blocks = tuple(
+            tuple(sum((r >> (len(o) - 1 - k)) % 2 << bit for k, bit in enumerate(o)) for r in range(grp_size))
+            for o in (order_p, order_q)
+        )
+        place = jnp.stack([me[0], grp])
+        biases = jnp.concatenate([gb_in.reshape(-1, 128), gb_back.reshape(-1, 128)])
+    grad_tokens, *grads = backward_call(
+        tokens, cotangent, resid, qkv, attended, lse, slot_col, w_qkv, w_out, vecs, gdis_back, place, biases, pack_blocks
     )
     output = combine_call(resid, slot_col, gate_col, outs_back)
-
-    def over_grp(v):
-        return lax.psum(v.astype(BF16), "grp").astype(F32)
-
-    def over_all(v):
-        return over_grp(lax.psum_scatter(v.astype(BF16), "ep", scatter_dimension=0, tiled=True))
-
-    return (
-        output,
-        grad_tokens,
-        over_all(gvec[0]),
-        over_all(gvec[1]),
-        over_all(gw_qkv),
-        over_all(gw_out),
-        over_all(gvec[2]),
-        over_all(gvec[3]),
-        over_all(gvec[4]),
-        over_grp(gw_in),
-        over_grp(gb_in),
-        over_grp(gw_back),
-        over_grp(gb_back),
-    )
+    if packed:
+        near, far = scatter_sums(grads, [order_p, order_q], grp_size)
+        parts = [near[0, d] for d in range(ep_size // 2)] + [far[0, d] for d in range(ep_size // 2)]
+        parts = exchange(parts)
+        total = parts[0].astype(F32)
+        for part in parts[1:]:
+            total = total + part.astype(F32)
+        pieces, offsets = [total.astype(BF16)], [0]
+        for bit in reversed(bits):
+            pieces = pieces + [swap(p, "grp", grp_size, 1 << bit) for p in pieces]
+            offsets = offsets + [o ^ (1 << bit) for o in offsets]
+        gw_qkv, gw_out, gvec, gb_in, gb_back = unpack_call(pieces, offsets, grp.reshape(1), width, exp_dev, hidden)
+        gvec = [gvec[k] for k in range(5)]
+    else:
+        def over_grp(v):
+            return lax.psum(v.astype(BF16), "grp").astype(F32)
+
+        def over_all(v):
+            return over_grp(lax.psum_scatter(v.astype(BF16), "ep", scatter_dimension=0, tiled=True))
+
+        gw_qkv, gw_out, gvec = grads
+        gw_qkv, gw_out, gb_in, gb_back = over_all(gw_qkv), over_all(gw_out), over_grp(gb_in), over_grp(gb_back)
+        gvec = [over_all(gvec[k]) for k in range(5)]
+    return (output, grad_tokens, gvec[0], gvec[1], gw_qkv, gw_out, gvec[2], gvec[3], gvec[4], gw_in, gb_in, gw_back, gb_back)
 
 
 def solution(mesh):

time: 427 us -> 359 us (0.84)
  starting transfers between devices: 21 us -> 84.8 us
  waiting for transfers between devices: 160 us -> 100 us
  blocking collectives: 40.9 us -> 0 us
  other arithmetic: 26 us -> 4.49 us
  Pallas kernels: 128 us -> 144 us
  between operations: 14.7 us -> 1.35 us
  local copies, waits for them, and re-layouts: 33.5 us -> 21.7 us
    ppermute x12 -> x48, starting transfers between devices: 20.9 us -> 84.8 us  [swap(): return lax.ppermute(array, axis, [(i, i ^ distance) for i in range(size)])]
    psum x1 -> x0, waiting for transfers between devices: 41.7 us -> none  [over_grp(): return lax.psum(v.astype(BF16), 'grp').astype(F32)]
    reduce_scatter x2 -> x0, waiting for transfers between devices: 28.6 us -> none  [over_all(): lax.psum_scatter(v.astype(BF16), 'ep', scatter_dimension=0, tiled=True)]
    psum x1 -> x0, blocking collectives: 22.9 us -> none  [over_grp(): return lax.psum(v.astype(BF16), 'grp').astype(F32)]
    convert_element_type x12 -> x1, other arithmetic: 19.5 us -> 0.04 us  [local(): pieces, offsets = ([total.astype(BF16)], [0])]
    unnamed x1 -> x0, blocking collectives: 18 us -> none
    pallas_call x1 -> x4, Pallas kernels: 25.7 us -> 42.6 us  [the longest x1 25.5 us: backward_call(): pl.pallas_call(functools.partial(backward_kernel, width // HD, ep_size, p...]
    ppermute x12 -> x48, waiting for transfers between devices: 90.1 us -> 100 us  [swap(): return lax.ppermute(array, axis, [(i, i ^ distance) for i in range(size)])]
  transfers between devices with their start and end apart: 15 -> 48, of which waited for: 8 -> 19; matrix products, arithmetic and copies ran while one was open for 6% -> 4% of each run, Pallas kernels for 20% -> 30%
where the time goes in v2:
time: 359 us; the launch traced here: 357 us
  Pallas kernels  144 us (40%)
  waiting for transfers between devices  100 us (28%)
  starting transfers between devices  84.8 us (24%)
  local copies, waits for them, and re-layouts  21.7 us (6%)
  other arithmetic  4.49 us (1%)
    ppermute x48, waiting for transfers between devices, swap(): return lax.ppermute(array, axis, [(i, i ^ distance) for i in range(size)])  100 us
    ppermute x48, starting transfers between devices, swap(): return lax.ppermute(array, axis, [(i, i ^ distance) for i in range(size)])  84.8 us
    pallas_call x4, Pallas kernels, expert_call(): pl.pallas_call(functools.partial(expert_kernel, count), grid=(exp_dev, hi...  48.5 us
    pallas_call x4, Pallas kernels, weight_call(): pl.pallas_call(functools.partial(weight_kernel, count, left_first), grid_...  28.8 us
    pallas_call x1, Pallas kernels, backward_call(): pl.pallas_call(functools.partial(backward_kernel, width // HD, ep_size, p...  25.5 us
    unnamed x106, local copies, waits for them, and re-layouts  15.8 us
    pallas_call x2, Pallas kernels, widen_call(): pl.pallas_call(functools.partial(widen_kernel, 2, count), grid_spec=pltpu...  14.9 us
    pallas_call x1, Pallas kernels, attention_call(): pl.pallas_call(functools.partial(attention_kernel, width // HD), grid=(n_...  14.1 us
  transfers between devices with their start and end apart: 48, of which 19 were waited for; matrix products, arithmetic and copies ran while one was open for 4% of the time, Pallas kernels for 30%

profile of v2, /device:TPU:0, one launch (start us, length us, event | category | flops | bytes accessed | tf_op | source)
XLA Modules:
  0.0 357.1 jit_solution(6881704068422072493)
XLA Ops:
  3.4 2.2 copy.31.cot_ref
  5.6 4.6 %route_and_dispatch_cotangent.1 = (f32[4,8,197]{2,1,0:T(8,128)}, f32[4,197,8]{2,1,0:T(8,128)}, f32[4,197,8]{2,1,0:T(8,128)}, bf16[2,248,512]{2,1,0:T(8,128)(2,1)...) custom-call(s32[1]{0:T(128)} %bitcast.5.me_ref, ...), custom_call_target="tpu_custom_call" | custom-call | flops 1000000 | bytes 4096 | tf_op jit(solution)/shard_map/route_and_dispatch_cotangent/pallas_call | solution.py:99
  10.2 5.1 %collective-permute-start.7 = (bf16[2,248,512]{2,1,0:T(8,128)(2,1)}, bf16[2,248,512]{2,1,0:T(8,128)(2,1)S(1)}, u32[]{:S(2)}, u32[]{:S(2)}) collective-permute-start(bf16[2,248,512]{2,1,0:T(8,128)(2,1)} %get-tuple-element.74), channel_id=1, source_target_pairs={{0,3},{1,2},{2,1},{3,0},{4,7},{5,6},{6,5},{7,4},{8,11},{9,10},{10,... | collective-permute-start | bytes 1523720 | tf_op jit(solution)/shard_map/ppermute | solution.py:475
  17.0 14.1 %attention_forward_and_dispatch.1 = (bf16[4,197,1536]{2,1,0:T(8,128)(2,1)}, bf16[4,197,512]{2,1,0:T(8,128)(2,1)}, f32[4,197,128]{2,1,0:T(8,128)}, f32[4,197,512]...) custom-call(bf16[4,197,512]{2,1,0:T(8,128)(2,1)} %copy.32.tok_ref, ...), custom_call_target="tpu_custom_call" | custom-call | flops 1000000 | bytes 4096 | tf_op jit(solution)/shard_map/attention_forward_and_dispatch/pallas_call | solution.py:173
  32.2 2.0 collective-permute-start.3
  35.6 35.6 %collective-permute-start = (bf16[2,248,512]{2,1,0:T(8,128)(2,1)}, bf16[2,248,512]{2,1,0:T(8,128)(2,1)S(1)}, u32[]{:S(2)}, u32[]{:S(2)}) collective-permute-start(bf16[2,248,512]{2,1,0:T(8,128)(2,1)} %get-tuple-element.67), channel_id=1, source_target_pairs={{0,1},{1,0},{2,3},{3,2},{4,5},{5,4},{6,7},{7,6},{8,9},{9,8},{10,11... | collective-permute-start | bytes 1523720 | tf_op jit(solution)/shard_map/ppermute | solution.py:475
  72.5 12.2 %experts.4 = (bf16[2,248,2048]{2,1,0:T(8,128)(2,1)}, bf16[2,248,2048]{2,1,0:T(8,128)(2,1)}, bf16[2,248,512]{2,1,0:T(8,128)(2,1)}, bf16[2,248,512]{2,1,0:T(8,128)(2,1)}) custom-call(bf16[2,248,512]{2,1,0:T(8,128)(2,1)} %get-tuple-element.64.refs_0_, bf16[2,248,512]{2,1,0:T(8,128)(2,1)} %get-tuple-element.65.refs_1_.refs_4_, bf16[2,512,2048]{2,1,0:T(8,128)(2,1)} %refs_2_.7, ...), custom_call_target="tpu_custom_call" | custom-call | flops 1000000 | bytes 4096 | tf_op jit(solution)/shard_map/experts/pallas_call | solution.py:239
  86.1 12.1 %experts.7 = (bf16[2,248,2048]{2,1,0:T(8,128)(2,1)}, bf16[2,248,2048]{2,1,0:T(8,128)(2,1)}, bf16[2,248,512]{2,1,0:T(8,128)(2,1)}, bf16[2,248,512]{2,1,0:T(8,128)(2,1)}) custom-call(bf16[2,248,512]{2,1,0:T(8,128)(2,1)} %copy-done.1, bf16[2,248,512]{2,1,0:T(8,128)(2,1)} %copy-done, bf16[2,512,2048]{2,1,0:T(8,128)(2,1)} %refs_2_.7, ...), custom_call_target="tpu_custom_call" | custom-call | flops 1000000 | bytes 4096 | tf_op jit(solution)/shard_map/experts/pallas_call | solution.py:239
  98.2 2.7 collective-permute-start.11
  100.9 13.3 %collective-permute-done.3.refs_0_.refs_2_ = bf16[2,248,512]{2,1,0:T(8,128)(2,1)S(1)} collective-permute-done((bf16[2,248,512]{2,1,0:T(8,128)(2,1)}, bf16[2,248,512]{2,1,0:T(8,128)(2,1)S(1)}, u32[]{:S(2)}, u32[]{:S(2)}) %collective-permute-start.3) | collective-permute-done | bytes 507936 | tf_op jit(solution)/shard_map/ppermute | solution.py:475
  115.0 12.1 %experts.6 = (bf16[2,248,2048]{2,1,0:T(8,128)(2,1)}, bf16[2,248,2048]{2,1,0:T(8,128)(2,1)}, bf16[2,248,512]{2,1,0:T(8,128)(2,1)}, bf16[2,248,512]{2,1,0:T(8,128)(2,1)}) custom-call(bf16[2,248,512]{2,1,0:T(8,128)(2,1)} %copy-done.2, bf16[2,248,512]{2,1,0:T(8,128)(2,1)} %copy-done.4, bf16[2,512,2048]{2,1,0:T(8,128)(2,1)} %refs_2_.7, ...), custom_call_target="tpu_custom_call" | custom-call | flops 1000000 | bytes 4096 | tf_op jit(solution)/shard_map/experts/pallas_call | solution.py:239
  128.8 12.1 %experts.5 = (bf16[2,248,2048]{2,1,0:T(8,128)(2,1)}, bf16[2,248,2048]{2,1,0:T(8,128)(2,1)}, bf16[2,248,512]{2,1,0:T(8,128)(2,1)}, bf16[2,248,512]{2,1,0:T(8,128)(2,1)}) custom-call(bf16[2,248,512]{2,1,0:T(8,128)(2,1)} %copy-done.3, bf16[2,248,512]{2,1,0:T(8,128)(2,1)} %copy-done.5, bf16[2,512,2048]{2,1,0:T(8,128)(2,1)} %refs_2_.7, ...), custom_call_target="tpu_custom_call" | custom-call | flops 1000000 | bytes 4096 | tf_op jit(solution)/shard_map/experts/pallas_call | solution.py:239
  140.9 3.3 collective-permute-start.9
  144.7 7.2 %expert_weight_gradient.7 = (bf16[4,512,512]{2,1,0:T(8,128)(2,1)}, f32[1,1,512]{2,1,0:T(1,128)}) custom-call(s32[2]{0:T(128)} %get-tuple-element.131.sel_ref, bf16[2,248,2048]{2,1,0:T(8,128)(2,1)} %get-tuple-element.82.refs_0_, bf16[2,248,2048]{2,1,0:T(8,128)(2,1)} %get-tuple-element.83.refs_1_, bf16[2,248,2048]{2,1,0:T(8,128)(2,1)} %get-tuple-element.84.refs_2_, ...), custom_call_target="tpu_custom_call" | custom-call | flops 1000000 | bytes 4096 | tf_op jit(solution)/shard_map/expert_weight_gradient/pallas_call | solution.py:291
  151.9 7.2 %expert_weight_gradient.6 = (bf16[4,512,512]{2,1,0:T(8,128)(2,1)}, f32[1,1,512]{2,1,0:T(1,128)}) custom-call(s32[2]{0:T(128)} %get-tuple-element.132.sel_ref.place_ref, bf16[2,248,2048]{2,1,0:T(8,128)(2,1)} %get-tuple-element.82.refs_0_, bf16[2,248,2048]{2,1,0:T(8,128)(2,1)} %get-tuple-element.83.refs_1_, bf16[2,248,2048]{2,1,0:T(8,128)(2,1)} %get-tuple-element.84.refs_2_, ...), custom_call_target="tpu_custom_call" | custom-call | flops 1000000 | bytes 4096 | tf_op jit(solution)/shard_map/expert_weight_gradient/pallas_call | solution.py:291
  159.1 7.2 %expert_weight_gradient.5 = (bf16[4,512,512]{2,1,0:T(8,128)(2,1)}, f32[1,1,2048]{2,1,0:T(1,128)}) custom-call(s32[2]{0:T(128)} %get-tuple-element.120.sel_ref, bf16[2,248,512]{2,1,0:T(8,128)(2,1)} %get-tuple-element.64.refs_0_, bf16[2,248,512]{2,1,0:T(8,128)(2,1)} %copy-done.3, bf16[2,248,512]{2,1,0:T(8,128)(2,1)} %copy-done.2, ...), custom_call_target="tpu_custom_call" | custom-call | flops 1000000 | bytes 4096 | tf_op jit(solution)/shard_map/expert_weight_gradient/pallas_call | solution.py:291
  166.3 7.2 %expert_weight_gradient.4 = (bf16[4,512,512]{2,1,0:T(8,128)(2,1)}, f32[1,1,2048]{2,1,0:T(1,128)}) custom-call(s32[2]{0:T(128)} %get-tuple-element.121.sel_ref.place_ref, bf16[2,248,512]{2,1,0:T(8,128)(2,1)} %get-tuple-element.64.refs_0_, bf16[2,248,512]{2,1,0:T(8,128)(2,1)} %copy-done.3, bf16[2,248,512]{2,1,0:T(8,128)(2,1)} %copy-done.2, ...), custom_call_target="tpu_custom_call" | custom-call | flops 1000000 | bytes 4096 | tf_op jit(solution)/shard_map/expert_weight_gradient/pallas_call | solution.py:291
  176.1 25.5 %attention_backward.1 = (bf16[4,197,512]{2,1,0:T(8,128)(2,1)}, bf16[8,2,16,2176]{3,2,1,0:T(8,128)(2,1)}, bf16[8,2,16,2176]{3,2,1,0:T(8,128)(2,1)}) custom-call(s32[2]{0:T(128)} %pad_add_fusion.place_ref, f32[40,128]{1,0:T(8,128)} %pad_maximum_fusion.bias_ref, bf16[4,197,512]{2,1,0:T(8,128)(2,1)} %copy.32.tok_ref, bf16[4,197,512]{2,1,0:T(8,128)(2,1)} %copy.31.cot_ref, ...), custom_call_target="tpu_custom_call" | custom-call | flops 1000000 | bytes 4096 | tf_op jit(solution)/shard_map/attention_backward/pallas_call | solution.py:438
  206.4 6.1 %collective-permute-done.12 = bf16[4,2,16,2176]{3,2,1,0:T(8,128)(2,1)S(1)} collective-permute-done((bf16[4,2,16,2176]{3,2,1,0:T(8,128)(2,1)S(1)}, bf16[4,2,16,2176]{3,2,1,0:T(8,128)(2,1)S(1)}, u32[]{:S(2)}, u32[]{:S(2)}) %collective-permute-start.12) | collective-permute-done | bytes 557088 | tf_op jit(solution)/shard_map/ppermute | solution.py:475
  212.5 1.5 collective-permute-start.17
  214.1 7.1 %collective-permute-done.17 = bf16[2,2,16,2176]{3,2,1,0:T(8,128)(2,1)S(1)} collective-permute-done((bf16[2,2,16,2176]{3,2,1,0:T(8,128)(2,1)S(1)}, bf16[2,2,16,2176]{3,2,1,0:T(8,128)(2,1)S(1)}, u32[]{:S(2)}, u32[]{:S(2)}) %collective-permute-start.17) | collective-permute-done | bytes 278560 | tf_op jit(solution)/shard_map/ppermute | solution.py:475
  221.2 1.5 collective-permute-start.13
  222.7 6.3 %collective-permute-done.13 = bf16[2,2,16,2176]{3,2,1,0:T(8,128)(2,1)S(1)} collective-permute-done((bf16[2,2,16,2176]{3,2,1,0:T(8,128)(2,1)S(1)}, bf16[2,2,16,2176]{3,2,1,0:T(8,128)(2,1)S(1)}, u32[]{:S(2)}, u32[]{:S(2)}) %collective-permute-start.13) | collective-permute-done | bytes 278560 | tf_op jit(solution)/shard_map/ppermute | solution.py:475
  229.1 1.5 collective-permute-start.18
  230.6 3.5 collective-permute-done.18
  234.1 1.5 collective-permute-start.14
  238.6 1.5 collective-permute-start.39
  240.7 2.6 collective-permute-start.19
  243.3 16.7 %collective-permute-done.29 = bf16[2,512,512]{2,1,0:T(8,128)(2,1)S(1)} collective-permute-done((bf16[2,512,512]{2,1,0:T(8,128)(2,1)S(1)}, bf16[2,512,512]{2,1,0:T(8,128)(2,1)S(1)}, u32[]{:S(2)}, u32[]{:S(2)}) %collective-permute-start.29) | collective-permute-done | bytes 1048608 | tf_op jit(solution)/shard_map/ppermute | solution.py:475
  260.1 1.5 collective-permute-start.30
  263.1 8.8 %collective-permute-done.30 = bf16[1,512,512]{2,1,0:T(8,128)(2,1)S(1)} collective-permute-done((bf16[1,512,512]{2,1,0:T(8,128)(2,1)S(1)}, bf16[1,512,512]{2,1,0:T(8,128)(2,1)S(1)}, u32[]{:S(2)}, u32[]{:S(2)}) %collective-permute-start.30) | collective-permute-done | bytes 524320 | tf_op jit(solution)/shard_map/ppermute | solution.py:475
  271.9 2.4 collective-permute-start.20
  277.2 1.5 collective-permute-start.31
  278.8 1.5 collective-permute-start.42
  280.9 6.3 %collective-permute-done.2.rest_1_ = bf16[2,248,512]{2,1,0:T(8,128)(2,1)S(1)} collective-permute-done((bf16[2,248,512]{2,1,0:T(8,128)(2,1)S(1)}, bf16[2,248,512]{2,1,0:T(8,128)(2,1)S(1)}, u32[]{:S(2)}, u32[]{:S(2)}) %collective-permute-start.2) | collective-permute-done | bytes 507936 | tf_op jit(solution)/shard_map/ppermute | solution.py:475
  289.9 9.6 %collective-permute-done.22.refs_2_ = bf16[16,2176]{1,0:T(8,128)(2,1)S(1)} collective-permute-done((bf16[16,2176]{1,0:T(8,128)(2,1)S(1)}, bf16[16,2176]{1,0:T(8,128)(2,1)S(1)}, u32[]{:S(2)}, u32[]{:S(2)}) %collective-permute-start.22) | collective-permute-done | bytes 69664 | tf_op jit(solution)/shard_map/ppermute | solution.py:475
  299.4 1.7 collective-permute-start.21
  301.1 2.6 collective-permute-done.21.refs_1_
  306.3 1.5 collective-permute-start.23
  307.8 2.8 collective-permute-done.23.refs_3_
  312.0 1.5 collective-permute-start.43
  313.5 1.7 collective-permute-start.33
  315.9 10.4 %collective-permute-done.43.refs_3_ = bf16[1,512,512]{2,1,0:T(8,128)(2,1)} collective-permute-done((bf16[1,512,512]{2,1,0:T(8,128)(2,1)S(1)}, bf16[1,512,512]{2,1,0:T(8,128)(2,1)}, u32[]{:S(2)}, u32[]{:S(2)}) %collective-permute-start.43) | collective-permute-done | bytes 524320 | tf_op jit(solution)/shard_map/ppermute | solution.py:475
  328.8 5.8 %combine_output.1 = bf16[4,197,512]{2,1,0:T(8,128)(2,1)} custom-call(f32[4,197,512]{2,1,0:T(8,128)} %get-tuple-element.61.resid_ref, f32[4,197,8]{2,1,0:T(8,128)} %get-tuple-element.62.slot_col_ref, f32[4,197,8]{2,1,0:T(8,128)} %get-tuple-element.63.gate_col_ref, bf16[2,248,512]{2,1,0:T(8,128)(2,1)} %get-tuple-element.66.rest_0_, ...), custom_call_target="tpu_custom_call" | custom-call | flops 1000000 | bytes 4096 | tf_op jit(solution)/shard_map/combine_output/pallas_call | solution.py:462
  334.8 2.5 copy.35
  338.6 2.1 parameter_gradient_results.1
  342.1 7.4 %expert_gradient_result.3 = f32[2,2048,512]{2,1,0:T(8,128)} custom-call(s32[2]{0:T(128)} %get-tuple-element.132.sel_ref.place_ref, bf16[1,512,512]{2,1,0:T(8,128)(2,1)} %copy-done.9, bf16[1,512,512]{2,1,0:T(8,128)(2,1)} %copy-done.17, bf16[1,512,512]{2,1,0:T(8,128)(2,1)} %copy-done.16, bf16[1,512,512]{2,1,0:T(8,128)(2,1)} %collective-permute-done.43.refs_3_, ...), custom_call_target="tpu_custom_call" | custom-call | flops 1000000 | bytes 4096 | tf_op jit(solution)/shard_map/expert_gradient_result/pallas_call | solution.py:513
  349.6 7.5 %expert_gradient_result.2 = f32[2,512,2048]{2,1,0:T(8,128)} custom-call(s32[2]{0:T(128)} %get-tuple-element.121.sel_ref.place_ref, bf16[1,512,512]{2,1,0:T(8,128)(2,1)} %copy-done.8, bf16[1,512,512]{2,1,0:T(8,128)(2,1)} %copy-done.15, bf16[1,512,512]{2,1,0:T(8,128)(2,1)} %copy-done.14, bf16[1,512,512]{2,1,0:T(8,128)(2,1)} %copy-done.18, ...), custom_call_target="tpu_custom_call" | custom-call | flops 1000000 | bytes 4096 | tf_op jit(solution)/shard_map/expert_gradient_result/pallas_call | solution.py:513
  (205 shorter events, 41.1 us)
Async XLA Ops:
  10.2 25.4 %collective-permute-start.7 = (bf16[2,248,512]{2,1,0:T(8,128)(2,1)}, bf16[2,248,512]{2,1,0:T(8,128)(2,1)S(1)}, u32[]{:S(2)}, u32[]{:S(2)}) collective-permute-start(bf16[2,248,512]{2,1,0:T(8,128)(2,1)} %get-tuple-element.74), channel_id=1, source_target_pairs={{0,3},{1,2},{2,1},{3,0},{4,7},{5,6},{6,5},{7,4},{8,11},{9,10},{10,... | collective-permute-start | bytes 1523720 | tf_op jit(solution)/shard_map/ppermute | solution.py:475
  31.1 54.2 %collective-permute-start.6 = (bf16[2,248,512]{2,1,0:T(8,128)(2,1)}, bf16[2,248,512]{2,1,0:T(8,128)(2,1)S(1)}, u32[]{:S(2)}, u32[]{:S(2)}) collective-permute-start(bf16[2,248,512]{2,1,0:T(8,128)(2,1)} %get-tuple-element.73), channel_id=1, source_target_pairs={{0,3},{1,2},{2,1},{3,0},{4,7},{5,6},{6,5},{7,4},{8,11},{9,10},{10,... | collective-permute-start | bytes 1523720 | tf_op jit(solution)/shard_map/ppermute | solution.py:475
  31.2 69.7 %collective-permute-start.4 = (bf16[2,248,512]{2,1,0:T(8,128)(2,1)}, bf16[2,248,512]{2,1,0:T(8,128)(2,1)S(1)}, u32[]{:S(2)}, u32[]{:S(2)}) collective-permute-start(bf16[2,248,512]{2,1,0:T(8,128)(2,1)} %get-tuple-element.71), channel_id=1, source_target_pairs={{0,2},{1,3},{2,0},{3,1},{4,6},{5,7},{6,4},{7,5},{8,10},{9,11},{10,... | collective-permute-start | bytes 1523720 | tf_op jit(solution)/shard_map/ppermute | solution.py:475
  32.2 82.0 %collective-permute-start.3 = (bf16[2,248,512]{2,1,0:T(8,128)(2,1)}, bf16[2,248,512]{2,1,0:T(8,128)(2,1)S(1)}, u32[]{:S(2)}, u32[]{:S(2)}) collective-permute-start(bf16[2,248,512]{2,1,0:T(8,128)(2,1)} %get-tuple-element.70), channel_id=1, source_target_pairs={{0,2},{1,3},{2,0},{3,1},{4,6},{5,7},{6,4},{7,5},{8,10},{9,11},{10,... | collective-permute-start | bytes 1523720 | tf_op jit(solution)/shard_map/ppermute | solution.py:475
  34.2 93.0 %collective-permute-start.1 = (bf16[2,248,512]{2,1,0:T(8,128)(2,1)}, bf16[2,248,512]{2,1,0:T(8,128)(2,1)S(1)}, u32[]{:S(2)}, u32[]{:S(2)}) collective-permute-start(bf16[2,248,512]{2,1,0:T(8,128)(2,1)} %get-tuple-element.68), channel_id=1, source_target_pairs={{0,1},{1,0},{2,3},{3,2},{4,5},{5,4},{6,7},{7,6},{8,9},{9,8},{10,11... | collective-permute-start | bytes 1523720 | tf_op jit(solution)/shard_map/ppermute | solution.py:475
  35.6 91.6 %collective-permute-start = (bf16[2,248,512]{2,1,0:T(8,128)(2,1)}, bf16[2,248,512]{2,1,0:T(8,128)(2,1)S(1)}, u32[]{:S(2)}, u32[]{:S(2)}) collective-permute-start(bf16[2,248,512]{2,1,0:T(8,128)(2,1)} %get-tuple-element.67), channel_id=1, source_target_pairs={{0,1},{1,0},{2,3},{3,2},{4,5},{5,4},{6,7},{7,6},{8,9},{9,8},{10,11... | collective-permute-start | bytes 1523720 | tf_op jit(solution)/shard_map/ppermute | solution.py:475
  98.2 76.7 %collective-permute-start.11 = (bf16[2,248,512]{2,1,0:T(8,128)(2,1)}, bf16[2,248,512]{2,1,0:T(8,128)(2,1)S(1)}, u32[]{:S(2)}, u32[]{:S(2)}) collective-permute-start(bf16[2,248,512]{2,1,0:T(8,128)(2,1)} %get-tuple-element.94), channel_id=1, source_target_pairs={{0,3},{1,2},{2,1},{3,0},{4,7},{5,6},{6,5},{7,4},{8,11},{9,10},{10,... | collective-permute-start | bytes 1523720 | tf_op jit(solution)/shard_map/ppermute | solution.py:475
  127.2 47.8 %collective-permute-start.10 = (bf16[2,248,512]{2,1,0:T(8,128)(2,1)}, bf16[2,248,512]{2,1,0:T(8,128)(2,1)S(1)}, u32[]{:S(2)}, u32[]{:S(2)}) collective-permute-start(bf16[2,248,512]{2,1,0:T(8,128)(2,1)} %get-tuple-element.93), channel_id=1, source_target_pairs={{0,2},{1,3},{2,0},{3,1},{4,6},{5,7},{6,4},{7,5},{8,10},{9,11},{10,... | collective-permute-start | bytes 1523720 | tf_op jit(solution)/shard_map/ppermute | solution.py:475
  140.9 34.1 %collective-permute-start.9 = (bf16[2,248,512]{2,1,0:T(8,128)(2,1)}, bf16[2,248,512]{2,1,0:T(8,128)(2,1)S(1)}, u32[]{:S(2)}, u32[]{:S(2)}) collective-permute-start(bf16[2,248,512]{2,1,0:T(8,128)(2,1)} %get-tuple-element.92), channel_id=1, source_target_pairs={{0,1},{1,0},{2,3},{3,2},{4,5},{5,4},{6,7},{7,6},{8,9},{9,8},{10,11... | collective-permute-start | bytes 1523720 | tf_op jit(solution)/shard_map/ppermute | solution.py:475
  202.9 3.2 collective-permute-start.16
  203.0 72.8 %collective-permute-start.8 = (bf16[2,248,512]{2,1,0:T(8,128)(2,1)S(1)}, bf16[2,248,512]{2,1,0:T(8,128)(2,1)S(1)}, u32[]{:S(2)}, u32[]{:S(2)}) collective-permute-start(bf16[2,248,512]{2,1,0:T(8,128)(2,1)S(1)} %copy-done.49), channel_id=1, source_target_pairs={{0,3},{1,2},{2,1},{3,0},{4,7},{5,6},{6,5},{7,4},{8,11},{9,10},{10,... | collective-permute-start | bytes 1523720 | tf_op jit(solution)/shard_map/ppermute | solution.py:475
  204.2 72.5 %collective-permute-start.5 = (bf16[2,248,512]{2,1,0:T(8,128)(2,1)}, bf16[2,248,512]{2,1,0:T(8,128)(2,1)S(1)}, u32[]{:S(2)}, u32[]{:S(2)}) collective-permute-start(bf16[2,248,512]{2,1,0:T(8,128)(2,1)} %get-tuple-element.72), channel_id=1, source_target_pairs={{0,2},{1,3},{2,0},{3,1},{4,6},{5,7},{6,4},{7,5},{8,10},{9,11},{10,... | collective-permute-start | bytes 1523720 | tf_op jit(solution)/shard_map/ppermute | solution.py:475
  204.5 31.1 %collective-permute-start.28 = (bf16[4,512,512]{2,1,0:T(8,128)(2,1)}, bf16[4,512,512]{2,1,0:T(8,128)(2,1)S(1)}, u32[]{:S(2)}, u32[]{:S(2)}) collective-permute-start(bf16[4,512,512]{2,1,0:T(8,128)(2,1)} %get-tuple-element.102), channel_id=1, source_target_pairs={{0,4},{4,0},{8,12},{12,8},{16,20},{20,16},{24,28},{28,24},{1,5},{5... | collective-permute-start | bytes 6291464 | tf_op jit(solution)/shard_map/ppermute | solution.py:475
  204.5 32.4 %collective-permute-start.38 = (bf16[4,512,512]{2,1,0:T(8,128)(2,1)S(1)}, bf16[4,512,512]{2,1,0:T(8,128)(2,1)S(1)}, u32[]{:S(2)}, u32[]{:S(2)}) collective-permute-start(bf16[4,512,512]{2,1,0:T(8,128)(2,1)S(1)} %copy-done.47), channel_id=1, source_target_pairs={{0,4},{4,0},{8,12},{12,8},{16,20},{20,16},{24,28},{28,24},{1,5},{5... | collective-permute-start | bytes 6291464 | tf_op jit(solution)/shard_map/ppermute | solution.py:475
  206.2 6.3 %collective-permute-start.12 = (bf16[4,2,16,2176]{3,2,1,0:T(8,128)(2,1)S(1)}, bf16[4,2,16,2176]{3,2,1,0:T(8,128)(2,1)S(1)}, u32[]{:S(2)}, u32[]{:S(2)}) collective-permute-start(bf16[4,2,16,2176]{3,2,1,0:T(8,128)(2,1)S(1)} %slice.88), channel_id=1, source_target_pairs={{0,4},{4,0},{8,12},{12,8},{16,20},{20,16},{24,28},{28,24},{1,5},{5... | collective-permute-start | bytes 1671176 | tf_op jit(solution)/shard_map/ppermute | solution.py:475
  212.5 8.7 %collective-permute-start.17 = (bf16[2,2,16,2176]{3,2,1,0:T(8,128)(2,1)S(1)}, bf16[2,2,16,2176]{3,2,1,0:T(8,128)(2,1)S(1)}, u32[]{:S(2)}, u32[]{:S(2)}) collective-permute-start(bf16[2,2,16,2176]{3,2,1,0:T(8,128)(2,1)S(1)} %slice.123), channel_id=1, source_target_pairs={{0,16},{4,20},{8,24},{12,28},{16,0},{20,4},{24,8},{28,12},{1,17},{... | collective-permute-start | bytes 835592 | tf_op jit(solution)/shard_map/ppermute | solution.py:475
  221.2 7.9 %collective-permute-start.13 = (bf16[2,2,16,2176]{3,2,1,0:T(8,128)(2,1)S(1)}, bf16[2,2,16,2176]{3,2,1,0:T(8,128)(2,1)S(1)}, u32[]{:S(2)}, u32[]{:S(2)}) collective-permute-start(bf16[2,2,16,2176]{3,2,1,0:T(8,128)(2,1)S(1)} %slice.117), channel_id=1, source_target_pairs={{0,8},{4,12},{8,0},{12,4},{16,24},{20,28},{24,16},{28,20},{1,9},{5... | collective-permute-start | bytes 835592 | tf_op jit(solution)/shard_map/ppermute | solution.py:475
  229.1 5.1 %collective-permute-start.18 = (bf16[1,2,16,2176]{3,2,1,0:T(8,128)(2,1)S(1)}, bf16[1,2,16,2176]{3,2,1,0:T(8,128)(2,1)S(1)}, u32[]{:S(2)}, u32[]{:S(2)}) collective-permute-start(bf16[1,2,16,2176]{3,2,1,0:T(8,128)(2,1)S(1)} %slice.125), channel_id=1, source_target_pairs={{0,8},{4,12},{8,0},{12,4},{16,24},{20,28},{24,16},{28,20},{1,9},{5... | collective-permute-start | bytes 417800 | tf_op jit(solution)/shard_map/ppermute | solution.py:475
  234.1 6.6 %collective-permute-start.14 = (bf16[1,2,16,2176]{3,2,1,0:T(8,128)(2,1)S(1)}, bf16[1,2,16,2176]{3,2,1,0:T(8,128)(2,1)S(1)}, u32[]{:S(2)}, u32[]{:S(2)}) collective-permute-start(bf16[1,2,16,2176]{3,2,1,0:T(8,128)(2,1)S(1)} %slice.119), channel_id=1, source_target_pairs={{0,16},{4,20},{8,24},{12,28},{16,0},{20,4},{24,8},{28,12},{1,17},{... | collective-permute-start | bytes 417800 | tf_op jit(solution)/shard_map/ppermute | solution.py:475
  236.4 23.6 %collective-permute-start.29 = (bf16[2,512,512]{2,1,0:T(8,128)(2,1)S(1)}, bf16[2,512,512]{2,1,0:T(8,128)(2,1)S(1)}, u32[]{:S(2)}, u32[]{:S(2)}) collective-permute-start(bf16[2,512,512]{2,1,0:T(8,128)(2,1)S(1)} %slice.129), channel_id=1, source_target_pairs={{0,16},{4,20},{8,24},{12,28},{16,0},{20,4},{24,8},{28,12},{1,17},{... | collective-permute-start | bytes 3145736 | tf_op jit(solution)/shard_map/ppermute | solution.py:475
  238.6 23.1 %collective-permute-start.39 = (bf16[2,512,512]{2,1,0:T(8,128)(2,1)S(1)}, bf16[2,512,512]{2,1,0:T(8,128)(2,1)S(1)}, u32[]{:S(2)}, u32[]{:S(2)}) collective-permute-start(bf16[2,512,512]{2,1,0:T(8,128)(2,1)S(1)} %slice.133), channel_id=1, source_target_pairs={{0,8},{4,12},{8,0},{12,4},{16,24},{20,28},{24,16},{28,20},{1,9},{5... | collective-permute-start | bytes 3145736 | tf_op jit(solution)/shard_map/ppermute | solution.py:475
  240.7 36.4 %collective-permute-start.19 = (bf16[16,2176]{1,0:T(8,128)(2,1)S(1)}, bf16[16,2176]{1,0:T(8,128)(2,1)S(1)}, u32[]{:S(2)}, u32[]{:S(2)}) collective-permute-start(bf16[16,2176]{1,0:T(8,128)(2,1)S(1)} %get-tuple-element.124), channel_id=1, source_target_pairs={{0,2},{1,3},{2,0},{3,1},{4,6},{5,7},{6,4},{7,5},{8,10},{9,11},{10,... | collective-permute-start | bytes 208904 | tf_op jit(solution)/shard_map/ppermute | solution.py:475
  260.1 11.8 %collective-permute-start.30 = (bf16[1,512,512]{2,1,0:T(8,128)(2,1)S(1)}, bf16[1,512,512]{2,1,0:T(8,128)(2,1)S(1)}, u32[]{:S(2)}, u32[]{:S(2)}) collective-permute-start(bf16[1,512,512]{2,1,0:T(8,128)(2,1)S(1)} %slice.131), channel_id=1, source_target_pairs={{0,8},{4,12},{8,0},{12,4},{16,24},{20,28},{24,16},{28,20},{1,9},{5... | collective-permute-start | bytes 1572872 | tf_op jit(solution)/shard_map/ppermute | solution.py:475
  261.8 12.6 %collective-permute-start.40 = (bf16[1,512,512]{2,1,0:T(8,128)(2,1)S(1)}, bf16[1,512,512]{2,1,0:T(8,128)(2,1)S(1)}, u32[]{:S(2)}, u32[]{:S(2)}) collective-permute-start(bf16[1,512,512]{2,1,0:T(8,128)(2,1)S(1)} %slice.135), channel_id=1, source_target_pairs={{0,16},{4,20},{8,24},{12,28},{16,0},{20,4},{24,8},{28,12},{1,17},{... | collective-permute-start | bytes 1572872 | tf_op jit(solution)/shard_map/ppermute | solution.py:475
  271.9 6.9 %collective-permute-start.20 = (bf16[16,2176]{1,0:T(8,128)(2,1)S(1)}, bf16[16,2176]{1,0:T(8,128)(2,1)S(1)}, u32[]{:S(2)}, u32[]{:S(2)}) collective-permute-start(bf16[16,2176]{1,0:T(8,128)(2,1)S(1)} %get-tuple-element.125), channel_id=1, source_target_pairs={{0,3},{1,2},{2,1},{3,0},{4,7},{5,6},{6,5},{7,4},{8,11},{9,10},{10,... | collective-permute-start | bytes 208904 | tf_op jit(solution)/shard_map/ppermute | solution.py:475
  274.4 5.9 %collective-permute-start.15 = (bf16[16,2176]{1,0:T(8,128)(2,1)S(1)}, bf16[16,2176]{1,0:T(8,128)(2,1)S(1)}, u32[]{:S(2)}, u32[]{:S(2)}) collective-permute-start(bf16[16,2176]{1,0:T(8,128)(2,1)S(1)} %slice_bitcast_fusion.2), channel_id=1, source_target_pairs={{0,1},{1,0},{2,3},{3,2},{4,5},{5,4},{6,7},{7,6},{8,9},{9,8},{10,11... | collective-permute-start | bytes 208904 | tf_op jit(solution)/shard_map/ppermute | solution.py:475
  275.9 11.3 %collective-permute-start.2 = (bf16[2,248,512]{2,1,0:T(8,128)(2,1)S(1)}, bf16[2,248,512]{2,1,0:T(8,128)(2,1)S(1)}, u32[]{:S(2)}, u32[]{:S(2)}) collective-permute-start(bf16[2,248,512]{2,1,0:T(8,128)(2,1)S(1)} %copy-done.48), channel_id=1, source_target_pairs={{0,1},{1,0},{2,3},{3,2},{4,5},{5,4},{6,7},{7,6},{8,9},{9,8},{10,11... | collective-permute-start | bytes 1523720 | tf_op jit(solution)/shard_map/ppermute | solution.py:475
  276.7 38.6 %collective-permute-start.32 = (bf16[1,512,512]{2,1,0:T(8,128)(2,1)S(1)}, bf16[1,512,512]{2,1,0:T(8,128)(2,1)S(1)}, u32[]{:S(2)}, u32[]{:S(2)}) collective-permute-start(bf16[1,512,512]{2,1,0:T(8,128)(2,1)S(1)} %slice_add_fusion.5.refs_0_), channel_id=1, source_target_pairs={{0,16},{4,20},{8,24},{12,28},{16,0},{20,4},{24,8},{28,12},{1,17},{... | collective-permute-start | bytes 1572872 | tf_op jit(solution)/shard_map/ppermute | solution.py:475
  277.2 36.3 %collective-permute-start.31 = (bf16[1,512,512]{2,1,0:T(8,128)(2,1)S(1)}, bf16[1,512,512]{2,1,0:T(8,128)(2,1)S(1)}, u32[]{:S(2)}, u32[]{:S(2)}) collective-permute-start(bf16[1,512,512]{2,1,0:T(8,128)(2,1)S(1)} %slice_add_fusion.5.refs_0_), channel_id=1, source_target_pairs={{0,8},{4,12},{8,0},{12,4},{16,24},{20,28},{24,16},{28,20},{1,9},{5... | collective-permute-start | bytes 1572872 | tf_op jit(solution)/shard_map/ppermute | solution.py:475
  278.8 36.4 %collective-permute-start.42 = (bf16[1,512,512]{2,1,0:T(8,128)(2,1)S(1)}, bf16[1,512,512]{2,1,0:T(8,128)(2,1)S(1)}, u32[]{:S(2)}, u32[]{:S(2)}) collective-permute-start(bf16[1,512,512]{2,1,0:T(8,128)(2,1)S(1)} %slice_add_fusion.4.refs_0_), channel_id=1, source_target_pairs={{0,8},{4,12},{8,0},{12,4},{16,24},{20,28},{24,16},{28,20},{1,9},{5... | collective-permute-start | bytes 1572872 | tf_op jit(solution)/shard_map/ppermute | solution.py:475
  280.3 31.7 %collective-permute-start.41 = (bf16[1,512,512]{2,1,0:T(8,128)(2,1)S(1)}, bf16[1,512,512]{2,1,0:T(8,128)(2,1)S(1)}, u32[]{:S(2)}, u32[]{:S(2)}) collective-permute-start(bf16[1,512,512]{2,1,0:T(8,128)(2,1)S(1)} %slice_add_fusion.4.refs_0_), channel_id=1, source_target_pairs={{0,16},{4,20},{8,24},{12,28},{16,0},{20,4},{24,8},{28,12},{1,17},{... | collective-permute-start | bytes 1572872 | tf_op jit(solution)/shard_map/ppermute | solution.py:475
  287.2 1.3 collective-permute-start.24
  288.4 11.0 %collective-permute-start.22 = (bf16[16,2176]{1,0:T(8,128)(2,1)S(1)}, bf16[16,2176]{1,0:T(8,128)(2,1)S(1)}, u32[]{:S(2)}, u32[]{:S(2)}) collective-permute-start(bf16[16,2176]{1,0:T(8,128)(2,1)S(1)} %fusion.2.refs_0_), channel_id=1, source_target_pairs={{0,8},{4,12},{8,0},{12,4},{16,24},{20,28},{24,16},{28,20},{1,9},{5... | collective-permute-start | bytes 208904 | tf_op jit(solution)/shard_map/ppermute | solution.py:475
  299.4 4.3 %collective-permute-start.21 = (bf16[16,2176]{1,0:T(8,128)(2,1)S(1)}, bf16[16,2176]{1,0:T(8,128)(2,1)S(1)}, u32[]{:S(2)}, u32[]{:S(2)}) collective-permute-start(bf16[16,2176]{1,0:T(8,128)(2,1)S(1)} %fusion.2.refs_0_), channel_id=1, source_target_pairs={{0,16},{4,20},{8,24},{12,28},{16,0},{20,4},{24,8},{28,12},{1,17},{... | collective-permute-start | bytes 208904 | tf_op jit(solution)/shard_map/ppermute | solution.py:475
  303.8 1.3 collective-permute-start.26
  305.0 1.3 collective-permute-start.25
  306.3 4.3 %collective-permute-start.23 = (bf16[16,2176]{1,0:T(8,128)(2,1)S(1)}, bf16[16,2176]{1,0:T(8,128)(2,1)S(1)}, u32[]{:S(2)}, u32[]{:S(2)}) collective-permute-start(bf16[16,2176]{1,0:T(8,128)(2,1)S(1)} %collective-permute-done.21.refs_1_), channel_id=1, source_target_pairs={{0,8},{4,12},{8,0},{12,4},{16,24},{20,28},{24,16},{28,20},{1,9},{5... | collective-permute-start | bytes 208904 | tf_op jit(solution)/shard_map/ppermute | solution.py:475
  310.6 1.3 collective-permute-start.27
  311.9 3.9 %collective-permute-start.44 = (bf16[1,512,512]{2,1,0:T(8,128)(2,1)S(1)}, bf16[1,512,512]{2,1,0:T(8,128)(2,1)S(1)}, u32[]{:S(2)}, u32[]{:S(2)}) collective-permute-start(bf16[1,512,512]{2,1,0:T(8,128)(2,1)S(1)} %slice_add_fusion.4.refs_0_), channel_id=1, source_target_pairs={{0,4},{4,0},{8,12},{12,8},{16,20},{20,16},{24,28},{28,24},{1,5},{5... | collective-permute-start | bytes 1572872 | tf_op jit(solution)/shard_map/ppermute | solution.py:475
  312.0 14.3 %collective-permute-start.43 = (bf16[1,512,512]{2,1,0:T(8,128)(2,1)S(1)}, bf16[1,512,512]{2,1,0:T(8,128)(2,1)}, u32[]{:S(2)}, u32[]{:S(2)}) collective-permute-start(bf16[1,512,512]{2,1,0:T(8,128)(2,1)S(1)} %collective-permute-done.41.refs_1_), channel_id=1, source_target_pairs={{0,8},{4,12},{8,0},{12,4},{16,24},{20,28},{24,16},{28,20},{1,9},{5... | collective-permute-start | bytes 1572872 | tf_op jit(solution)/shard_map/ppermute | solution.py:475
  313.5 14.0 %collective-permute-start.33 = (bf16[1,512,512]{2,1,0:T(8,128)(2,1)S(1)}, bf16[1,512,512]{2,1,0:T(8,128)(2,1)S(1)}, u32[]{:S(2)}, u32[]{:S(2)}) collective-permute-start(bf16[1,512,512]{2,1,0:T(8,128)(2,1)S(1)} %collective-permute-done.31.refs_1_), channel_id=1, source_target_pairs={{0,16},{4,20},{8,24},{12,28},{16,0},{20,4},{24,8},{28,12},{1,17},{... | collective-permute-start | bytes 1572872 | tf_op jit(solution)/shard_map/ppermute | solution.py:475
  315.3 12.2 %collective-permute-start.46 = (bf16[1,512,512]{2,1,0:T(8,128)(2,1)S(1)}, bf16[1,512,512]{2,1,0:T(8,128)(2,1)S(1)}, u32[]{:S(2)}, u32[]{:S(2)}) collective-permute-start(bf16[1,512,512]{2,1,0:T(8,128)(2,1)S(1)} %collective-permute-done.42.refs_2_), channel_id=1, source_target_pairs={{0,4},{4,0},{8,12},{12,8},{16,20},{20,16},{24,28},{28,24},{1,5},{5... | collective-permute-start | bytes 1572872 | tf_op jit(solution)/shard_map/ppermute | solution.py:475
  315.3 12.7 %collective-permute-start.45 = (bf16[1,512,512]{2,1,0:T(8,128)(2,1)S(1)}, bf16[1,512,512]{2,1,0:T(8,128)(2,1)S(1)}, u32[]{:S(2)}, u32[]{:S(2)}) collective-permute-start(bf16[1,512,512]{2,1,0:T(8,128)(2,1)S(1)} %collective-permute-done.41.refs_1_), channel_id=1, source_target_pairs={{0,4},{4,0},{8,12},{12,8},{16,20},{20,16},{24,28},{28,24},{1,5},{5... | collective-permute-start | bytes 1572872 | tf_op jit(solution)/shard_map/ppermute | solution.py:475
  315.8 33.8 %collective-permute-start.34 = (bf16[1,512,512]{2,1,0:T(8,128)(2,1)S(1)}, bf16[1,512,512]{2,1,0:T(8,128)(2,1)}, u32[]{:S(2)}, u32[]{:S(2)}) collective-permute-start(bf16[1,512,512]{2,1,0:T(8,128)(2,1)S(1)} %slice_add_fusion.5.refs_0_), channel_id=1, source_target_pairs={{0,4},{4,0},{8,12},{12,8},{16,20},{20,16},{24,28},{28,24},{1,5},{5... | collective-permute-start | bytes 1572872 | tf_op jit(solution)/shard_map/ppermute | solution.py:475
  326.3 15.8 %collective-permute-start.47 = (bf16[1,512,512]{2,1,0:T(8,128)(2,1)}, bf16[1,512,512]{2,1,0:T(8,128)(2,1)}, u32[]{:S(2)}, u32[]{:S(2)}) collective-permute-start(bf16[1,512,512]{2,1,0:T(8,128)(2,1)} %collective-permute-done.43.refs_3_), channel_id=1, source_target_pairs={{0,4},{4,0},{8,12},{12,8},{16,20},{20,16},{24,28},{28,24},{1,5},{5... | collective-permute-start | bytes 1572872 | tf_op jit(solution)/shard_map/ppermute | solution.py:475
  327.5 22.1 %collective-permute-start.35 = (bf16[1,512,512]{2,1,0:T(8,128)(2,1)S(1)}, bf16[1,512,512]{2,1,0:T(8,128)(2,1)}, u32[]{:S(2)}, u32[]{:S(2)}) collective-permute-start(bf16[1,512,512]{2,1,0:T(8,128)(2,1)S(1)} %collective-permute-done.31.refs_1_), channel_id=1, source_target_pairs={{0,4},{4,0},{8,12},{12,8},{16,20},{20,16},{24,28},{28,24},{1,5},{5... | collective-permute-start | bytes 1572872 | tf_op jit(solution)/shard_map/ppermute | solution.py:475
  327.5 22.1 %collective-permute-start.36 = (bf16[1,512,512]{2,1,0:T(8,128)(2,1)S(1)}, bf16[1,512,512]{2,1,0:T(8,128)(2,1)}, u32[]{:S(2)}, u32[]{:S(2)}) collective-permute-start(bf16[1,512,512]{2,1,0:T(8,128)(2,1)S(1)} %collective-permute-done.32.refs_2_), channel_id=1, source_target_pairs={{0,4},{4,0},{8,12},{12,8},{16,20},{20,16},{24,28},{28,24},{1,5},{5... | collective-permute-start | bytes 1572872 | tf_op jit(solution)/shard_map/ppermute | solution.py:475
  328.0 21.6 %collective-permute-start.37 = (bf16[1,512,512]{2,1,0:T(8,128)(2,1)S(1)}, bf16[1,512,512]{2,1,0:T(8,128)(2,1)}, u32[]{:S(2)}, u32[]{:S(2)}) collective-permute-start(bf16[1,512,512]{2,1,0:T(8,128)(2,1)S(1)} %collective-permute-done.33.refs_3_), channel_id=1, source_target_pairs={{0,4},{4,0},{8,12},{12,8},{16,20},{20,16},{24,28},{28,24},{1,5},{5... | collective-permute-start | bytes 1572872 | tf_op jit(solution)/shard_map/ppermute | solution.py:475
  (50 other events, 1058.6 us)

commit v3 on v2

--- a/solution.py
+++ b/solution.py
@@ -13,7 +13,10 @@
 F32 = jnp.float32
 VMEM_LIMIT = 60 * 1024 * 1024
 GELU_C = 0.7978845608028654
-COST = pl.CostEstimate(flops=10**6, bytes_accessed=2**12, transcendentals=0)
+
+
+def cost(microseconds):
+    return pl.CostEstimate(flops=int(microseconds * 10**9), bytes_accessed=2**12, transcendentals=0)
 
 
 def dot_nn(a, b):
@@ -55,10 +58,24 @@
     )
 
 
-def route_kernel(exp_dev, me_ref, routes_ref, gates_ref, cot_ref, slot_row_ref, slot_col_ref, gate_col_ref, *rest):
+def dispatch_rows(place, slots, values, source_refs, e):
+    total = None
+    for i, source in enumerate(source_refs):
+        value = 1.0 if values is None else values[i][e : e + 1, :]
+        pick = jnp.where(place == slots[i][e : e + 1, :], value, 0.0).astype(BF16)
+        part = dot_nn(pick, source[...])
+        total = part if total is None else total + part
+    return total.astype(BF16)
+
+
+def slot_places(capp, seq):
+    return lax.broadcasted_iota(jnp.int32, (capp, seq), 0).astype(F32)
+
+
+def route_kernel(exp_dev, me_ref, routes_ref, gates_ref, cot_ref, info_ref, slot_col_ref, gate_col_ref, *rest):
     out_refs, scratch = rest[:-1], rest[-1]
     n_img, seq, width = cot_ref.shape
-    experts = slot_row_ref.shape[1]
+    experts = info_ref.shape[2]
     capp = out_refs[0].shape[1]
     me = me_ref[0]
     expert = lax.broadcasted_iota(jnp.int32, (experts, seq), 0)
@@ -77,18 +94,16 @@
         carry = carry + jnp.sum(member, axis=1, keepdims=True)
         slots.append(slot)
         gate_rows.append(gate)
-        slot_row_ref[i] = slot
+        info_ref[0, i] = slot
+        info_ref[1, i] = gate
         scratch[0, 0:experts, 0:seq] = slot
         scratch[1, 0:experts, 0:seq] = gate
         slot_col_ref[i] = jnp.transpose(scratch[0])[:seq, :experts]
         gate_col_ref[i] = jnp.transpose(scratch[1])[:seq, :experts]
-    place = lax.broadcasted_iota(jnp.int32, (capp, seq), 0).astype(F32)
-    for e in range(experts):
-        total = jnp.zeros((capp, width), F32)
-        for i in range(n_img):
-            pick = jnp.where(place == slots[i][e : e + 1, :], gate_rows[i][e : e + 1, :], 0.0)
-            total = total + dot_nn(pick.astype(BF16), cot_ref[i])
-        out_refs[e // exp_dev][e % exp_dev] = total.astype(BF16)
+    place = slot_places(capp, seq)
+    sources = [cot_ref.at[i] for i in range(n_img)]
+    for e in range(len(out_refs) * exp_dev):
+        out_refs[e // exp_dev][e % exp_dev] = dispatch_rows(place, slots, gate_rows, sources, e)
 
 
 def route_call(me, routes, gates, cotangent, ep_size, exp_dev, capp):
@@ -99,22 +114,48 @@
     return pl.pallas_call(
         functools.partial(route_kernel, exp_dev),
         in_specs=[pl.BlockSpec(memory_space=pltpu.SMEM)] + [pl.BlockSpec(memory_space=pltpu.VMEM)] * 3,
-        out_specs=[pl.BlockSpec(memory_space=pltpu.VMEM)] * (3 + ep_size),
+        out_specs=[pl.BlockSpec(memory_space=pltpu.VMEM)] * (3 + ep_size // 2),
         out_shape=[
-            jax.ShapeDtypeStruct((n_img, experts, seq), F32),
+            jax.ShapeDtypeStruct((2, n_img, experts, seq), F32),
             jax.ShapeDtypeStruct((n_img, seq, experts), F32),
             jax.ShapeDtypeStruct((n_img, seq, experts), F32),
         ]
-        + [chunk] * ep_size,
+        + [chunk] * (ep_size // 2),
         scratch_shapes=[pltpu.VMEM((2, 128, seq_pad), F32)],
         compiler_params=params(),
-        cost_estimate=COST,
+        cost_estimate=cost(4),
         name="route_and_dispatch_cotangent",
     )(me, routes.transpose(2, 0, 1), gates.transpose(2, 0, 1), cotangent)
 
 
+def gateway_kernel(exp_dev, info_ref, cot_ref, *out_refs):
+    n_img, seq, width = cot_ref.shape
+    capp = out_refs[0].shape[1]
+    place = slot_places(capp, seq)
+    slots = [info_ref[0, i] for i in range(n_img)]
+    gate_rows = [info_ref[1, i] for i in range(n_img)]
+    sources = [cot_ref.at[i] for i in range(n_img)]
+    half = len(out_refs)
+    for j in range(half):
+        for k in range(exp_dev):
+            out_refs[j][k] = dispatch_rows(place, slots, gate_rows, sources, (half ^ j) * exp_dev + k)
+
+
+def gateway_call(info, cotangent, ep_size, exp_dev, capp):
+    chunk = jax.ShapeDtypeStruct((exp_dev, capp, cotangent.shape[2]), BF16)
+    return pl.pallas_call(
+        functools.partial(gateway_kernel, exp_dev),
+        in_specs=[pl.BlockSpec(memory_space=pltpu.VMEM)] * 2,
+        out_specs=[pl.BlockSpec(memory_space=pltpu.VMEM)] * (ep_size // 2),
+        out_shape=[chunk] * (ep_size // 2),
+        compiler_params=params(),
+        cost_estimate=cost(3),
+        name="dispatch_far_cotangent",
+    )(info, cotangent)
+
+
 def attention_kernel(
-    heads, tok_ref, w_qkv_ref, w_out_ref, vec_ref, slot_row_ref, qkv_ref, att_ref, lse_ref, resid_ref, *rest
+    heads, tok_ref, w_qkv_ref, w_out_ref, vec_ref, info_ref, qkv_ref, att_ref, lse_ref, resid_ref, *rest
 ):
     out_refs, second_ref = rest[:-1], rest[-1]
     img = pl.program_id(0)
@@ -157,23 +198,21 @@
     @pl.when(img == pl.num_programs(0) - 1)
     def _():
         n_img = second_ref.shape[0]
-        place = lax.broadcasted_iota(jnp.int32, (capp, seq), 0).astype(F32)
+        place = slot_places(capp, seq)
+        slots = [info_ref[0, i] for i in range(n_img)]
+        sources = [second_ref.at[i] for i in range(n_img)]
         for e in range(len(out_refs) * exp_dev):
-            total = jnp.zeros((capp, width), F32)
-            for i in range(n_img):
-                pick = jnp.where(place == slot_row_ref[i, e : e + 1, :], 1.0, 0.0)
-                total = total + dot_nn(pick.astype(BF16), second_ref[i])
-            out_refs[e // exp_dev][e % exp_dev] = total.astype(BF16)
-
-
-def attention_call(tokens, w_qkv, w_out, vecs, slot_row, ep_size, exp_dev, capp):
+            out_refs[e // exp_dev][e % exp_dev] = dispatch_rows(place, slots, None, sources, e)
+
+
+def attention_call(tokens, w_qkv, w_out, vecs, info, ep_size, exp_dev, capp):
     n_img, seq, width = tokens.shape
     chunk = jax.ShapeDtypeStruct((exp_dev, capp, width), BF16)
     image = lambda *tail: pl.BlockSpec((1,) + tail, lambda i: (i, 0, 0))
     return pl.pallas_call(
         functools.partial(attention_kernel, width // HD),
         grid=(n_img,),
-        in_specs=[image(seq, width), whole(w_qkv.shape), whole(w_out.shape), whole(vecs.shape), whole(slot_row.shape)],
+        in_specs=[image(seq, width), whole(w_qkv.shape), whole(w_out.shape), whole(vecs.shape), whole(info.shape)],
         out_specs=[image(seq, 3 * width), image(seq, width), image(seq, 128), image(seq, width)]
         + [whole(chunk.shape)] * ep_size,
         out_shape=[
@@ -185,125 +224,152 @@
         + [chunk] * ep_size,
         scratch_shapes=[pltpu.VMEM((n_img, seq, width), BF16)],
         compiler_params=params("arbitrary"),
-        cost_estimate=COST,
+        cost_estimate=cost(14),
         name="attention_forward_and_dispatch",
-    )(tokens, w_qkv, w_out, vecs, slot_row)
-
-
-def expert_kernel(count, *refs):
+    )(tokens, w_qkv, w_out, vecs, info)
+
+
+def expert_kernel(count, carried, blocks, tile, sel_ref, *refs):
     x_refs, g_refs = refs[:count], refs[count : 2 * count]
-    w_in_ref, w_back_ref, b_in_ref, b_back_ref = refs[2 * count : 2 * count + 4]
-    outs = refs[2 * count + 4 :]
-    act_refs, gpre_refs, out_refs, gdis_refs = (outs[k * count : (k + 1) * count] for k in range(4))
-    acc_out, acc_dis = outs[4 * count :]
-    step = pl.program_id(1)
-    w_in = w_in_ref[0]
-    w_back = w_back_ref[0]
-    for n in range(count):
-        pre = dot_nn(x_refs[n][0], w_in) + b_in_ref[0]
-        square = pre * pre
-        bent = jnp.tanh(pre * (GELU_C + (GELU_C * 0.044715) * square))
-        half = 0.5 + 0.5 * bent
-        act = (pre * half).astype(BF16)
-        slope = half + (pre * (0.5 - 0.5 * bent * bent)) * (GELU_C + (3 * GELU_C * 0.044715) * square)
-        gpre = (dot_nt(g_refs[n][0], w_back) * slope).astype(BF16)
-        act_refs[n][0] = act
-        gpre_refs[n][0] = gpre
-        part_dis = dot_nt(gpre, w_in)
-        part_out = dot_nn(act, w_back)
-
-        @pl.when(step == 0)
-        def _():
-            acc_dis[n] = part_dis
-            acc_out[n] = part_out + b_back_ref[0]
-
-        @pl.when(step > 0)
-        def _():
-            acc_dis[n] += part_dis
-            acc_out[n] += part_out
-
-        @pl.when(step == pl.num_programs(1) - 1)
-        def _():
-            gdis_refs[n][0] = acc_dis[n].astype(BF16)
-            out_refs[n][0] = acc_out[n].astype(BF16)
-
-
-def expert_call(xs, gs, w_in, w_back, b_in, b_back, tile):
+    w_in_hbm, w_back_hbm, b_in_ref, b_back_ref = refs[2 * count : 2 * count + 4]
+    before = refs[2 * count + 4 : 2 * count + 4 + carried]
+    outs = refs[2 * count + 4 + carried :]
+    out_refs, gdis_refs = outs[:count], outs[count : 2 * count]
+    sums, (gb_in_ref, gb_back_ref) = outs[2 * count : 2 * count + 4], outs[2 * count + 4 : 2 * count + 6]
+    w_in_buf, w_back_buf, back_buf, in_buf, acc_out, acc_dis, load_sem, sum_sem, store_sem = outs[2 * count + 6 :]
+    exp_dev, _, hidden = w_in_buf.shape
+    block = hidden // blocks
+    steps = [(l, t) for l in range(exp_dev) for t in range(hidden // tile)]
+
+    def loads(l, t):
+        e = sel_ref[0] ^ l
+        span = pl.ds(t * tile, tile)
+        return [
+            pltpu.make_async_copy(w_in_hbm.at[e, :, span], w_in_buf.at[l, :, span], load_sem.at[l, t, 0]),
+            pltpu.make_async_copy(w_back_hbm.at[e, span, :], w_back_buf.at[l, span, :], load_sem.at[l, t, 1]),
+        ]
+
+    def blocks_of(t):
+        return range(t * tile // block, (t + 1) * tile // block)
+
+    def sum_loads(l, t):
+        return [
+            copy
+            for b in blocks_of(t)
+            for copy in (
+                pltpu.make_async_copy(before[2 * l].at[b ^ sel_ref[1]], back_buf.at[l, b], sum_sem.at[l, b, 0]),
+                pltpu.make_async_copy(before[2 * l + 1].at[b ^ sel_ref[2]], in_buf.at[l, b], sum_sem.at[l, b, 1]),
+            )
+        ]
+
+    def stores(l, t):
+        return [
+            copy
+            for b in blocks_of(t)
+            for copy in (
+                pltpu.make_async_copy(back_buf.at[l, b], sums[2 * l].at[b ^ sel_ref[1]], store_sem.at[l, b, 0]),
+                pltpu.make_async_copy(in_buf.at[l, b], sums[2 * l + 1].at[b ^ sel_ref[2]], store_sem.at[l, b, 1]),
+            )
+        ]
+
+    for l, t in steps:
+        for copy in loads(l, t):
+            copy.start()
+    if carried:
+        for l, t in steps:
+            for copy in sum_loads(l, t):
+                copy.start()
+    for l, t in steps:
+        e = sel_ref[0] ^ l
+        span = slice(t * tile, (t + 1) * tile)
+        for copy in loads(l, t):
+            copy.wait()
+        w_in, w_back = w_in_buf[l, :, span], w_back_buf[l, span, :]
+        gw_back = gw_in = gb_in = None
+        for n in range(count):
+            x, g = x_refs[n][e], g_refs[n][e]
+            pre = dot_nn(x, w_in) + b_in_ref[e, :, span]
+            square = pre * pre
+            bent = jnp.tanh(pre * (GELU_C + (GELU_C * 0.044715) * square))
+            half = 0.5 + 0.5 * bent
+            act = (pre * half).astype(BF16)
+            slope = half + (pre * (0.5 - 0.5 * bent * bent)) * (GELU_C + (3 * GELU_C * 0.044715) * square)
+            gpre = (dot_nt(g, w_back) * slope).astype(BF16)
+            part_dis, part_out = dot_nt(gpre, w_in), dot_nn(act, w_back)
+            if t == 0:
+                part_out = part_out + b_back_ref[e]
+            else:
+                part_dis, part_out = part_dis + acc_dis[n], part_out + acc_out[n]
+            if span.stop == hidden:
+                gdis_refs[n][e] = part_dis.astype(BF16)
+                out_refs[n][e] = part_out.astype(BF16)
+            else:
+                acc_dis[n] = part_dis
+                acc_out[n] = part_out
+            one = (dot_tn(act, g), dot_tn(x, gpre), jnp.sum(gpre.astype(F32), axis=0, keepdims=True))
+            gw_back = one[0] if n == 0 else gw_back + one[0]
+            gw_in = one[1] if n == 0 else gw_in + one[1]
+            gb_in = one[2] if n == 0 else gb_in + one[2]
+        gb_in_ref[e, :, span] = gb_in
+        if carried:
+            for copy in sum_loads(l, t):
+                copy.wait()
+        for b in blocks_of(t):
+            at = slice(b * block - t * tile, (b + 1) * block - t * tile)
+            back, into = gw_back[at, :], gw_in[:, at]
+            if carried:
+                back, into = back + back_buf[l, b].astype(F32), into + in_buf[l, b].astype(F32)
+            back_buf[l, b] = back.astype(BF16)
+            in_buf[l, b] = into.astype(BF16)
+        for copy in stores(l, t):
+            copy.start()
+    for e in range(exp_dev):
+        total = jnp.sum(g_refs[0][e].astype(F32), axis=0, keepdims=True)
+        for n in range(1, count):
+            total = total + jnp.sum(g_refs[n][e].astype(F32), axis=0, keepdims=True)
+        gb_back_ref[e] = total
+    for l, t in steps:
+        for copy in stores(l, t):
+            copy.wait()
+
+
+def expert_call(xs, gs, w_in, w_back, b_in, b_back, place, blocks, before, microseconds):
     count = len(xs)
     exp_dev, capp, width = xs[0].shape
     hidden = w_in.shape[2]
-    rows = pl.BlockSpec((1, capp, width), lambda e, f: (e, 0, 0))
-    wide = pl.BlockSpec((1, capp, tile), lambda e, f: (e, 0, f))
+    block = hidden // blocks
+    tile = max(block, min(hidden, 512))
     narrow = jax.ShapeDtypeStruct((exp_dev, capp, width), BF16)
-    broad = jax.ShapeDtypeStruct((exp_dev, capp, hidden), BF16)
+    shapes = [jax.ShapeDtypeStruct((blocks, block, width), BF16), jax.ShapeDtypeStruct((blocks, width, block), BF16)] * 2
+    held = pl.BlockSpec(memory_space=pltpu.VMEM)
+    remote = pl.BlockSpec(memory_space=pl.ANY)
     res = pl.pallas_call(
-        functools.partial(expert_kernel, count),
-        grid=(exp_dev, hidden // tile),
-        in_specs=[rows] * (2 * count)
-        + [
-            pl.BlockSpec((1, width, tile), lambda e, f: (e, 0, f)),
-            pl.BlockSpec((1, tile, width), lambda e, f: (e, f, 0)),
-            pl.BlockSpec((1, 1, tile), lambda e, f: (e, 0, f)),
-            pl.BlockSpec((1, 1, width), lambda e, f: (e, 0, 0)),
+        functools.partial(expert_kernel, count, len(before), blocks, tile),
+        in_specs=[pl.BlockSpec(memory_space=pltpu.SMEM)]
+        + [held] * (2 * count)
+        + [remote] * 2
+        + [held] * 2
+        + [remote] * len(before),
+        out_specs=[held] * (2 * count) + [remote] * 4 + [held] * 2,
+        out_shape=[narrow] * (2 * count)
+        + shapes
+        + [jax.ShapeDtypeStruct((exp_dev, 1, hidden), F32), jax.ShapeDtypeStruct((exp_dev, 1, width), F32)],
+        scratch_shapes=[
+            pltpu.VMEM((exp_dev, width, hidden), BF16),
+            pltpu.VMEM((exp_dev, hidden, width), BF16),
+            pltpu.VMEM((exp_dev, blocks, block, width), BF16),
+            pltpu.VMEM((exp_dev, blocks, width, block), BF16),
+            pltpu.VMEM((count, capp, width), F32),
+            pltpu.VMEM((count, capp, width), F32),
+            pltpu.SemaphoreType.DMA((exp_dev, blocks, 2)),
+            pltpu.SemaphoreType.DMA((exp_dev, blocks, 2)),
+            pltpu.SemaphoreType.DMA((exp_dev, blocks, 2)),
         ],
-        out_specs=[wide] * (2 * count) + [rows] * (2 * count),
-        out_shape=[broad] * (2 * count) + [narrow] * (2 * count),
-        scratch_shapes=[pltpu.VMEM((count, capp, width), F32)] * 2,
-        compiler_params=params("arbitrary", "arbitrary"),
-        cost_estimate=COST,
+        compiler_params=params(),
+        cost_estimate=cost(microseconds),
         name="experts",
-    )(*xs, *gs, w_in, w_back, b_in, b_back)
-    return [res[k * count : (k + 1) * count] for k in range(4)]
-
-
-def weight_kernel(count, left_first, sel_ref, *refs):
-    a_refs, b_refs = refs[:count], refs[count : 2 * count]
-    out_ref, bias_ref = refs[2 * count :]
-    total = dot_tn(a_refs[0][0], b_refs[0][0])
-    for n in range(1, count):
-        total = total + dot_tn(a_refs[n][0], b_refs[n][0])
-    out_ref[0] = total.astype(BF16)
-    if left_first:
-        @pl.when(pl.program_id(0) == 0)
-        def _():
-            bias = jnp.sum(b_refs[0][0].astype(F32), axis=0, keepdims=True)
-            for n in range(1, count):
-                bias = bias + jnp.sum(b_refs[n][0].astype(F32), axis=0, keepdims=True)
-            bias_ref[0] = bias
-    else:
-        bias = jnp.sum(b_refs[0][0].astype(F32), axis=0, keepdims=True)
-        for n in range(1, count):
-            bias = bias + jnp.sum(b_refs[n][0].astype(F32), axis=0, keepdims=True)
-        bias_ref[0] = bias
-
-
-def weight_call(lefts, rights, which, blocks, left_first):
-    count = len(lefts)
-    _, capp, m = lefts[0].shape
-    n = rights[0].shape[2]
-    if left_first:
-        m = m // blocks
-    else:
-        n = n // blocks
-    left_at = (lambda r, s: (s[0], 0, r ^ s[1])) if left_first else (lambda r, s: (s[0], 0, 0))
-    right_at = (lambda r, s: (s[0], 0, 0)) if left_first else (lambda r, s: (s[0], 0, r ^ s[1]))
-    bias_at = (lambda r, s: (0, 0, 0)) if left_first else (lambda r, s: (0, 0, r ^ s[1]))
-    return pl.pallas_call(
-        functools.partial(weight_kernel, count, left_first),
-        grid_spec=pltpu.PrefetchScalarGridSpec(
-            num_scalar_prefetch=1,
-            grid=(blocks,),
-            in_specs=[pl.BlockSpec((1, capp, m), left_at)] * count + [pl.BlockSpec((1, capp, n), right_at)] * count,
-            out_specs=[pl.BlockSpec((1, m, n), lambda r, s: (r, 0, 0)), pl.BlockSpec((1, 1, n), bias_at)],
-        ),
-        out_shape=[
-            jax.ShapeDtypeStruct((blocks, m, n), BF16),
-            jax.ShapeDtypeStruct((1, 1, rights[0].shape[2]), F32),
-        ],
-        compiler_params=params("arbitrary"),
-        cost_estimate=COST,
-        name="expert_weight_gradient",
-    )(which, *lefts, *rights)
+    )(place, *xs, *gs, w_in, w_back, b_in, b_back, *before)
+    return res[:count], res[count : 2 * count], res[2 * count : 2 * count + 4], res[2 * count + 4 :]
 
 
 def gather_rows(slot_col, value_col, chunk_refs, capp):
@@ -445,7 +511,7 @@
         out_shape=[jax.ShapeDtypeStruct(tokens.shape, BF16)] + outs,
         scratch_shapes=scratch,
         compiler_params=params("arbitrary"),
-        cost_estimate=COST,
+        cost_estimate=cost(25),
         name="attention_backward",
     )(place, biases, tokens, cotangent, resid, qkv, attended, lse, slot_col, w_qkv, w_out, vecs, *chunks)
 
@@ -466,7 +532,7 @@
         out_specs=image(resid),
         out_shape=jax.ShapeDtypeStruct(resid.shape, BF16),
         compiler_params=params("arbitrary"),
-        cost_estimate=COST,
+        cost_estimate=cost(5),
         name="combine_output",
     )(resid, slot_col, gate_col, *chunks)
 
@@ -482,12 +548,10 @@
     return number
 
 
-def scatter_sums(arrays, orders, size):
-    for step in range(len(orders[0])):
-        halves = [a.shape[0] // 2 for a in arrays]
-        came = [swap(a[h:], "grp", size, 1 << o[step]) for a, h, o in zip(arrays, halves, orders)]
-        arrays = [a[:h] + c for a, h, c in zip(arrays, halves, came)]
-    return arrays
+def scatter_step(arrays, bits, size):
+    halves = [a.shape[0] // 2 for a in arrays]
+    came = [swap(a[h:], "grp", size, 1 << bit) for a, h, bit in zip(arrays, halves, bits)]
+    return [a[:h] + c for a, h, c in zip(arrays, halves, came)]
 
 
 def gather_sums(block, order, size):
@@ -520,7 +584,7 @@
         ),
         out_shape=jax.ShapeDtypeStruct(shape, F32),
         compiler_params=params("arbitrary", "arbitrary"),
-        cost_estimate=COST,
+        cost_estimate=cost(5),
         name="expert_gradient_result",
     )(place, *own, *other)
 
@@ -553,7 +617,7 @@
         out_shape=[jax.ShapeDtypeStruct(v, F32) for v in shapes],
         scratch_shapes=[pltpu.VMEM((rows, 128), F32)],
         compiler_params=params(),
-        cost_estimate=COST,
+        cost_estimate=cost(5),
         name="parameter_gradient_results",
     )(place, *pieces)
 
@@ -588,49 +652,58 @@
     me = lax.axis_index("ep").astype(jnp.int32).reshape(1)
     vecs = jnp.stack([ln1_gain, ln1_bias, out_bias, ln2_gain, ln2_bias] + [jnp.zeros_like(ln1_gain)] * 3)
 
-    def exchange(chunks):
-        return [chunks[0]] + [swap(chunks[d], "ep", ep_size, d) for d in range(1, ep_size)]
-
-    slot_row, slot_col, gate_col, *g_send = route_call(me, routes, gates, cotangent, ep_size, exp_dev, capp)
-    g_all = exchange(g_send)
-    qkv, attended, lse, resid, *x_send = attention_call(tokens, w_qkv, w_out, vecs, slot_row, ep_size, exp_dev, capp)
-    x_all = exchange(x_send)
-    b_in, b_back = in_bias[:, None, :], back_bias[:, None, :]
-    acts, gpres, outs, gdis = [], [], [], []
-    for d in range(ep_size):
-        a, p, o, g = expert_call(x_all[d : d + 1], g_all[d : d + 1], w_in, w_back, b_in, b_back, 512)
-        acts += a
-        gpres += p
-        outs += o
-        gdis += g
-    gdis_back = exchange(gdis)
-    outs_back = exchange(outs)
     grp_size = lax.axis_size("grp")
     grp = lax.axis_index("grp").astype(jnp.int32)
     bits = list(range(grp_size.bit_length() - 1))
     order_a, order_b = bits[1:], bits[:0:-1]
     blocks = grp_size // 2
     core = grp % 2
-    place_a = jnp.stack([core, digits(grp, order_a)])
-    place_b = jnp.stack([core, digits(grp, order_b)])
-    flip = jnp.array([1, 0], jnp.int32)
-    gwb_far, gbb_far = weight_call(acts, g_all, place_a ^ flip, blocks, True)
-    gwi_far, gbi_far = weight_call(x_all, gpres, place_b ^ flip, blocks, False)
-    gwb_far = swap(gwb_far, "grp", grp_size, 1)
-    gwi_far = swap(gwi_far, "grp", grp_size, 1)
-    gwb, gbb = weight_call(acts, g_all, place_a, blocks, True)
-    gwi, gbi = weight_call(x_all, gpres, place_b, blocks, False)
-    sum_b, sum_i = scatter_sums([gwb + gwb_far, gwi + gwi_far], [order_a, order_b], grp_size)
+    block_a, block_b = digits(grp, order_a), digits(grp, order_b)
+    half = ep_size // 2
+
+    def over_ep(array, distance):
+        return swap(array, "ep", ep_size, distance)
+
+    cot_far = over_ep(cotangent, half)
+    info, slot_col, gate_col, *g_all = route_call(me, routes, gates, cotangent, ep_size, exp_dev, capp)
+    info_far = over_ep(info, half)
+    g_all = [g_all[0]] + [over_ep(g_all[d], d) for d in range(1, half)]
+    qkv, attended, lse, resid, *x_send = attention_call(tokens, w_qkv, w_out, vecs, info, ep_size, exp_dev, capp)
+    x_all = [x_send[0]]
+    for d in range(1, ep_size):
+        send, = after([x_send[d]], *([cot_far] if d == half else [x_all[-1]] if d > half else []))
+        x_all.append(over_ep(send, d))
+    far = gateway_call(info_far, cot_far, ep_size, exp_dev, capp)
+    g_all = g_all + [far[0]] + [over_ep(far[j], j) for j in range(1, half)]
+    g_all[0], = after(g_all[:1], *far)
+    b_in, b_back = in_bias[:, None, :], back_bias[:, None, :]
+    place_e = jnp.stack([1 - core, block_a, block_b])
+    steps = [list(range(half))] + [[d] for d in range(half, ep_size)]
+    outs, gdis, gdis_back, sums, bias_sums = [], [], [], (), None
+    for number, step in enumerate(steps):
+        xs, gs = [x_all[d] for d in step], [g_all[d] for d in step]
+        if number == len(steps) - 1:
+            xs = after(xs, *gdis_back[:half])
+        o, g, sums, sums_b = expert_call(xs, gs, w_in, w_back, b_in, b_back, place_e, blocks, tuple(sums), 4 + 6 * len(step))
+        outs, gdis = outs + list(o), gdis + list(g)
+        for d in step:
+            send, = after([gdis[d]], *([x_all[-1]] if d >= half else []))
+            gdis_back.append(over_ep(send, d) if d else send)
+        bias_sums = sums_b if number == 0 else [a + b for a, b in zip(bias_sums, sums_b)]
+    gb_in, gb_back = bias_sums[0][:, 0], bias_sums[1][:, 0]
+    far_b, far_i, near_b, near_i = sums
+    state = [near_b + swap(far_b, "grp", grp_size, 1), near_i + swap(far_i, "grp", grp_size, 1)]
+    stages = [state]
+    for step in range(len(order_a)):
+        state = scatter_step(state, [order_a[step], order_b[step]], grp_size)
+        stages.append(state)
+    sum_b, sum_i = state
+    resid_late, = after([resid], *stages[len(stages) // 2])
     all_b, all_i = gather_sums(sum_b, order_a, grp_size), gather_sums(sum_i, order_b, grp_size)
     oth_b = [swap(p, "grp", grp_size, 1) for p in all_b]
     oth_i = [swap(p, "grp", grp_size, 1) for p in all_i]
-    gw_back = widen_call(all_b, oth_b, place_a, 0, w_back.shape)
-    gw_in = widen_call(all_i, oth_i, place_b, 1, w_in.shape)
-
-    def by_expert(near, far):
-        return jnp.where(core == 0, jnp.concatenate([near, far]), jnp.concatenate([far, near]))[:, 0]
-
-    gb_in, gb_back = by_expert(gbi, gbi_far), by_expert(gbb, gbb_far)
+    gw_back = widen_call(all_b, oth_b, jnp.stack([core, block_a]), 0, w_back.shape)
+    gw_in = widen_call(all_i, oth_i, jnp.stack([core, block_b]), 1, w_in.shape)
     hidden = w_in.shape[2]
     packed = width // ep_size == 128 and 128 % (16 * grp_size) == 0
     place, biases, pack_blocks = None, None, ()
@@ -643,16 +716,22 @@
         place = jnp.stack([me[0], grp])
         biases = jnp.concatenate([gb_in.reshape(-1, 128), gb_back.reshape(-1, 128)])
     grad_tokens, *grads = backward_call(
-        tokens, cotangent, resid, qkv, attended, lse, slot_col, w_qkv, w_out, vecs, gdis_back, place, biases, pack_blocks
+        tokens, cotangent, resid_late, qkv, attended, lse, slot_col, w_qkv, w_out, vecs, gdis_back, place, biases, pack_blocks
     )
+    outs_back = [outs[0]]
+    for d in range(1, ep_size):
+        send, = after([outs[d]], *gdis_back, *([outs_back[-1]] if d > half else []))
+        outs_back.append(over_ep(send, d))
     output = combine_call(resid, slot_col, gate_col, outs_back)
+    grads = after(grads, sum_b, sum_i, *outs_back[: half + 1])
     if packed:
-        near, far = scatter_sums(grads, [order_p, order_q], grp_size)
+        for bits_now in zip(order_p, order_q):
+            grads = scatter_step(grads, bits_now, grp_size)
+        near, far = after(grads, *outs_back)
         parts = [near[0, d] for d in range(ep_size // 2)] + [far[0, d] for d in range(ep_size // 2)]
-        parts = exchange(parts)
         total = parts[0].astype(F32)
-        for part in parts[1:]:
-            total = total + part.astype(F32)
+        for d in range(1, ep_size):
+            total = total + over_ep(parts[d], d).astype(F32)
         pieces, offsets = [total.astype(BF16)], [0]
         for bit in reversed(bits):
             pieces = pieces + [swap(p, "grp", grp_size, 1 << bit) for p in pieces]

time: 359 us -> 324 us (0.903)
  starting transfers between devices: 84.8 us -> 53.5 us
  Pallas kernels: 144 us -> 124 us
  waiting for transfers between devices: 100 us -> 113 us
    ppermute x48 -> x49, starting transfers between devices: 84.8 us -> 53.5 us  [swap(): return lax.ppermute(array, axis, [(i, i ^ distance) for i in range(size)])]
    pallas_call x8 -> x4, Pallas kernels: 77.3 us -> 57.8 us  [the longest x3 54.6 us: expert_call(): pl.pallas_call(functools.partial(expert_kernel, count, len(before), block...]
    ppermute x48 -> x49, waiting for transfers between devices: 100 us -> 113 us  [swap(): return lax.ppermute(array, axis, [(i, i ^ distance) for i in range(size)])]
    unnamed x106 -> x108, local copies, waits for them, and re-layouts: 15.8 us -> 15 us
  transfers between devices with their start and end apart: 48 -> 49, of which waited for: 19 -> 15; matrix products, arithmetic and copies ran while one was open for 4% -> 7% of each run, Pallas kernels for 30% -> 32%
where the time goes in v3:
time: 324 us; the launch traced here: 319 us
  Pallas kernels  124 us (38%)
  waiting for transfers between devices  113 us (35%)
  starting transfers between devices  53.5 us (17%)
  local copies, waits for them, and re-layouts  20.5 us (6%)
  other arithmetic  6.12 us (2%)
    ppermute x49, waiting for transfers between devices, swap(): return lax.ppermute(array, axis, [(i, i ^ distance) for i in range(size)])  113 us
    pallas_call x3, Pallas kernels, expert_call(): pl.pallas_call(functools.partial(expert_kernel, count, len(before), block...  54.6 us
    ppermute x49, starting transfers between devices, swap(): return lax.ppermute(array, axis, [(i, i ^ distance) for i in range(size)])  53.5 us
    pallas_call x1, Pallas kernels, backward_call(): pl.pallas_call(functools.partial(backward_kernel, width // HD, ep_size, p...  25.2 us
    unnamed x108, local copies, waits for them, and re-layouts  15 us
    pallas_call x2, Pallas kernels, widen_call(): pl.pallas_call(functools.partial(widen_kernel, 2, count), grid_spec=pltpu...  14.9 us
    pallas_call x1, Pallas kernels, attention_call(): pl.pallas_call(functools.partial(attention_kernel, width // HD), grid=(n_...  14.6 us
  transfers between devices with their start and end apart: 49, of which 15 were waited for; matrix products, arithmetic and copies ran while one was open for 7% of the time, Pallas kernels for 32%

profile of v3, /device:TPU:0, one launch (start us, length us, event | category | flops | bytes accessed | tf_op | source)
XLA Modules:
  0.0 319.0 jit_solution(18201139114830745978)
XLA Ops:
  0.6 4.1 %collective-permute-start.2 = (bf16[4,197,512]{2,0,1:T(4,128)(2,1)}, bf16[4,197,512]{2,0,1:T(4,128)(2,1)S(1)}, u32[]{:S(2)}, u32[]{:S(2)}) collective-permute-start(bf16[4,197,512]{2,0,1:T(4,128)(2,1)} %param.29), channel_id=1, source_target_pairs={{0,2},{1,3},{2,0},{3,1},{4,6},{5,7},{6,4},{7,5},{8,10},{9,11},{10,... | collective-permute-start | bytes 2420744 | tf_op jit(solution)/shard_map/ppermute | solution.py:541
  4.7 2.2 copy.39.cot_ref
  8.3 1.3 copy.48
  9.6 3.6 %route_and_dispatch_cotangent.1 = (f32[2,4,8,197]{3,2,1,0:T(8,128)}, f32[4,197,8]{2,1,0:T(8,128)}, f32[4,197,8]{2,1,0:T(8,128)}, bf16[2,248,512]{2,1,0:T(8,128)(2,1)}, bf16[2,248,512]{2,1,0:T(8,128)(2,1)}) custom-call(s32[1]{0:T(128)} %bitcast.5.me_ref, s32[2,4,197]{2,1,0:T(4,128)} %bitcast.40, f32[2,4,197]{2,1,0:T(4,128)} %bitcast.41, ...), custom_call_target="tpu_custom_call" | custom-call | flops 4000000000 | bytes 4096 | tf_op jit(solution)/shard_map/route_and_dispatch_cotangent/pallas_call | solution.py:114
  13.2 1.6 collective-permute-start.3
  16.5 14.6 %attention_forward_and_dispatch.1 = (bf16[4,197,1536]{2,1,0:T(8,128)(2,1)}, bf16[4,197,512]{2,1,0:T(8,128)(2,1)}, f32[4,197,128]{2,1,0:T(8,128)}, f32[4,197,512]...) custom-call(bf16[4,197,512]{2,1,0:T(8,128)(2,1)} %copy.40.tok_ref, ...), custom_call_target="tpu_custom_call" | custom-call | flops 14000000000 | bytes 4096 | tf_op jit(solution)/shard_map/attention_forward_and_dispatch/pallas_call | solution.py:212
  33.5 7.6 %collective-permute-done.2 = bf16[4,197,512]{2,0,1:T(4,128)(2,1)S(1)} collective-permute-done((bf16[4,197,512]{2,0,1:T(4,128)(2,1)}, bf16[4,197,512]{2,0,1:T(4,128)(2,1)S(1)}, u32[]{:S(2)}, u32[]{:S(2)}) %collective-permute-start.2) | collective-permute-done | bytes 806944 | tf_op jit(solution)/shard_map/ppermute | solution.py:541
  42.1 3.3 %collective-permute-done.1.info_ref = f32[2,4,8,197]{3,2,1,0:T(8,128)S(1)} collective-permute-done((f32[2,4,8,197]{3,2,1,0:T(8,128)S(1)}, f32[2,4,8,197]{3,2,1,0:T(8,128)S(1)}, u32[]{:S(2)}, u32[]{:S(2)}) %collective-permute-start.1) | collective-permute-done | bytes 50464 | tf_op jit(solution)/shard_map/ppermute | solution.py:541
  46.0 3.2 %dispatch_far_cotangent.1 = (bf16[2,248,512]{2,1,0:T(8,128)(2,1)}, bf16[2,248,512]{2,1,0:T(8,128)(2,1)}) custom-call(f32[2,4,8,197]{3,2,1,0:T(8,128)} %copy-done.50, bf16[4,197,512]{2,1,0:T(8,128)(2,1)} %copy.41.cot_ref), custom_call_target="tpu_custom_call" | custom-call | flops 3000000000 | bytes 4096 | tf_op jit(solution)/shard_map/dispatch_far_cotangent/pallas_call | solution.py:146
  49.2 2.4 collective-permute-start.8
  52.6 14.6 %collective-permute-done.refs_1_ = bf16[2,248,512]{2,1,0:T(8,128)(2,1)S(1)} collective-permute-done((bf16[2,248,512]{2,1,0:T(8,128)(2,1)}, bf16[2,248,512]{2,1,0:T(8,128)(2,1)S(1)}, u32[]{:S(2)}, u32[]{:S(2)}) %collective-permute-start) | collective-permute-done | bytes 507936 | tf_op jit(solution)/shard_map/ppermute | solution.py:541
  68.0 23.7 %experts.3 = (bf16[2,248,512]{2,1,0:T(8,128)(2,1)}, bf16[2,248,512]{2,1,0:T(8,128)(2,1)}, bf16[2,248,512]{2,1,0:T(8,128)(2,1)}, bf16[2,248,512]{2,1,0:T(8,128)(2...) custom-call(s32[3]{0:T(128)} %pad_add_fusion.sel_ref, ...), custom_call_target="tpu_custom_call" | custom-call | flops 16000000000 | bytes 4096 | tf_op jit(solution)/shard_map/experts/pallas_call | solution.py:346
  92.9 15.6 %experts.4 = (bf16[2,248,512]{2,1,0:T(8,128)(2,1)}, bf16[2,248,512]{2,1,0:T(8,128)(2,1)}, bf16[4,512,512]{2,1,0:T(8,128)(2,1)}, bf16[4,512,512]{2,1,0:T(8,128)(2...) custom-call(s32[3]{0:T(128)} %pad_add_fusion.sel_ref, ...), custom_call_target="tpu_custom_call" | custom-call | flops 10000000000 | bytes 4096 | tf_op jit(solution)/shard_map/experts/pallas_call | solution.py:346
  108.5 3.3 %collective-permute-done.4.rest_1_ = bf16[2,248,512]{2,1,0:T(8,128)(2,1)S(1)} collective-permute-done((bf16[2,248,512]{2,1,0:T(8,128)(2,1)}, bf16[2,248,512]{2,1,0:T(8,128)(2,1)S(1)}, u32[]{:S(2)}, u32[]{:S(2)}) %collective-permute-start.4) | collective-permute-done | bytes 507936 | tf_op jit(solution)/shard_map/ppermute | solution.py:541
  112.8 15.3 %experts.5 = (bf16[2,248,512]{2,1,0:T(8,128)(2,1)}, bf16[2,248,512]{2,1,0:T(8,128)(2,1)}, bf16[4,512,512]{2,1,0:T(8,128)(2,1)}, bf16[4,512,512]{2,1,0:T(8,128)(2...) custom-call(s32[3]{0:T(128)} %pad_add_fusion.sel_ref, ...), custom_call_target="tpu_custom_call" | custom-call | flops 10000000000 | bytes 4096 | tf_op jit(solution)/shard_map/experts/pallas_call | solution.py:346
  128.7 3.9 %collective-permute-done.13 = bf16[4,512,512]{2,1,0:T(8,128)(2,1)S(1)} collective-permute-done((bf16[4,512,512]{2,1,0:T(8,128)(2,1)}, bf16[4,512,512]{2,1,0:T(8,128)(2,1)S(1)}, u32[]{:S(2)}, u32[]{:S(2)}) %collective-permute-start.13) | collective-permute-done | bytes 2097184 | tf_op jit(solution)/shard_map/ppermute | solution.py:541
  132.5 2.3 add.84
  134.9 1.6 collective-permute-start.14
  137.1 1.4 collective-permute-start.7
  138.5 2.2 collective-permute-start.9
  141.6 1.5 collective-permute-start.16
  143.9 30.0 %collective-permute-done.7.rest_2_ = bf16[2,248,512]{2,1,0:T(8,128)(2,1)S(1)} collective-permute-done((bf16[2,248,512]{2,1,0:T(8,128)(2,1)S(1)}, bf16[2,248,512]{2,1,0:T(8,128)(2,1)S(1)}, u32[]{:S(2)}, u32[]{:S(2)}) %collective-permute-start.7) | collective-permute-done | bytes 507936 | tf_op jit(solution)/shard_map/ppermute | solution.py:541
  173.9 10.7 %collective-permute-start.10 = (bf16[2,248,512]{2,1,0:T(8,128)(2,1)}, bf16[2,248,512]{2,1,0:T(8,128)(2,1)}, u32[]{:S(2)}, u32[]{:S(2)}) collective-permute-start(bf16[2,248,512]{2,1,0:T(8,128)(2,1)} %get-tuple-element.108), channel_id=1, source_target_pairs={{0,1},{1,0},{2,3},{3,2},{4,5},{5,4},{6,7},{7,6},{8,9},{9,8},{10,11... | collective-permute-start | bytes 1523720 | tf_op jit(solution)/shard_map/ppermute | solution.py:541
  184.8 1.5 collective-permute-start.17
  187.7 25.2 %attention_backward.1 = (bf16[4,197,512]{2,1,0:T(8,128)(2,1)}, bf16[8,2,16,2176]{3,2,1,0:T(8,128)(2,1)}, bf16[8,2,16,2176]{3,2,1,0:T(8,128)(2,1)}) custom-call(s32[2]{0:T(128)} %pad_add_fusion.1.place_ref, f32[40,128]{1,0:T(8,128)} %pad_maximum_fusion.bias_ref, bf16[4,197,512]{2,1,0:T(8,128)(2,1)} %copy.40.tok_ref, bf16[4,197,512]{2,1,0:T(8,128)(2,1)} %copy.39.cot_ref, ...), custom_call_target="tpu_custom_call" | custom-call | flops 24999999488 | bytes 4096 | tf_op jit(solution)/shard_map/attention_backward/pallas_call | solution.py:504
  213.1 1.4 copy-done.2
  214.6 2.4 collective-permute-start.12
  217.1 1.5 collective-permute-start.35
  221.3 6.6 %collective-permute-done.23 = bf16[2,2,16,2176]{3,2,1,0:T(8,128)(2,1)S(1)} collective-permute-done((bf16[2,2,16,2176]{3,2,1,0:T(8,128)(2,1)S(1)}, bf16[2,2,16,2176]{3,2,1,0:T(8,128)(2,1)S(1)}, u32[]{:S(2)}, u32[]{:S(2)}) %collective-permute-start.23) | collective-permute-done | bytes 278560 | tf_op jit(solution)/shard_map/ppermute | solution.py:541
  228.6 9.2 %collective-permute-done.20 = bf16[2,2,16,2176]{3,2,1,0:T(8,128)(2,1)S(1)} collective-permute-done((bf16[2,2,16,2176]{3,2,1,0:T(8,128)(2,1)S(1)}, bf16[2,2,16,2176]{3,2,1,0:T(8,128)(2,1)S(1)}, u32[]{:S(2)}, u32[]{:S(2)}) %collective-permute-start.20) | collective-permute-done | bytes 278560 | tf_op jit(solution)/shard_map/ppermute | solution.py:541
  238.5 1.5 collective-permute-done.24
  240.0 3.0 collective-permute-done.21
  245.2 2.4 collective-permute-start.27
  247.5 1.5 collective-permute-start.43
  249.6 1.5 collective-permute-start.36
  251.7 1.5 collective-permute-start.28
  253.2 5.4 %collective-permute-done.43.refs_2_ = bf16[1,512,512]{2,1,0:T(8,128)(2,1)S(1)} collective-permute-done((bf16[1,512,512]{2,1,0:T(8,128)(2,1)S(1)}, bf16[1,512,512]{2,1,0:T(8,128)(2,1)S(1)}, u32[]{:S(2)}, u32[]{:S(2)}) %collective-permute-start.43) | collective-permute-done | bytes 524320 | tf_op jit(solution)/shard_map/ppermute | solution.py:541
  258.7 1.5 collective-permute-start.29
  260.2 3.7 %collective-permute-done.42.refs_1_ = bf16[1,512,512]{2,1,0:T(8,128)(2,1)S(1)} collective-permute-done((bf16[1,512,512]{2,1,0:T(8,128)(2,1)S(1)}, bf16[1,512,512]{2,1,0:T(8,128)(2,1)S(1)}, u32[]{:S(2)}, u32[]{:S(2)}) %collective-permute-start.42) | collective-permute-done | bytes 524320 | tf_op jit(solution)/shard_map/ppermute | solution.py:541
  263.9 19.2 %collective-permute-done.28.refs_1_ = bf16[16,2176]{1,0:T(8,128)(2,1)S(1)} collective-permute-done((bf16[16,2176]{1,0:T(8,128)(2,1)S(1)}, bf16[16,2176]{1,0:T(8,128)(2,1)S(1)}, u32[]{:S(2)}, u32[]{:S(2)}) %collective-permute-start.28) | collective-permute-done | bytes 69664 | tf_op jit(solution)/shard_map/ppermute | solution.py:541
  285.3 1.6 collective-permute-start.44
  287.7 5.9 %combine_output.1 = bf16[4,197,512]{2,1,0:T(8,128)(2,1)} custom-call(f32[4,197,512]{2,1,0:T(8,128)} %get-tuple-element.123.resid_ref, f32[4,197,8]{2,1,0:T(8,128)} %get-tuple-element.78.slot_col_ref, f32[4,197,8]{2,1,0:T(8,128)} %get-tuple-element.79.gate_col_ref, bf16[2,248,512]{2,1,0:T(8,128)(2,1)} %get-tuple-element.87.rest_0_, ...), custom_call_target="tpu_custom_call" | custom-call | flops 5000000000 | bytes 4096 | tf_op jit(solution)/shard_map/combine_output/pallas_call | solution.py:528
  293.7 2.6 copy.44
  296.3 1.3 copy.45
  298.2 2.1 parameter_gradient_results.1
  301.5 1.4 slice_bitcast_fusion.3
  302.9 7.4 %expert_gradient_result.2 = f32[2,512,2048]{2,1,0:T(8,128)} custom-call(s32[2]{0:T(128)} %get-tuple-element.172.place_ref, bf16[1,512,512]{2,1,0:T(8,128)(2,1)} %copy-done.6, bf16[1,512,512]{2,1,0:T(8,128)(2,1)} %copy-done.21, bf16[1,512,512]{2,1,0:T(8,128)(2,1)} %collective-permute-done.36.refs_2_, bf16[1,512,512]{2,1,0:T(8,128)(2,1)} %copy-done.24, ...), custom_call_target="tpu_custom_call" | custom-call | flops 5000000000 | bytes 4096 | tf_op jit(solution)/shard_map/expert_gradient_result/pallas_call | solution.py:577
  311.4 7.4 %expert_gradient_result.3 = f32[2,2048,512]{2,1,0:T(8,128)} custom-call(s32[2]{0:T(128)} %get-tuple-element.173.place_ref, bf16[1,512,512]{2,1,0:T(8,128)(2,1)} %copy-done.5, bf16[1,512,512]{2,1,0:T(8,128)(2,1)} %copy-done.23, bf16[1,512,512]{2,1,0:T(8,128)(2,1)} %copy-done.22, bf16[1,512,512]{2,1,0:T(8,128)(2,1)} %collective-permute-done.44.refs_3_, ...), custom_call_target="tpu_custom_call" | custom-call | flops 5000000000 | bytes 4096 | tf_op jit(solution)/shard_map/expert_gradient_result/pallas_call | solution.py:577
  (207 shorter events, 28.7 us)
Async XLA Ops:
  0.6 40.4 %collective-permute-start.2 = (bf16[4,197,512]{2,0,1:T(4,128)(2,1)}, bf16[4,197,512]{2,0,1:T(4,128)(2,1)S(1)}, u32[]{:S(2)}, u32[]{:S(2)}) collective-permute-start(bf16[4,197,512]{2,0,1:T(4,128)(2,1)} %param.29), channel_id=1, source_target_pairs={{0,2},{1,3},{2,0},{3,1},{4,6},{5,7},{6,4},{7,5},{8,10},{9,11},{10,... | collective-permute-start | bytes 2420744 | tf_op jit(solution)/shard_map/ppermute | solution.py:541
  13.2 39.4 %collective-permute-start.3 = (bf16[2,248,512]{2,1,0:T(8,128)(2,1)}, bf16[2,248,512]{2,1,0:T(8,128)(2,1)S(1)}, u32[]{:S(2)}, u32[]{:S(2)}) collective-permute-start(bf16[2,248,512]{2,1,0:T(8,128)(2,1)} %get-tuple-element.86), channel_id=1, source_target_pairs={{0,1},{1,0},{2,3},{3,2},{4,5},{5,4},{6,7},{7,6},{8,9},{9,8},{10,11... | collective-permute-start | bytes 1523720 | tf_op jit(solution)/shard_map/ppermute | solution.py:541
  31.1 36.1 %collective-permute-start = (bf16[2,248,512]{2,1,0:T(8,128)(2,1)}, bf16[2,248,512]{2,1,0:T(8,128)(2,1)S(1)}, u32[]{:S(2)}, u32[]{:S(2)}) collective-permute-start(bf16[2,248,512]{2,1,0:T(8,128)(2,1)} %get-tuple-element.81), channel_id=1, source_target_pairs={{0,1},{1,0},{2,3},{3,2},{4,5},{5,4},{6,7},{7,6},{8,9},{9,8},{10,11... | collective-permute-start | bytes 1523720 | tf_op jit(solution)/shard_map/ppermute | solution.py:541
  31.7 13.7 %collective-permute-start.1 = (f32[2,4,8,197]{3,2,1,0:T(8,128)S(1)}, f32[2,4,8,197]{3,2,1,0:T(8,128)S(1)}, u32[]{:S(2)}, u32[]{:S(2)}) collective-permute-start(f32[2,4,8,197]{3,2,1,0:T(8,128)S(1)} %copy-done.49), channel_id=1, source_target_pairs={{0,2},{1,3},{2,0},{3,1},{4,6},{5,7},{6,4},{7,5},{8,10},{9,11},{10,... | collective-permute-start | bytes 151304 | tf_op jit(solution)/shard_map/ppermute | solution.py:541
  49.2 62.6 %collective-permute-start.8 = (bf16[2,248,512]{2,1,0:T(8,128)(2,1)}, bf16[2,248,512]{2,1,0:T(8,128)(2,1)S(1)}, u32[]{:S(2)}, u32[]{:S(2)}) collective-permute-start(bf16[2,248,512]{2,1,0:T(8,128)(2,1)} %get-tuple-element.84), channel_id=1, source_target_pairs={{0,1},{1,0},{2,3},{3,2},{4,5},{5,4},{6,7},{7,6},{8,9},{9,8},{10,11... | collective-permute-start | bytes 1523720 | tf_op jit(solution)/shard_map/ppermute | solution.py:541
  51.6 40.2 %collective-permute-start.5 = (bf16[2,248,512]{2,1,0:T(8,128)(2,1)S(1)}, bf16[2,248,512]{2,1,0:T(8,128)(2,1)S(1)}, u32[]{:S(2)}, u32[]{:S(2)}) collective-permute-start(bf16[2,248,512]{2,1,0:T(8,128)(2,1)S(1)} %copy-done.33), channel_id=1, source_target_pairs={{0,2},{1,3},{2,0},{3,1},{4,6},{5,7},{6,4},{7,5},{8,10},{9,11},{10,... | collective-permute-start | bytes 1523720 | tf_op jit(solution)/shard_map/ppermute | solution.py:541
  91.7 20.1 %collective-permute-start.4 = (bf16[2,248,512]{2,1,0:T(8,128)(2,1)}, bf16[2,248,512]{2,1,0:T(8,128)(2,1)S(1)}, u32[]{:S(2)}, u32[]{:S(2)}) collective-permute-start(bf16[2,248,512]{2,1,0:T(8,128)(2,1)} %get-tuple-element.90), channel_id=1, source_target_pairs={{0,1},{1,0},{2,3},{3,2},{4,5},{5,4},{6,7},{7,6},{8,9},{9,8},{10,11... | collective-permute-start | bytes 1523720 | tf_op jit(solution)/shard_map/ppermute | solution.py:541
  91.8 20.0 %collective-permute-start.6 = (bf16[2,248,512]{2,1,0:T(8,128)(2,1)S(1)}, bf16[2,248,512]{2,1,0:T(8,128)(2,1)S(1)}, u32[]{:S(2)}, u32[]{:S(2)}) collective-permute-start(bf16[2,248,512]{2,1,0:T(8,128)(2,1)S(1)} %copy-done.30), channel_id=1, source_target_pairs={{0,3},{1,2},{2,1},{3,0},{4,7},{5,6},{6,5},{7,4},{8,11},{9,10},{10,... | collective-permute-start | bytes 1523720 | tf_op jit(solution)/shard_map/ppermute | solution.py:541
  128.1 4.4 %collective-permute-start.13 = (bf16[4,512,512]{2,1,0:T(8,128)(2,1)}, bf16[4,512,512]{2,1,0:T(8,128)(2,1)S(1)}, u32[]{:S(2)}, u32[]{:S(2)}) collective-permute-start(bf16[4,512,512]{2,1,0:T(8,128)(2,1)} %get-tuple-element.120), channel_id=1, source_target_pairs={{0,4},{4,0},{8,12},{12,8},{16,20},{20,16},{24,28},{28,24},{1,5},{5... | collective-permute-start | bytes 6291464 | tf_op jit(solution)/shard_map/ppermute | solution.py:541
  128.2 12.5 %collective-permute-start.15 = (bf16[4,512,512]{2,1,0:T(8,128)(2,1)}, bf16[4,512,512]{2,1,0:T(8,128)(2,1)S(1)}, u32[]{:S(2)}, u32[]{:S(2)}) collective-permute-start(bf16[4,512,512]{2,1,0:T(8,128)(2,1)} %get-tuple-element.122), channel_id=1, source_target_pairs={{0,4},{4,0},{8,12},{12,8},{16,20},{20,16},{24,28},{28,24},{1,5},{5... | collective-permute-start | bytes 6291464 | tf_op jit(solution)/shard_map/ppermute | solution.py:541
  134.9 49.7 %collective-permute-start.14 = (bf16[2,512,512]{2,1,0:T(8,128)(2,1)S(1)}, bf16[2,512,512]{2,1,0:T(8,128)(2,1)S(1)}, u32[]{:S(2)}, u32[]{:S(2)}) collective-permute-start(bf16[2,512,512]{2,1,0:T(8,128)(2,1)S(1)} %slice.117), channel_id=1, source_target_pairs={{0,8},{4,12},{8,0},{12,4},{16,24},{20,28},{24,16},{28,20},{1,9},{5... | collective-permute-start | bytes 3145736 | tf_op jit(solution)/shard_map/ppermute | solution.py:541
  137.1 36.7 %collective-permute-start.7 = (bf16[2,248,512]{2,1,0:T(8,128)(2,1)S(1)}, bf16[2,248,512]{2,1,0:T(8,128)(2,1)S(1)}, u32[]{:S(2)}, u32[]{:S(2)}) collective-permute-start(bf16[2,248,512]{2,1,0:T(8,128)(2,1)S(1)} %copy-done.35), channel_id=1, source_target_pairs={{0,2},{1,3},{2,0},{3,1},{4,6},{5,7},{6,4},{7,5},{8,10},{9,11},{10,... | collective-permute-start | bytes 1523720 | tf_op jit(solution)/shard_map/ppermute | solution.py:541
  138.5 35.4 %collective-permute-start.9 = (bf16[2,248,512]{2,1,0:T(8,128)(2,1)S(1)}, bf16[2,248,512]{2,1,0:T(8,128)(2,1)S(1)}, u32[]{:S(2)}, u32[]{:S(2)}) collective-permute-start(bf16[2,248,512]{2,1,0:T(8,128)(2,1)S(1)} %copy-done.39), channel_id=1, source_target_pairs={{0,3},{1,2},{2,1},{3,0},{4,7},{5,6},{6,5},{7,4},{8,11},{9,10},{10,... | collective-permute-start | bytes 1523720 | tf_op jit(solution)/shard_map/ppermute | solution.py:541
  141.6 44.7 %collective-permute-start.16 = (bf16[2,512,512]{2,1,0:T(8,128)(2,1)S(1)}, bf16[2,512,512]{2,1,0:T(8,128)(2,1)S(1)}, u32[]{:S(2)}, u32[]{:S(2)}) collective-permute-start(bf16[2,512,512]{2,1,0:T(8,128)(2,1)S(1)} %slice.119), channel_id=1, source_target_pairs={{0,16},{4,20},{8,24},{12,28},{16,0},{20,4},{24,8},{28,12},{1,17},{... | collective-permute-start | bytes 3145736 | tf_op jit(solution)/shard_map/ppermute | solution.py:541
  173.9 39.2 %collective-permute-start.10 = (bf16[2,248,512]{2,1,0:T(8,128)(2,1)}, bf16[2,248,512]{2,1,0:T(8,128)(2,1)}, u32[]{:S(2)}, u32[]{:S(2)}) collective-permute-start(bf16[2,248,512]{2,1,0:T(8,128)(2,1)} %get-tuple-element.108), channel_id=1, source_target_pairs={{0,1},{1,0},{2,3},{3,2},{4,5},{5,4},{6,7},{7,6},{8,9},{9,8},{10,11... | collective-permute-start | bytes 1523720 | tf_op jit(solution)/shard_map/ppermute | solution.py:541
  184.6 28.5 %collective-permute-start.11 = (bf16[2,248,512]{2,1,0:T(8,128)(2,1)}, bf16[2,248,512]{2,1,0:T(8,128)(2,1)}, u32[]{:S(2)}, u32[]{:S(2)}) collective-permute-start(bf16[2,248,512]{2,1,0:T(8,128)(2,1)} %get-tuple-element.110), channel_id=1, source_target_pairs={{0,2},{1,3},{2,0},{3,1},{4,6},{5,7},{6,4},{7,5},{8,10},{9,11},{10,... | collective-permute-start | bytes 1523720 | tf_op jit(solution)/shard_map/ppermute | solution.py:541
  184.8 28.2 %collective-permute-start.17 = (bf16[1,512,512]{2,1,0:T(8,128)(2,1)S(1)}, bf16[1,512,512]{2,1,0:T(8,128)(2,1)S(1)}, u32[]{:S(2)}, u32[]{:S(2)}) collective-permute-start(bf16[1,512,512]{2,1,0:T(8,128)(2,1)S(1)} %slice.121), channel_id=1, source_target_pairs={{0,16},{4,20},{8,24},{12,28},{16,0},{20,4},{24,8},{28,12},{1,17},{... | collective-permute-start | bytes 1572872 | tf_op jit(solution)/shard_map/ppermute | solution.py:541
  187.2 25.8 %collective-permute-start.18 = (bf16[1,512,512]{2,1,0:T(8,128)(2,1)}, bf16[1,512,512]{2,1,0:T(8,128)(2,1)S(1)}, u32[]{:S(2)}, u32[]{:S(2)}) collective-permute-start(bf16[1,512,512]{2,1,0:T(8,128)(2,1)} %slice.123), channel_id=1, source_target_pairs={{0,8},{4,12},{8,0},{12,4},{16,24},{20,28},{24,16},{28,20},{1,9},{5... | collective-permute-start | bytes 1572872 | tf_op jit(solution)/shard_map/ppermute | solution.py:541
  214.6 4.2 %collective-permute-start.22 = (bf16[4,2,16,2176]{3,2,1,0:T(8,128)(2,1)S(1)}, bf16[4,2,16,2176]{3,2,1,0:T(8,128)(2,1)S(1)}, u32[]{:S(2)}, u32[]{:S(2)}) collective-permute-start(bf16[4,2,16,2176]{3,2,1,0:T(8,128)(2,1)S(1)} %slice.102), channel_id=1, source_target_pairs={{0,4},{4,0},{8,12},{12,8},{16,20},{20,16},{24,28},{28,24},{1,5},{5... | collective-permute-start | bytes 1671176 | tf_op jit(solution)/shard_map/ppermute | solution.py:541
  214.6 28.4 %collective-permute-start.12 = (bf16[2,248,512]{2,1,0:T(8,128)(2,1)S(1)}, bf16[2,248,512]{2,1,0:T(8,128)(2,1)S(1)}, u32[]{:S(2)}, u32[]{:S(2)}) collective-permute-start(bf16[2,248,512]{2,1,0:T(8,128)(2,1)S(1)} %copy-done.28), channel_id=1, source_target_pairs={{0,3},{1,2},{2,1},{3,0},{4,7},{5,6},{6,5},{7,4},{8,11},{9,10},{10,... | collective-permute-start | bytes 1523720 | tf_op jit(solution)/shard_map/ppermute | solution.py:541
  217.1 32.0 %collective-permute-start.35 = (bf16[1,512,512]{2,1,0:T(8,128)(2,1)S(1)}, bf16[1,512,512]{2,1,0:T(8,128)(2,1)S(1)}, u32[]{:S(2)}, u32[]{:S(2)}) collective-permute-start(bf16[1,512,512]{2,1,0:T(8,128)(2,1)S(1)} %slice_add_fusion.4.refs_0_), channel_id=1, source_target_pairs={{0,8},{4,12},{8,0},{12,4},{16,24},{20,28},{24,16},{28,20},{1,9},{5... | collective-permute-start | bytes 1572872 | tf_op jit(solution)/shard_map/ppermute | solution.py:541
  218.7 2.0 collective-permute-start.19
  218.8 9.1 %collective-permute-start.23 = (bf16[2,2,16,2176]{3,2,1,0:T(8,128)(2,1)S(1)}, bf16[2,2,16,2176]{3,2,1,0:T(8,128)(2,1)S(1)}, u32[]{:S(2)}, u32[]{:S(2)}) collective-permute-start(bf16[2,2,16,2176]{3,2,1,0:T(8,128)(2,1)S(1)} %slice.129), channel_id=1, source_target_pairs={{0,16},{4,20},{8,24},{12,28},{16,0},{20,4},{24,8},{28,12},{1,17},{... | collective-permute-start | bytes 835592 | tf_op jit(solution)/shard_map/ppermute | solution.py:541
  220.8 17.0 %collective-permute-start.20 = (bf16[2,2,16,2176]{3,2,1,0:T(8,128)(2,1)S(1)}, bf16[2,2,16,2176]{3,2,1,0:T(8,128)(2,1)S(1)}, u32[]{:S(2)}, u32[]{:S(2)}) collective-permute-start(bf16[2,2,16,2176]{3,2,1,0:T(8,128)(2,1)S(1)} %slice.125), channel_id=1, source_target_pairs={{0,8},{4,12},{8,0},{12,4},{16,24},{20,28},{24,16},{28,20},{1,9},{5... | collective-permute-start | bytes 835592 | tf_op jit(solution)/shard_map/ppermute | solution.py:541
  228.0 12.0 %collective-permute-start.24 = (bf16[1,2,16,2176]{3,2,1,0:T(8,128)(2,1)S(1)}, bf16[1,2,16,2176]{3,2,1,0:T(8,128)(2,1)S(1)}, u32[]{:S(2)}, u32[]{:S(2)}) collective-permute-start(bf16[1,2,16,2176]{3,2,1,0:T(8,128)(2,1)S(1)} %slice.131), channel_id=1, source_target_pairs={{0,8},{4,12},{8,0},{12,4},{16,24},{20,28},{24,16},{28,20},{1,9},{5... | collective-permute-start | bytes 417800 | tf_op jit(solution)/shard_map/ppermute | solution.py:541
  237.9 5.1 %collective-permute-start.21 = (bf16[1,2,16,2176]{3,2,1,0:T(8,128)(2,1)S(1)}, bf16[1,2,16,2176]{3,2,1,0:T(8,128)(2,1)S(1)}, u32[]{:S(2)}, u32[]{:S(2)}) collective-permute-start(bf16[1,2,16,2176]{3,2,1,0:T(8,128)(2,1)S(1)} %slice.127), channel_id=1, source_target_pairs={{0,16},{4,20},{8,24},{12,28},{16,0},{20,4},{24,8},{28,12},{1,17},{... | collective-permute-start | bytes 417800 | tf_op jit(solution)/shard_map/ppermute | solution.py:541
  243.1 6.6 %collective-permute-start.25 = (bf16[16,2176]{1,0:T(8,128)(2,1)S(1)}, bf16[16,2176]{1,0:T(8,128)(2,1)S(1)}, u32[]{:S(2)}, u32[]{:S(2)}) collective-permute-start(bf16[16,2176]{1,0:T(8,128)(2,1)S(1)} %slice_bitcast_fusion.2), channel_id=1, source_target_pairs={{0,1},{1,0},{2,3},{3,2},{4,5},{5,4},{6,7},{7,6},{8,9},{9,8},{10,11... | collective-permute-start | bytes 208904 | tf_op jit(solution)/shard_map/ppermute | solution.py:541
  244.2 6.8 %collective-permute-start.26 = (bf16[16,2176]{1,0:T(8,128)(2,1)S(1)}, bf16[16,2176]{1,0:T(8,128)(2,1)S(1)}, u32[]{:S(2)}, u32[]{:S(2)}) collective-permute-start(bf16[16,2176]{1,0:T(8,128)(2,1)S(1)} %get-tuple-element.165), channel_id=1, source_target_pairs={{0,2},{1,3},{2,0},{3,1},{4,6},{5,7},{6,4},{7,5},{8,10},{9,11},{10,... | collective-permute-start | bytes 208904 | tf_op jit(solution)/shard_map/ppermute | solution.py:541
  245.2 6.5 %collective-permute-start.27 = (bf16[16,2176]{1,0:T(8,128)(2,1)S(1)}, bf16[16,2176]{1,0:T(8,128)(2,1)S(1)}, u32[]{:S(2)}, u32[]{:S(2)}) collective-permute-start(bf16[16,2176]{1,0:T(8,128)(2,1)S(1)} %get-tuple-element.166), channel_id=1, source_target_pairs={{0,3},{1,2},{2,1},{3,0},{4,7},{5,6},{6,5},{7,4},{8,11},{9,10},{10,... | collective-permute-start | bytes 208904 | tf_op jit(solution)/shard_map/ppermute | solution.py:541
  247.5 11.1 %collective-permute-start.43 = (bf16[1,512,512]{2,1,0:T(8,128)(2,1)S(1)}, bf16[1,512,512]{2,1,0:T(8,128)(2,1)S(1)}, u32[]{:S(2)}, u32[]{:S(2)}) collective-permute-start(bf16[1,512,512]{2,1,0:T(8,128)(2,1)S(1)} %slice_add_fusion.5.refs_0_), channel_id=1, source_target_pairs={{0,8},{4,12},{8,0},{12,4},{16,24},{20,28},{24,16},{28,20},{1,9},{5... | collective-permute-start | bytes 1572872 | tf_op jit(solution)/shard_map/ppermute | solution.py:541
  249.1 14.9 %collective-permute-start.42 = (bf16[1,512,512]{2,1,0:T(8,128)(2,1)S(1)}, bf16[1,512,512]{2,1,0:T(8,128)(2,1)S(1)}, u32[]{:S(2)}, u32[]{:S(2)}) collective-permute-start(bf16[1,512,512]{2,1,0:T(8,128)(2,1)S(1)} %slice_add_fusion.5.refs_0_), channel_id=1, source_target_pairs={{0,16},{4,20},{8,24},{12,28},{16,0},{20,4},{24,8},{28,12},{1,17},{... | collective-permute-start | bytes 1572872 | tf_op jit(solution)/shard_map/ppermute | solution.py:541
  249.6 33.5 %collective-permute-start.36 = (bf16[1,512,512]{2,1,0:T(8,128)(2,1)S(1)}, bf16[1,512,512]{2,1,0:T(8,128)(2,1)}, u32[]{:S(2)}, u32[]{:S(2)}) collective-permute-start(bf16[1,512,512]{2,1,0:T(8,128)(2,1)S(1)} %slice_add_fusion.4.refs_0_), channel_id=1, source_target_pairs={{0,16},{4,20},{8,24},{12,28},{16,0},{20,4},{24,8},{28,12},{1,17},{... | collective-permute-start | bytes 1572872 | tf_op jit(solution)/shard_map/ppermute | solution.py:541
  251.1 33.4 %collective-permute-start.37 = (bf16[1,512,512]{2,1,0:T(8,128)(2,1)S(1)}, bf16[1,512,512]{2,1,0:T(8,128)(2,1)S(1)}, u32[]{:S(2)}, u32[]{:S(2)}) collective-permute-start(bf16[1,512,512]{2,1,0:T(8,128)(2,1)S(1)} %collective-permute-done.35.refs_1_), channel_id=1, source_target_pairs={{0,16},{4,20},{8,24},{12,28},{16,0},{20,4},{24,8},{28,12},{1,17},{... | collective-permute-start | bytes 1572872 | tf_op jit(solution)/shard_map/ppermute | solution.py:541
  251.7 31.4 %collective-permute-start.28 = (bf16[16,2176]{1,0:T(8,128)(2,1)S(1)}, bf16[16,2176]{1,0:T(8,128)(2,1)S(1)}, u32[]{:S(2)}, u32[]{:S(2)}) collective-permute-start(bf16[16,2176]{1,0:T(8,128)(2,1)S(1)} %fusion.2.refs_0_), channel_id=1, source_target_pairs={{0,16},{4,20},{8,24},{12,28},{16,0},{20,4},{24,8},{28,12},{1,17},{... | collective-permute-start | bytes 208904 | tf_op jit(solution)/shard_map/ppermute | solution.py:541
  258.7 25.0 %collective-permute-start.29 = (bf16[16,2176]{1,0:T(8,128)(2,1)S(1)}, bf16[16,2176]{1,0:T(8,128)(2,1)S(1)}, u32[]{:S(2)}, u32[]{:S(2)}) collective-permute-start(bf16[16,2176]{1,0:T(8,128)(2,1)S(1)} %fusion.2.refs_0_), channel_id=1, source_target_pairs={{0,8},{4,12},{8,0},{12,4},{16,24},{20,28},{24,16},{28,20},{1,9},{5... | collective-permute-start | bytes 208904 | tf_op jit(solution)/shard_map/ppermute | solution.py:541
  263.9 21.0 %collective-permute-start.31 = (bf16[16,2176]{1,0:T(8,128)(2,1)S(1)}, bf16[16,2176]{1,0:T(8,128)(2,1)S(1)}, u32[]{:S(2)}, u32[]{:S(2)}) collective-permute-start(bf16[16,2176]{1,0:T(8,128)(2,1)S(1)} %fusion.2.refs_0_), channel_id=1, source_target_pairs={{0,4},{4,0},{8,12},{12,8},{16,20},{20,16},{24,28},{28,24},{1,5},{5... | collective-permute-start | bytes 208904 | tf_op jit(solution)/shard_map/ppermute | solution.py:541
  283.1 3.8 %collective-permute-start.32 = (bf16[16,2176]{1,0:T(8,128)(2,1)S(1)}, bf16[16,2176]{1,0:T(8,128)(2,1)S(1)}, u32[]{:S(2)}, u32[]{:S(2)}) collective-permute-start(bf16[16,2176]{1,0:T(8,128)(2,1)S(1)} %collective-permute-done.28.refs_1_), channel_id=1, source_target_pairs={{0,4},{4,0},{8,12},{12,8},{16,20},{20,16},{24,28},{28,24},{1,5},{5... | collective-permute-start | bytes 208904 | tf_op jit(solution)/shard_map/ppermute | solution.py:541
  283.1 4.6 %collective-permute-start.30 = (bf16[16,2176]{1,0:T(8,128)(2,1)S(1)}, bf16[16,2176]{1,0:T(8,128)(2,1)S(1)}, u32[]{:S(2)}, u32[]{:S(2)}) collective-permute-start(bf16[16,2176]{1,0:T(8,128)(2,1)S(1)} %collective-permute-done.28.refs_1_), channel_id=1, source_target_pairs={{0,8},{4,12},{8,0},{12,4},{16,24},{20,28},{24,16},{28,20},{1,9},{5... | collective-permute-start | bytes 208904 | tf_op jit(solution)/shard_map/ppermute | solution.py:541
  284.5 15.9 %collective-permute-start.38 = (bf16[1,512,512]{2,1,0:T(8,128)(2,1)S(1)}, bf16[1,512,512]{2,1,0:T(8,128)(2,1)}, u32[]{:S(2)}, u32[]{:S(2)}) collective-permute-start(bf16[1,512,512]{2,1,0:T(8,128)(2,1)S(1)} %slice_add_fusion.4.refs_0_), channel_id=1, source_target_pairs={{0,4},{4,0},{8,12},{12,8},{16,20},{20,16},{24,28},{28,24},{1,5},{5... | collective-permute-start | bytes 1572872 | tf_op jit(solution)/shard_map/ppermute | solution.py:541
  284.9 16.5 %collective-permute-start.39 = (bf16[1,512,512]{2,1,0:T(8,128)(2,1)S(1)}, bf16[1,512,512]{2,1,0:T(8,128)(2,1)}, u32[]{:S(2)}, u32[]{:S(2)}) collective-permute-start(bf16[1,512,512]{2,1,0:T(8,128)(2,1)S(1)} %collective-permute-done.35.refs_1_), channel_id=1, source_target_pairs={{0,4},{4,0},{8,12},{12,8},{16,20},{20,16},{24,28},{28,24},{1,5},{5... | collective-permute-start | bytes 1572872 | tf_op jit(solution)/shard_map/ppermute | solution.py:541
  285.3 15.6 %collective-permute-start.44 = (bf16[1,512,512]{2,1,0:T(8,128)(2,1)S(1)}, bf16[1,512,512]{2,1,0:T(8,128)(2,1)}, u32[]{:S(2)}, u32[]{:S(2)}) collective-permute-start(bf16[1,512,512]{2,1,0:T(8,128)(2,1)S(1)} %collective-permute-done.42.refs_1_), channel_id=1, source_target_pairs={{0,8},{4,12},{8,0},{12,4},{16,24},{20,28},{24,16},{28,20},{1,9},{5... | collective-permute-start | bytes 1572872 | tf_op jit(solution)/shard_map/ppermute | solution.py:541
  286.9 14.1 %collective-permute-start.40 = (bf16[1,512,512]{2,1,0:T(8,128)(2,1)}, bf16[1,512,512]{2,1,0:T(8,128)(2,1)}, u32[]{:S(2)}, u32[]{:S(2)}) collective-permute-start(bf16[1,512,512]{2,1,0:T(8,128)(2,1)} %collective-permute-done.36.refs_2_), channel_id=1, source_target_pairs={{0,4},{4,0},{8,12},{12,8},{16,20},{20,16},{24,28},{28,24},{1,5},{5... | collective-permute-start | bytes 1572872 | tf_op jit(solution)/shard_map/ppermute | solution.py:541
  287.7 9.8 %collective-permute-start.34 = (bf16[16,2176]{1,0:T(8,128)(2,1)S(1)}, bf16[16,2176]{1,0:T(8,128)(2,1)S(1)}, u32[]{:S(2)}, u32[]{:S(2)}) collective-permute-start(bf16[16,2176]{1,0:T(8,128)(2,1)S(1)} %collective-permute-done.30.refs_3_), channel_id=1, source_target_pairs={{0,4},{4,0},{8,12},{12,8},{16,20},{20,16},{24,28},{28,24},{1,5},{5... | collective-permute-start | bytes 208904 | tf_op jit(solution)/shard_map/ppermute | solution.py:541
  297.6 5.3 %collective-permute-start.41 = (bf16[1,512,512]{2,1,0:T(8,128)(2,1)S(1)}, bf16[1,512,512]{2,1,0:T(8,128)(2,1)}, u32[]{:S(2)}, u32[]{:S(2)}) collective-permute-start(bf16[1,512,512]{2,1,0:T(8,128)(2,1)S(1)} %copy-done.25), channel_id=1, source_target_pairs={{0,4},{4,0},{8,12},{12,8},{16,20},{20,16},{24,28},{28,24},{1,5},{5... | collective-permute-start | bytes 1572872 | tf_op jit(solution)/shard_map/ppermute | solution.py:541
  300.4 10.0 %collective-permute-start.45 = (bf16[1,512,512]{2,1,0:T(8,128)(2,1)S(1)}, bf16[1,512,512]{2,1,0:T(8,128)(2,1)S(1)}, u32[]{:S(2)}, u32[]{:S(2)}) collective-permute-start(bf16[1,512,512]{2,1,0:T(8,128)(2,1)S(1)} %slice_add_fusion.5.refs_0_), channel_id=1, source_target_pairs={{0,4},{4,0},{8,12},{12,8},{16,20},{20,16},{24,28},{28,24},{1,5},{5... | collective-permute-start | bytes 1572872 | tf_op jit(solution)/shard_map/ppermute | solution.py:541
  300.9 9.5 %collective-permute-start.46 = (bf16[1,512,512]{2,1,0:T(8,128)(2,1)S(1)}, bf16[1,512,512]{2,1,0:T(8,128)(2,1)}, u32[]{:S(2)}, u32[]{:S(2)}) collective-permute-start(bf16[1,512,512]{2,1,0:T(8,128)(2,1)S(1)} %collective-permute-done.42.refs_1_), channel_id=1, source_target_pairs={{0,4},{4,0},{8,12},{12,8},{16,20},{20,16},{24,28},{28,24},{1,5},{5... | collective-permute-start | bytes 1572872 | tf_op jit(solution)/shard_map/ppermute | solution.py:541
  301.0 9.4 %collective-permute-start.47 = (bf16[1,512,512]{2,1,0:T(8,128)(2,1)S(1)}, bf16[1,512,512]{2,1,0:T(8,128)(2,1)}, u32[]{:S(2)}, u32[]{:S(2)}) collective-permute-start(bf16[1,512,512]{2,1,0:T(8,128)(2,1)S(1)} %collective-permute-done.43.refs_2_), channel_id=1, source_target_pairs={{0,4},{4,0},{8,12},{12,8},{16,20},{20,16},{24,28},{28,24},{1,5},{5... | collective-permute-start | bytes 1572872 | tf_op jit(solution)/shard_map/ppermute | solution.py:541
  301.4 9.0 %collective-permute-start.48 = (bf16[1,512,512]{2,1,0:T(8,128)(2,1)}, bf16[1,512,512]{2,1,0:T(8,128)(2,1)S(1)}, u32[]{:S(2)}, u32[]{:S(2)}) collective-permute-start(bf16[1,512,512]{2,1,0:T(8,128)(2,1)} %collective-permute-done.44.refs_3_), channel_id=1, source_target_pairs={{0,4},{4,0},{8,12},{12,8},{16,20},{20,16},{24,28},{28,24},{1,5},{5... | collective-permute-start | bytes 1572872 | tf_op jit(solution)/shard_map/ppermute | solution.py:541
  (52 other events, 638.1 us)

commit v4 on v3

--- a/solution.py
+++ b/solution.py
@@ -11,7 +11,7 @@
 NORM_EPS = 1e-06
 BF16 = jnp.bfloat16
 F32 = jnp.float32
-VMEM_LIMIT = 60 * 1024 * 1024
+VMEM_LIMIT = 64 * 1024 * 1024
 GELU_C = 0.7978845608028654
 
 
@@ -86,11 +86,11 @@
     carry = jnp.zeros((experts, 1), F32)
     slots, gate_rows = [], []
     for i in range(n_img):
-        hit0 = expert == routes_ref[0, i : i + 1, :]
-        hit1 = expert == routes_ref[1, i : i + 1, :]
+        hit0 = expert == routes_ref[i, 0:1, :]
+        hit1 = expert == routes_ref[i, 1:2, :]
         member = jnp.where(hit0 | hit1, 1.0, 0.0)
         slot = jnp.where(member > 0.5, dot_nn(member.astype(BF16), tri) + carry, -1.0)
-        gate = jnp.where(hit0, gates_ref[0, i : i + 1, :], jnp.where(hit1, gates_ref[1, i : i + 1, :], 0.0))
+        gate = jnp.where(hit0, gates_ref[i, 0:1, :], jnp.where(hit1, gates_ref[i, 1:2, :], 0.0))
         carry = carry + jnp.sum(member, axis=1, keepdims=True)
         slots.append(slot)
         gate_rows.append(gate)
@@ -125,7 +125,7 @@
         compiler_params=params(),
         cost_estimate=cost(4),
         name="route_and_dispatch_cotangent",
-    )(me, routes.transpose(2, 0, 1), gates.transpose(2, 0, 1), cotangent)
+    )(me, routes.transpose(0, 2, 1), gates.transpose(0, 2, 1), cotangent)
 
 
 def gateway_kernel(exp_dev, info_ref, cot_ref, *out_refs):
@@ -292,8 +292,9 @@
             square = pre * pre
             bent = jnp.tanh(pre * (GELU_C + (GELU_C * 0.044715) * square))
             half = 0.5 + 0.5 * bent
-            act = (pre * half).astype(BF16)
-            slope = half + (pre * (0.5 - 0.5 * bent * bent)) * (GELU_C + (3 * GELU_C * 0.044715) * square)
+            value = pre * half
+            act = value.astype(BF16)
+            slope = half + (value - value * half) * (2 * GELU_C + (6 * GELU_C * 0.044715) * square)
             gpre = (dot_nt(g, w_back) * slope).astype(BF16)
             part_dis, part_out = dot_nt(gpre, w_in), dot_nn(act, w_back)
             if t == 0:
@@ -561,32 +562,34 @@
     return pieces
 
 
-def widen_kernel(exp_dev, count, place_ref, *refs):
-    piece_refs, out_ref = refs[: exp_dev * count], refs[-1]
-    for e in range(exp_dev):
-        for r in range(count):
-            @pl.when((pl.program_id(0) == e) & (pl.program_id(1) == r))
-            def _():
-                out_ref[0] = piece_refs[e * count + r][0].astype(F32)
-
-
-def widen_call(own, other, place, axis, shape):
-    count = len(own)
-    _, m, n = own[0].shape
-    at = (lambda l, r, s: (l ^ s[0], r ^ s[1], 0)) if axis == 0 else (lambda l, r, s: (l ^ s[0], 0, r ^ s[1]))
+def widen_kernel(count, place_ref, *refs):
+    piece_refs, out_ref = refs[:count], refs[-1]
+    for r in range(count):
+        @pl.when(pl.program_id(0) == r)
+        def _():
+            out_ref[0] = piece_refs[r][0].astype(F32)
+
+
+def widen_call(pieces, expert, first, axis, shape, base):
+    count = len(pieces)
+    _, m, n = pieces[0].shape
+    at = (lambda r, s: (s[0], r ^ s[1], 0)) if axis == 0 else (lambda r, s: (s[0], 0, r ^ s[1]))
+    extra = [] if base is None else [base]
     return pl.pallas_call(
-        functools.partial(widen_kernel, 2, count),
+        functools.partial(widen_kernel, count),
         grid_spec=pltpu.PrefetchScalarGridSpec(
             num_scalar_prefetch=1,
-            grid=(2, count),
-            in_specs=[pl.BlockSpec((1, m, n), lambda l, r, s: (0, 0, 0))] * (2 * count),
+            grid=(count,),
+            in_specs=[pl.BlockSpec((1, m, n), lambda r, s: (0, 0, 0))] * count
+            + [pl.BlockSpec(memory_space=pl.ANY)] * len(extra),
             out_specs=pl.BlockSpec((1, m, n), at),
         ),
         out_shape=jax.ShapeDtypeStruct(shape, F32),
-        compiler_params=params("arbitrary", "arbitrary"),
-        cost_estimate=cost(5),
+        input_output_aliases={1 + count: 0} if extra else {},
+        compiler_params=params("arbitrary"),
+        cost_estimate=cost(4),
         name="expert_gradient_result",
-    )(place, *own, *other)
+    )(jnp.stack([expert, first]), *pieces, *extra)
 
 
 def unpack_kernel(width, exp_dev, hidden, offsets, place_ref, *refs):
@@ -669,41 +672,46 @@
     info_far = over_ep(info, half)
     g_all = [g_all[0]] + [over_ep(g_all[d], d) for d in range(1, half)]
     qkv, attended, lse, resid, *x_send = attention_call(tokens, w_qkv, w_out, vecs, info, ep_size, exp_dev, capp)
-    x_all = [x_send[0]]
-    for d in range(1, ep_size):
-        send, = after([x_send[d]], *([cot_far] if d == half else [x_all[-1]] if d > half else []))
-        x_all.append(over_ep(send, d))
-    far = gateway_call(info_far, cot_far, ep_size, exp_dev, capp)
-    g_all = g_all + [far[0]] + [over_ep(far[j], j) for j in range(1, half)]
-    g_all[0], = after(g_all[:1], *far)
     b_in, b_back = in_bias[:, None, :], back_bias[:, None, :]
     place_e = jnp.stack([1 - core, block_a, block_b])
-    steps = [list(range(half))] + [[d] for d in range(half, ep_size)]
+    x_all = [x_send[0]] + [over_ep(x_send[d], d) for d in range(1, half + 1)]
+    groups = [[0], list(range(1, half + 1))] + [[d] for d in range(half + 1, ep_size)]
     outs, gdis, gdis_back, sums, bias_sums = [], [], [], (), None
-    for number, step in enumerate(steps):
-        xs, gs = [x_all[d] for d in step], [g_all[d] for d in step]
-        if number == len(steps) - 1:
-            xs = after(xs, *gdis_back[:half])
-        o, g, sums, sums_b = expert_call(xs, gs, w_in, w_back, b_in, b_back, place_e, blocks, tuple(sums), 4 + 6 * len(step))
+    for number, group in enumerate(groups):
+        if number == 1:
+            info_far, = after([info_far], sums[0])
+            far = gateway_call(info_far, cot_far, ep_size, exp_dev, capp)
+            g_all = g_all + [far[0]] + [over_ep(far[j], j) for j in range(1, half)]
+            for d in range(half + 1, ep_size):
+                send, = after([x_send[d]], *far, *x_all[1:d])
+                x_all.append(over_ep(send, d))
+        xs, gs = [x_all[d] for d in group], [g_all[d] for d in group]
+        if number == 0:
+            xs = after(xs, *g_all[1:])
+        o, g, sums, sums_b = expert_call(xs, gs, w_in, w_back, b_in, b_back, place_e, blocks, tuple(sums), 10 * len(group))
         outs, gdis = outs + list(o), gdis + list(g)
-        for d in step:
+        for d in group:
             send, = after([gdis[d]], *([x_all[-1]] if d >= half else []))
             gdis_back.append(over_ep(send, d) if d else send)
         bias_sums = sums_b if number == 0 else [a + b for a, b in zip(bias_sums, sums_b)]
     gb_in, gb_back = bias_sums[0][:, 0], bias_sums[1][:, 0]
     far_b, far_i, near_b, near_i = sums
+    far_i, = after([far_i], gdis_back[half])
     state = [near_b + swap(far_b, "grp", grp_size, 1), near_i + swap(far_i, "grp", grp_size, 1)]
     stages = [state]
     for step in range(len(order_a)):
         state = scatter_step(state, [order_a[step], order_b[step]], grp_size)
         stages.append(state)
     sum_b, sum_i = state
-    resid_late, = after([resid], *stages[len(stages) // 2])
+    early = stages[len(stages) // 2]
+    resid_late, = after([resid], *early)
     all_b, all_i = gather_sums(sum_b, order_a, grp_size), gather_sums(sum_i, order_b, grp_size)
     oth_b = [swap(p, "grp", grp_size, 1) for p in all_b]
     oth_i = [swap(p, "grp", grp_size, 1) for p in all_i]
-    gw_back = widen_call(all_b, oth_b, jnp.stack([core, block_a]), 0, w_back.shape)
-    gw_in = widen_call(all_i, oth_i, jnp.stack([core, block_b]), 1, w_in.shape)
+    gw_back = widen_call(all_b, core, block_a, 0, w_back.shape, None)
+    gw_in = widen_call(all_i, core, block_b, 1, w_in.shape, None)
+    gw_back = widen_call(oth_b, 1 - core, block_a, 0, w_back.shape, gw_back)
+    gw_in = widen_call(oth_i, 1 - core, block_b, 1, w_in.shape, gw_in)
     hidden = w_in.shape[2]
     packed = width // ep_size == 128 and 128 % (16 * grp_size) == 0
     place, biases, pack_blocks = None, None, ()
@@ -720,7 +728,7 @@
     )
     outs_back = [outs[0]]
     for d in range(1, ep_size):
-        send, = after([outs[d]], *gdis_back, *([outs_back[-1]] if d > half else []))
+        send, = after([outs[d]], *early, *gdis_back, *([outs_back[-1]] if d > half else []))
         outs_back.append(over_ep(send, d))
     output = combine_call(resid, slot_col, gate_col, outs_back)
     grads = after(grads, sum_b, sum_i, *outs_back[: half + 1])

time: 324 us -> 289 us (0.89)
  waiting for transfers between devices: 113 us -> 74.8 us
  starting transfers between devices: 53.5 us -> 45.1 us
  other arithmetic: 6.12 us -> 13.2 us
  Pallas kernels: 124 us -> 128 us
    ppermute x49, waiting for transfers between devices: 113 us -> 74.8 us  [swap(): return lax.ppermute(array, axis, [(i, i ^ distance) for i in range(size)])]
    ppermute x49, starting transfers between devices: 53.5 us -> 45.1 us  [swap(): return lax.ppermute(array, axis, [(i, i ^ distance) for i in range(size)])]
    unnamed x108 -> x42, local copies, waits for them, and re-layouts: 15 us -> 10.1 us
    add x10, other arithmetic: 0.57 us -> 4.83 us  [scatter_step(): return [a[:h] + c for a, h, c in zip(arrays, halves, came)]]
    pallas_call x2 -> x4, Pallas kernels: 14.9 us -> 18.6 us  [widen_call(): pl.pallas_call(functools.partial(widen_kernel, count), grid_spec=pltpu.Pr...]
  transfers between devices with their start and end apart: 49 -> 49, of which waited for: 15 -> 14; matrix products, arithmetic and copies ran while one was open for 7% -> 11% of each run, Pallas kernels for 32% -> 43%
where the time goes in v4:
time: 289 us; the launch traced here: 283 us
  Pallas kernels  128 us (44%)
  waiting for transfers between devices  74.8 us (26%)
  starting transfers between devices  45.1 us (16%)
  local copies, waits for them, and re-layouts  21.1 us (7%)
  other arithmetic  13.2 us (5%)
    ppermute x49, waiting for transfers between devices, swap(): return lax.ppermute(array, axis, [(i, i ^ distance) for i in range(size)])  74.8 us
    pallas_call x3, Pallas kernels, expert_call(): pl.pallas_call(functools.partial(expert_kernel, count, len(before), block...  54.8 us
    ppermute x49, starting transfers between devices, swap(): return lax.ppermute(array, axis, [(i, i ^ distance) for i in range(size)])  45.1 us
    pallas_call x1, Pallas kernels, backward_call(): pl.pallas_call(functools.partial(backward_kernel, width // HD, ep_size, p...  25.2 us
    pallas_call x4, Pallas kernels, widen_call(): pl.pallas_call(functools.partial(widen_kernel, count), grid_spec=pltpu.Pr...  18.6 us
    pallas_call x1, Pallas kernels, attention_call(): pl.pallas_call(functools.partial(attention_kernel, width // HD), grid=(n_...  14.6 us
    unnamed x42, local copies, waits for them, and re-layouts  10.1 us
    pallas_call x1, Pallas kernels, combine_call(): pl.pallas_call(functools.partial(combine_kernel, len(chunks)), grid=(n_im...  5.85 us
  transfers between devices with their start and end apart: 49, of which 14 were waited for; matrix products, arithmetic and copies ran while one was open for 11% of the time, Pallas kernels for 43%

profile of v4, /device:TPU:0, one launch (start us, length us, event | category | flops | bytes accessed | tf_op | source)
XLA Modules:
  0.0 283.3 jit_solution(13077105025646658513)
XLA Ops:
  0.6 4.1 %collective-permute-start.4 = (bf16[4,197,512]{2,0,1:T(4,128)(2,1)}, bf16[4,197,512]{2,0,1:T(4,128)(2,1)}, u32[]{:S(2)}, u32[]{:S(2)}) collective-permute-start(bf16[4,197,512]{2,0,1:T(4,128)(2,1)} %param.29), channel_id=1, source_target_pairs={{0,2},{1,3},{2,0},{3,1},{4,6},{5,7},{6,4},{7,5},{8,10},{9,11},{10,... | collective-permute-start | bytes 2420744 | tf_op jit(solution)/shard_map/ppermute | solution.py:542
  4.7 2.2 copy.37.cot_ref
  7.0 3.5 %route_and_dispatch_cotangent.1 = (f32[2,4,8,197]{3,2,1,0:T(8,128)}, f32[4,197,8]{2,1,0:T(8,128)}, f32[4,197,8]{2,1,0:T(8,128)}, bf16[2,248,512]{2,1,0:T(8,128)(2,1)}, bf16[2,248,512]{2,1,0:T(8,128)(2,1)}) custom-call(s32[1]{0:T(128)} %bitcast.5.me_ref, s32[4,2,197]{2,1,0:T(2,128)} %bitcast.41, f32[4,2,197]{2,1,0:T(2,128)} %bitcast.42, ...), custom_call_target="tpu_custom_call" | custom-call | flops 4000000000 | bytes 4096 | tf_op jit(solution)/shard_map/route_and_dispatch_cotangent/pallas_call | solution.py:114
  10.5 1.9 collective-permute-start
  12.4 2.2 copy.38.tok_ref
  16.0 14.6 %attention_forward_and_dispatch.1 = (bf16[4,197,1536]{2,1,0:T(8,128)(2,1)}, bf16[4,197,512]{2,1,0:T(8,128)(2,1)}, f32[4,197,128]{2,1,0:T(8,128)}, f32[4,197,512]...) custom-call(bf16[4,197,512]{2,1,0:T(8,128)(2,1)} %copy.38.tok_ref, ...), custom_call_target="tpu_custom_call" | custom-call | flops 14000000000 | bytes 4096 | tf_op jit(solution)/shard_map/attention_forward_and_dispatch/pallas_call | solution.py:212
  30.7 2.9 %collective-permute-start.2 = (bf16[2,248,512]{2,1,0:T(8,128)(2,1)}, bf16[2,248,512]{2,1,0:T(8,128)(2,1)}, u32[]{:S(2)}, u32[]{:S(2)}) collective-permute-start(bf16[2,248,512]{2,1,0:T(8,128)(2,1)} %get-tuple-element.86), channel_id=1, source_target_pairs={{0,2},{1,3},{2,0},{3,1},{4,6},{5,7},{6,4},{7,5},{8,10},{9,11},{10,... | collective-permute-start | bytes 1523720 | tf_op jit(solution)/shard_map/ppermute | solution.py:542
  36.9 14.3 %experts.3 = (bf16[2,248,512]{2,1,0:T(8,128)(2,1)}, bf16[2,248,512]{2,1,0:T(8,128)(2,1)}, bf16[4,512,512]{2,1,0:T(8,128)(2,1)}, bf16[4,512,512]{2,1,0:T(8,128)(2...) custom-call(s32[3]{0:T(128)} %pad_add_fusion.sel_ref, ...), custom_call_target="tpu_custom_call" | custom-call | flops 10000000000 | bytes 4096 | tf_op jit(solution)/shard_map/experts/pallas_call | solution.py:347
  51.2 2.2 copy.39.cot_ref
  53.4 3.2 %dispatch_far_cotangent.1 = (bf16[2,248,512]{2,1,0:T(8,128)(2,1)}, bf16[2,248,512]{2,1,0:T(8,128)(2,1)}) custom-call(f32[2,4,8,197]{3,2,1,0:T(8,128)} %collective-permute-done.3.info_ref, bf16[4,197,512]{2,1,0:T(8,128)(2,1)} %copy.39.cot_ref), custom_call_target="tpu_custom_call" | custom-call | flops 3000000000 | bytes 4096 | tf_op jit(solution)/shard_map/dispatch_far_cotangent/pallas_call | solution.py:146
  56.6 1.6 collective-permute-start.6
  58.4 6.6 %collective-permute-done.2.refs_1_ = bf16[2,248,512]{2,1,0:T(8,128)(2,1)} collective-permute-done((bf16[2,248,512]{2,1,0:T(8,128)(2,1)}, bf16[2,248,512]{2,1,0:T(8,128)(2,1)}, u32[]{:S(2)}, u32[]{:S(2)}) %collective-permute-start.2) | collective-permute-done | bytes 507936 | tf_op jit(solution)/shard_map/ppermute | solution.py:542
  65.1 3.5 %collective-permute-start.5 = (bf16[2,248,512]{2,1,0:T(8,128)(2,1)}, bf16[2,248,512]{2,1,0:T(8,128)(2,1)}, u32[]{:S(2)}, u32[]{:S(2)}) collective-permute-start(bf16[2,248,512]{2,1,0:T(8,128)(2,1)} %get-tuple-element.96), channel_id=1, source_target_pairs={{0,3},{1,2},{2,1},{3,0},{4,7},{5,6},{6,5},{7,4},{8,11},{9,10},{10,... | collective-permute-start | bytes 1523720 | tf_op jit(solution)/shard_map/ppermute | solution.py:542
  68.6 25.4 %experts.4 = (bf16[2,248,512]{2,1,0:T(8,128)(2,1)}, bf16[2,248,512]{2,1,0:T(8,128)(2,1)}, bf16[2,248,512]{2,1,0:T(8,128)(2,1)}, bf16[2,248,512]{2,1,0:T(8,128)(2...) custom-call(s32[3]{0:T(128)} %pad_add_fusion.sel_ref, ...), custom_call_target="tpu_custom_call" | custom-call | flops 20000000000 | bytes 4096 | tf_op jit(solution)/shard_map/experts/pallas_call | solution.py:347
  94.1 15.1 %experts.5 = (bf16[2,248,512]{2,1,0:T(8,128)(2,1)}, bf16[2,248,512]{2,1,0:T(8,128)(2,1)}, bf16[4,512,512]{2,1,0:T(8,128)(2,1)}, bf16[4,512,512]{2,1,0:T(8,128)(2...) custom-call(s32[3]{0:T(128)} %pad_add_fusion.sel_ref, ...), custom_call_target="tpu_custom_call" | custom-call | flops 10000000000 | bytes 4096 | tf_op jit(solution)/shard_map/experts/pallas_call | solution.py:347
  109.3 7.7 %collective-permute-done.9.rest_2_ = bf16[2,248,512]{2,1,0:T(8,128)(2,1)} collective-permute-done((bf16[2,248,512]{2,1,0:T(8,128)(2,1)}, bf16[2,248,512]{2,1,0:T(8,128)(2,1)}, u32[]{:S(2)}, u32[]{:S(2)}) %collective-permute-start.9) | collective-permute-done | bytes 507936 | tf_op jit(solution)/shard_map/ppermute | solution.py:542
  117.0 2.3 add.80
  119.4 1.5 collective-permute-start.8
  121.5 2.7 collective-permute-start.13
  125.1 1.6 collective-permute-start.11
  127.4 17.6 %collective-permute-done.8 = bf16[2,512,512]{2,1,0:T(8,128)(2,1)S(1)} collective-permute-done((bf16[2,512,512]{2,1,0:T(8,128)(2,1)S(1)}, bf16[2,512,512]{2,1,0:T(8,128)(2,1)S(1)}, u32[]{:S(2)}, u32[]{:S(2)}) %collective-permute-start.8) | collective-permute-done | bytes 1048608 | tf_op jit(solution)/shard_map/ppermute | solution.py:542
  146.0 1.5 collective-permute-start.17
  147.5 3.8 %collective-permute-done.11 = bf16[2,512,512]{2,1,0:T(8,128)(2,1)S(1)} collective-permute-done((bf16[2,512,512]{2,1,0:T(8,128)(2,1)S(1)}, bf16[2,512,512]{2,1,0:T(8,128)(2,1)S(1)}, u32[]{:S(2)}, u32[]{:S(2)}) %collective-permute-start.11) | collective-permute-done | bytes 1048608 | tf_op jit(solution)/shard_map/ppermute | solution.py:542
  155.8 25.2 %attention_backward.1 = (bf16[4,197,512]{2,1,0:T(8,128)(2,1)}, bf16[8,2,16,2176]{3,2,1,0:T(8,128)(2,1)}, bf16[8,2,16,2176]{3,2,1,0:T(8,128)(2,1)}) custom-call(s32[2]{0:T(128)} %pad_add_fusion.1.place_ref, f32[40,128]{1,0:T(8,128)} %pad_maximum_fusion.bias_ref, bf16[4,197,512]{2,1,0:T(8,128)(2,1)} %copy.38.tok_ref, bf16[4,197,512]{2,1,0:T(8,128)(2,1)} %copy.37.cot_ref, ...), custom_call_target="tpu_custom_call" | custom-call | flops 24999999488 | bytes 4096 | tf_op jit(solution)/shard_map/attention_backward/pallas_call | solution.py:505
  181.0 2.2 slice_add_fusion.5.refs_0_
  183.2 2.2 slice_add_fusion.4.refs_0_
  188.6 1.5 collective-permute-start.43
  190.1 3.0 %collective-permute-start.16 = (bf16[2,248,512]{2,1,0:T(8,128)(2,1)S(1)}, bf16[2,248,512]{2,1,0:T(8,128)(2,1)S(1)}, u32[]{:S(2)}, u32[]{:S(2)}) collective-permute-start(bf16[2,248,512]{2,1,0:T(8,128)(2,1)S(1)} %copy-done.13), channel_id=1, source_target_pairs={{0,3},{1,2},{2,1},{3,0},{4,7},{5,6},{6,5},{7,4},{8,11},{9,10},{10,... | collective-permute-start | bytes 1523720 | tf_op jit(solution)/shard_map/ppermute | solution.py:542
  193.1 1.8 collective-permute-start.36
  197.3 11.8 %collective-permute-done.23 = bf16[2,2,16,2176]{3,2,1,0:T(8,128)(2,1)S(1)} collective-permute-done((bf16[2,2,16,2176]{3,2,1,0:T(8,128)(2,1)S(1)}, bf16[2,2,16,2176]{3,2,1,0:T(8,128)(2,1)S(1)}, u32[]{:S(2)}, u32[]{:S(2)}) %collective-permute-start.23) | collective-permute-done | bytes 278560 | tf_op jit(solution)/shard_map/ppermute | solution.py:542
  209.1 1.5 collective-permute-start.24
  210.7 3.3 %collective-permute-done.20 = bf16[2,2,16,2176]{3,2,1,0:T(8,128)(2,1)S(1)} collective-permute-done((bf16[2,2,16,2176]{3,2,1,0:T(8,128)(2,1)S(1)}, bf16[2,2,16,2176]{3,2,1,0:T(8,128)(2,1)S(1)}, u32[]{:S(2)}, u32[]{:S(2)}) %collective-permute-start.20) | collective-permute-done | bytes 278560 | tf_op jit(solution)/shard_map/ppermute | solution.py:542
  214.2 1.9 collective-permute-done.24
  216.1 3.1 %collective-permute-done.21 = bf16[1,2,16,2176]{3,2,1,0:T(8,128)(2,1)S(1)} collective-permute-done((bf16[1,2,16,2176]{3,2,1,0:T(8,128)(2,1)S(1)}, bf16[1,2,16,2176]{3,2,1,0:T(8,128)(2,1)S(1)}, u32[]{:S(2)}, u32[]{:S(2)}) %collective-permute-start.21) | collective-permute-done | bytes 139296 | tf_op jit(solution)/shard_map/ppermute | solution.py:542
  221.2 3.9 %collective-permute-start.27 = (bf16[16,2176]{1,0:T(8,128)(2,1)}, bf16[16,2176]{1,0:T(8,128)(2,1)}, u32[]{:S(2)}, u32[]{:S(2)}) collective-permute-start(bf16[16,2176]{1,0:T(8,128)(2,1)} %get-tuple-element.166), channel_id=1, source_target_pairs={{0,3},{1,2},{2,1},{3,0},{4,7},{5,6},{6,5},{7,4},{8,11},{9,10},{10,... | collective-permute-start | bytes 208904 | tf_op jit(solution)/shard_map/ppermute | solution.py:542
  225.0 5.9 %combine_output.1 = bf16[4,197,512]{2,1,0:T(8,128)(2,1)} custom-call(f32[4,197,512]{2,1,0:T(8,128)} %get-tuple-element.123.resid_ref, f32[4,197,8]{2,1,0:T(8,128)} %get-tuple-element.78.slot_col_ref, f32[4,197,8]{2,1,0:T(8,128)} %get-tuple-element.79.gate_col_ref, bf16[2,248,512]{2,1,0:T(8,128)(2,1)} %get-tuple-element.84.rest_0_, ...), custom_call_target="tpu_custom_call" | custom-call | flops 5000000000 | bytes 4096 | tf_op jit(solution)/shard_map/combine_output/pallas_call | solution.py:529
  230.9 2.4 copy.42
  233.3 1.8 collective-permute-start.45
  235.6 1.9 collective-permute-start.40
  237.5 1.6 fusion.2.refs_0_
  239.1 9.4 %collective-permute-done.45.refs_2_ = bf16[1,512,512]{2,1,0:T(8,128)(2,1)} collective-permute-done((bf16[1,512,512]{2,1,0:T(8,128)(2,1)}, bf16[1,512,512]{2,1,0:T(8,128)(2,1)}, u32[]{:S(2)}, u32[]{:S(2)}) %collective-permute-start.45) | collective-permute-done | bytes 524320 | tf_op jit(solution)/shard_map/ppermute | solution.py:542
  249.0 5.9 %collective-permute-done.47.refs_3_ = bf16[1,512,512]{2,1,0:T(8,128)(2,1)} collective-permute-done((bf16[1,512,512]{2,1,0:T(8,128)(2,1)}, bf16[1,512,512]{2,1,0:T(8,128)(2,1)}, u32[]{:S(2)}, u32[]{:S(2)}) %collective-permute-start.47) | collective-permute-done | bytes 524320 | tf_op jit(solution)/shard_map/ppermute | solution.py:542
  255.4 4.6 %expert_gradient_result.6.refs_4_ = f32[2,2048,512]{2,1,0:T(8,128)} custom-call(s32[2]{0:T(128)} %pad_add_fusion.5.place_ref, bf16[1,512,512]{2,1,0:T(8,128)(2,1)} %slice_add_fusion.5.refs_0_, bf16[1,512,512]{2,1,0:T(8,128)(2,1)} %collective-permute-done.43.refs_1_, bf16[1,512,512]{2,1,0:T(8,128)(2,1)} %collective-permute-done.45.refs_2_, ...), custom_call_target="tpu_custom_call" | custom-call | flops 4000000000 | bytes 4096 | tf_op jit(solution)/shard_map/expert_gradient_result/pallas_call | solution.py:578
  260.1 1.4 collective-permute-done.40.refs_3_
  263.5 4.6 %expert_gradient_result.4.refs_4_ = f32[2,512,2048]{2,1,0:T(8,128)} custom-call(s32[2]{0:T(128)} %pad_add_fusion.2.place_ref, bf16[1,512,512]{2,1,0:T(8,128)(2,1)} %slice_add_fusion.4.refs_0_, bf16[1,512,512]{2,1,0:T(8,128)(2,1)} %collective-permute-done.36.refs_1_, bf16[1,512,512]{2,1,0:T(8,128)(2,1)} %collective-permute-done.38.refs_2_, ...), custom_call_target="tpu_custom_call" | custom-call | flops 4000000000 | bytes 4096 | tf_op jit(solution)/shard_map/expert_gradient_result/pallas_call | solution.py:578
  269.3 4.6 %expert_gradient_result.7 = f32[2,2048,512]{2,1,0:T(8,128)} custom-call(s32[2]{0:T(128)} %get-tuple-element.173.place_ref, bf16[1,512,512]{2,1,0:T(8,128)(2,1)} %collective-permute-done.42.refs_0_, bf16[1,512,512]{2,1,0:T(8,128)(2,1)} %collective-permute-done.44.refs_1_, ...), custom_call_target="tpu_custom_call", output_to_operand_aliasing={{}: (5, {})} | custom-call | flops 4000000000 | bytes 4096 | tf_op jit(solution)/shard_map/expert_gradient_result/pallas_call | solution.py:578
  274.9 2.1 parameter_gradient_results.1
  278.5 4.7 %expert_gradient_result.5 = f32[2,512,2048]{2,1,0:T(8,128)} custom-call(s32[2]{0:T(128)} %get-tuple-element.172.place_ref, bf16[1,512,512]{2,1,0:T(8,128)(2,1)} %collective-permute-done.35.refs_0_, bf16[1,512,512]{2,1,0:T(8,128)(2,1)} %collective-permute-done.37.refs_1_, ...), custom_call_target="tpu_custom_call", output_to_operand_aliasing={{}: (5, {})} | custom-call | flops 4000000000 | bytes 4096 | tf_op jit(solution)/shard_map/expert_gradient_result/pallas_call | solution.py:578
  (145 shorter events, 27.6 us)
Async XLA Ops:
  0.6 50.6 %collective-permute-start.4 = (bf16[4,197,512]{2,0,1:T(4,128)(2,1)}, bf16[4,197,512]{2,0,1:T(4,128)(2,1)}, u32[]{:S(2)}, u32[]{:S(2)}) collective-permute-start(bf16[4,197,512]{2,0,1:T(4,128)(2,1)} %param.29), channel_id=1, source_target_pairs={{0,2},{1,3},{2,0},{3,1},{4,6},{5,7},{6,4},{7,5},{8,10},{9,11},{10,... | collective-permute-start | bytes 2420744 | tf_op jit(solution)/shard_map/ppermute | solution.py:542
  10.5 40.7 %collective-permute-start.3 = (f32[2,4,8,197]{3,2,1,0:T(8,128)}, f32[2,4,8,197]{3,2,1,0:T(8,128)}, u32[]{:S(2)}, u32[]{:S(2)}) collective-permute-start(f32[2,4,8,197]{3,2,1,0:T(8,128)} %get-tuple-element.76.info_ref), channel_id=1, source_target_pairs={{0,2},{1,3},{2,0},{3,1},{4,6},{5,7},{6,4},{7,5},{8,10},{9,11},{10,... | collective-permute-start | bytes 151304 | tf_op jit(solution)/shard_map/ppermute | solution.py:542
  10.5 26.4 %collective-permute-start = (bf16[2,248,512]{2,1,0:T(8,128)(2,1)}, bf16[2,248,512]{2,1,0:T(8,128)(2,1)}, u32[]{:S(2)}, u32[]{:S(2)}) collective-permute-start(bf16[2,248,512]{2,1,0:T(8,128)(2,1)} %get-tuple-element.81), channel_id=1, source_target_pairs={{0,1},{1,0},{2,3},{3,2},{4,5},{5,4},{6,7},{7,6},{8,9},{9,8},{10,11... | collective-permute-start | bytes 1523720 | tf_op jit(solution)/shard_map/ppermute | solution.py:542
  30.5 27.9 %collective-permute-start.1 = (bf16[2,248,512]{2,1,0:T(8,128)(2,1)}, bf16[2,248,512]{2,1,0:T(8,128)(2,1)}, u32[]{:S(2)}, u32[]{:S(2)}) collective-permute-start(bf16[2,248,512]{2,1,0:T(8,128)(2,1)} %get-tuple-element.85), channel_id=1, source_target_pairs={{0,1},{1,0},{2,3},{3,2},{4,5},{5,4},{6,7},{7,6},{8,9},{9,8},{10,11... | collective-permute-start | bytes 1523720 | tf_op jit(solution)/shard_map/ppermute | solution.py:542
  30.7 34.3 %collective-permute-start.2 = (bf16[2,248,512]{2,1,0:T(8,128)(2,1)}, bf16[2,248,512]{2,1,0:T(8,128)(2,1)}, u32[]{:S(2)}, u32[]{:S(2)}) collective-permute-start(bf16[2,248,512]{2,1,0:T(8,128)(2,1)} %get-tuple-element.86), channel_id=1, source_target_pairs={{0,2},{1,3},{2,0},{3,1},{4,6},{5,7},{6,4},{7,5},{8,10},{9,11},{10,... | collective-permute-start | bytes 1523720 | tf_op jit(solution)/shard_map/ppermute | solution.py:542
  56.6 37.5 %collective-permute-start.6 = (bf16[2,248,512]{2,1,0:T(8,128)(2,1)}, bf16[2,248,512]{2,1,0:T(8,128)(2,1)}, u32[]{:S(2)}, u32[]{:S(2)}) collective-permute-start(bf16[2,248,512]{2,1,0:T(8,128)(2,1)} %get-tuple-element.95), channel_id=1, source_target_pairs={{0,1},{1,0},{2,3},{3,2},{4,5},{5,4},{6,7},{7,6},{8,9},{9,8},{10,11... | collective-permute-start | bytes 1523720 | tf_op jit(solution)/shard_map/ppermute | solution.py:542
  65.1 29.0 %collective-permute-start.5 = (bf16[2,248,512]{2,1,0:T(8,128)(2,1)}, bf16[2,248,512]{2,1,0:T(8,128)(2,1)}, u32[]{:S(2)}, u32[]{:S(2)}) collective-permute-start(bf16[2,248,512]{2,1,0:T(8,128)(2,1)} %get-tuple-element.96), channel_id=1, source_target_pairs={{0,3},{1,2},{2,1},{3,0},{4,7},{5,6},{6,5},{7,4},{8,11},{9,10},{10,... | collective-permute-start | bytes 1523720 | tf_op jit(solution)/shard_map/ppermute | solution.py:542
  94.0 23.0 %collective-permute-start.9 = (bf16[2,248,512]{2,1,0:T(8,128)(2,1)}, bf16[2,248,512]{2,1,0:T(8,128)(2,1)}, u32[]{:S(2)}, u32[]{:S(2)}) collective-permute-start(bf16[2,248,512]{2,1,0:T(8,128)(2,1)} %get-tuple-element.106), channel_id=1, source_target_pairs={{0,2},{1,3},{2,0},{3,1},{4,6},{5,7},{6,4},{7,5},{8,10},{9,11},{10,... | collective-permute-start | bytes 1523720 | tf_op jit(solution)/shard_map/ppermute | solution.py:542
  109.2 7.8 %collective-permute-start.7 = (bf16[4,512,512]{2,1,0:T(8,128)(2,1)}, bf16[4,512,512]{2,1,0:T(8,128)(2,1)S(1)}, u32[]{:S(2)}, u32[]{:S(2)}) collective-permute-start(bf16[4,512,512]{2,1,0:T(8,128)(2,1)} %get-tuple-element.102), channel_id=1, source_target_pairs={{0,4},{4,0},{8,12},{12,8},{16,20},{20,16},{24,28},{28,24},{1,5},{5... | collective-permute-start | bytes 6291464 | tf_op jit(solution)/shard_map/ppermute | solution.py:542
  117.0 7.2 %collective-permute-start.10 = (bf16[4,512,512]{2,1,0:T(8,128)(2,1)}, bf16[4,512,512]{2,1,0:T(8,128)(2,1)S(1)}, u32[]{:S(2)}, u32[]{:S(2)}) collective-permute-start(bf16[4,512,512]{2,1,0:T(8,128)(2,1)} %get-tuple-element.107), channel_id=1, source_target_pairs={{0,4},{4,0},{8,12},{12,8},{16,20},{20,16},{24,28},{28,24},{1,5},{5... | collective-permute-start | bytes 6291464 | tf_op jit(solution)/shard_map/ppermute | solution.py:542
  119.4 25.6 %collective-permute-start.8 = (bf16[2,512,512]{2,1,0:T(8,128)(2,1)S(1)}, bf16[2,512,512]{2,1,0:T(8,128)(2,1)S(1)}, u32[]{:S(2)}, u32[]{:S(2)}) collective-permute-start(bf16[2,512,512]{2,1,0:T(8,128)(2,1)S(1)} %slice.117), channel_id=1, source_target_pairs={{0,8},{4,12},{8,0},{12,4},{16,24},{20,28},{24,16},{28,20},{1,9},{5... | collective-permute-start | bytes 3145736 | tf_op jit(solution)/shard_map/ppermute | solution.py:542
  121.5 31.2 %collective-permute-start.12 = (bf16[2,248,512]{2,1,0:T(8,128)(2,1)S(1)}, bf16[2,248,512]{2,1,0:T(8,128)(2,1)S(1)}, u32[]{:S(2)}, u32[]{:S(2)}) collective-permute-start(bf16[2,248,512]{2,1,0:T(8,128)(2,1)S(1)} %copy-done.14), channel_id=1, source_target_pairs={{0,1},{1,0},{2,3},{3,2},{4,5},{5,4},{6,7},{7,6},{8,9},{9,8},{10,11... | collective-permute-start | bytes 1523720 | tf_op jit(solution)/shard_map/ppermute | solution.py:542
  121.5 31.2 %collective-permute-start.13 = (bf16[2,248,512]{2,1,0:T(8,128)(2,1)S(1)}, bf16[2,248,512]{2,1,0:T(8,128)(2,1)S(1)}, u32[]{:S(2)}, u32[]{:S(2)}) collective-permute-start(bf16[2,248,512]{2,1,0:T(8,128)(2,1)S(1)} %copy-done.16), channel_id=1, source_target_pairs={{0,3},{1,2},{2,1},{3,0},{4,7},{5,6},{6,5},{7,4},{8,11},{9,10},{10,... | collective-permute-start | bytes 1523720 | tf_op jit(solution)/shard_map/ppermute | solution.py:542
  125.1 26.1 %collective-permute-start.11 = (bf16[2,512,512]{2,1,0:T(8,128)(2,1)S(1)}, bf16[2,512,512]{2,1,0:T(8,128)(2,1)S(1)}, u32[]{:S(2)}, u32[]{:S(2)}) collective-permute-start(bf16[2,512,512]{2,1,0:T(8,128)(2,1)S(1)} %slice.119), channel_id=1, source_target_pairs={{0,16},{4,20},{8,24},{12,28},{16,0},{20,4},{24,8},{28,12},{1,17},{... | collective-permute-start | bytes 3145736 | tf_op jit(solution)/shard_map/ppermute | solution.py:542
  146.0 35.0 %collective-permute-start.17 = (bf16[1,512,512]{2,1,0:T(8,128)(2,1)}, bf16[1,512,512]{2,1,0:T(8,128)(2,1)}, u32[]{:S(2)}, u32[]{:S(2)}) collective-permute-start(bf16[1,512,512]{2,1,0:T(8,128)(2,1)} %slice.121), channel_id=1, source_target_pairs={{0,16},{4,20},{8,24},{12,28},{16,0},{20,4},{24,8},{28,12},{1,17},{... | collective-permute-start | bytes 1572872 | tf_op jit(solution)/shard_map/ppermute | solution.py:542
  152.5 30.7 %collective-permute-start.18 = (bf16[1,512,512]{2,1,0:T(8,128)(2,1)}, bf16[1,512,512]{2,1,0:T(8,128)(2,1)}, u32[]{:S(2)}, u32[]{:S(2)}) collective-permute-start(bf16[1,512,512]{2,1,0:T(8,128)(2,1)} %slice.123), channel_id=1, source_target_pairs={{0,8},{4,12},{8,0},{12,4},{16,24},{20,28},{24,16},{28,20},{1,9},{5... | collective-permute-start | bytes 1572872 | tf_op jit(solution)/shard_map/ppermute | solution.py:542
  154.4 31.0 %collective-permute-start.14 = (bf16[2,248,512]{2,1,0:T(8,128)(2,1)}, bf16[2,248,512]{2,1,0:T(8,128)(2,1)}, u32[]{:S(2)}, u32[]{:S(2)}) collective-permute-start(bf16[2,248,512]{2,1,0:T(8,128)(2,1)} %get-tuple-element.112), channel_id=1, source_target_pairs={{0,1},{1,0},{2,3},{3,2},{4,5},{5,4},{6,7},{7,6},{8,9},{9,8},{10,11... | collective-permute-start | bytes 1523720 | tf_op jit(solution)/shard_map/ppermute | solution.py:542
  155.8 29.6 %collective-permute-start.15 = (bf16[2,248,512]{2,1,0:T(8,128)(2,1)}, bf16[2,248,512]{2,1,0:T(8,128)(2,1)}, u32[]{:S(2)}, u32[]{:S(2)}) collective-permute-start(bf16[2,248,512]{2,1,0:T(8,128)(2,1)} %get-tuple-element.114), channel_id=1, source_target_pairs={{0,2},{1,3},{2,0},{3,1},{4,6},{5,7},{6,4},{7,5},{8,10},{9,11},{10,... | collective-permute-start | bytes 1523720 | tf_op jit(solution)/shard_map/ppermute | solution.py:542
  185.4 9.6 %collective-permute-start.22 = (bf16[4,2,16,2176]{3,2,1,0:T(8,128)(2,1)S(1)}, bf16[4,2,16,2176]{3,2,1,0:T(8,128)(2,1)S(1)}, u32[]{:S(2)}, u32[]{:S(2)}) collective-permute-start(bf16[4,2,16,2176]{3,2,1,0:T(8,128)(2,1)S(1)} %slice.102), channel_id=1, source_target_pairs={{0,4},{4,0},{8,12},{12,8},{16,20},{20,16},{24,28},{28,24},{1,5},{5... | collective-permute-start | bytes 1671176 | tf_op jit(solution)/shard_map/ppermute | solution.py:542
  188.6 44.8 %collective-permute-start.43 = (bf16[1,512,512]{2,1,0:T(8,128)(2,1)}, bf16[1,512,512]{2,1,0:T(8,128)(2,1)}, u32[]{:S(2)}, u32[]{:S(2)}) collective-permute-start(bf16[1,512,512]{2,1,0:T(8,128)(2,1)} %slice_add_fusion.5.refs_0_), channel_id=1, source_target_pairs={{0,16},{4,20},{8,24},{12,28},{16,0},{20,4},{24,8},{28,12},{1,17},{... | collective-permute-start | bytes 1572872 | tf_op jit(solution)/shard_map/ppermute | solution.py:542
  190.1 29.1 %collective-permute-start.16 = (bf16[2,248,512]{2,1,0:T(8,128)(2,1)S(1)}, bf16[2,248,512]{2,1,0:T(8,128)(2,1)S(1)}, u32[]{:S(2)}, u32[]{:S(2)}) collective-permute-start(bf16[2,248,512]{2,1,0:T(8,128)(2,1)S(1)} %copy-done.13), channel_id=1, source_target_pairs={{0,3},{1,2},{2,1},{3,0},{4,7},{5,6},{6,5},{7,4},{8,11},{9,10},{10,... | collective-permute-start | bytes 1523720 | tf_op jit(solution)/shard_map/ppermute | solution.py:542
  193.1 42.1 %collective-permute-start.36 = (bf16[1,512,512]{2,1,0:T(8,128)(2,1)}, bf16[1,512,512]{2,1,0:T(8,128)(2,1)}, u32[]{:S(2)}, u32[]{:S(2)}) collective-permute-start(bf16[1,512,512]{2,1,0:T(8,128)(2,1)} %slice_add_fusion.4.refs_0_), channel_id=1, source_target_pairs={{0,8},{4,12},{8,0},{12,4},{16,24},{20,28},{24,16},{28,20},{1,9},{5... | collective-permute-start | bytes 1572872 | tf_op jit(solution)/shard_map/ppermute | solution.py:542
  195.1 14.0 %collective-permute-start.23 = (bf16[2,2,16,2176]{3,2,1,0:T(8,128)(2,1)S(1)}, bf16[2,2,16,2176]{3,2,1,0:T(8,128)(2,1)S(1)}, u32[]{:S(2)}, u32[]{:S(2)}) collective-permute-start(bf16[2,2,16,2176]{3,2,1,0:T(8,128)(2,1)S(1)} %slice.129), channel_id=1, source_target_pairs={{0,16},{4,20},{8,24},{12,28},{16,0},{20,4},{24,8},{28,12},{1,17},{... | collective-permute-start | bytes 835592 | tf_op jit(solution)/shard_map/ppermute | solution.py:542
  197.0 17.0 %collective-permute-start.20 = (bf16[2,2,16,2176]{3,2,1,0:T(8,128)(2,1)S(1)}, bf16[2,2,16,2176]{3,2,1,0:T(8,128)(2,1)S(1)}, u32[]{:S(2)}, u32[]{:S(2)}) collective-permute-start(bf16[2,2,16,2176]{3,2,1,0:T(8,128)(2,1)S(1)} %slice.125), channel_id=1, source_target_pairs={{0,8},{4,12},{8,0},{12,4},{16,24},{20,28},{24,16},{28,20},{1,9},{5... | collective-permute-start | bytes 835592 | tf_op jit(solution)/shard_map/ppermute | solution.py:542
  209.1 6.9 %collective-permute-start.24 = (bf16[1,2,16,2176]{3,2,1,0:T(8,128)(2,1)S(1)}, bf16[1,2,16,2176]{3,2,1,0:T(8,128)(2,1)S(1)}, u32[]{:S(2)}, u32[]{:S(2)}) collective-permute-start(bf16[1,2,16,2176]{3,2,1,0:T(8,128)(2,1)S(1)} %slice.131), channel_id=1, source_target_pairs={{0,8},{4,12},{8,0},{12,4},{16,24},{20,28},{24,16},{28,20},{1,9},{5... | collective-permute-start | bytes 417800 | tf_op jit(solution)/shard_map/ppermute | solution.py:542
  214.1 5.1 %collective-permute-start.21 = (bf16[1,2,16,2176]{3,2,1,0:T(8,128)(2,1)S(1)}, bf16[1,2,16,2176]{3,2,1,0:T(8,128)(2,1)S(1)}, u32[]{:S(2)}, u32[]{:S(2)}) collective-permute-start(bf16[1,2,16,2176]{3,2,1,0:T(8,128)(2,1)S(1)} %slice.127), channel_id=1, source_target_pairs={{0,16},{4,20},{8,24},{12,28},{16,0},{20,4},{24,8},{28,12},{1,17},{... | collective-permute-start | bytes 417800 | tf_op jit(solution)/shard_map/ppermute | solution.py:542
  220.6 14.5 %collective-permute-start.25 = (bf16[16,2176]{1,0:T(8,128)(2,1)}, bf16[16,2176]{1,0:T(8,128)(2,1)}, u32[]{:S(2)}, u32[]{:S(2)}) collective-permute-start(bf16[16,2176]{1,0:T(8,128)(2,1)} %slice_bitcast_fusion.2), channel_id=1, source_target_pairs={{0,1},{1,0},{2,3},{3,2},{4,5},{5,4},{6,7},{7,6},{8,9},{9,8},{10,11... | collective-permute-start | bytes 208904 | tf_op jit(solution)/shard_map/ppermute | solution.py:542
  220.7 14.8 %collective-permute-start.26 = (bf16[16,2176]{1,0:T(8,128)(2,1)}, bf16[16,2176]{1,0:T(8,128)(2,1)}, u32[]{:S(2)}, u32[]{:S(2)}) collective-permute-start(bf16[16,2176]{1,0:T(8,128)(2,1)} %get-tuple-element.165), channel_id=1, source_target_pairs={{0,2},{1,3},{2,0},{3,1},{4,6},{5,7},{6,4},{7,5},{8,10},{9,11},{10,... | collective-permute-start | bytes 208904 | tf_op jit(solution)/shard_map/ppermute | solution.py:542
  221.2 14.4 %collective-permute-start.27 = (bf16[16,2176]{1,0:T(8,128)(2,1)}, bf16[16,2176]{1,0:T(8,128)(2,1)}, u32[]{:S(2)}, u32[]{:S(2)}) collective-permute-start(bf16[16,2176]{1,0:T(8,128)(2,1)} %get-tuple-element.166), channel_id=1, source_target_pairs={{0,3},{1,2},{2,1},{3,0},{4,7},{5,6},{6,5},{7,4},{8,11},{9,10},{10,... | collective-permute-start | bytes 208904 | tf_op jit(solution)/shard_map/ppermute | solution.py:542
  233.3 15.2 %collective-permute-start.45 = (bf16[1,512,512]{2,1,0:T(8,128)(2,1)}, bf16[1,512,512]{2,1,0:T(8,128)(2,1)}, u32[]{:S(2)}, u32[]{:S(2)}) collective-permute-start(bf16[1,512,512]{2,1,0:T(8,128)(2,1)} %slice_add_fusion.5.refs_0_), channel_id=1, source_target_pairs={{0,8},{4,12},{8,0},{12,4},{16,24},{20,28},{24,16},{28,20},{1,9},{5... | collective-permute-start | bytes 1572872 | tf_op jit(solution)/shard_map/ppermute | solution.py:542
  235.2 13.4 %collective-permute-start.42 = (bf16[1,512,512]{2,1,0:T(8,128)(2,1)}, bf16[1,512,512]{2,1,0:T(8,128)(2,1)}, u32[]{:S(2)}, u32[]{:S(2)}) collective-permute-start(bf16[1,512,512]{2,1,0:T(8,128)(2,1)} %slice_add_fusion.5.refs_0_), channel_id=1, source_target_pairs={{0,4},{4,0},{8,12},{12,8},{16,20},{20,16},{24,28},{28,24},{1,5},{5... | collective-permute-start | bytes 1572872 | tf_op jit(solution)/shard_map/ppermute | solution.py:542
  235.2 19.8 %collective-permute-start.38 = (bf16[1,512,512]{2,1,0:T(8,128)(2,1)}, bf16[1,512,512]{2,1,0:T(8,128)(2,1)}, u32[]{:S(2)}, u32[]{:S(2)}) collective-permute-start(bf16[1,512,512]{2,1,0:T(8,128)(2,1)} %slice_add_fusion.4.refs_0_), channel_id=1, source_target_pairs={{0,16},{4,20},{8,24},{12,28},{16,0},{20,4},{24,8},{28,12},{1,17},{... | collective-permute-start | bytes 1572872 | tf_op jit(solution)/shard_map/ppermute | solution.py:542
  235.5 19.4 %collective-permute-start.47 = (bf16[1,512,512]{2,1,0:T(8,128)(2,1)}, bf16[1,512,512]{2,1,0:T(8,128)(2,1)}, u32[]{:S(2)}, u32[]{:S(2)}) collective-permute-start(bf16[1,512,512]{2,1,0:T(8,128)(2,1)} %collective-permute-done.43.refs_1_), channel_id=1, source_target_pairs={{0,8},{4,12},{8,0},{12,4},{16,24},{20,28},{24,16},{28,20},{1,9},{5... | collective-permute-start | bytes 1572872 | tf_op jit(solution)/shard_map/ppermute | solution.py:542
  235.6 26.0 %collective-permute-start.40 = (bf16[1,512,512]{2,1,0:T(8,128)(2,1)}, bf16[1,512,512]{2,1,0:T(8,128)(2,1)}, u32[]{:S(2)}, u32[]{:S(2)}) collective-permute-start(bf16[1,512,512]{2,1,0:T(8,128)(2,1)} %collective-permute-done.36.refs_1_), channel_id=1, source_target_pairs={{0,16},{4,20},{8,24},{12,28},{16,0},{20,4},{24,8},{28,12},{1,17},{... | collective-permute-start | bytes 1572872 | tf_op jit(solution)/shard_map/ppermute | solution.py:542
  248.5 19.7 %collective-permute-start.44 = (bf16[1,512,512]{2,1,0:T(8,128)(2,1)}, bf16[1,512,512]{2,1,0:T(8,128)(2,1)}, u32[]{:S(2)}, u32[]{:S(2)}) collective-permute-start(bf16[1,512,512]{2,1,0:T(8,128)(2,1)} %collective-permute-done.43.refs_1_), channel_id=1, source_target_pairs={{0,4},{4,0},{8,12},{12,8},{16,20},{20,16},{24,28},{28,24},{1,5},{5... | collective-permute-start | bytes 1572872 | tf_op jit(solution)/shard_map/ppermute | solution.py:542
  248.5 19.7 %collective-permute-start.46 = (bf16[1,512,512]{2,1,0:T(8,128)(2,1)}, bf16[1,512,512]{2,1,0:T(8,128)(2,1)}, u32[]{:S(2)}, u32[]{:S(2)}) collective-permute-start(bf16[1,512,512]{2,1,0:T(8,128)(2,1)} %collective-permute-done.45.refs_2_), channel_id=1, source_target_pairs={{0,4},{4,0},{8,12},{12,8},{16,20},{20,16},{24,28},{28,24},{1,5},{5... | collective-permute-start | bytes 1572872 | tf_op jit(solution)/shard_map/ppermute | solution.py:542
  254.9 13.8 %collective-permute-start.48 = (bf16[1,512,512]{2,1,0:T(8,128)(2,1)}, bf16[1,512,512]{2,1,0:T(8,128)(2,1)}, u32[]{:S(2)}, u32[]{:S(2)}) collective-permute-start(bf16[1,512,512]{2,1,0:T(8,128)(2,1)} %collective-permute-done.47.refs_3_), channel_id=1, source_target_pairs={{0,4},{4,0},{8,12},{12,8},{16,20},{20,16},{24,28},{28,24},{1,5},{5... | collective-permute-start | bytes 1572872 | tf_op jit(solution)/shard_map/ppermute | solution.py:542
  254.9 7.6 %collective-permute-start.28 = (bf16[16,2176]{1,0:T(8,128)(2,1)}, bf16[16,2176]{1,0:T(8,128)(2,1)}, u32[]{:S(2)}, u32[]{:S(2)}) collective-permute-start(bf16[16,2176]{1,0:T(8,128)(2,1)} %fusion.2.refs_0_), channel_id=1, source_target_pairs={{0,16},{4,20},{8,24},{12,28},{16,0},{20,4},{24,8},{28,12},{1,17},{... | collective-permute-start | bytes 208904 | tf_op jit(solution)/shard_map/ppermute | solution.py:542
  261.5 7.3 %collective-permute-start.29 = (bf16[16,2176]{1,0:T(8,128)(2,1)}, bf16[16,2176]{1,0:T(8,128)(2,1)}, u32[]{:S(2)}, u32[]{:S(2)}) collective-permute-start(bf16[16,2176]{1,0:T(8,128)(2,1)} %fusion.2.refs_0_), channel_id=1, source_target_pairs={{0,8},{4,12},{8,0},{12,4},{16,24},{20,28},{24,16},{28,20},{1,9},{5... | collective-permute-start | bytes 208904 | tf_op jit(solution)/shard_map/ppermute | solution.py:542
  262.5 6.7 %collective-permute-start.30 = (bf16[16,2176]{1,0:T(8,128)(2,1)}, bf16[16,2176]{1,0:T(8,128)(2,1)}, u32[]{:S(2)}, u32[]{:S(2)}) collective-permute-start(bf16[16,2176]{1,0:T(8,128)(2,1)} %collective-permute-done.28.refs_1_), channel_id=1, source_target_pairs={{0,8},{4,12},{8,0},{12,4},{16,24},{20,28},{24,16},{28,20},{1,9},{5... | collective-permute-start | bytes 208904 | tf_op jit(solution)/shard_map/ppermute | solution.py:542
  268.2 10.2 %collective-permute-start.35 = (bf16[1,512,512]{2,1,0:T(8,128)(2,1)}, bf16[1,512,512]{2,1,0:T(8,128)(2,1)}, u32[]{:S(2)}, u32[]{:S(2)}) collective-permute-start(bf16[1,512,512]{2,1,0:T(8,128)(2,1)} %slice_add_fusion.4.refs_0_), channel_id=1, source_target_pairs={{0,4},{4,0},{8,12},{12,8},{16,20},{20,16},{24,28},{28,24},{1,5},{5... | collective-permute-start | bytes 1572872 | tf_op jit(solution)/shard_map/ppermute | solution.py:542
  268.2 5.8 %collective-permute-start.31 = (bf16[16,2176]{1,0:T(8,128)(2,1)}, bf16[16,2176]{1,0:T(8,128)(2,1)}, u32[]{:S(2)}, u32[]{:S(2)}) collective-permute-start(bf16[16,2176]{1,0:T(8,128)(2,1)} %fusion.2.refs_0_), channel_id=1, source_target_pairs={{0,4},{4,0},{8,12},{12,8},{16,20},{20,16},{24,28},{28,24},{1,5},{5... | collective-permute-start | bytes 208904 | tf_op jit(solution)/shard_map/ppermute | solution.py:542
  268.7 5.8 %collective-permute-start.32 = (bf16[16,2176]{1,0:T(8,128)(2,1)}, bf16[16,2176]{1,0:T(8,128)(2,1)}, u32[]{:S(2)}, u32[]{:S(2)}) collective-permute-start(bf16[16,2176]{1,0:T(8,128)(2,1)} %collective-permute-done.28.refs_1_), channel_id=1, source_target_pairs={{0,4},{4,0},{8,12},{12,8},{16,20},{20,16},{24,28},{28,24},{1,5},{5... | collective-permute-start | bytes 208904 | tf_op jit(solution)/shard_map/ppermute | solution.py:542
  268.8 5.6 %collective-permute-start.33 = (bf16[16,2176]{1,0:T(8,128)(2,1)}, bf16[16,2176]{1,0:T(8,128)(2,1)}, u32[]{:S(2)}, u32[]{:S(2)}) collective-permute-start(bf16[16,2176]{1,0:T(8,128)(2,1)} %collective-permute-done.29.refs_2_), channel_id=1, source_target_pairs={{0,4},{4,0},{8,12},{12,8},{16,20},{20,16},{24,28},{28,24},{1,5},{5... | collective-permute-start | bytes 208904 | tf_op jit(solution)/shard_map/ppermute | solution.py:542
  269.2 5.7 %collective-permute-start.34 = (bf16[16,2176]{1,0:T(8,128)(2,1)}, bf16[16,2176]{1,0:T(8,128)(2,1)}, u32[]{:S(2)}, u32[]{:S(2)}) collective-permute-start(bf16[16,2176]{1,0:T(8,128)(2,1)} %collective-permute-done.30.refs_3_), channel_id=1, source_target_pairs={{0,4},{4,0},{8,12},{12,8},{16,20},{20,16},{24,28},{28,24},{1,5},{5... | collective-permute-start | bytes 208904 | tf_op jit(solution)/shard_map/ppermute | solution.py:542
  274.0 4.5 %collective-permute-start.39 = (bf16[1,512,512]{2,1,0:T(8,128)(2,1)}, bf16[1,512,512]{2,1,0:T(8,128)(2,1)}, u32[]{:S(2)}, u32[]{:S(2)}) collective-permute-start(bf16[1,512,512]{2,1,0:T(8,128)(2,1)} %collective-permute-done.38.refs_2_), channel_id=1, source_target_pairs={{0,4},{4,0},{8,12},{12,8},{16,20},{20,16},{24,28},{28,24},{1,5},{5... | collective-permute-start | bytes 1572872 | tf_op jit(solution)/shard_map/ppermute | solution.py:542
  274.4 4.0 %collective-permute-start.37 = (bf16[1,512,512]{2,1,0:T(8,128)(2,1)}, bf16[1,512,512]{2,1,0:T(8,128)(2,1)}, u32[]{:S(2)}, u32[]{:S(2)}) collective-permute-start(bf16[1,512,512]{2,1,0:T(8,128)(2,1)} %collective-permute-done.36.refs_1_), channel_id=1, source_target_pairs={{0,4},{4,0},{8,12},{12,8},{16,20},{20,16},{24,28},{28,24},{1,5},{5... | collective-permute-start | bytes 1572872 | tf_op jit(solution)/shard_map/ppermute | solution.py:542
  274.5 4.0 %collective-permute-start.41 = (bf16[1,512,512]{2,1,0:T(8,128)(2,1)}, bf16[1,512,512]{2,1,0:T(8,128)(2,1)}, u32[]{:S(2)}, u32[]{:S(2)}) collective-permute-start(bf16[1,512,512]{2,1,0:T(8,128)(2,1)} %collective-permute-done.40.refs_3_), channel_id=1, source_target_pairs={{0,4},{4,0},{8,12},{12,8},{16,20},{20,16},{24,28},{28,24},{1,5},{5... | collective-permute-start | bytes 1572872 | tf_op jit(solution)/shard_map/ppermute | solution.py:542
  (20 other events, 66.7 us)

commit v5 on v4

--- a/solution.py
+++ b/solution.py
@@ -11,7 +11,7 @@
 NORM_EPS = 1e-06
 BF16 = jnp.bfloat16
 F32 = jnp.float32
-VMEM_LIMIT = 64 * 1024 * 1024
+MIB = 1024 * 1024
 GELU_C = 0.7978845608028654
 
 
@@ -52,10 +52,8 @@
     return pl.BlockSpec(tuple(shape), lambda *_: zeros)
 
 
-def params(*semantics):
-    return pltpu.CompilerParams(
-        dimension_semantics=semantics or None, vmem_limit_bytes=VMEM_LIMIT
-    )
+def params(mebibytes, *semantics):
+    return pltpu.CompilerParams(dimension_semantics=semantics or None, vmem_limit_bytes=mebibytes * MIB)
 
 
 def dispatch_rows(place, slots, values, source_refs, e):
@@ -122,7 +120,7 @@
         ]
         + [chunk] * (ep_size // 2),
         scratch_shapes=[pltpu.VMEM((2, 128, seq_pad), F32)],
-        compiler_params=params(),
+        compiler_params=params(16),
         cost_estimate=cost(4),
         name="route_and_dispatch_cotangent",
     )(me, routes.transpose(0, 2, 1), gates.transpose(0, 2, 1), cotangent)
@@ -148,7 +146,7 @@
         in_specs=[pl.BlockSpec(memory_space=pltpu.VMEM)] * 2,
         out_specs=[pl.BlockSpec(memory_space=pltpu.VMEM)] * (ep_size // 2),
         out_shape=[chunk] * (ep_size // 2),
-        compiler_params=params(),
+        compiler_params=params(16),
         cost_estimate=cost(3),
         name="dispatch_far_cotangent",
     )(info, cotangent)
@@ -223,7 +221,7 @@
         ]
         + [chunk] * ep_size,
         scratch_shapes=[pltpu.VMEM((n_img, seq, width), BF16)],
-        compiler_params=params("arbitrary"),
+        compiler_params=params(32, "arbitrary"),
         cost_estimate=cost(14),
         name="attention_forward_and_dispatch",
     )(tokens, w_qkv, w_out, vecs, info)
@@ -231,107 +229,60 @@
 
 def expert_kernel(count, carried, blocks, tile, sel_ref, *refs):
     x_refs, g_refs = refs[:count], refs[count : 2 * count]
-    w_in_hbm, w_back_hbm, b_in_ref, b_back_ref = refs[2 * count : 2 * count + 4]
+    w_in_ref, w_back_ref, b_in_ref, b_back_ref = refs[2 * count : 2 * count + 4]
     before = refs[2 * count + 4 : 2 * count + 4 + carried]
     outs = refs[2 * count + 4 + carried :]
     out_refs, gdis_refs = outs[:count], outs[count : 2 * count]
     sums, (gb_in_ref, gb_back_ref) = outs[2 * count : 2 * count + 4], outs[2 * count + 4 : 2 * count + 6]
-    w_in_buf, w_back_buf, back_buf, in_buf, acc_out, acc_dis, load_sem, sum_sem, store_sem = outs[2 * count + 6 :]
-    exp_dev, _, hidden = w_in_buf.shape
+    acc_out, acc_dis = outs[2 * count + 6 :]
+    exp_dev, _, hidden = w_in_ref.shape
     block = hidden // blocks
-    steps = [(l, t) for l in range(exp_dev) for t in range(hidden // tile)]
-
-    def loads(l, t):
+    for l in range(exp_dev):
         e = sel_ref[0] ^ l
-        span = pl.ds(t * tile, tile)
-        return [
-            pltpu.make_async_copy(w_in_hbm.at[e, :, span], w_in_buf.at[l, :, span], load_sem.at[l, t, 0]),
-            pltpu.make_async_copy(w_back_hbm.at[e, span, :], w_back_buf.at[l, span, :], load_sem.at[l, t, 1]),
-        ]
-
-    def blocks_of(t):
-        return range(t * tile // block, (t + 1) * tile // block)
-
-    def sum_loads(l, t):
-        return [
-            copy
-            for b in blocks_of(t)
-            for copy in (
-                pltpu.make_async_copy(before[2 * l].at[b ^ sel_ref[1]], back_buf.at[l, b], sum_sem.at[l, b, 0]),
-                pltpu.make_async_copy(before[2 * l + 1].at[b ^ sel_ref[2]], in_buf.at[l, b], sum_sem.at[l, b, 1]),
-            )
-        ]
-
-    def stores(l, t):
-        return [
-            copy
-            for b in blocks_of(t)
-            for copy in (
-                pltpu.make_async_copy(back_buf.at[l, b], sums[2 * l].at[b ^ sel_ref[1]], store_sem.at[l, b, 0]),
-                pltpu.make_async_copy(in_buf.at[l, b], sums[2 * l + 1].at[b ^ sel_ref[2]], store_sem.at[l, b, 1]),
-            )
-        ]
-
-    for l, t in steps:
-        for copy in loads(l, t):
-            copy.start()
-    if carried:
-        for l, t in steps:
-            for copy in sum_loads(l, t):
-                copy.start()
-    for l, t in steps:
-        e = sel_ref[0] ^ l
-        span = slice(t * tile, (t + 1) * tile)
-        for copy in loads(l, t):
-            copy.wait()
-        w_in, w_back = w_in_buf[l, :, span], w_back_buf[l, span, :]
-        gw_back = gw_in = gb_in = None
-        for n in range(count):
-            x, g = x_refs[n][e], g_refs[n][e]
-            pre = dot_nn(x, w_in) + b_in_ref[e, :, span]
-            square = pre * pre
-            bent = jnp.tanh(pre * (GELU_C + (GELU_C * 0.044715) * square))
-            half = 0.5 + 0.5 * bent
-            value = pre * half
-            act = value.astype(BF16)
-            slope = half + (value - value * half) * (2 * GELU_C + (6 * GELU_C * 0.044715) * square)
-            gpre = (dot_nt(g, w_back) * slope).astype(BF16)
-            part_dis, part_out = dot_nt(gpre, w_in), dot_nn(act, w_back)
-            if t == 0:
-                part_out = part_out + b_back_ref[e]
-            else:
-                part_dis, part_out = part_dis + acc_dis[n], part_out + acc_out[n]
-            if span.stop == hidden:
-                gdis_refs[n][e] = part_dis.astype(BF16)
-                out_refs[n][e] = part_out.astype(BF16)
-            else:
-                acc_dis[n] = part_dis
-                acc_out[n] = part_out
-            one = (dot_tn(act, g), dot_tn(x, gpre), jnp.sum(gpre.astype(F32), axis=0, keepdims=True))
-            gw_back = one[0] if n == 0 else gw_back + one[0]
-            gw_in = one[1] if n == 0 else gw_in + one[1]
-            gb_in = one[2] if n == 0 else gb_in + one[2]
-        gb_in_ref[e, :, span] = gb_in
-        if carried:
-            for copy in sum_loads(l, t):
-                copy.wait()
-        for b in blocks_of(t):
-            at = slice(b * block - t * tile, (b + 1) * block - t * tile)
-            back, into = gw_back[at, :], gw_in[:, at]
-            if carried:
-                back, into = back + back_buf[l, b].astype(F32), into + in_buf[l, b].astype(F32)
-            back_buf[l, b] = back.astype(BF16)
-            in_buf[l, b] = into.astype(BF16)
-        for copy in stores(l, t):
-            copy.start()
-    for e in range(exp_dev):
+        own = pl.ds(e, 1)
+        for t in range(hidden // tile):
+            span = slice(t * tile, (t + 1) * tile)
+            w_in, w_back = w_in_ref[e, :, span], w_back_ref[e, span, :]
+            gw_back = gw_in = gb_in = None
+            for n in range(count):
+                x, g = x_refs[n][e], g_refs[n][e]
+                pre = dot_nn(x, w_in) + b_in_ref[own, span]
+                square = pre * pre
+                bent = jnp.tanh(pre * (GELU_C + (GELU_C * 0.044715) * square))
+                half = 0.5 + 0.5 * bent
+                value = pre * half
+                act = value.astype(BF16)
+                slope = half + (value - value * half) * (2 * GELU_C + (6 * GELU_C * 0.044715) * square)
+                gpre = (dot_nt(g, w_back) * slope).astype(BF16)
+                part_dis, part_out = dot_nt(gpre, w_in), dot_nn(act, w_back)
+                if t == 0:
+                    part_out = part_out + b_back_ref[own, :]
+                else:
+                    part_dis, part_out = part_dis + acc_dis[n], part_out + acc_out[n]
+                if span.stop == hidden:
+                    gdis_refs[n][e] = part_dis.astype(BF16)
+                    out_refs[n][e] = part_out.astype(BF16)
+                else:
+                    acc_dis[n] = part_dis
+                    acc_out[n] = part_out
+                one = (dot_tn(act, g), dot_tn(x, gpre), jnp.sum(gpre.astype(F32), axis=0, keepdims=True))
+                gw_back = one[0] if n == 0 else gw_back + one[0]
+                gw_in = one[1] if n == 0 else gw_in + one[1]
+                gb_in = one[2] if n == 0 else gb_in + one[2]
+            gb_in_ref[own, span] = gb_in
+            for b in range(t * tile // block, (t + 1) * tile // block):
+                at = slice(b * block - t * tile, (b + 1) * block - t * tile)
+                at_back, at_in = b ^ sel_ref[1], b ^ sel_ref[2]
+                back, into = gw_back[at, :], gw_in[:, at]
+                if carried:
+                    back = back + before[2 * l][at_back].astype(F32)
+                    into = into + before[2 * l + 1][at_in].astype(F32)
+                sums[2 * l][at_back] = back.astype(BF16)
+                sums[2 * l + 1][at_in] = into.astype(BF16)
         total = jnp.sum(g_refs[0][e].astype(F32), axis=0, keepdims=True)
         for n in range(1, count):
             total = total + jnp.sum(g_refs[n][e].astype(F32), axis=0, keepdims=True)
-        gb_back_ref[e] = total
-    for l, t in steps:
-        for copy in stores(l, t):
-            copy.wait()
+        gb_back_ref[own, :] = total
 
 
 def expert_call(xs, gs, w_in, w_back, b_in, b_back, place, blocks, before, microseconds):
@@ -339,34 +290,21 @@
     exp_dev, capp, width = xs[0].shape
     hidden = w_in.shape[2]
     block = hidden // blocks
-    tile = max(block, min(hidden, 512))
+    tile = max(block, min(hidden, 1024))
     narrow = jax.ShapeDtypeStruct((exp_dev, capp, width), BF16)
     shapes = [jax.ShapeDtypeStruct((blocks, block, width), BF16), jax.ShapeDtypeStruct((blocks, width, block), BF16)] * 2
     held = pl.BlockSpec(memory_space=pltpu.VMEM)
-    remote = pl.BlockSpec(memory_space=pl.ANY)
+    first = 1 + 2 * count + 4
     res = pl.pallas_call(
         functools.partial(expert_kernel, count, len(before), blocks, tile),
-        in_specs=[pl.BlockSpec(memory_space=pltpu.SMEM)]
-        + [held] * (2 * count)
-        + [remote] * 2
-        + [held] * 2
-        + [remote] * len(before),
-        out_specs=[held] * (2 * count) + [remote] * 4 + [held] * 2,
+        in_specs=[pl.BlockSpec(memory_space=pltpu.SMEM)] + [held] * (2 * count + 4 + len(before)),
+        out_specs=[held] * (2 * count + 6),
         out_shape=[narrow] * (2 * count)
         + shapes
-        + [jax.ShapeDtypeStruct((exp_dev, 1, hidden), F32), jax.ShapeDtypeStruct((exp_dev, 1, width), F32)],
-        scratch_shapes=[
-            pltpu.VMEM((exp_dev, width, hidden), BF16),
-            pltpu.VMEM((exp_dev, hidden, width), BF16),
-            pltpu.VMEM((exp_dev, blocks, block, width), BF16),
-            pltpu.VMEM((exp_dev, blocks, width, block), BF16),
-            pltpu.VMEM((count, capp, width), F32),
-            pltpu.VMEM((count, capp, width), F32),
-            pltpu.SemaphoreType.DMA((exp_dev, blocks, 2)),
-            pltpu.SemaphoreType.DMA((exp_dev, blocks, 2)),
-            pltpu.SemaphoreType.DMA((exp_dev, blocks, 2)),
-        ],
-        compiler_params=params(),
+        + [jax.ShapeDtypeStruct(b_in.shape, F32), jax.ShapeDtypeStruct(b_back.shape, F32)],
+        scratch_shapes=[pltpu.VMEM((count, capp, width), F32)] * 2,
+        input_output_aliases={first + k: 2 * count + k for k in range(len(before))},
+        compiler_params=params(30),
         cost_estimate=cost(microseconds),
         name="experts",
     )(place, *xs, *gs, w_in, w_back, b_in, b_back, *before)
@@ -511,7 +449,7 @@
         out_specs=[image(tokens)] + [whole(v.shape) for v in outs],
         out_shape=[jax.ShapeDtypeStruct(tokens.shape, BF16)] + outs,
         scratch_shapes=scratch,
-        compiler_params=params("arbitrary"),
+        compiler_params=params(40, "arbitrary"),
         cost_estimate=cost(25),
         name="attention_backward",
     )(place, biases, tokens, cotangent, resid, qkv, attended, lse, slot_col, w_qkv, w_out, vecs, *chunks)
@@ -532,7 +470,7 @@
         in_specs=[image(a) for a in (resid, slot_col, gate_col)] + [whole(c.shape) for c in chunks],
         out_specs=image(resid),
         out_shape=jax.ShapeDtypeStruct(resid.shape, BF16),
-        compiler_params=params("arbitrary"),
+        compiler_params=params(16, "arbitrary"),
         cost_estimate=cost(5),
         name="combine_output",
     )(resid, slot_col, gate_col, *chunks)
@@ -586,7 +524,7 @@
         ),
         out_shape=jax.ShapeDtypeStruct(shape, F32),
         input_output_aliases={1 + count: 0} if extra else {},
-        compiler_params=params("arbitrary"),
+        compiler_params=params(16, "arbitrary"),
         cost_estimate=cost(4),
         name="expert_gradient_result",
     )(jnp.stack([expert, first]), *pieces, *extra)
@@ -619,7 +557,7 @@
         out_specs=[pl.BlockSpec(memory_space=pltpu.VMEM)] * len(shapes),
         out_shape=[jax.ShapeDtypeStruct(v, F32) for v in shapes],
         scratch_shapes=[pltpu.VMEM((rows, 128), F32)],
-        compiler_params=params(),
+        compiler_params=params(16),
         cost_estimate=cost(5),
         name="parameter_gradient_results",
     )(place, *pieces)
@@ -672,10 +610,9 @@
     info_far = over_ep(info, half)
     g_all = [g_all[0]] + [over_ep(g_all[d], d) for d in range(1, half)]
     qkv, attended, lse, resid, *x_send = attention_call(tokens, w_qkv, w_out, vecs, info, ep_size, exp_dev, capp)
-    b_in, b_back = in_bias[:, None, :], back_bias[:, None, :]
     place_e = jnp.stack([1 - core, block_a, block_b])
     x_all = [x_send[0]] + [over_ep(x_send[d], d) for d in range(1, half + 1)]
-    groups = [[0], list(range(1, half + 1))] + [[d] for d in range(half + 1, ep_size)]
+    groups = [[0]] + [list(range(d, min(d + 2, half + 1))) for d in range(1, half + 1, 2)] + [[d] for d in range(half + 1, ep_size)]
     outs, gdis, gdis_back, sums, bias_sums = [], [], [], (), None
     for number, group in enumerate(groups):
         if number == 1:
@@ -688,13 +625,13 @@
         xs, gs = [x_all[d] for d in group], [g_all[d] for d in group]
         if number == 0:
             xs = after(xs, *g_all[1:])
-        o, g, sums, sums_b = expert_call(xs, gs, w_in, w_back, b_in, b_back, place_e, blocks, tuple(sums), 10 * len(group))
+        o, g, sums, sums_b = expert_call(xs, gs, w_in, w_back, in_bias, back_bias, place_e, blocks, tuple(sums), 10 * len(group))
         outs, gdis = outs + list(o), gdis + list(g)
         for d in group:
             send, = after([gdis[d]], *([x_all[-1]] if d >= half else []))
             gdis_back.append(over_ep(send, d) if d else send)
         bias_sums = sums_b if number == 0 else [a + b for a, b in zip(bias_sums, sums_b)]
-    gb_in, gb_back = bias_sums[0][:, 0], bias_sums[1][:, 0]
+    gb_in, gb_back = bias_sums
     far_b, far_i, near_b, near_i = sums
     far_i, = after([far_i], gdis_back[half])
     state = [near_b + swap(far_b, "grp", grp_size, 1), near_i + swap(far_i, "grp", grp_size, 1)]

time: 289 us -> 259 us (0.90)
  Pallas kernels: 128 us -> 88.3 us
  waiting for transfers between devices: 74.8 us -> 82.7 us
  other arithmetic: 13.2 us -> 5.55 us
  starting transfers between devices: 45.1 us -> 50.9 us
  local copies, waits for them, and re-layouts: 21.1 us -> 25 us
    pallas_call x3, Pallas kernels: 54.8 us -> 35 us  [expert_call(): pl.pallas_call(functools.partial(expert_kernel, count, len(before), block...]
    unnamed x42 -> x104, local copies, waits for them, and re-layouts: 10.1 us -> 20.3 us
    ppermute x49, waiting for transfers between devices: 74.8 us -> 82.7 us  [swap(): return lax.ppermute(array, axis, [(i, i ^ distance) for i in range(size)])]
    pallas_call x4, Pallas kernels: 18.6 us -> 12 us  [widen_call(): pl.pallas_call(functools.partial(widen_kernel, count), grid_spec=pltpu.Pr...]
    ppermute x49, starting transfers between devices: 45.1 us -> 50.9 us  [swap(): return lax.ppermute(array, axis, [(i, i ^ distance) for i in range(size)])]
    pallas_call x1, Pallas kernels: 25.2 us -> 22 us  [backward_call(): pl.pallas_call(functools.partial(backward_kernel, width // HD, ep_size, p...]
    pallas_call x1, Pallas kernels: 5.85 us -> 2.94 us  [combine_call(): pl.pallas_call(functools.partial(combine_kernel, len(chunks)), grid=(n_im...]
  transfers between devices with their start and end apart: 49 -> 49, of which waited for: 14 -> 18; matrix products, arithmetic and copies ran while one was open for 11% -> 6% of each run, Pallas kernels for 43% -> 34%
where the time goes in v5:
time: 259 us; the launch traced here: 254 us
  Pallas kernels  88.3 us (34%)
  waiting for transfers between devices  82.7 us (32%)
  starting transfers between devices  50.9 us (20%)
  local copies, waits for them, and re-layouts  25 us (10%)
  other arithmetic  5.55 us (2%)
    ppermute x49, waiting for transfers between devices, swap(): return lax.ppermute(array, axis, [(i, i ^ distance) for i in range(size)])  82.7 us
    ppermute x49, starting transfers between devices, swap(): return lax.ppermute(array, axis, [(i, i ^ distance) for i in range(size)])  50.9 us
    pallas_call x3, Pallas kernels, expert_call(): pl.pallas_call(functools.partial(expert_kernel, count, len(before), block...  35 us
    pallas_call x1, Pallas kernels, backward_call(): pl.pallas_call(functools.partial(backward_kernel, width // HD, ep_size, p...  22 us
    unnamed x104, local copies, waits for them, and re-layouts  20.3 us
    pallas_call x4, Pallas kernels, widen_call(): pl.pallas_call(functools.partial(widen_kernel, count), grid_spec=pltpu.Pr...  12 us
    pallas_call x1, Pallas kernels, attention_call(): pl.pallas_call(functools.partial(attention_kernel, width // HD), grid=(n_...  11.9 us
  transfers between devices with their start and end apart: 49, of which 18 were waited for; matrix products, arithmetic and copies ran while one was open for 6% of the time, Pallas kernels for 34%

profile of v5, /device:TPU:0, one launch (start us, length us, event | category | flops | bytes accessed | tf_op | source)
XLA Modules:
  0.0 254.3 jit_solution(10727536009763754044)
XLA Ops:
  0.6 4.1 %collective-permute-start.4 = (bf16[4,197,512]{2,0,1:T(4,128)(2,1)}, bf16[4,197,512]{2,0,1:T(4,128)(2,1)}, u32[]{:S(2)}, u32[]{:S(2)}) collective-permute-start(bf16[4,197,512]{2,0,1:T(4,128)(2,1)} %param.29), channel_id=1, source_target_pairs={{0,2},{1,3},{2,0},{3,1},{4,6},{5,7},{6,4},{7,5},{8,10},{9,11},{10,... | collective-permute-start | bytes 2420744 | tf_op jit(solution)/shard_map/ppermute | solution.py:480
  4.7 1.3 copy.45.cot_ref
  7.5 2.2 route_and_dispatch_cotangent.1
  9.7 1.9 collective-permute-start
  13.0 11.9 %attention_forward_and_dispatch.1 = (bf16[4,197,1536]{2,1,0:T(8,128)(2,1)S(1)}, bf16[4,197,512]{2,1,0:T(8,128)(2,1)S(1)}, f32[4,197,128]{2,1,0:T(8,128)S(1)}, f3...) custom-call(bf16[4,197,512]{2,1,0:T(8,128)(2,1)S(1)} %copy.46.tok_re, ...), custom_call_target="tpu_custom_call" | custom-call | flops 14000000000 | bytes 4096 | tf_op jit(solution)/shard_map/attention_forward_and_dispatch/pallas_call | solution.py:210
  26.9 1.4 copy-done.32
  31.2 2.5 %collective-permute-start.2 = (bf16[2,248,512]{2,1,0:T(8,128)(2,1)}, bf16[2,248,512]{2,1,0:T(8,128)(2,1)}, u32[]{:S(2)}, u32[]{:S(2)}) collective-permute-start(bf16[2,248,512]{2,1,0:T(8,128)(2,1)} %get-tuple-element.86), channel_id=1, source_target_pairs={{0,2},{1,3},{2,0},{3,1},{4,6},{5,7},{6,4},{7,5},{8,10},{9,11},{10,... | collective-permute-start | bytes 1523720 | tf_op jit(solution)/shard_map/ppermute | solution.py:480
  33.8 1.9 collective-permute-done.refs_2_
  35.8 2.2 copy-done
  38.0 2.2 copy-done.2
  42.2 8.1 %experts.3 = (bf16[2,248,512]{2,1,0:T(8,128)(2,1)S(1)}, bf16[2,248,512]{2,1,0:T(8,128)(2,1)S(1)}, bf16[4,512,512]{2,1,0:T(8,128)(2,1)S(1)}, bf16[4,512,512]{2,1,...) custom-call(s32[3]{0:T(128)S(1)} %pad_add_fusion.sel_ref, ...), custom_call_target="tpu_custom_call" | custom-call | flops 10000000000 | bytes 4096 | tf_op jit(solution)/shard_map/experts/pallas_call | solution.py:298
  51.1 1.5 copy.47.cot_ref
  53.9 2.6 %collective-permute-start.6 = (bf16[2,248,512]{2,1,0:T(8,128)(2,1)S(1)}, bf16[2,248,512]{2,1,0:T(8,128)(2,1)S(1)}, u32[]{:S(2)}, u32[]{:S(2)}) collective-permute-start(bf16[2,248,512]{2,1,0:T(8,128)(2,1)S(1)} %get-tuple-element.95), channel_id=1, source_target_pairs={{0,1},{1,0},{2,3},{3,2},{4,5},{5,4},{6,7},{7,6},{8,9},{9,8},{10,11... | collective-permute-start | bytes 1523720 | tf_op jit(solution)/shard_map/ppermute | solution.py:480
  56.4 3.0 %collective-permute-done.1.refs_0_ = bf16[2,248,512]{2,1,0:T(8,128)(2,1)} collective-permute-done((bf16[2,248,512]{2,1,0:T(8,128)(2,1)}, bf16[2,248,512]{2,1,0:T(8,128)(2,1)}, u32[]{:S(2)}, u32[]{:S(2)}) %collective-permute-start.1) | collective-permute-done | bytes 507936 | tf_op jit(solution)/shard_map/ppermute | solution.py:480
  59.4 5.6 %collective-permute-done.2.refs_1_ = bf16[2,248,512]{2,1,0:T(8,128)(2,1)} collective-permute-done((bf16[2,248,512]{2,1,0:T(8,128)(2,1)}, bf16[2,248,512]{2,1,0:T(8,128)(2,1)}, u32[]{:S(2)}, u32[]{:S(2)}) %collective-permute-start.2) | collective-permute-done | bytes 507936 | tf_op jit(solution)/shard_map/ppermute | solution.py:480
  65.1 3.5 %collective-permute-start.5 = (bf16[2,248,512]{2,1,0:T(8,128)(2,1)S(1)}, bf16[2,248,512]{2,1,0:T(8,128)(2,1)S(1)}, u32[]{:S(2)}, u32[]{:S(2)}) collective-permute-start(bf16[2,248,512]{2,1,0:T(8,128)(2,1)S(1)} %copy-done.14), channel_id=1, source_target_pairs={{0,3},{1,2},{2,1},{3,0},{4,7},{5,6},{6,5},{7,4},{8,11},{9,10},{10,... | collective-permute-start | bytes 1523720 | tf_op jit(solution)/shard_map/ppermute | solution.py:480
  68.6 18.2 %experts.4 = (bf16[2,248,512]{2,1,0:T(8,128)(2,1)S(1)}, bf16[2,248,512]{2,1,0:T(8,128)(2,1)S(1)}, bf16[2,248,512]{2,1,0:T(8,128)(2,1)}, bf16[2,248,512]{2,1,0:T(...) custom-call(s32[3]{0:T(128)S(1)} %pad_add_fusion.sel_ref, ...), custom_call_target="tpu_custom_call", output_to_operand_aliasing={{4}: (9, {}), {5}: (10, {}), {6}: (11, {}), {7}: (12, {})} | custom-call | flops 20000000000 | bytes 4096 | tf_op jit(solution)/shard_map/experts/pallas_call | solution.py:298
  86.8 3.0 %collective-permute-start.9 = (bf16[2,248,512]{2,1,0:T(8,128)(2,1)S(1)}, bf16[2,248,512]{2,1,0:T(8,128)(2,1)S(1)}, u32[]{:S(2)}, u32[]{:S(2)}) collective-permute-start(bf16[2,248,512]{2,1,0:T(8,128)(2,1)S(1)} %get-tuple-element.106), channel_id=1, source_target_pairs={{0,2},{1,3},{2,0},{3,1},{4,6},{5,7},{6,4},{7,5},{8,10},{9,11},{10,... | collective-permute-start | bytes 1523720 | tf_op jit(solution)/shard_map/ppermute | solution.py:480
  89.8 8.8 %experts.5 = (bf16[2,248,512]{2,1,0:T(8,128)(2,1)S(1)}, bf16[2,248,512]{2,1,0:T(8,128)(2,1)S(1)}, bf16[4,512,512]{2,1,0:T(8,128)(2,1)S(1)}, bf16[4,512,512]{2,1,...) custom-call(s32[3]{0:T(128)S(1)} %pad_add_fusion.sel_ref, ...), custom_call_target="tpu_custom_call", output_to_operand_aliasing={{2}: (7, {}), {3}: (8, {}), {4}: (9, {}), {5}: (10, {})} | custom-call | flops 10000000000 | bytes 4096 | tf_op jit(solution)/shard_map/experts/pallas_call | solution.py:298
  98.7 13.2 %collective-permute-done.9.rest_2_ = bf16[2,248,512]{2,1,0:T(8,128)(2,1)S(1)} collective-permute-done((bf16[2,248,512]{2,1,0:T(8,128)(2,1)S(1)}, bf16[2,248,512]{2,1,0:T(8,128)(2,1)S(1)}, u32[]{:S(2)}, u32[]{:S(2)}) %collective-permute-start.9) | collective-permute-done | bytes 507936 | tf_op jit(solution)/shard_map/ppermute | solution.py:480
  113.9 1.5 collective-permute-start.8
  118.5 1.5 collective-permute-start.11
  120.0 2.4 collective-permute-start.13
  122.4 17.3 %collective-permute-done.8 = bf16[2,512,512]{2,1,0:T(8,128)(2,1)} collective-permute-done((bf16[2,512,512]{2,1,0:T(8,128)(2,1)}, bf16[2,512,512]{2,1,0:T(8,128)(2,1)}, u32[]{:S(2)}, u32[]{:S(2)}) %collective-permute-start.8) | collective-permute-done | bytes 1048608 | tf_op jit(solution)/shard_map/ppermute | solution.py:480
  139.7 1.8 slice_add_fusion.1
  141.6 1.6 collective-permute-start.17
  144.0 1.6 slice_add_fusion
  145.7 1.6 collective-permute-start.18
  148.1 2.1 collective-permute-start.15
  150.3 22.0 %attention_backward.1 = (bf16[4,197,512]{2,1,0:T(8,128)(2,1)S(1)}, bf16[8,2,16,2176]{3,2,1,0:T(8,128)(2,1)S(1)}, bf16[8,2,16,2176]{3,2,1,0:T(8,128)(2,1)S(1)}) custom-call(s32[2]{0:T(128)S(1)} %pad_add_fusion.1.place_ref, f32[40,128]{1,0:T(8,128)S(1)} %pad_maximum_fusion.bias_ref, bf16[4,197,512]{2,1,0:T(8,128)(2,1)S(1)} %copy.46.tok_ref, ...), custom_call_target="tpu_custom_call" | custom-call | flops 24999999488 | bytes 4096 | tf_op jit(solution)/shard_map/attention_backward/pallas_call | solution.py:443
  172.8 1.3 copy.51
  174.1 1.5 collective-permute-start.43
  175.6 1.6 collective-permute-start.16
  179.0 1.3 collective-permute-done.19
  181.5 12.9 %collective-permute-done.23 = bf16[2,2,16,2176]{3,2,1,0:T(8,128)(2,1)S(1)} collective-permute-done((bf16[2,2,16,2176]{3,2,1,0:T(8,128)(2,1)S(1)}, bf16[2,2,16,2176]{3,2,1,0:T(8,128)(2,1)S(1)}, u32[]{:S(2)}, u32[]{:S(2)}) %collective-permute-start.23) | collective-permute-done | bytes 278560 | tf_op jit(solution)/shard_map/ppermute | solution.py:480
  195.4 1.7 collective-permute-done.20
  197.6 2.4 collective-permute-done.24
  200.0 2.2 collective-permute-done.21
  202.6 3.1 %collective-permute-start.26 = (bf16[16,2176]{1,0:T(8,128)(2,1)S(1)}, bf16[16,2176]{1,0:T(8,128)(2,1)S(1)}, u32[]{:S(2)}, u32[]{:S(2)}) collective-permute-start(bf16[16,2176]{1,0:T(8,128)(2,1)S(1)} %get-tuple-element.165), channel_id=1, source_target_pairs={{0,2},{1,3},{2,0},{3,1},{4,6},{5,7},{6,4},{7,5},{8,10},{9,11},{10,... | collective-permute-start | bytes 208904 | tf_op jit(solution)/shard_map/ppermute | solution.py:480
  206.7 2.9 %combine_output.1 = bf16[4,197,512]{2,1,0:T(8,128)(2,1)S(1)} custom-call(f32[4,197,512]{2,1,0:T(8,128)S(1)} %copy-done.23, f32[4,197,8]{2,1,0:T(8,128)S(1)} %copy-done.29, f32[4,197,8]{2,1,0:T(8,128)S(1)} %copy-done.31, bf16[2,248,512]{2,1,0:T(8,128)(2,1)S(1)} %copy-done.25, bf16[2,248,512]{2,1,0:T(8,128)(2,1)S(1)} %collective-permute-done.14.rest_1_, ...), custom_call_target="tpu_custom_call" | custom-call | flops 5000000000 | bytes 4096 | tf_op jit(solution)/shard_map/combine_output/pallas_call | solution.py:467
  209.7 1.3 copy.50
  213.5 1.6 collective-permute-start.40
  215.2 10.7 %collective-permute-done.45.refs_2_ = bf16[1,512,512]{2,1,0:T(8,128)(2,1)S(1)} collective-permute-done((bf16[1,512,512]{2,1,0:T(8,128)(2,1)S(1)}, bf16[1,512,512]{2,1,0:T(8,128)(2,1)S(1)}, u32[]{:S(2)}, u32[]{:S(2)}) %collective-permute-start.45) | collective-permute-done | bytes 524320 | tf_op jit(solution)/shard_map/ppermute | solution.py:480
  226.4 6.7 %collective-permute-done.47.refs_3_ = bf16[1,512,512]{2,1,0:T(8,128)(2,1)S(1)} collective-permute-done((bf16[1,512,512]{2,1,0:T(8,128)(2,1)S(1)}, bf16[1,512,512]{2,1,0:T(8,128)(2,1)S(1)}, u32[]{:S(2)}, u32[]{:S(2)}) %collective-permute-start.47) | collective-permute-done | bytes 524320 | tf_op jit(solution)/shard_map/ppermute | solution.py:480
  233.9 3.0 %expert_gradient_result.6.refs_4_ = f32[2,2048,512]{2,1,0:T(8,128)} custom-call(s32[2]{0:T(128)S(1)} %pad_add_fusion.5.place_ref, bf16[1,512,512]{2,1,0:T(8,128)(2,1)S(1)} %slice_add_fusion.5.refs_0_, bf16[1,512,512]{2,1,0:T(8,128)(2,1)S(1)} %collective-permute-done.43.refs_1_, bf16[1,512,512]{2,1,0:T(8,128)(2,1)S(1)} %collective-permute-done.45.refs_2_, ...), custom_call_target="tpu_custom_call" | custom-call | flops 4000000000 | bytes 4096 | tf_op jit(solution)/shard_map/expert_gradient_result/pallas_call | solution.py:516
  240.2 3.0 %expert_gradient_result.4.refs_4_ = f32[2,512,2048]{2,1,0:T(8,128)} custom-call(s32[2]{0:T(128)S(1)} %pad_add_fusion.2.place_ref, bf16[1,512,512]{2,1,0:T(8,128)(2,1)S(1)} %slice_add_fusion.4.refs_0_, bf16[1,512,512]{2,1,0:T(8,128)(2,1)S(1)} %collective-permute-done.36.refs_1_, bf16[1,512,512]{2,1,0:T(8,128)(2,1)S(1)} %collective-permute-done.38.refs_2_, ...), custom_call_target="tpu_custom_call" | custom-call | flops 4000000000 | bytes 4096 | tf_op jit(solution)/shard_map/expert_gradient_result/pallas_call | solution.py:516
  244.3 3.0 %expert_gradient_result.7 = f32[2,2048,512]{2,1,0:T(8,128)} custom-call(s32[2]{0:T(128)S(1)} %get-tuple-element.173.place_ref, bf16[1,512,512]{2,1,0:T(8,128)(2,1)S(1)} %collective-permute-done.42.refs_0_, bf16[1,512,512]{2,1,0:T(8,128)(2,1)S(1)} %collective-permute-done.44.refs_1_, ...), custom_call_target="tpu_custom_call", output_to_operand_aliasing={{}: (5, {})} | custom-call | flops 4000000000 | bytes 4096 | tf_op jit(solution)/shard_map/expert_gradient_result/pallas_call | solution.py:516
  250.8 3.0 %expert_gradient_result.5 = f32[2,512,2048]{2,1,0:T(8,128)} custom-call(s32[2]{0:T(128)S(1)} %get-tuple-element.172.place_ref, bf16[1,512,512]{2,1,0:T(8,128)(2,1)S(1)} %collective-permute-done.35.refs_0_, bf16[1,512,512]{2,1,0:T(8,128)(2,1)S(1)} %collective-permute-done.37.refs_1_, ...), custom_call_target="tpu_custom_call", output_to_operand_aliasing={{}: (5, {})} | custom-call | flops 4000000000 | bytes 4096 | tf_op jit(solution)/shard_map/expert_gradient_result/pallas_call | solution.py:516
  (207 shorter events, 36.7 us)
Async XLA Ops:
  0.6 50.5 %collective-permute-start.4 = (bf16[4,197,512]{2,0,1:T(4,128)(2,1)}, bf16[4,197,512]{2,0,1:T(4,128)(2,1)}, u32[]{:S(2)}, u32[]{:S(2)}) collective-permute-start(bf16[4,197,512]{2,0,1:T(4,128)(2,1)} %param.29), channel_id=1, source_target_pairs={{0,2},{1,3},{2,0},{3,1},{4,6},{5,7},{6,4},{7,5},{8,10},{9,11},{10,... | collective-permute-start | bytes 2420744 | tf_op jit(solution)/shard_map/ppermute | solution.py:480
  9.7 41.4 %collective-permute-start.3 = (f32[2,4,8,197]{3,2,1,0:T(8,128)S(1)}, f32[2,4,8,197]{3,2,1,0:T(8,128)S(1)}, u32[]{:S(2)}, u32[]{:S(2)}) collective-permute-start(f32[2,4,8,197]{3,2,1,0:T(8,128)S(1)} %get-tuple-element.76.info_ref), channel_id=1, source_target_pairs={{0,2},{1,3},{2,0},{3,1},{4,6},{5,7},{6,4},{7,5},{8,10},{9,11},{10,... | collective-permute-start | bytes 151304 | tf_op jit(solution)/shard_map/ppermute | solution.py:480
  9.7 26.0 %collective-permute-start = (bf16[2,248,512]{2,1,0:T(8,128)(2,1)}, bf16[2,248,512]{2,1,0:T(8,128)(2,1)}, u32[]{:S(2)}, u32[]{:S(2)}) collective-permute-start(bf16[2,248,512]{2,1,0:T(8,128)(2,1)} %get-tuple-element.81), channel_id=1, source_target_pairs={{0,1},{1,0},{2,3},{3,2},{4,5},{5,4},{6,7},{7,6},{8,9},{9,8},{10,11... | collective-permute-start | bytes 1523720 | tf_op jit(solution)/shard_map/ppermute | solution.py:480
  30.7 28.7 %collective-permute-start.1 = (bf16[2,248,512]{2,1,0:T(8,128)(2,1)}, bf16[2,248,512]{2,1,0:T(8,128)(2,1)}, u32[]{:S(2)}, u32[]{:S(2)}) collective-permute-start(bf16[2,248,512]{2,1,0:T(8,128)(2,1)} %get-tuple-element.85), channel_id=1, source_target_pairs={{0,1},{1,0},{2,3},{3,2},{4,5},{5,4},{6,7},{7,6},{8,9},{9,8},{10,11... | collective-permute-start | bytes 1523720 | tf_op jit(solution)/shard_map/ppermute | solution.py:480
  31.2 33.8 %collective-permute-start.2 = (bf16[2,248,512]{2,1,0:T(8,128)(2,1)}, bf16[2,248,512]{2,1,0:T(8,128)(2,1)}, u32[]{:S(2)}, u32[]{:S(2)}) collective-permute-start(bf16[2,248,512]{2,1,0:T(8,128)(2,1)} %get-tuple-element.86), channel_id=1, source_target_pairs={{0,2},{1,3},{2,0},{3,1},{4,6},{5,7},{6,4},{7,5},{8,10},{9,11},{10,... | collective-permute-start | bytes 1523720 | tf_op jit(solution)/shard_map/ppermute | solution.py:480
  53.9 35.9 %collective-permute-start.6 = (bf16[2,248,512]{2,1,0:T(8,128)(2,1)S(1)}, bf16[2,248,512]{2,1,0:T(8,128)(2,1)S(1)}, u32[]{:S(2)}, u32[]{:S(2)}) collective-permute-start(bf16[2,248,512]{2,1,0:T(8,128)(2,1)S(1)} %get-tuple-element.95), channel_id=1, source_target_pairs={{0,1},{1,0},{2,3},{3,2},{4,5},{5,4},{6,7},{7,6},{8,9},{9,8},{10,11... | collective-permute-start | bytes 1523720 | tf_op jit(solution)/shard_map/ppermute | solution.py:480
  65.1 21.7 %collective-permute-start.5 = (bf16[2,248,512]{2,1,0:T(8,128)(2,1)S(1)}, bf16[2,248,512]{2,1,0:T(8,128)(2,1)S(1)}, u32[]{:S(2)}, u32[]{:S(2)}) collective-permute-start(bf16[2,248,512]{2,1,0:T(8,128)(2,1)S(1)} %copy-done.14), channel_id=1, source_target_pairs={{0,3},{1,2},{2,1},{3,0},{4,7},{5,6},{6,5},{7,4},{8,11},{9,10},{10,... | collective-permute-start | bytes 1523720 | tf_op jit(solution)/shard_map/ppermute | solution.py:480
  86.8 25.2 %collective-permute-start.9 = (bf16[2,248,512]{2,1,0:T(8,128)(2,1)S(1)}, bf16[2,248,512]{2,1,0:T(8,128)(2,1)S(1)}, u32[]{:S(2)}, u32[]{:S(2)}) collective-permute-start(bf16[2,248,512]{2,1,0:T(8,128)(2,1)S(1)} %get-tuple-element.106), channel_id=1, source_target_pairs={{0,2},{1,3},{2,0},{3,1},{4,6},{5,7},{6,4},{7,5},{8,10},{9,11},{10,... | collective-permute-start | bytes 1523720 | tf_op jit(solution)/shard_map/ppermute | solution.py:480
  98.6 13.3 %collective-permute-start.7 = (bf16[4,512,512]{2,1,0:T(8,128)(2,1)S(1)}, bf16[4,512,512]{2,1,0:T(8,128)(2,1)S(1)}, u32[]{:S(2)}, u32[]{:S(2)}) collective-permute-start(bf16[4,512,512]{2,1,0:T(8,128)(2,1)S(1)} %get-tuple-element.102), channel_id=1, source_target_pairs={{0,4},{4,0},{8,12},{12,8},{16,20},{20,16},{24,28},{28,24},{1,5},{5... | collective-permute-start | bytes 6291464 | tf_op jit(solution)/shard_map/ppermute | solution.py:480
  111.9 4.2 %collective-permute-start.10 = (bf16[4,512,512]{2,1,0:T(8,128)(2,1)S(1)}, bf16[4,512,512]{2,1,0:T(8,128)(2,1)S(1)}, u32[]{:S(2)}, u32[]{:S(2)}) collective-permute-start(bf16[4,512,512]{2,1,0:T(8,128)(2,1)S(1)} %get-tuple-element.107), channel_id=1, source_target_pairs={{0,4},{4,0},{8,12},{12,8},{16,20},{20,16},{24,28},{28,24},{1,5},{5... | collective-permute-start | bytes 6291464 | tf_op jit(solution)/shard_map/ppermute | solution.py:480
  113.9 25.8 %collective-permute-start.8 = (bf16[2,512,512]{2,1,0:T(8,128)(2,1)}, bf16[2,512,512]{2,1,0:T(8,128)(2,1)}, u32[]{:S(2)}, u32[]{:S(2)}) collective-permute-start(bf16[2,512,512]{2,1,0:T(8,128)(2,1)} %slice.117), channel_id=1, source_target_pairs={{0,8},{4,12},{8,0},{12,4},{16,24},{20,28},{24,16},{28,20},{1,9},{5... | collective-permute-start | bytes 3145736 | tf_op jit(solution)/shard_map/ppermute | solution.py:480
  115.5 31.8 %collective-permute-start.12 = (bf16[2,248,512]{2,1,0:T(8,128)(2,1)}, bf16[2,248,512]{2,1,0:T(8,128)(2,1)}, u32[]{:S(2)}, u32[]{:S(2)}) collective-permute-start(bf16[2,248,512]{2,1,0:T(8,128)(2,1)} %get-tuple-element.109), channel_id=1, source_target_pairs={{0,1},{1,0},{2,3},{3,2},{4,5},{5,4},{6,7},{7,6},{8,9},{9,8},{10,11... | collective-permute-start | bytes 1523720 | tf_op jit(solution)/shard_map/ppermute | solution.py:480
  118.5 25.5 %collective-permute-start.11 = (bf16[2,512,512]{2,1,0:T(8,128)(2,1)}, bf16[2,512,512]{2,1,0:T(8,128)(2,1)}, u32[]{:S(2)}, u32[]{:S(2)}) collective-permute-start(bf16[2,512,512]{2,1,0:T(8,128)(2,1)} %slice.119), channel_id=1, source_target_pairs={{0,16},{4,20},{8,24},{12,28},{16,0},{20,4},{24,8},{28,12},{1,17},{... | collective-permute-start | bytes 3145736 | tf_op jit(solution)/shard_map/ppermute | solution.py:480
  120.0 27.2 %collective-permute-start.13 = (bf16[2,248,512]{2,1,0:T(8,128)(2,1)}, bf16[2,248,512]{2,1,0:T(8,128)(2,1)S(1)}, u32[]{:S(2)}, u32[]{:S(2)}) collective-permute-start(bf16[2,248,512]{2,1,0:T(8,128)(2,1)} %copy-done.17), channel_id=1, source_target_pairs={{0,3},{1,2},{2,1},{3,0},{4,7},{5,6},{6,5},{7,4},{8,11},{9,10},{10,... | collective-permute-start | bytes 1523720 | tf_op jit(solution)/shard_map/ppermute | solution.py:480
  141.6 30.6 %collective-permute-start.17 = (bf16[1,512,512]{2,1,0:T(8,128)(2,1)S(1)}, bf16[1,512,512]{2,1,0:T(8,128)(2,1)S(1)}, u32[]{:S(2)}, u32[]{:S(2)}) collective-permute-start(bf16[1,512,512]{2,1,0:T(8,128)(2,1)S(1)} %slice.121), channel_id=1, source_target_pairs={{0,16},{4,20},{8,24},{12,28},{16,0},{20,4},{24,8},{28,12},{1,17},{... | collective-permute-start | bytes 1572872 | tf_op jit(solution)/shard_map/ppermute | solution.py:480
  145.7 26.7 %collective-permute-start.18 = (bf16[1,512,512]{2,1,0:T(8,128)(2,1)S(1)}, bf16[1,512,512]{2,1,0:T(8,128)(2,1)S(1)}, u32[]{:S(2)}, u32[]{:S(2)}) collective-permute-start(bf16[1,512,512]{2,1,0:T(8,128)(2,1)S(1)} %slice.123), channel_id=1, source_target_pairs={{0,8},{4,12},{8,0},{12,4},{16,24},{20,28},{24,16},{28,20},{1,9},{5... | collective-permute-start | bytes 1572872 | tf_op jit(solution)/shard_map/ppermute | solution.py:480
  147.2 25.2 %collective-permute-start.14 = (bf16[2,248,512]{2,1,0:T(8,128)(2,1)S(1)}, bf16[2,248,512]{2,1,0:T(8,128)(2,1)S(1)}, u32[]{:S(2)}, u32[]{:S(2)}) collective-permute-start(bf16[2,248,512]{2,1,0:T(8,128)(2,1)S(1)} %copy-done.12), channel_id=1, source_target_pairs={{0,1},{1,0},{2,3},{3,2},{4,5},{5,4},{6,7},{7,6},{8,9},{9,8},{10,11... | collective-permute-start | bytes 1523720 | tf_op jit(solution)/shard_map/ppermute | solution.py:480
  148.1 24.4 %collective-permute-start.15 = (bf16[2,248,512]{2,1,0:T(8,128)(2,1)S(1)}, bf16[2,248,512]{2,1,0:T(8,128)(2,1)S(1)}, u32[]{:S(2)}, u32[]{:S(2)}) collective-permute-start(bf16[2,248,512]{2,1,0:T(8,128)(2,1)S(1)} %copy-done.10), channel_id=1, source_target_pairs={{0,2},{1,3},{2,0},{3,1},{4,6},{5,7},{6,4},{7,5},{8,10},{9,11},{10,... | collective-permute-start | bytes 1523720 | tf_op jit(solution)/shard_map/ppermute | solution.py:480
  172.5 5.8 %collective-permute-start.22 = (bf16[4,2,16,2176]{3,2,1,0:T(8,128)(2,1)S(1)}, bf16[4,2,16,2176]{3,2,1,0:T(8,128)(2,1)S(1)}, u32[]{:S(2)}, u32[]{:S(2)}) collective-permute-start(bf16[4,2,16,2176]{3,2,1,0:T(8,128)(2,1)S(1)} %slice.102), channel_id=1, source_target_pairs={{0,4},{4,0},{8,12},{12,8},{16,20},{20,16},{24,28},{28,24},{1,5},{5... | collective-permute-start | bytes 1671176 | tf_op jit(solution)/shard_map/ppermute | solution.py:480
  174.1 36.9 %collective-permute-start.43 = (bf16[1,512,512]{2,1,0:T(8,128)(2,1)S(1)}, bf16[1,512,512]{2,1,0:T(8,128)(2,1)S(1)}, u32[]{:S(2)}, u32[]{:S(2)}) collective-permute-start(bf16[1,512,512]{2,1,0:T(8,128)(2,1)S(1)} %slice_add_fusion.5.refs_0_), channel_id=1, source_target_pairs={{0,16},{4,20},{8,24},{12,28},{16,0},{20,4},{24,8},{28,12},{1,17},{... | collective-permute-start | bytes 1572872 | tf_op jit(solution)/shard_map/ppermute | solution.py:480
  175.6 26.6 %collective-permute-start.16 = (bf16[2,248,512]{2,1,0:T(8,128)(2,1)S(1)}, bf16[2,248,512]{2,1,0:T(8,128)(2,1)S(1)}, u32[]{:S(2)}, u32[]{:S(2)}) collective-permute-start(bf16[2,248,512]{2,1,0:T(8,128)(2,1)S(1)} %copy-done.8), channel_id=1, source_target_pairs={{0,3},{1,2},{2,1},{3,0},{4,7},{5,6},{6,5},{7,4},{8,11},{9,10},{10,... | collective-permute-start | bytes 1523720 | tf_op jit(solution)/shard_map/ppermute | solution.py:480
  177.2 34.9 %collective-permute-start.36 = (bf16[1,512,512]{2,1,0:T(8,128)(2,1)S(1)}, bf16[1,512,512]{2,1,0:T(8,128)(2,1)S(1)}, u32[]{:S(2)}, u32[]{:S(2)}) collective-permute-start(bf16[1,512,512]{2,1,0:T(8,128)(2,1)S(1)} %slice_add_fusion.4.refs_0_), channel_id=1, source_target_pairs={{0,8},{4,12},{8,0},{12,4},{16,24},{20,28},{24,16},{28,20},{1,9},{5... | collective-permute-start | bytes 1572872 | tf_op jit(solution)/shard_map/ppermute | solution.py:480
  178.5 15.9 %collective-permute-start.23 = (bf16[2,2,16,2176]{3,2,1,0:T(8,128)(2,1)S(1)}, bf16[2,2,16,2176]{3,2,1,0:T(8,128)(2,1)S(1)}, u32[]{:S(2)}, u32[]{:S(2)}) collective-permute-start(bf16[2,2,16,2176]{3,2,1,0:T(8,128)(2,1)S(1)} %slice.129), channel_id=1, source_target_pairs={{0,16},{4,20},{8,24},{12,28},{16,0},{20,4},{24,8},{28,12},{1,17},{... | collective-permute-start | bytes 835592 | tf_op jit(solution)/shard_map/ppermute | solution.py:480
  180.4 16.6 %collective-permute-start.20 = (bf16[2,2,16,2176]{3,2,1,0:T(8,128)(2,1)S(1)}, bf16[2,2,16,2176]{3,2,1,0:T(8,128)(2,1)S(1)}, u32[]{:S(2)}, u32[]{:S(2)}) collective-permute-start(bf16[2,2,16,2176]{3,2,1,0:T(8,128)(2,1)S(1)} %slice.125), channel_id=1, source_target_pairs={{0,8},{4,12},{8,0},{12,4},{16,24},{20,28},{24,16},{28,20},{1,9},{5... | collective-permute-start | bytes 835592 | tf_op jit(solution)/shard_map/ppermute | solution.py:480
  194.5 5.5 %collective-permute-start.24 = (bf16[1,2,16,2176]{3,2,1,0:T(8,128)(2,1)S(1)}, bf16[1,2,16,2176]{3,2,1,0:T(8,128)(2,1)S(1)}, u32[]{:S(2)}, u32[]{:S(2)}) collective-permute-start(bf16[1,2,16,2176]{3,2,1,0:T(8,128)(2,1)S(1)} %slice.131), channel_id=1, source_target_pairs={{0,8},{4,12},{8,0},{12,4},{16,24},{20,28},{24,16},{28,20},{1,9},{5... | collective-permute-start | bytes 417800 | tf_op jit(solution)/shard_map/ppermute | solution.py:480
  197.1 5.1 %collective-permute-start.21 = (bf16[1,2,16,2176]{3,2,1,0:T(8,128)(2,1)S(1)}, bf16[1,2,16,2176]{3,2,1,0:T(8,128)(2,1)S(1)}, u32[]{:S(2)}, u32[]{:S(2)}) collective-permute-start(bf16[1,2,16,2176]{3,2,1,0:T(8,128)(2,1)S(1)} %slice.127), channel_id=1, source_target_pairs={{0,16},{4,20},{8,24},{12,28},{16,0},{20,4},{24,8},{28,12},{1,17},{... | collective-permute-start | bytes 417800 | tf_op jit(solution)/shard_map/ppermute | solution.py:480
  202.3 9.9 %collective-permute-start.25 = (bf16[16,2176]{1,0:T(8,128)(2,1)S(1)}, bf16[16,2176]{1,0:T(8,128)(2,1)S(1)}, u32[]{:S(2)}, u32[]{:S(2)}) collective-permute-start(bf16[16,2176]{1,0:T(8,128)(2,1)S(1)} %slice_bitcast_fusion.2), channel_id=1, source_target_pairs={{0,1},{1,0},{2,3},{3,2},{4,5},{5,4},{6,7},{7,6},{8,9},{9,8},{10,11... | collective-permute-start | bytes 208904 | tf_op jit(solution)/shard_map/ppermute | solution.py:480
  202.6 9.9 %collective-permute-start.26 = (bf16[16,2176]{1,0:T(8,128)(2,1)S(1)}, bf16[16,2176]{1,0:T(8,128)(2,1)S(1)}, u32[]{:S(2)}, u32[]{:S(2)}) collective-permute-start(bf16[16,2176]{1,0:T(8,128)(2,1)S(1)} %get-tuple-element.165), channel_id=1, source_target_pairs={{0,2},{1,3},{2,0},{3,1},{4,6},{5,7},{6,4},{7,5},{8,10},{9,11},{10,... | collective-permute-start | bytes 208904 | tf_op jit(solution)/shard_map/ppermute | solution.py:480
  205.7 7.8 %collective-permute-start.27 = (bf16[16,2176]{1,0:T(8,128)(2,1)S(1)}, bf16[16,2176]{1,0:T(8,128)(2,1)S(1)}, u32[]{:S(2)}, u32[]{:S(2)}) collective-permute-start(bf16[16,2176]{1,0:T(8,128)(2,1)S(1)} %get-tuple-element.166), channel_id=1, source_target_pairs={{0,3},{1,2},{2,1},{3,0},{4,7},{5,6},{6,5},{7,4},{8,11},{9,10},{10,... | collective-permute-start | bytes 208904 | tf_op jit(solution)/shard_map/ppermute | solution.py:480
  211.0 14.9 %collective-permute-start.45 = (bf16[1,512,512]{2,1,0:T(8,128)(2,1)S(1)}, bf16[1,512,512]{2,1,0:T(8,128)(2,1)S(1)}, u32[]{:S(2)}, u32[]{:S(2)}) collective-permute-start(bf16[1,512,512]{2,1,0:T(8,128)(2,1)S(1)} %slice_add_fusion.5.refs_0_), channel_id=1, source_target_pairs={{0,8},{4,12},{8,0},{12,4},{16,24},{20,28},{24,16},{28,20},{1,9},{5... | collective-permute-start | bytes 1572872 | tf_op jit(solution)/shard_map/ppermute | solution.py:480
  212.2 13.7 %collective-permute-start.42 = (bf16[1,512,512]{2,1,0:T(8,128)(2,1)S(1)}, bf16[1,512,512]{2,1,0:T(8,128)(2,1)S(1)}, u32[]{:S(2)}, u32[]{:S(2)}) collective-permute-start(bf16[1,512,512]{2,1,0:T(8,128)(2,1)S(1)} %slice_add_fusion.5.refs_0_), channel_id=1, source_target_pairs={{0,4},{4,0},{8,12},{12,8},{16,20},{20,16},{24,28},{28,24},{1,5},{5... | collective-permute-start | bytes 1572872 | tf_op jit(solution)/shard_map/ppermute | solution.py:480
  212.2 20.9 %collective-permute-start.38 = (bf16[1,512,512]{2,1,0:T(8,128)(2,1)S(1)}, bf16[1,512,512]{2,1,0:T(8,128)(2,1)S(1)}, u32[]{:S(2)}, u32[]{:S(2)}) collective-permute-start(bf16[1,512,512]{2,1,0:T(8,128)(2,1)S(1)} %slice_add_fusion.4.refs_0_), channel_id=1, source_target_pairs={{0,16},{4,20},{8,24},{12,28},{16,0},{20,4},{24,8},{28,12},{1,17},{... | collective-permute-start | bytes 1572872 | tf_op jit(solution)/shard_map/ppermute | solution.py:480
  212.5 20.6 %collective-permute-start.47 = (bf16[1,512,512]{2,1,0:T(8,128)(2,1)S(1)}, bf16[1,512,512]{2,1,0:T(8,128)(2,1)S(1)}, u32[]{:S(2)}, u32[]{:S(2)}) collective-permute-start(bf16[1,512,512]{2,1,0:T(8,128)(2,1)S(1)} %collective-permute-done.43.refs_1_), channel_id=1, source_target_pairs={{0,8},{4,12},{8,0},{12,4},{16,24},{20,28},{24,16},{28,20},{1,9},{5... | collective-permute-start | bytes 1572872 | tf_op jit(solution)/shard_map/ppermute | solution.py:480
  213.5 24.6 %collective-permute-start.40 = (bf16[1,512,512]{2,1,0:T(8,128)(2,1)S(1)}, bf16[1,512,512]{2,1,0:T(8,128)(2,1)S(1)}, u32[]{:S(2)}, u32[]{:S(2)}) collective-permute-start(bf16[1,512,512]{2,1,0:T(8,128)(2,1)S(1)} %collective-permute-done.36.refs_1_), channel_id=1, source_target_pairs={{0,16},{4,20},{8,24},{12,28},{16,0},{20,4},{24,8},{28,12},{1,17},{... | collective-permute-start | bytes 1572872 | tf_op jit(solution)/shard_map/ppermute | solution.py:480
  225.9 17.4 %collective-permute-start.44 = (bf16[1,512,512]{2,1,0:T(8,128)(2,1)S(1)}, bf16[1,512,512]{2,1,0:T(8,128)(2,1)S(1)}, u32[]{:S(2)}, u32[]{:S(2)}) collective-permute-start(bf16[1,512,512]{2,1,0:T(8,128)(2,1)S(1)} %collective-permute-done.43.refs_1_), channel_id=1, source_target_pairs={{0,4},{4,0},{8,12},{12,8},{16,20},{20,16},{24,28},{28,24},{1,5},{5... | collective-permute-start | bytes 1572872 | tf_op jit(solution)/shard_map/ppermute | solution.py:480
  225.9 17.4 %collective-permute-start.46 = (bf16[1,512,512]{2,1,0:T(8,128)(2,1)S(1)}, bf16[1,512,512]{2,1,0:T(8,128)(2,1)S(1)}, u32[]{:S(2)}, u32[]{:S(2)}) collective-permute-start(bf16[1,512,512]{2,1,0:T(8,128)(2,1)S(1)} %collective-permute-done.45.refs_2_), channel_id=1, source_target_pairs={{0,4},{4,0},{8,12},{12,8},{16,20},{20,16},{24,28},{28,24},{1,5},{5... | collective-permute-start | bytes 1572872 | tf_op jit(solution)/shard_map/ppermute | solution.py:480
  233.1 10.7 %collective-permute-start.48 = (bf16[1,512,512]{2,1,0:T(8,128)(2,1)S(1)}, bf16[1,512,512]{2,1,0:T(8,128)(2,1)S(1)}, u32[]{:S(2)}, u32[]{:S(2)}) collective-permute-start(bf16[1,512,512]{2,1,0:T(8,128)(2,1)S(1)} %collective-permute-done.47.refs_3_), channel_id=1, source_target_pairs={{0,4},{4,0},{8,12},{12,8},{16,20},{20,16},{24,28},{28,24},{1,5},{5... | collective-permute-start | bytes 1572872 | tf_op jit(solution)/shard_map/ppermute | solution.py:480
  233.1 6.1 %collective-permute-start.28 = (bf16[16,2176]{1,0:T(8,128)(2,1)S(1)}, bf16[16,2176]{1,0:T(8,128)(2,1)S(1)}, u32[]{:S(2)}, u32[]{:S(2)}) collective-permute-start(bf16[16,2176]{1,0:T(8,128)(2,1)S(1)} %fusion.2.refs_0_), channel_id=1, source_target_pairs={{0,16},{4,20},{8,24},{12,28},{16,0},{20,4},{24,8},{28,12},{1,17},{... | collective-permute-start | bytes 208904 | tf_op jit(solution)/shard_map/ppermute | solution.py:480
  238.2 5.6 %collective-permute-start.29 = (bf16[16,2176]{1,0:T(8,128)(2,1)S(1)}, bf16[16,2176]{1,0:T(8,128)(2,1)S(1)}, u32[]{:S(2)}, u32[]{:S(2)}) collective-permute-start(bf16[16,2176]{1,0:T(8,128)(2,1)S(1)} %fusion.2.refs_0_), channel_id=1, source_target_pairs={{0,8},{4,12},{8,0},{12,4},{16,24},{20,28},{24,16},{28,20},{1,9},{5... | collective-permute-start | bytes 208904 | tf_op jit(solution)/shard_map/ppermute | solution.py:480
  239.2 5.0 %collective-permute-start.30 = (bf16[16,2176]{1,0:T(8,128)(2,1)S(1)}, bf16[16,2176]{1,0:T(8,128)(2,1)S(1)}, u32[]{:S(2)}, u32[]{:S(2)}) collective-permute-start(bf16[16,2176]{1,0:T(8,128)(2,1)S(1)} %collective-permute-done.28.refs_1_), channel_id=1, source_target_pairs={{0,8},{4,12},{8,0},{12,4},{16,24},{20,28},{24,16},{28,20},{1,9},{5... | collective-permute-start | bytes 208904 | tf_op jit(solution)/shard_map/ppermute | solution.py:480
  243.2 6.6 %collective-permute-start.35 = (bf16[1,512,512]{2,1,0:T(8,128)(2,1)S(1)}, bf16[1,512,512]{2,1,0:T(8,128)(2,1)S(1)}, u32[]{:S(2)}, u32[]{:S(2)}) collective-permute-start(bf16[1,512,512]{2,1,0:T(8,128)(2,1)S(1)} %slice_add_fusion.4.refs_0_), channel_id=1, source_target_pairs={{0,4},{4,0},{8,12},{12,8},{16,20},{20,16},{24,28},{28,24},{1,5},{5... | collective-permute-start | bytes 1572872 | tf_op jit(solution)/shard_map/ppermute | solution.py:480
  243.3 4.1 %collective-permute-start.31 = (bf16[16,2176]{1,0:T(8,128)(2,1)S(1)}, bf16[16,2176]{1,0:T(8,128)(2,1)S(1)}, u32[]{:S(2)}, u32[]{:S(2)}) collective-permute-start(bf16[16,2176]{1,0:T(8,128)(2,1)S(1)} %fusion.2.refs_0_), channel_id=1, source_target_pairs={{0,4},{4,0},{8,12},{12,8},{16,20},{20,16},{24,28},{28,24},{1,5},{5... | collective-permute-start | bytes 208904 | tf_op jit(solution)/shard_map/ppermute | solution.py:480
  243.8 4.1 %collective-permute-start.32 = (bf16[16,2176]{1,0:T(8,128)(2,1)S(1)}, bf16[16,2176]{1,0:T(8,128)(2,1)S(1)}, u32[]{:S(2)}, u32[]{:S(2)}) collective-permute-start(bf16[16,2176]{1,0:T(8,128)(2,1)S(1)} %collective-permute-done.28.refs_1_), channel_id=1, source_target_pairs={{0,4},{4,0},{8,12},{12,8},{16,20},{20,16},{24,28},{28,24},{1,5},{5... | collective-permute-start | bytes 208904 | tf_op jit(solution)/shard_map/ppermute | solution.py:480
  243.8 4.0 %collective-permute-start.33 = (bf16[16,2176]{1,0:T(8,128)(2,1)S(1)}, bf16[16,2176]{1,0:T(8,128)(2,1)S(1)}, u32[]{:S(2)}, u32[]{:S(2)}) collective-permute-start(bf16[16,2176]{1,0:T(8,128)(2,1)S(1)} %collective-permute-done.29.refs_2_), channel_id=1, source_target_pairs={{0,4},{4,0},{8,12},{12,8},{16,20},{20,16},{24,28},{28,24},{1,5},{5... | collective-permute-start | bytes 208904 | tf_op jit(solution)/shard_map/ppermute | solution.py:480
  244.3 4.0 %collective-permute-start.34 = (bf16[16,2176]{1,0:T(8,128)(2,1)S(1)}, bf16[16,2176]{1,0:T(8,128)(2,1)S(1)}, u32[]{:S(2)}, u32[]{:S(2)}) collective-permute-start(bf16[16,2176]{1,0:T(8,128)(2,1)S(1)} %collective-permute-done.30.refs_3_), channel_id=1, source_target_pairs={{0,4},{4,0},{8,12},{12,8},{16,20},{20,16},{24,28},{28,24},{1,5},{5... | collective-permute-start | bytes 208904 | tf_op jit(solution)/shard_map/ppermute | solution.py:480
  247.4 2.5 collective-permute-start.39
  247.8 2.3 collective-permute-start.37
  247.9 3.0 %collective-permute-start.41 = (bf16[1,512,512]{2,1,0:T(8,128)(2,1)S(1)}, bf16[1,512,512]{2,1,0:T(8,128)(2,1)S(1)}, u32[]{:S(2)}, u32[]{:S(2)}) collective-permute-start(bf16[1,512,512]{2,1,0:T(8,128)(2,1)S(1)} %collective-permute-done.40.refs_3_), channel_id=1, source_target_pairs={{0,4},{4,0},{8,12},{12,8},{16,20},{20,16},{24,28},{28,24},{1,5},{5... | collective-permute-start | bytes 1572872 | tf_op jit(solution)/shard_map/ppermute | solution.py:480
  (51 other events, 346.3 us)

commit v6 on v5

--- a/solution.py
+++ b/solution.py
@@ -214,10 +214,10 @@
         out_specs=[image(seq, 3 * width), image(seq, width), image(seq, 128), image(seq, width)]
         + [whole(chunk.shape)] * ep_size,
         out_shape=[
-            jax.ShapeDtypeStruct((n_img, seq, 3 * width), BF16),
-            jax.ShapeDtypeStruct((n_img, seq, width), BF16),
-            jax.ShapeDtypeStruct((n_img, seq, 128), F32),
-            jax.ShapeDtypeStruct((n_img, seq, width), F32),
+            pltpu.HBM((n_img, seq, 3 * width), BF16),
+            pltpu.HBM((n_img, seq, width), BF16),
+            pltpu.HBM((n_img, seq, 128), F32),
+            pltpu.HBM((n_img, seq, width), F32),
         ]
         + [chunk] * ep_size,
         scratch_shapes=[pltpu.VMEM((n_img, seq, width), BF16)],
@@ -328,7 +328,7 @@
     heads, ep_size, pack_blocks, place_ref, bias_ref, tok_ref, cot_ref, resid_ref, qkv_ref, att_ref, lse_ref, slot_col_ref, w_qkv_ref, w_out_ref, vec_ref, *rest
 ):
     chunk_refs = rest[:ep_size]
-    packed = len(pack_blocks)
+    packed = 1 if pack_blocks else 0
     gtok_ref = rest[ep_size]
     pack_refs = rest[ep_size + 1 : ep_size + 1 + packed]
     gw_qkv_ref, gw_out_ref, gvec_ref, gqkv_ref = rest[ep_size + 1 + packed : ep_size + 5 + packed]
@@ -403,7 +403,7 @@
     @pl.when(img == pl.num_programs(0) - 1)
     def _():
         small_ref = rest[-1]
-        blocks, per_pack, rows = pack_refs[0].shape[:3]
+        blocks, _, rows = pack_refs[0].shape[:3]
         per_ep = width // ep_size
         biases = bias_ref.shape[0]
         small_ref[...] = jnp.zeros(small_ref.shape, F32)
@@ -412,19 +412,19 @@
             small_ref[0:8, :] = gvec_ref[:, pl.ds(pl.multiple_of(owner * per_ep, per_ep), per_ep)]
             small_ref[8 : 8 + biases, :] = bias_ref[...] if j == 0 else jnp.zeros(bias_ref.shape, F32)
             for r in range(blocks):
-                block = pack_blocks[j // per_pack][r] ^ place_ref[1]
+                block = pack_blocks[r] ^ place_ref[1]
                 start = pl.multiple_of(owner * per_ep + block * rows, rows)
-                into = pack_refs[j // per_pack]
-                into[r, j % per_pack, :, 0 : 3 * width] = gw_qkv_ref[pl.ds(start, rows), :].astype(BF16)
-                into[r, j % per_pack, :, 3 * width : 4 * width] = gw_out_ref[pl.ds(start, rows), :].astype(BF16)
+                into = pack_refs[0]
+                into[r, j, :, 0 : 3 * width] = gw_qkv_ref[pl.ds(start, rows), :].astype(BF16)
+                into[r, j, :, 3 * width : 4 * width] = gw_out_ref[pl.ds(start, rows), :].astype(BF16)
                 small = small_ref[pl.ds(pl.multiple_of(block * rows, rows), rows), :]
-                into[r, j % per_pack, :, 4 * width :] = small.astype(BF16)
+                into[r, j, :, 4 * width :] = small.astype(BF16)
 
 
 def backward_call(tokens, cotangent, resid, qkv, attended, lse, slot_col, w_qkv, w_out, vecs, chunks, place, biases, pack_blocks):
     n_img, seq, width = tokens.shape
     ep_size = len(chunks)
-    packed = len(pack_blocks)
+    packed = 1 if pack_blocks else 0
     image = lambda arr: pl.BlockSpec((1,) + arr.shape[1:], lambda i: (i, 0, 0))
     sums = [
         jax.ShapeDtypeStruct(w_qkv.shape, F32),
@@ -433,9 +433,9 @@
     ]
     scratch = [pltpu.VMEM((seq, 3 * width), BF16)]
     if packed:
-        grp_size = len(pack_blocks[0])
-        pack = (grp_size, ep_size // 2, width // (ep_size * grp_size), 4 * width + 128)
-        outs = [jax.ShapeDtypeStruct(pack, BF16)] * 2
+        grp_size = len(pack_blocks)
+        pack = (grp_size, ep_size, width // (ep_size * grp_size), 4 * width + 128)
+        outs = [jax.ShapeDtypeStruct(pack, BF16)]
         scratch = [pltpu.VMEM(v.shape, F32) for v in sums] + scratch + [pltpu.VMEM((width // ep_size, 128), F32)]
     else:
         outs = sums
@@ -452,7 +452,7 @@
         compiler_params=params(40, "arbitrary"),
         cost_estimate=cost(25),
         name="attention_backward",
-    )(place, biases, tokens, cotangent, resid, qkv, attended, lse, slot_col, w_qkv, w_out, vecs, *chunks)
+    )(place, biases, tokens, cotangent, *(pltpu.with_memory_space_constraint(a, pltpu.HBM) for a in (resid, qkv, attended, lse)), slot_col, w_qkv, w_out, vecs, *chunks)
 
 
 def combine_kernel(ep_size, resid_ref, slot_col_ref, gate_col_ref, *rest):
@@ -496,34 +496,36 @@
 def gather_sums(block, order, size):
     pieces = [block]
     for bit in reversed(order):
-        pieces = pieces + [swap(p, "grp", size, 1 << bit) for p in pieces]
+        held = pieces[0] if len(pieces) == 1 else jnp.concatenate(pieces)
+        pieces = pieces + [swap(held, "grp", size, 1 << bit)]
     return pieces
 
 
-def widen_kernel(count, place_ref, *refs):
-    piece_refs, out_ref = refs[:count], refs[-1]
-    for r in range(count):
-        @pl.when(pl.program_id(0) == r)
-        def _():
-            out_ref[0] = piece_refs[r][0].astype(F32)
+def widen_kernel(starts, place_ref, *refs):
+    piece_refs, out_ref = refs[: len(starts)], refs[-1]
+    for start, piece_ref in zip(starts, piece_refs):
+        for k in range(piece_ref.shape[0]):
+            @pl.when(pl.program_id(0) == start + k)
+            def _():
+                out_ref[0] = piece_ref[k].astype(F32)
 
 
 def widen_call(pieces, expert, first, axis, shape, base):
-    count = len(pieces)
+    starts = [sum(p.shape[0] for p in pieces[:k]) for k in range(len(pieces))]
+    count = sum(p.shape[0] for p in pieces)
     _, m, n = pieces[0].shape
     at = (lambda r, s: (s[0], r ^ s[1], 0)) if axis == 0 else (lambda r, s: (s[0], 0, r ^ s[1]))
     extra = [] if base is None else [base]
     return pl.pallas_call(
-        functools.partial(widen_kernel, count),
+        functools.partial(widen_kernel, starts),
         grid_spec=pltpu.PrefetchScalarGridSpec(
             num_scalar_prefetch=1,
             grid=(count,),
-            in_specs=[pl.BlockSpec((1, m, n), lambda r, s: (0, 0, 0))] * count
-            + [pl.BlockSpec(memory_space=pl.ANY)] * len(extra),
+            in_specs=[whole(p.shape) for p in pieces] + [pl.BlockSpec(memory_space=pl.ANY)] * len(extra),
             out_specs=pl.BlockSpec((1, m, n), at),
         ),
         out_shape=jax.ShapeDtypeStruct(shape, F32),
-        input_output_aliases={1 + count: 0} if extra else {},
+        input_output_aliases={1 + len(pieces): 0} if extra else {},
         compiler_params=params(16, "arbitrary"),
         cost_estimate=cost(4),
         name="expert_gradient_result",
@@ -633,7 +635,6 @@
         bias_sums = sums_b if number == 0 else [a + b for a, b in zip(bias_sums, sums_b)]
     gb_in, gb_back = bias_sums
     far_b, far_i, near_b, near_i = sums
-    far_i, = after([far_i], gdis_back[half])
     state = [near_b + swap(far_b, "grp", grp_size, 1), near_i + swap(far_i, "grp", grp_size, 1)]
     stages = [state]
     for step in range(len(order_a)):
@@ -643,21 +644,11 @@
     early = stages[len(stages) // 2]
     resid_late, = after([resid], *early)
     all_b, all_i = gather_sums(sum_b, order_a, grp_size), gather_sums(sum_i, order_b, grp_size)
-    oth_b = [swap(p, "grp", grp_size, 1) for p in all_b]
-    oth_i = [swap(p, "grp", grp_size, 1) for p in all_i]
-    gw_back = widen_call(all_b, core, block_a, 0, w_back.shape, None)
-    gw_in = widen_call(all_i, core, block_b, 1, w_in.shape, None)
-    gw_back = widen_call(oth_b, 1 - core, block_a, 0, w_back.shape, gw_back)
-    gw_in = widen_call(oth_i, 1 - core, block_b, 1, w_in.shape, gw_in)
     hidden = w_in.shape[2]
     packed = width // ep_size == 128 and 128 % (16 * grp_size) == 0
     place, biases, pack_blocks = None, None, ()
     if packed:
-        order_p, order_q = [0] + order_a, [0] + order_b
-        pack_blocks = tuple(
-            tuple(sum((r >> (len(o) - 1 - k)) % 2 << bit for k, bit in enumerate(o)) for r in range(grp_size))
-            for o in (order_p, order_q)
-        )
+        pack_blocks = tuple(range(0, grp_size, 2)) + tuple(range(1, grp_size, 2))
         place = jnp.stack([me[0], grp])
         biases = jnp.concatenate([gb_in.reshape(-1, 128), gb_back.reshape(-1, 128)])
     grad_tokens, *grads = backward_call(
@@ -670,17 +661,21 @@
     output = combine_call(resid, slot_col, gate_col, outs_back)
     grads = after(grads, sum_b, sum_i, *outs_back[: half + 1])
     if packed:
-        for bits_now in zip(order_p, order_q):
-            grads = scatter_step(grads, bits_now, grp_size)
-        near, far = after(grads, *outs_back)
-        parts = [near[0, d] for d in range(ep_size // 2)] + [far[0, d] for d in range(ep_size // 2)]
-        total = parts[0].astype(F32)
+        chips = grp_size // 2
+        pack = grads[0][:chips] + swap(grads[0][chips:], "grp", grp_size, 1)
+        pack, = after([pack], all_b[1], all_i[1])
+        share = pack[0].astype(F32)
+        for c in range(1, chips):
+            share = share + swap(pack[c], "grp", grp_size, 2 * c).astype(F32)
+        share, *_ = after([share.astype(BF16)], *outs_back)
+        total = share[0].astype(F32)
         for d in range(1, ep_size):
-            total = total + over_ep(parts[d], d).astype(F32)
-        pieces, offsets = [total.astype(BF16)], [0]
-        for bit in reversed(bits):
-            pieces = pieces + [swap(p, "grp", grp_size, 1 << bit) for p in pieces]
-            offsets = offsets + [o ^ (1 << bit) for o in offsets]
+            total = total + over_ep(share[d], d).astype(F32)
+        total, *_ = after([total.astype(BF16)], all_b[-1], all_i[-1])
+        late = total
+        pieces = [total] + [swap(total, "grp", grp_size, 2 * c) for c in range(1, chips)]
+        offsets = tuple(range(0, grp_size, 2)) + tuple(range(1, grp_size, 2))
+        pieces = pieces + [swap(p, "grp", grp_size, 1) for p in pieces]
         gw_qkv, gw_out, gvec, gb_in, gb_back = unpack_call(pieces, offsets, grp.reshape(1), width, exp_dev, hidden)
         gvec = [gvec[k] for k in range(5)]
     else:
@@ -691,8 +686,15 @@
             return over_grp(lax.psum_scatter(v.astype(BF16), "ep", scatter_dimension=0, tiled=True))
 
         gw_qkv, gw_out, gvec = grads
+        late = gw_qkv
         gw_qkv, gw_out, gb_in, gb_back = over_all(gw_qkv), over_all(gw_out), over_grp(gb_in), over_grp(gb_back)
         gvec = [over_all(gvec[k]) for k in range(5)]
+    oth_b = [swap(p, "grp", grp_size, 1) for p in after(all_b, late)]
+    oth_i = [swap(p, "grp", grp_size, 1) for p in after(all_i, late)]
+    gw_back = widen_call(all_b, core, block_a, 0, w_back.shape, None)
+    gw_in = widen_call(all_i, core, block_b, 1, w_in.shape, None)
+    gw_back = widen_call(oth_b, 1 - core, block_a, 0, w_back.shape, gw_back)
+    gw_in = widen_call(oth_i, 1 - core, block_b, 1, w_in.shape, gw_in)
     return (output, grad_tokens, gvec[0], gvec[1], gw_qkv, gw_out, gvec[2], gvec[3], gvec[4], gw_in, gb_in, gw_back, gb_back)
 
 

time: 259 us -> 256 us (0.988)
  waiting for transfers between devices: 82.7 us -> 67.3 us
  starting transfers between devices: 50.9 us -> 65.9 us
  local copies, waits for them, and re-layouts: 25 us -> 21.3 us
    ppermute x49 -> x43, waiting for transfers between devices: 82.7 us -> 67.3 us  [swap(): return lax.ppermute(array, axis, [(i, i ^ distance) for i in range(size)])]
    ppermute x49 -> x43, starting transfers between devices: 50.9 us -> 65.9 us  [swap(): return lax.ppermute(array, axis, [(i, i ^ distance) for i in range(size)])]
    unnamed x104 -> x88, local copies, waits for them, and re-layouts: 20.3 us -> 16.8 us
  transfers between devices with their start and end apart: 49 -> 43, of which waited for: 18 -> 16; matrix products, arithmetic and copies ran while one was open for 6% -> 6% of each run, Pallas kernels for 34% -> 31%
where the time goes in v6:
time: 256 us; the launch traced here: 251 us
  Pallas kernels  89.7 us (35%)
  waiting for transfers between devices  67.3 us (26%)
  starting transfers between devices  65.9 us (26%)
  local copies, waits for them, and re-layouts  21.3 us (8%)
  other arithmetic  5.34 us (2%)
    ppermute x43, waiting for transfers between devices, swap(): return lax.ppermute(array, axis, [(i, i ^ distance) for i in range(size)])  67.3 us
    ppermute x43, starting transfers between devices, swap(): return lax.ppermute(array, axis, [(i, i ^ distance) for i in range(size)])  65.9 us
    pallas_call x3, Pallas kernels, expert_call(): pl.pallas_call(functools.partial(expert_kernel, count, len(before), block...  35.1 us
    pallas_call x1, Pallas kernels, backward_call(): pl.pallas_call(functools.partial(backward_kernel, width // HD, ep_size, p...  22.7 us
    unnamed x88, local copies, waits for them, and re-layouts  16.8 us
    pallas_call x1, Pallas kernels, attention_call(): pl.pallas_call(functools.partial(attention_kernel, width // HD), grid=(n_...  12.4 us
    pallas_call x4, Pallas kernels, widen_call(): pl.pallas_call(functools.partial(widen_kernel, starts), grid_spec=pltpu.P...  12.1 us
  transfers between devices with their start and end apart: 43, of which 16 were waited for; matrix products, arithmetic and copies ran while one was open for 6% of the time, Pallas kernels for 31%

profile of v6, /device:TPU:0, one launch (start us, length us, event | category | flops | bytes accessed | tf_op | source)
XLA Modules:
  0.0 251.4 jit_solution(10585781858477418646)
XLA Ops:
  0.6 4.1 %collective-permute-start.4 = (bf16[4,197,512]{2,0,1:T(4,128)(2,1)}, bf16[4,197,512]{2,0,1:T(4,128)(2,1)}, u32[]{:S(2)}, u32[]{:S(2)}) collective-permute-start(bf16[4,197,512]{2,0,1:T(4,128)(2,1)} %param.29), channel_id=1, source_target_pairs={{0,2},{1,3},{2,0},{3,1},{4,6},{5,7},{6,4},{7,5},{8,10},{9,11},{10,... | collective-permute-start | bytes 2420744 | tf_op jit(solution)/shard_map/ppermute | solution.py:480
  4.7 1.3 copy.45.cot_ref
  7.5 2.2 route_and_dispatch_cotangent.1
  10.5 1.9 collective-permute-start
  13.8 12.4 %attention_forward_and_dispatch.1 = (bf16[4,197,1536]{2,1,0:T(8,128)(2,1)}, bf16[4,197,512]{2,1,0:T(8,128)(2,1)}, f32[4,197,128]{2,1,0:T(8,128)}, f32[4,197,512]...) custom-call(bf16[4,197,512]{2,1,0:T(8,128)(2,1)S(1)} %copy.46.tok_re, ...), custom_call_target="tpu_custom_call" | custom-call | flops 14000000000 | bytes 4096 | tf_op jit(solution)/shard_map/attention_forward_and_dispatch/pallas_call | solution.py:210
  28.2 2.7 %collective-permute-start.2 = (bf16[2,248,512]{2,1,0:T(8,128)(2,1)}, bf16[2,248,512]{2,1,0:T(8,128)(2,1)}, u32[]{:S(2)}, u32[]{:S(2)}) collective-permute-start(bf16[2,248,512]{2,1,0:T(8,128)(2,1)} %get-tuple-element.90), channel_id=1, source_target_pairs={{0,2},{1,3},{2,0},{3,1},{4,6},{5,7},{6,4},{7,5},{8,10},{9,11},{10,... | collective-permute-start | bytes 1523720 | tf_op jit(solution)/shard_map/ppermute | solution.py:480
  30.9 4.9 %collective-permute-done.refs_2_ = bf16[2,248,512]{2,1,0:T(8,128)(2,1)} collective-permute-done((bf16[2,248,512]{2,1,0:T(8,128)(2,1)}, bf16[2,248,512]{2,1,0:T(8,128)(2,1)}, u32[]{:S(2)}, u32[]{:S(2)}) %collective-permute-start) | collective-permute-done | bytes 507936 | tf_op jit(solution)/shard_map/ppermute | solution.py:480
  35.8 2.2 copy-done
  38.0 2.2 copy-done.2
  42.2 8.1 %experts.3 = (bf16[2,248,512]{2,1,0:T(8,128)(2,1)S(1)}, bf16[2,248,512]{2,1,0:T(8,128)(2,1)S(1)}, bf16[4,512,512]{2,1,0:T(8,128)(2,1)S(1)}, bf16[4,512,512]{2,1,...) custom-call(s32[3]{0:T(128)S(1)} %pad_add_fusion.sel_ref, ...), custom_call_target="tpu_custom_call" | custom-call | flops 10000000000 | bytes 4096 | tf_op jit(solution)/shard_map/experts/pallas_call | solution.py:298
  51.1 1.5 copy.47.cot_ref
  53.9 2.6 %collective-permute-start.6 = (bf16[2,248,512]{2,1,0:T(8,128)(2,1)S(1)}, bf16[2,248,512]{2,1,0:T(8,128)(2,1)S(1)}, u32[]{:S(2)}, u32[]{:S(2)}) collective-permute-start(bf16[2,248,512]{2,1,0:T(8,128)(2,1)S(1)} %get-tuple-element.99), channel_id=1, source_target_pairs={{0,1},{1,0},{2,3},{3,2},{4,5},{5,4},{6,7},{7,6},{8,9},{9,8},{10,11... | collective-permute-start | bytes 1523720 | tf_op jit(solution)/shard_map/ppermute | solution.py:480
  56.4 3.0 %collective-permute-done.1.refs_0_ = bf16[2,248,512]{2,1,0:T(8,128)(2,1)} collective-permute-done((bf16[2,248,512]{2,1,0:T(8,128)(2,1)}, bf16[2,248,512]{2,1,0:T(8,128)(2,1)}, u32[]{:S(2)}, u32[]{:S(2)}) %collective-permute-start.1) | collective-permute-done | bytes 507936 | tf_op jit(solution)/shard_map/ppermute | solution.py:480
  59.4 5.6 %collective-permute-done.2.refs_1_ = bf16[2,248,512]{2,1,0:T(8,128)(2,1)} collective-permute-done((bf16[2,248,512]{2,1,0:T(8,128)(2,1)}, bf16[2,248,512]{2,1,0:T(8,128)(2,1)}, u32[]{:S(2)}, u32[]{:S(2)}) %collective-permute-start.2) | collective-permute-done | bytes 507936 | tf_op jit(solution)/shard_map/ppermute | solution.py:480
  65.1 3.5 %collective-permute-start.5 = (bf16[2,248,512]{2,1,0:T(8,128)(2,1)S(1)}, bf16[2,248,512]{2,1,0:T(8,128)(2,1)S(1)}, u32[]{:S(2)}, u32[]{:S(2)}) collective-permute-start(bf16[2,248,512]{2,1,0:T(8,128)(2,1)S(1)} %copy-done.14), channel_id=1, source_target_pairs={{0,3},{1,2},{2,1},{3,0},{4,7},{5,6},{6,5},{7,4},{8,11},{9,10},{10,... | collective-permute-start | bytes 1523720 | tf_op jit(solution)/shard_map/ppermute | solution.py:480
  68.6 18.2 %experts.4 = (bf16[2,248,512]{2,1,0:T(8,128)(2,1)S(1)}, bf16[2,248,512]{2,1,0:T(8,128)(2,1)S(1)}, bf16[2,248,512]{2,1,0:T(8,128)(2,1)}, bf16[2,248,512]{2,1,0:T(...) custom-call(s32[3]{0:T(128)S(1)} %pad_add_fusion.sel_ref, ...), custom_call_target="tpu_custom_call", output_to_operand_aliasing={{4}: (9, {}), {5}: (10, {}), {6}: (11, {}), {7}: (12, {})} | custom-call | flops 20000000000 | bytes 4096 | tf_op jit(solution)/shard_map/experts/pallas_call | solution.py:298
  86.9 8.8 %experts.5 = (bf16[2,248,512]{2,1,0:T(8,128)(2,1)S(1)}, bf16[2,248,512]{2,1,0:T(8,128)(2,1)S(1)}, bf16[4,512,512]{2,1,0:T(8,128)(2,1)S(1)}, bf16[4,512,512]{2,1,...) custom-call(s32[3]{0:T(128)S(1)} %pad_add_fusion.sel_ref, ...), custom_call_target="tpu_custom_call", output_to_operand_aliasing={{2}: (7, {}), {3}: (8, {}), {4}: (9, {}), {5}: (10, {})} | custom-call | flops 10000000000 | bytes 4096 | tf_op jit(solution)/shard_map/experts/pallas_call | solution.py:298
  96.3 3.6 %collective-permute-done.7 = bf16[4,512,512]{2,1,0:T(8,128)(2,1)S(1)} collective-permute-done((bf16[4,512,512]{2,1,0:T(8,128)(2,1)S(1)}, bf16[4,512,512]{2,1,0:T(8,128)(2,1)S(1)}, u32[]{:S(2)}, u32[]{:S(2)}) %collective-permute-start.7) | collective-permute-done | bytes 2097184 | tf_op jit(solution)/shard_map/ppermute | solution.py:480
  101.7 1.5 collective-permute-start.8
  103.3 3.2 %collective-permute-start.11 = (bf16[2,248,512]{2,1,0:T(8,128)(2,1)}, bf16[2,248,512]{2,1,0:T(8,128)(2,1)}, u32[]{:S(2)}, u32[]{:S(2)}) collective-permute-start(bf16[2,248,512]{2,1,0:T(8,128)(2,1)} %get-tuple-element.110), channel_id=1, source_target_pairs={{0,1},{1,0},{2,3},{3,2},{4,5},{5,4},{6,7},{7,6},{8,9},{9,8},{10,11... | collective-permute-start | bytes 1523720 | tf_op jit(solution)/shard_map/ppermute | solution.py:480
  109.5 1.5 collective-permute-start.10
  111.1 1.9 collective-permute-start.13
  113.0 14.3 %collective-permute-done.8 = bf16[2,512,512]{2,1,0:T(8,128)(2,1)} collective-permute-done((bf16[2,512,512]{2,1,0:T(8,128)(2,1)}, bf16[2,512,512]{2,1,0:T(8,128)(2,1)}, u32[]{:S(2)}, u32[]{:S(2)}) %collective-permute-start.8) | collective-permute-done | bytes 1048608 | tf_op jit(solution)/shard_map/ppermute | solution.py:480
  127.3 1.6 slice_add_fusion.2
  129.0 1.6 collective-permute-start.17
  130.6 5.3 %collective-permute-done.10 = bf16[2,512,512]{2,1,0:T(8,128)(2,1)} collective-permute-done((bf16[2,512,512]{2,1,0:T(8,128)(2,1)}, bf16[2,512,512]{2,1,0:T(8,128)(2,1)}, u32[]{:S(2)}, u32[]{:S(2)}) %collective-permute-start.10) | collective-permute-done | bytes 1048608 | tf_op jit(solution)/shard_map/ppermute | solution.py:480
  135.9 1.3 slice_add_fusion.1
  137.3 6.7 %collective-permute-done.12.rest_2_ = bf16[2,248,512]{2,1,0:T(8,128)(2,1)} collective-permute-done((bf16[2,248,512]{2,1,0:T(8,128)(2,1)}, bf16[2,248,512]{2,1,0:T(8,128)(2,1)}, u32[]{:S(2)}, u32[]{:S(2)}) %collective-permute-start.12) | collective-permute-done | bytes 507936 | tf_op jit(solution)/shard_map/ppermute | solution.py:480
  144.0 9.9 %collective-permute-start.14 = (bf16[2,248,512]{2,1,0:T(8,128)(2,1)S(1)}, bf16[2,248,512]{2,1,0:T(8,128)(2,1)S(1)}, u32[]{:S(2)}, u32[]{:S(2)}) collective-permute-start(bf16[2,248,512]{2,1,0:T(8,128)(2,1)S(1)} %copy-done.12), channel_id=1, source_target_pairs={{0,1},{1,0},{2,3},{3,2},{4,5},{5,4},{6,7},{7,6},{8,9},{9,8},{10,11... | collective-permute-start | bytes 1523720 | tf_op jit(solution)/shard_map/ppermute | solution.py:480
  154.5 22.7 %attention_backward.1 = (bf16[4,197,512]{2,1,0:T(8,128)(2,1)S(1)}, bf16[8,4,16,2176]{3,2,1,0:T(8,128)(2,1)S(1)}) custom-call(s32[2]{0:T(128)S(1)} %pad_add_fusion.1.place_ref, f32[40,128]{1,0:T(8,128)S(1)} %pad_maximum_fusion.2.bias_ref, bf16[4,197,512]{2,1,0:T(8,128)(2,1)S(1)} %copy.46.tok_ref, bf16[4,197,512]{2,1,0:T(8,128)(2,1)S(1)} %copy.45.cot_ref, ...), custom_call_target="tpu_custom_call" | custom-call | flops 24999999488 | bytes 4096 | tf_op jit(solution)/shard_map/attention_backward/pallas_call | solution.py:443
  178.0 1.5 collective-permute-start.20
  180.9 11.4 %collective-permute-done.20.refs_1_ = bf16[1,512,512]{2,1,0:T(8,128)(2,1)S(1)} collective-permute-done((bf16[1,512,512]{2,1,0:T(8,128)(2,1)S(1)}, bf16[1,512,512]{2,1,0:T(8,128)(2,1)S(1)}, u32[]{:S(2)}, u32[]{:S(2)}) %collective-permute-start.20) | collective-permute-done | bytes 524320 | tf_op jit(solution)/shard_map/ppermute | solution.py:480
  195.7 1.5 collective-permute-start.23
  198.6 2.2 collective-permute-start.16
  200.9 1.5 collective-permute-start.28
  203.8 5.5 %collective-permute-done.24 = bf16[4,16,2176]{2,1,0:T(8,128)(2,1)S(1)} collective-permute-done((bf16[4,16,2176]{2,1,0:T(8,128)(2,1)S(1)}, bf16[4,16,2176]{2,1,0:T(8,128)(2,1)S(1)}, u32[]{:S(2)}, u32[]{:S(2)}) %collective-permute-start.24) | collective-permute-done | bytes 278560 | tf_op jit(solution)/shard_map/ppermute | solution.py:480
  209.3 1.3 collective-permute-done.23
  210.7 1.8 collective-permute-done.16.rest_3_
  212.6 10.5 %collective-permute-start.25 = (bf16[16,2176]{1,0:T(8,128)(2,1)S(1)}, bf16[16,2176]{1,0:T(8,128)(2,1)S(1)}, u32[]{:S(2)}, u32[]{:S(2)}) collective-permute-start(bf16[16,2176]{1,0:T(8,128)(2,1)S(1)} %get-tuple-element.176), channel_id=1, source_target_pairs={{0,1},{1,0},{2,3},{3,2},{4,5},{5,4},{6,7},{7,6},{8,9},{9,8},{10,11... | collective-permute-start | bytes 208904 | tf_op jit(solution)/shard_map/ppermute | solution.py:480
  223.1 2.6 %collective-permute-start.27 = (bf16[16,2176]{1,0:T(8,128)(2,1)S(1)}, bf16[16,2176]{1,0:T(8,128)(2,1)S(1)}, u32[]{:S(2)}, u32[]{:S(2)}) collective-permute-start(bf16[16,2176]{1,0:T(8,128)(2,1)S(1)} %get-tuple-element.177), channel_id=1, source_target_pairs={{0,3},{1,2},{2,1},{3,0},{4,7},{5,6},{6,5},{7,4},{8,11},{9,10},{10,... | collective-permute-start | bytes 208904 | tf_op jit(solution)/shard_map/ppermute | solution.py:480
  225.7 3.0 %combine_output.1 = bf16[4,197,512]{2,1,0:T(8,128)(2,1)S(1)} custom-call(f32[4,197,512]{2,1,0:T(8,128)S(1)} %copy-done.20, f32[4,197,8]{2,1,0:T(8,128)S(1)} %copy-done.26, f32[4,197,8]{2,1,0:T(8,128)S(1)} %copy-done.28, bf16[2,248,512]{2,1,0:T(8,128)(2,1)S(1)} %copy-done.22, bf16[2,248,512]{2,1,0:T(8,128)(2,1)S(1)} %collective-permute-done.14.rest_1_, ...), custom_call_target="tpu_custom_call" | custom-call | flops 5000000000 | bytes 4096 | tf_op jit(solution)/shard_map/combine_output/pallas_call | solution.py:467
  228.7 1.3 copy.50
  230.0 1.5 collective-permute-done.26
  231.6 2.1 collective-permute-start.32
  235.2 3.0 %expert_gradient_result.4.refs_3_ = f32[2,512,2048]{2,1,0:T(8,128)} custom-call(s32[2]{0:T(128)S(1)} %pad_add_fusion.2.place_ref, bf16[1,512,512]{2,1,0:T(8,128)(2,1)S(1)} %slice_add_fusion.3.refs_0_, bf16[1,512,512]{2,1,0:T(8,128)(2,1)S(1)} %collective-permute-done.21.refs_1_, bf16[2,512,512]{2,1,0:T(8,128)(2,1)S(1)} %collective-permute-done.29.refs_2_), custom_call_target="tpu_custom_call" | custom-call | flops 4000000000 | bytes 4096 | tf_op jit(solution)/shard_map/expert_gradient_result/pallas_call | solution.py:519
  239.3 3.0 %expert_gradient_result.6.refs_3_ = f32[2,2048,512]{2,1,0:T(8,128)} custom-call(s32[2]{0:T(128)S(1)} %pad_add_fusion.5.place_ref, bf16[1,512,512]{2,1,0:T(8,128)(2,1)S(1)} %slice_add_fusion.4.refs_0_, bf16[1,512,512]{2,1,0:T(8,128)(2,1)S(1)} %collective-permute-done.20.refs_1_, bf16[2,512,512]{2,1,0:T(8,128)(2,1)S(1)} %collective-permute-done.28.refs_2_), custom_call_target="tpu_custom_call" | custom-call | flops 4000000000 | bytes 4096 | tf_op jit(solution)/shard_map/expert_gradient_result/pallas_call | solution.py:519
  244.9 3.0 %expert_gradient_result.5 = f32[2,512,2048]{2,1,0:T(8,128)} custom-call(s32[2]{0:T(128)S(1)} %get-tuple-element.184.place_ref, bf16[1,512,512]{2,1,0:T(8,128)(2,1)S(1)} %collective-permute-done.37.refs_0_, bf16[1,512,512]{2,1,0:T(8,128)(2,1)S(1)} %collective-permute-done.38.refs_1_, ...), custom_call_target="tpu_custom_call", output_to_operand_aliasing={{}: (4, {})} | custom-call | flops 4000000000 | bytes 4096 | tf_op jit(solution)/shard_map/expert_gradient_result/pallas_call | solution.py:519
  247.9 3.0 %expert_gradient_result.7 = f32[2,2048,512]{2,1,0:T(8,128)} custom-call(s32[2]{0:T(128)S(1)} %get-tuple-element.185.place_ref, bf16[1,512,512]{2,1,0:T(8,128)(2,1)S(1)} %collective-permute-done.40.refs_0_, bf16[1,512,512]{2,1,0:T(8,128)(2,1)S(1)} %collective-permute-done.41.refs_1_, ...), custom_call_target="tpu_custom_call", output_to_operand_aliasing={{}: (4, {})} | custom-call | flops 4000000000 | bytes 4096 | tf_op jit(solution)/shard_map/expert_gradient_result/pallas_call | solution.py:519
  (172 shorter events, 29.4 us)
Async XLA Ops:
  0.6 50.5 %collective-permute-start.4 = (bf16[4,197,512]{2,0,1:T(4,128)(2,1)}, bf16[4,197,512]{2,0,1:T(4,128)(2,1)}, u32[]{:S(2)}, u32[]{:S(2)}) collective-permute-start(bf16[4,197,512]{2,0,1:T(4,128)(2,1)} %param.29), channel_id=1, source_target_pairs={{0,2},{1,3},{2,0},{3,1},{4,6},{5,7},{6,4},{7,5},{8,10},{9,11},{10,... | collective-permute-start | bytes 2420744 | tf_op jit(solution)/shard_map/ppermute | solution.py:480
  10.5 40.6 %collective-permute-start.3 = (f32[2,4,8,197]{3,2,1,0:T(8,128)S(1)}, f32[2,4,8,197]{3,2,1,0:T(8,128)S(1)}, u32[]{:S(2)}, u32[]{:S(2)}) collective-permute-start(f32[2,4,8,197]{3,2,1,0:T(8,128)S(1)} %get-tuple-element.80.info_ref), channel_id=1, source_target_pairs={{0,2},{1,3},{2,0},{3,1},{4,6},{5,7},{6,4},{7,5},{8,10},{9,11},{10,... | collective-permute-start | bytes 151304 | tf_op jit(solution)/shard_map/ppermute | solution.py:480
  10.5 25.2 %collective-permute-start = (bf16[2,248,512]{2,1,0:T(8,128)(2,1)}, bf16[2,248,512]{2,1,0:T(8,128)(2,1)}, u32[]{:S(2)}, u32[]{:S(2)}) collective-permute-start(bf16[2,248,512]{2,1,0:T(8,128)(2,1)} %get-tuple-element.85), channel_id=1, source_target_pairs={{0,1},{1,0},{2,3},{3,2},{4,5},{5,4},{6,7},{7,6},{8,9},{9,8},{10,11... | collective-permute-start | bytes 1523720 | tf_op jit(solution)/shard_map/ppermute | solution.py:480
  27.8 31.6 %collective-permute-start.1 = (bf16[2,248,512]{2,1,0:T(8,128)(2,1)}, bf16[2,248,512]{2,1,0:T(8,128)(2,1)}, u32[]{:S(2)}, u32[]{:S(2)}) collective-permute-start(bf16[2,248,512]{2,1,0:T(8,128)(2,1)} %get-tuple-element.89), channel_id=1, source_target_pairs={{0,1},{1,0},{2,3},{3,2},{4,5},{5,4},{6,7},{7,6},{8,9},{9,8},{10,11... | collective-permute-start | bytes 1523720 | tf_op jit(solution)/shard_map/ppermute | solution.py:480
  28.2 36.9 %collective-permute-start.2 = (bf16[2,248,512]{2,1,0:T(8,128)(2,1)}, bf16[2,248,512]{2,1,0:T(8,128)(2,1)}, u32[]{:S(2)}, u32[]{:S(2)}) collective-permute-start(bf16[2,248,512]{2,1,0:T(8,128)(2,1)} %get-tuple-element.90), channel_id=1, source_target_pairs={{0,2},{1,3},{2,0},{3,1},{4,6},{5,7},{6,4},{7,5},{8,10},{9,11},{10,... | collective-permute-start | bytes 1523720 | tf_op jit(solution)/shard_map/ppermute | solution.py:480
  53.9 33.0 %collective-permute-start.6 = (bf16[2,248,512]{2,1,0:T(8,128)(2,1)S(1)}, bf16[2,248,512]{2,1,0:T(8,128)(2,1)S(1)}, u32[]{:S(2)}, u32[]{:S(2)}) collective-permute-start(bf16[2,248,512]{2,1,0:T(8,128)(2,1)S(1)} %get-tuple-element.99), channel_id=1, source_target_pairs={{0,1},{1,0},{2,3},{3,2},{4,5},{5,4},{6,7},{7,6},{8,9},{9,8},{10,11... | collective-permute-start | bytes 1523720 | tf_op jit(solution)/shard_map/ppermute | solution.py:480
  65.1 21.8 %collective-permute-start.5 = (bf16[2,248,512]{2,1,0:T(8,128)(2,1)S(1)}, bf16[2,248,512]{2,1,0:T(8,128)(2,1)S(1)}, u32[]{:S(2)}, u32[]{:S(2)}) collective-permute-start(bf16[2,248,512]{2,1,0:T(8,128)(2,1)S(1)} %copy-done.14), channel_id=1, source_target_pairs={{0,3},{1,2},{2,1},{3,0},{4,7},{5,6},{6,5},{7,4},{8,11},{9,10},{10,... | collective-permute-start | bytes 1523720 | tf_op jit(solution)/shard_map/ppermute | solution.py:480
  95.7 4.2 %collective-permute-start.7 = (bf16[4,512,512]{2,1,0:T(8,128)(2,1)S(1)}, bf16[4,512,512]{2,1,0:T(8,128)(2,1)S(1)}, u32[]{:S(2)}, u32[]{:S(2)}) collective-permute-start(bf16[4,512,512]{2,1,0:T(8,128)(2,1)S(1)} %get-tuple-element.106), channel_id=1, source_target_pairs={{0,4},{4,0},{8,12},{12,8},{16,20},{20,16},{24,28},{28,24},{1,5},{5... | collective-permute-start | bytes 6291464 | tf_op jit(solution)/shard_map/ppermute | solution.py:480
  95.8 11.3 %collective-permute-start.9 = (bf16[4,512,512]{2,1,0:T(8,128)(2,1)S(1)}, bf16[4,512,512]{2,1,0:T(8,128)(2,1)S(1)}, u32[]{:S(2)}, u32[]{:S(2)}) collective-permute-start(bf16[4,512,512]{2,1,0:T(8,128)(2,1)S(1)} %get-tuple-element.108), channel_id=1, source_target_pairs={{0,4},{4,0},{8,12},{12,8},{16,20},{20,16},{24,28},{28,24},{1,5},{5... | collective-permute-start | bytes 6291464 | tf_op jit(solution)/shard_map/ppermute | solution.py:480
  101.7 25.5 %collective-permute-start.8 = (bf16[2,512,512]{2,1,0:T(8,128)(2,1)}, bf16[2,512,512]{2,1,0:T(8,128)(2,1)}, u32[]{:S(2)}, u32[]{:S(2)}) collective-permute-start(bf16[2,512,512]{2,1,0:T(8,128)(2,1)} %slice.93), channel_id=1, source_target_pairs={{0,8},{4,12},{8,0},{12,4},{16,24},{20,28},{24,16},{28,20},{1,9},{5... | collective-permute-start | bytes 3145736 | tf_op jit(solution)/shard_map/ppermute | solution.py:480
  103.3 34.0 %collective-permute-start.11 = (bf16[2,248,512]{2,1,0:T(8,128)(2,1)}, bf16[2,248,512]{2,1,0:T(8,128)(2,1)}, u32[]{:S(2)}, u32[]{:S(2)}) collective-permute-start(bf16[2,248,512]{2,1,0:T(8,128)(2,1)} %get-tuple-element.110), channel_id=1, source_target_pairs={{0,1},{1,0},{2,3},{3,2},{4,5},{5,4},{6,7},{7,6},{8,9},{9,8},{10,11... | collective-permute-start | bytes 1523720 | tf_op jit(solution)/shard_map/ppermute | solution.py:480
  106.5 37.5 %collective-permute-start.12 = (bf16[2,248,512]{2,1,0:T(8,128)(2,1)}, bf16[2,248,512]{2,1,0:T(8,128)(2,1)}, u32[]{:S(2)}, u32[]{:S(2)}) collective-permute-start(bf16[2,248,512]{2,1,0:T(8,128)(2,1)} %get-tuple-element.112), channel_id=1, source_target_pairs={{0,2},{1,3},{2,0},{3,1},{4,6},{5,7},{6,4},{7,5},{8,10},{9,11},{10,... | collective-permute-start | bytes 1523720 | tf_op jit(solution)/shard_map/ppermute | solution.py:480
  109.5 26.4 %collective-permute-start.10 = (bf16[2,512,512]{2,1,0:T(8,128)(2,1)}, bf16[2,512,512]{2,1,0:T(8,128)(2,1)}, u32[]{:S(2)}, u32[]{:S(2)}) collective-permute-start(bf16[2,512,512]{2,1,0:T(8,128)(2,1)} %slice.95), channel_id=1, source_target_pairs={{0,16},{4,20},{8,24},{12,28},{16,0},{20,4},{24,8},{28,12},{1,17},{... | collective-permute-start | bytes 3145736 | tf_op jit(solution)/shard_map/ppermute | solution.py:480
  111.1 33.0 %collective-permute-start.13 = (bf16[2,248,512]{2,1,0:T(8,128)(2,1)}, bf16[2,248,512]{2,1,0:T(8,128)(2,1)S(1)}, u32[]{:S(2)}, u32[]{:S(2)}) collective-permute-start(bf16[2,248,512]{2,1,0:T(8,128)(2,1)} %copy-done.15), channel_id=1, source_target_pairs={{0,3},{1,2},{2,1},{3,0},{4,7},{5,6},{6,5},{7,4},{8,11},{9,10},{10,... | collective-permute-start | bytes 1523720 | tf_op jit(solution)/shard_map/ppermute | solution.py:480
  129.0 25.0 %copy-start.10 = (bf16[2,248,512]{2,1,0:T(8,128)(2,1)S(1)}, bf16[2,248,512]{2,1,0:T(8,128)(2,1)}, u32[]{:S(2)}) copy-start(bf16[2,248,512]{2,1,0:T(8,128)(2,1)} %copy-done.9) | copy-start | bytes 1523716
  129.0 25.5 %copy-start.6 = (bf16[512,512]{1,0:T(8,128)(2,1)S(1)}, bf16[512,512]{1,0:T(8,128)(2,1)}, u32[]{:S(2)}) copy-start(bf16[512,512]{1,0:T(8,128)(2,1)} %w_out_ref.3) | copy-start | bytes 1572868
  129.0 25.5 %copy-start.26 = (f32[4,197,8]{2,1,0:T(8,128)S(1)}, f32[4,197,8]{2,1,0:T(8,128)}, u32[]{:S(2)}) copy-start(f32[4,197,8]{2,1,0:T(8,128)} %copy-done.25) | copy-start | bytes 75652
  129.0 25.5 %copy-start.30 = (bf16[2,248,512]{2,1,0:T(8,128)(2,1)S(1)}, bf16[2,248,512]{2,1,0:T(8,128)(2,1)}, u32[]{:S(2)}) copy-start(bf16[2,248,512]{2,1,0:T(8,128)(2,1)} %copy-done.29) | copy-start | bytes 1523716
  129.0 48.3 %collective-permute-start.17 = (bf16[1,512,512]{2,1,0:T(8,128)(2,1)S(1)}, bf16[1,512,512]{2,1,0:T(8,128)(2,1)S(1)}, u32[]{:S(2)}, u32[]{:S(2)}) collective-permute-start(bf16[1,512,512]{2,1,0:T(8,128)(2,1)S(1)} %slice.97), channel_id=1, source_target_pairs={{0,16},{4,20},{8,24},{12,28},{16,0},{20,4},{24,8},{28,12},{1,17},{... | collective-permute-start | bytes 1572872 | tf_op jit(solution)/shard_map/ppermute | solution.py:480
  144.0 33.4 %collective-permute-start.14 = (bf16[2,248,512]{2,1,0:T(8,128)(2,1)S(1)}, bf16[2,248,512]{2,1,0:T(8,128)(2,1)S(1)}, u32[]{:S(2)}, u32[]{:S(2)}) collective-permute-start(bf16[2,248,512]{2,1,0:T(8,128)(2,1)S(1)} %copy-done.12), channel_id=1, source_target_pairs={{0,1},{1,0},{2,3},{3,2},{4,5},{5,4},{6,7},{7,6},{8,9},{9,8},{10,11... | collective-permute-start | bytes 1523720 | tf_op jit(solution)/shard_map/ppermute | solution.py:480
  154.0 23.7 %collective-permute-start.15 = (bf16[2,248,512]{2,1,0:T(8,128)(2,1)S(1)}, bf16[2,248,512]{2,1,0:T(8,128)(2,1)S(1)}, u32[]{:S(2)}, u32[]{:S(2)}) collective-permute-start(bf16[2,248,512]{2,1,0:T(8,128)(2,1)S(1)} %copy-done.10), channel_id=1, source_target_pairs={{0,2},{1,3},{2,0},{3,1},{4,6},{5,7},{6,4},{7,5},{8,10},{9,11},{10,... | collective-permute-start | bytes 1523720 | tf_op jit(solution)/shard_map/ppermute | solution.py:480
  154.0 23.4 %collective-permute-start.18 = (bf16[1,512,512]{2,1,0:T(8,128)(2,1)S(1)}, bf16[1,512,512]{2,1,0:T(8,128)(2,1)S(1)}, u32[]{:S(2)}, u32[]{:S(2)}) collective-permute-start(bf16[1,512,512]{2,1,0:T(8,128)(2,1)S(1)} %slice.99), channel_id=1, source_target_pairs={{0,8},{4,12},{8,0},{12,4},{16,24},{20,28},{24,16},{28,20},{1,9},{5... | collective-permute-start | bytes 1572872 | tf_op jit(solution)/shard_map/ppermute | solution.py:480
  177.8 3.0 %collective-permute-start.19 = (bf16[4,4,16,2176]{3,2,1,0:T(8,128)(2,1)S(1)}, bf16[4,4,16,2176]{3,2,1,0:T(8,128)(2,1)S(1)}, u32[]{:S(2)}, u32[]{:S(2)}) collective-permute-start(bf16[4,4,16,2176]{3,2,1,0:T(8,128)(2,1)S(1)} %slice.78), channel_id=1, source_target_pairs={{0,4},{4,0},{8,12},{12,8},{16,20},{20,16},{24,28},{28,24},{1,5},{5... | collective-permute-start | bytes 3342344 | tf_op jit(solution)/shard_map/ppermute | solution.py:480
  178.0 14.3 %collective-permute-start.20 = (bf16[1,512,512]{2,1,0:T(8,128)(2,1)S(1)}, bf16[1,512,512]{2,1,0:T(8,128)(2,1)S(1)}, u32[]{:S(2)}, u32[]{:S(2)}) collective-permute-start(bf16[1,512,512]{2,1,0:T(8,128)(2,1)S(1)} %slice_add_fusion.4.refs_0_), channel_id=1, source_target_pairs={{0,16},{4,20},{8,24},{12,28},{16,0},{20,4},{24,8},{28,12},{1,17},{... | collective-permute-start | bytes 1572872 | tf_op jit(solution)/shard_map/ppermute | solution.py:480
  179.6 14.0 %collective-permute-start.21 = (bf16[1,512,512]{2,1,0:T(8,128)(2,1)S(1)}, bf16[1,512,512]{2,1,0:T(8,128)(2,1)S(1)}, u32[]{:S(2)}, u32[]{:S(2)}) collective-permute-start(bf16[1,512,512]{2,1,0:T(8,128)(2,1)S(1)} %slice_add_fusion.3.refs_0_), channel_id=1, source_target_pairs={{0,8},{4,12},{8,0},{12,4},{16,24},{20,28},{24,16},{28,20},{1,9},{5... | collective-permute-start | bytes 1572872 | tf_op jit(solution)/shard_map/ppermute | solution.py:480
  193.7 9.7 %collective-permute-start.22 = (bf16[4,16,2176]{2,1,0:T(8,128)(2,1)S(1)}, bf16[4,16,2176]{2,1,0:T(8,128)(2,1)S(1)}, u32[]{:S(2)}, u32[]{:S(2)}) collective-permute-start(bf16[4,16,2176]{2,1,0:T(8,128)(2,1)S(1)} %get-tuple-element.173), channel_id=1, source_target_pairs={{0,8},{4,12},{8,0},{12,4},{16,24},{20,28},{24,16},{28,20},{1,9},{5... | collective-permute-start | bytes 835592 | tf_op jit(solution)/shard_map/ppermute | solution.py:480
  194.9 14.3 %collective-permute-start.24 = (bf16[4,16,2176]{2,1,0:T(8,128)(2,1)S(1)}, bf16[4,16,2176]{2,1,0:T(8,128)(2,1)S(1)}, u32[]{:S(2)}, u32[]{:S(2)}) collective-permute-start(bf16[4,16,2176]{2,1,0:T(8,128)(2,1)S(1)} %get-tuple-element.174), channel_id=1, source_target_pairs={{0,24},{4,28},{8,16},{12,20},{16,8},{20,12},{24,0},{28,4},{1,25},{... | collective-permute-start | bytes 835592 | tf_op jit(solution)/shard_map/ppermute | solution.py:480
  195.7 14.9 %collective-permute-start.23 = (bf16[4,16,2176]{2,1,0:T(8,128)(2,1)S(1)}, bf16[4,16,2176]{2,1,0:T(8,128)(2,1)S(1)}, u32[]{:S(2)}, u32[]{:S(2)}) collective-permute-start(bf16[4,16,2176]{2,1,0:T(8,128)(2,1)S(1)} %get-tuple-element.175), channel_id=1, source_target_pairs={{0,16},{4,20},{8,24},{12,28},{16,0},{20,4},{24,8},{28,12},{1,17},{... | collective-permute-start | bytes 835592 | tf_op jit(solution)/shard_map/ppermute | solution.py:480
  198.6 13.9 %collective-permute-start.16 = (bf16[2,248,512]{2,1,0:T(8,128)(2,1)S(1)}, bf16[2,248,512]{2,1,0:T(8,128)(2,1)S(1)}, u32[]{:S(2)}, u32[]{:S(2)}) collective-permute-start(bf16[2,248,512]{2,1,0:T(8,128)(2,1)S(1)} %copy-done.8), channel_id=1, source_target_pairs={{0,3},{1,2},{2,1},{3,0},{4,7},{5,6},{6,5},{7,4},{8,11},{9,10},{10,... | collective-permute-start | bytes 1523720 | tf_op jit(solution)/shard_map/ppermute | solution.py:480
  200.9 24.9 %copy-start.20 = (f32[4,197,512]{2,1,0:T(8,128)S(1)}, f32[4,197,512]{2,1,0:T(8,128)}, u32[]{:S(2)}) copy-start(f32[4,197,512]{2,1,0:T(8,128)} %get-tuple-element.126.resid_ref) | copy-start | bytes 4841476
  200.9 30.7 %collective-permute-start.28 = (bf16[2,512,512]{2,1,0:T(8,128)(2,1)S(1)}, bf16[2,512,512]{2,1,0:T(8,128)(2,1)S(1)}, u32[]{:S(2)}, u32[]{:S(2)}) collective-permute-start(bf16[2,512,512]{2,1,0:T(8,128)(2,1)S(1)} %pad_maximum_fusion), channel_id=1, source_target_pairs={{0,8},{4,12},{8,0},{12,4},{16,24},{20,28},{24,16},{28,20},{1,9},{5... | collective-permute-start | bytes 3145736 | tf_op jit(solution)/shard_map/ppermute | solution.py:480
  203.3 28.3 %collective-permute-start.29 = (bf16[2,512,512]{2,1,0:T(8,128)(2,1)S(1)}, bf16[2,512,512]{2,1,0:T(8,128)(2,1)S(1)}, u32[]{:S(2)}, u32[]{:S(2)}) collective-permute-start(bf16[2,512,512]{2,1,0:T(8,128)(2,1)S(1)} %pad_maximum_fusion.1), channel_id=1, source_target_pairs={{0,16},{4,20},{8,24},{12,28},{16,0},{20,4},{24,8},{28,12},{1,17},{... | collective-permute-start | bytes 3145736 | tf_op jit(solution)/shard_map/ppermute | solution.py:480
  212.6 17.4 %collective-permute-start.25 = (bf16[16,2176]{1,0:T(8,128)(2,1)S(1)}, bf16[16,2176]{1,0:T(8,128)(2,1)S(1)}, u32[]{:S(2)}, u32[]{:S(2)}) collective-permute-start(bf16[16,2176]{1,0:T(8,128)(2,1)S(1)} %get-tuple-element.176), channel_id=1, source_target_pairs={{0,1},{1,0},{2,3},{3,2},{4,5},{5,4},{6,7},{7,6},{8,9},{9,8},{10,11... | collective-permute-start | bytes 208904 | tf_op jit(solution)/shard_map/ppermute | solution.py:480
  223.1 6.9 %collective-permute-start.27 = (bf16[16,2176]{1,0:T(8,128)(2,1)S(1)}, bf16[16,2176]{1,0:T(8,128)(2,1)S(1)}, u32[]{:S(2)}, u32[]{:S(2)}) collective-permute-start(bf16[16,2176]{1,0:T(8,128)(2,1)S(1)} %get-tuple-element.177), channel_id=1, source_target_pairs={{0,3},{1,2},{2,1},{3,0},{4,7},{5,6},{6,5},{7,4},{8,11},{9,10},{10,... | collective-permute-start | bytes 208904 | tf_op jit(solution)/shard_map/ppermute | solution.py:480
  225.7 5.8 %collective-permute-start.26 = (bf16[16,2176]{1,0:T(8,128)(2,1)S(1)}, bf16[16,2176]{1,0:T(8,128)(2,1)S(1)}, u32[]{:S(2)}, u32[]{:S(2)}) collective-permute-start(bf16[16,2176]{1,0:T(8,128)(2,1)S(1)} %get-tuple-element.178), channel_id=1, source_target_pairs={{0,2},{1,3},{2,0},{3,1},{4,6},{5,7},{6,4},{7,5},{8,10},{9,11},{10,... | collective-permute-start | bytes 208904 | tf_op jit(solution)/shard_map/ppermute | solution.py:480
  231.6 6.6 %collective-permute-start.33 = (bf16[16,2176]{1,0:T(8,128)(2,1)S(1)}, bf16[16,2176]{1,0:T(8,128)(2,1)S(1)}, u32[]{:S(2)}, u32[]{:S(2)}) collective-permute-start(bf16[16,2176]{1,0:T(8,128)(2,1)S(1)} %fusion.5.refs_0_), channel_id=1, source_target_pairs={{0,4},{4,0},{8,12},{12,8},{16,20},{20,16},{24,28},{28,24},{1,5},{5... | collective-permute-start | bytes 208904 | tf_op jit(solution)/shard_map/ppermute | solution.py:480
  231.6 7.1 %collective-permute-start.32 = (bf16[16,2176]{1,0:T(8,128)(2,1)S(1)}, bf16[16,2176]{1,0:T(8,128)(2,1)S(1)}, u32[]{:S(2)}, u32[]{:S(2)}) collective-permute-start(bf16[16,2176]{1,0:T(8,128)(2,1)S(1)} %fusion.5.refs_0_), channel_id=1, source_target_pairs={{0,24},{4,28},{8,16},{12,20},{16,8},{20,12},{24,0},{28,4},{1,25},{... | collective-permute-start | bytes 208904 | tf_op jit(solution)/shard_map/ppermute | solution.py:480
  233.7 5.1 %collective-permute-start.31 = (bf16[16,2176]{1,0:T(8,128)(2,1)S(1)}, bf16[16,2176]{1,0:T(8,128)(2,1)S(1)}, u32[]{:S(2)}, u32[]{:S(2)}) collective-permute-start(bf16[16,2176]{1,0:T(8,128)(2,1)S(1)} %fusion.5.refs_0_), channel_id=1, source_target_pairs={{0,16},{4,20},{8,24},{12,28},{16,0},{20,4},{24,8},{28,12},{1,17},{... | collective-permute-start | bytes 208904 | tf_op jit(solution)/shard_map/ppermute | solution.py:480
  234.6 4.6 %collective-permute-start.30 = (bf16[16,2176]{1,0:T(8,128)(2,1)S(1)}, bf16[16,2176]{1,0:T(8,128)(2,1)S(1)}, u32[]{:S(2)}, u32[]{:S(2)}) collective-permute-start(bf16[16,2176]{1,0:T(8,128)(2,1)S(1)} %fusion.5.refs_0_), channel_id=1, source_target_pairs={{0,8},{4,12},{8,0},{12,4},{16,24},{20,28},{24,16},{28,20},{1,9},{5... | collective-permute-start | bytes 208904 | tf_op jit(solution)/shard_map/ppermute | solution.py:480
  235.2 9.1 %collective-permute-start.37 = (bf16[1,512,512]{2,1,0:T(8,128)(2,1)S(1)}, bf16[1,512,512]{2,1,0:T(8,128)(2,1)S(1)}, u32[]{:S(2)}, u32[]{:S(2)}) collective-permute-start(bf16[1,512,512]{2,1,0:T(8,128)(2,1)S(1)} %slice_add_fusion.3.refs_0_), channel_id=1, source_target_pairs={{0,4},{4,0},{8,12},{12,8},{16,20},{20,16},{24,28},{28,24},{1,5},{5... | collective-permute-start | bytes 1572872 | tf_op jit(solution)/shard_map/ppermute | solution.py:480
  238.2 6.7 %collective-permute-start.39 = (bf16[2,512,512]{2,1,0:T(8,128)(2,1)S(1)}, bf16[2,512,512]{2,1,0:T(8,128)(2,1)S(1)}, u32[]{:S(2)}, u32[]{:S(2)}) collective-permute-start(bf16[2,512,512]{2,1,0:T(8,128)(2,1)S(1)} %collective-permute-done.29.refs_2_), channel_id=1, source_target_pairs={{0,4},{4,0},{8,12},{12,8},{16,20},{20,16},{24,28},{28,24},{1,5},{5... | collective-permute-start | bytes 3145736 | tf_op jit(solution)/shard_map/ppermute | solution.py:480
  238.7 3.6 %collective-permute-start.36 = (bf16[16,2176]{1,0:T(8,128)(2,1)S(1)}, bf16[16,2176]{1,0:T(8,128)(2,1)S(1)}, u32[]{:S(2)}, u32[]{:S(2)}) collective-permute-start(bf16[16,2176]{1,0:T(8,128)(2,1)S(1)} %collective-permute-done.32.refs_3_), channel_id=1, source_target_pairs={{0,4},{4,0},{8,12},{12,8},{16,20},{20,16},{24,28},{28,24},{1,5},{5... | collective-permute-start | bytes 208904 | tf_op jit(solution)/shard_map/ppermute | solution.py:480
  238.8 4.0 %collective-permute-start.35 = (bf16[16,2176]{1,0:T(8,128)(2,1)S(1)}, bf16[16,2176]{1,0:T(8,128)(2,1)S(1)}, u32[]{:S(2)}, u32[]{:S(2)}) collective-permute-start(bf16[16,2176]{1,0:T(8,128)(2,1)S(1)} %collective-permute-done.31.refs_2_), channel_id=1, source_target_pairs={{0,4},{4,0},{8,12},{12,8},{16,20},{20,16},{24,28},{28,24},{1,5},{5... | collective-permute-start | bytes 208904 | tf_op jit(solution)/shard_map/ppermute | solution.py:480
  239.2 3.6 %collective-permute-start.34 = (bf16[16,2176]{1,0:T(8,128)(2,1)S(1)}, bf16[16,2176]{1,0:T(8,128)(2,1)S(1)}, u32[]{:S(2)}, u32[]{:S(2)}) collective-permute-start(bf16[16,2176]{1,0:T(8,128)(2,1)S(1)} %collective-permute-done.30.refs_1_), channel_id=1, source_target_pairs={{0,4},{4,0},{8,12},{12,8},{16,20},{20,16},{24,28},{28,24},{1,5},{5... | collective-permute-start | bytes 208904 | tf_op jit(solution)/shard_map/ppermute | solution.py:480
  242.3 2.6 %collective-permute-start.38 = (bf16[1,512,512]{2,1,0:T(8,128)(2,1)S(1)}, bf16[1,512,512]{2,1,0:T(8,128)(2,1)S(1)}, u32[]{:S(2)}, u32[]{:S(2)}) collective-permute-start(bf16[1,512,512]{2,1,0:T(8,128)(2,1)S(1)} %collective-permute-done.21.refs_1_), channel_id=1, source_target_pairs={{0,4},{4,0},{8,12},{12,8},{16,20},{20,16},{24,28},{28,24},{1,5},{5... | collective-permute-start | bytes 1572872 | tf_op jit(solution)/shard_map/ppermute | solution.py:480
  242.8 5.1 %collective-permute-start.40 = (bf16[1,512,512]{2,1,0:T(8,128)(2,1)S(1)}, bf16[1,512,512]{2,1,0:T(8,128)(2,1)S(1)}, u32[]{:S(2)}, u32[]{:S(2)}) collective-permute-start(bf16[1,512,512]{2,1,0:T(8,128)(2,1)S(1)} %slice_add_fusion.4.refs_0_), channel_id=1, source_target_pairs={{0,4},{4,0},{8,12},{12,8},{16,20},{20,16},{24,28},{28,24},{1,5},{5... | collective-permute-start | bytes 1572872 | tf_op jit(solution)/shard_map/ppermute | solution.py:480
  242.8 5.1 %collective-permute-start.42 = (bf16[2,512,512]{2,1,0:T(8,128)(2,1)S(1)}, bf16[2,512,512]{2,1,0:T(8,128)(2,1)S(1)}, u32[]{:S(2)}, u32[]{:S(2)}) collective-permute-start(bf16[2,512,512]{2,1,0:T(8,128)(2,1)S(1)} %collective-permute-done.28.refs_2_), channel_id=1, source_target_pairs={{0,4},{4,0},{8,12},{12,8},{16,20},{20,16},{24,28},{28,24},{1,5},{5... | collective-permute-start | bytes 3145736 | tf_op jit(solution)/shard_map/ppermute | solution.py:480
  244.3 3.6 %collective-permute-start.41 = (bf16[1,512,512]{2,1,0:T(8,128)(2,1)S(1)}, bf16[1,512,512]{2,1,0:T(8,128)(2,1)S(1)}, u32[]{:S(2)}, u32[]{:S(2)}) collective-permute-start(bf16[1,512,512]{2,1,0:T(8,128)(2,1)S(1)} %collective-permute-done.20.refs_1_), channel_id=1, source_target_pairs={{0,4},{4,0},{8,12},{12,8},{16,20},{20,16},{24,28},{28,24},{1,5},{5... | collective-permute-start | bytes 1572872 | tf_op jit(solution)/shard_map/ppermute | solution.py:480
  (37 other events, 285.2 us)

commit v7 on v6

--- a/solution.py
+++ b/solution.py
@@ -667,7 +667,7 @@
         share = pack[0].astype(F32)
         for c in range(1, chips):
             share = share + swap(pack[c], "grp", grp_size, 2 * c).astype(F32)
-        share, *_ = after([share.astype(BF16)], *outs_back)
+        share, *_ = after([share.astype(BF16)], *outs_back[: half + 1])
         total = share[0].astype(F32)
         for d in range(1, ep_size):
             total = total + over_ep(share[d], d).astype(F32)

time: 256 us -> 256 us (level)
  transfers between devices with their start and end apart: 43 -> 43, of which waited for: 16 -> 14; matrix products, arithmetic and copies ran while one was open for 6% -> 6% of each run, Pallas kernels for 31% -> 31%
where the time goes in v7:
time: 256 us; the launch traced here: 251 us
  Pallas kernels  89.7 us (35%)
  starting transfers between devices  68.2 us (27%)
  waiting for transfers between devices  65 us (25%)
  local copies, waits for them, and re-layouts  21.3 us (8%)
  other arithmetic  5.34 us (2%)
    ppermute x43, starting transfers between devices, swap(): return lax.ppermute(array, axis, [(i, i ^ distance) for i in range(size)])  68.2 us
    ppermute x43, waiting for transfers between devices, swap(): return lax.ppermute(array, axis, [(i, i ^ distance) for i in range(size)])  65 us
    pallas_call x3, Pallas kernels, expert_call(): pl.pallas_call(functools.partial(expert_kernel, count, len(before), block...  35.1 us
    pallas_call x1, Pallas kernels, backward_call(): pl.pallas_call(functools.partial(backward_kernel, width // HD, ep_size, p...  22.7 us
    unnamed x88, local copies, waits for them, and re-layouts  16.8 us
    pallas_call x1, Pallas kernels, attention_call(): pl.pallas_call(functools.partial(attention_kernel, width // HD), grid=(n_...  12.4 us
    pallas_call x4, Pallas kernels, widen_call(): pl.pallas_call(functools.partial(widen_kernel, starts), grid_spec=pltpu.P...  12.1 us
  transfers between devices with their start and end apart: 43, of which 14 were waited for; matrix products, arithmetic and copies ran while one was open for 6% of the time, Pallas kernels for 31%

profile of v7, /device:TPU:0, one launch (start us, length us, event | category | flops | bytes accessed | tf_op | source)
XLA Modules:
  0.0 251.3 jit_solution(11296829612549125908)
XLA Ops:
  0.6 4.1 %collective-permute-start.4 = (bf16[4,197,512]{2,0,1:T(4,128)(2,1)}, bf16[4,197,512]{2,0,1:T(4,128)(2,1)}, u32[]{:S(2)}, u32[]{:S(2)}) collective-permute-start(bf16[4,197,512]{2,0,1:T(4,128)(2,1)} %param.29), channel_id=1, source_target_pairs={{0,2},{1,3},{2,0},{3,1},{4,6},{5,7},{6,4},{7,5},{8,10},{9,11},{10,... | collective-permute-start | bytes 2420744 | tf_op jit(solution)/shard_map/ppermute | solution.py:480
  4.7 1.3 copy.45.cot_ref
  7.5 2.2 route_and_dispatch_cotangent.1
  10.5 1.9 collective-permute-start
  13.8 12.4 %attention_forward_and_dispatch.1 = (bf16[4,197,1536]{2,1,0:T(8,128)(2,1)}, bf16[4,197,512]{2,1,0:T(8,128)(2,1)}, f32[4,197,128]{2,1,0:T(8,128)}, f32[4,197,512]...) custom-call(bf16[4,197,512]{2,1,0:T(8,128)(2,1)S(1)} %copy.46.tok_re, ...), custom_call_target="tpu_custom_call" | custom-call | flops 14000000000 | bytes 4096 | tf_op jit(solution)/shard_map/attention_forward_and_dispatch/pallas_call | solution.py:210
  28.2 2.7 %collective-permute-start.2 = (bf16[2,248,512]{2,1,0:T(8,128)(2,1)}, bf16[2,248,512]{2,1,0:T(8,128)(2,1)}, u32[]{:S(2)}, u32[]{:S(2)}) collective-permute-start(bf16[2,248,512]{2,1,0:T(8,128)(2,1)} %get-tuple-element.90), channel_id=1, source_target_pairs={{0,2},{1,3},{2,0},{3,1},{4,6},{5,7},{6,4},{7,5},{8,10},{9,11},{10,... | collective-permute-start | bytes 1523720 | tf_op jit(solution)/shard_map/ppermute | solution.py:480
  30.9 4.9 %collective-permute-done.refs_2_ = bf16[2,248,512]{2,1,0:T(8,128)(2,1)} collective-permute-done((bf16[2,248,512]{2,1,0:T(8,128)(2,1)}, bf16[2,248,512]{2,1,0:T(8,128)(2,1)}, u32[]{:S(2)}, u32[]{:S(2)}) %collective-permute-start) | collective-permute-done | bytes 507936 | tf_op jit(solution)/shard_map/ppermute | solution.py:480
  35.8 2.2 copy-done
  38.0 2.2 copy-done.2
  42.2 8.1 %experts.3 = (bf16[2,248,512]{2,1,0:T(8,128)(2,1)S(1)}, bf16[2,248,512]{2,1,0:T(8,128)(2,1)S(1)}, bf16[4,512,512]{2,1,0:T(8,128)(2,1)S(1)}, bf16[4,512,512]{2,1,...) custom-call(s32[3]{0:T(128)S(1)} %pad_add_fusion.sel_ref, ...), custom_call_target="tpu_custom_call" | custom-call | flops 10000000000 | bytes 4096 | tf_op jit(solution)/shard_map/experts/pallas_call | solution.py:298
  51.1 1.5 copy.47.cot_ref
  53.9 2.6 %collective-permute-start.6 = (bf16[2,248,512]{2,1,0:T(8,128)(2,1)S(1)}, bf16[2,248,512]{2,1,0:T(8,128)(2,1)S(1)}, u32[]{:S(2)}, u32[]{:S(2)}) collective-permute-start(bf16[2,248,512]{2,1,0:T(8,128)(2,1)S(1)} %get-tuple-element.99), channel_id=1, source_target_pairs={{0,1},{1,0},{2,3},{3,2},{4,5},{5,4},{6,7},{7,6},{8,9},{9,8},{10,11... | collective-permute-start | bytes 1523720 | tf_op jit(solution)/shard_map/ppermute | solution.py:480
  56.4 3.0 %collective-permute-done.1.refs_0_ = bf16[2,248,512]{2,1,0:T(8,128)(2,1)} collective-permute-done((bf16[2,248,512]{2,1,0:T(8,128)(2,1)}, bf16[2,248,512]{2,1,0:T(8,128)(2,1)}, u32[]{:S(2)}, u32[]{:S(2)}) %collective-permute-start.1) | collective-permute-done | bytes 507936 | tf_op jit(solution)/shard_map/ppermute | solution.py:480
  59.4 5.6 %collective-permute-done.2.refs_1_ = bf16[2,248,512]{2,1,0:T(8,128)(2,1)} collective-permute-done((bf16[2,248,512]{2,1,0:T(8,128)(2,1)}, bf16[2,248,512]{2,1,0:T(8,128)(2,1)}, u32[]{:S(2)}, u32[]{:S(2)}) %collective-permute-start.2) | collective-permute-done | bytes 507936 | tf_op jit(solution)/shard_map/ppermute | solution.py:480
  65.1 3.5 %collective-permute-start.5 = (bf16[2,248,512]{2,1,0:T(8,128)(2,1)S(1)}, bf16[2,248,512]{2,1,0:T(8,128)(2,1)S(1)}, u32[]{:S(2)}, u32[]{:S(2)}) collective-permute-start(bf16[2,248,512]{2,1,0:T(8,128)(2,1)S(1)} %copy-done.14), channel_id=1, source_target_pairs={{0,3},{1,2},{2,1},{3,0},{4,7},{5,6},{6,5},{7,4},{8,11},{9,10},{10,... | collective-permute-start | bytes 1523720 | tf_op jit(solution)/shard_map/ppermute | solution.py:480
  68.6 18.2 %experts.4 = (bf16[2,248,512]{2,1,0:T(8,128)(2,1)S(1)}, bf16[2,248,512]{2,1,0:T(8,128)(2,1)S(1)}, bf16[2,248,512]{2,1,0:T(8,128)(2,1)}, bf16[2,248,512]{2,1,0:T(...) custom-call(s32[3]{0:T(128)S(1)} %pad_add_fusion.sel_ref, ...), custom_call_target="tpu_custom_call", output_to_operand_aliasing={{4}: (9, {}), {5}: (10, {}), {6}: (11, {}), {7}: (12, {})} | custom-call | flops 20000000000 | bytes 4096 | tf_op jit(solution)/shard_map/experts/pallas_call | solution.py:298
  86.9 8.8 %experts.5 = (bf16[2,248,512]{2,1,0:T(8,128)(2,1)S(1)}, bf16[2,248,512]{2,1,0:T(8,128)(2,1)S(1)}, bf16[4,512,512]{2,1,0:T(8,128)(2,1)S(1)}, bf16[4,512,512]{2,1,...) custom-call(s32[3]{0:T(128)S(1)} %pad_add_fusion.sel_ref, ...), custom_call_target="tpu_custom_call", output_to_operand_aliasing={{2}: (7, {}), {3}: (8, {}), {4}: (9, {}), {5}: (10, {})} | custom-call | flops 10000000000 | bytes 4096 | tf_op jit(solution)/shard_map/experts/pallas_call | solution.py:298
  96.3 3.6 %collective-permute-done.7 = bf16[4,512,512]{2,1,0:T(8,128)(2,1)S(1)} collective-permute-done((bf16[4,512,512]{2,1,0:T(8,128)(2,1)S(1)}, bf16[4,512,512]{2,1,0:T(8,128)(2,1)S(1)}, u32[]{:S(2)}, u32[]{:S(2)}) %collective-permute-start.7) | collective-permute-done | bytes 2097184 | tf_op jit(solution)/shard_map/ppermute | solution.py:480
  101.7 1.5 collective-permute-start.8
  103.3 3.2 %collective-permute-start.11 = (bf16[2,248,512]{2,1,0:T(8,128)(2,1)}, bf16[2,248,512]{2,1,0:T(8,128)(2,1)}, u32[]{:S(2)}, u32[]{:S(2)}) collective-permute-start(bf16[2,248,512]{2,1,0:T(8,128)(2,1)} %get-tuple-element.110), channel_id=1, source_target_pairs={{0,1},{1,0},{2,3},{3,2},{4,5},{5,4},{6,7},{7,6},{8,9},{9,8},{10,11... | collective-permute-start | bytes 1523720 | tf_op jit(solution)/shard_map/ppermute | solution.py:480
  109.5 1.5 collective-permute-start.10
  111.1 1.9 collective-permute-start.13
  113.0 14.3 %collective-permute-done.8 = bf16[2,512,512]{2,1,0:T(8,128)(2,1)} collective-permute-done((bf16[2,512,512]{2,1,0:T(8,128)(2,1)}, bf16[2,512,512]{2,1,0:T(8,128)(2,1)}, u32[]{:S(2)}, u32[]{:S(2)}) %collective-permute-start.8) | collective-permute-done | bytes 1048608 | tf_op jit(solution)/shard_map/ppermute | solution.py:480
  127.3 1.6 slice_add_fusion.2
  129.0 1.6 collective-permute-start.17
  130.6 5.3 %collective-permute-done.10 = bf16[2,512,512]{2,1,0:T(8,128)(2,1)} collective-permute-done((bf16[2,512,512]{2,1,0:T(8,128)(2,1)}, bf16[2,512,512]{2,1,0:T(8,128)(2,1)}, u32[]{:S(2)}, u32[]{:S(2)}) %collective-permute-start.10) | collective-permute-done | bytes 1048608 | tf_op jit(solution)/shard_map/ppermute | solution.py:480
  135.9 1.3 slice_add_fusion.1
  137.3 6.7 %collective-permute-done.12.rest_2_ = bf16[2,248,512]{2,1,0:T(8,128)(2,1)} collective-permute-done((bf16[2,248,512]{2,1,0:T(8,128)(2,1)}, bf16[2,248,512]{2,1,0:T(8,128)(2,1)}, u32[]{:S(2)}, u32[]{:S(2)}) %collective-permute-start.12) | collective-permute-done | bytes 507936 | tf_op jit(solution)/shard_map/ppermute | solution.py:480
  144.0 9.9 %collective-permute-start.14 = (bf16[2,248,512]{2,1,0:T(8,128)(2,1)S(1)}, bf16[2,248,512]{2,1,0:T(8,128)(2,1)S(1)}, u32[]{:S(2)}, u32[]{:S(2)}) collective-permute-start(bf16[2,248,512]{2,1,0:T(8,128)(2,1)S(1)} %copy-done.12), channel_id=1, source_target_pairs={{0,1},{1,0},{2,3},{3,2},{4,5},{5,4},{6,7},{7,6},{8,9},{9,8},{10,11... | collective-permute-start | bytes 1523720 | tf_op jit(solution)/shard_map/ppermute | solution.py:480
  154.5 22.7 %attention_backward.1 = (bf16[4,197,512]{2,1,0:T(8,128)(2,1)S(1)}, bf16[8,4,16,2176]{3,2,1,0:T(8,128)(2,1)S(1)}) custom-call(s32[2]{0:T(128)S(1)} %pad_add_fusion.1.place_ref, f32[40,128]{1,0:T(8,128)S(1)} %pad_maximum_fusion.2.bias_ref, bf16[4,197,512]{2,1,0:T(8,128)(2,1)S(1)} %copy.46.tok_ref, bf16[4,197,512]{2,1,0:T(8,128)(2,1)S(1)} %copy.45.cot_ref, ...), custom_call_target="tpu_custom_call" | custom-call | flops 24999999488 | bytes 4096 | tf_op jit(solution)/shard_map/attention_backward/pallas_call | solution.py:443
  178.0 1.5 collective-permute-start.20
  180.9 11.4 %collective-permute-done.20.refs_1_ = bf16[1,512,512]{2,1,0:T(8,128)(2,1)S(1)} collective-permute-done((bf16[1,512,512]{2,1,0:T(8,128)(2,1)S(1)}, bf16[1,512,512]{2,1,0:T(8,128)(2,1)S(1)}, u32[]{:S(2)}, u32[]{:S(2)}) %collective-permute-start.20) | collective-permute-done | bytes 524320 | tf_op jit(solution)/shard_map/ppermute | solution.py:480
  195.7 1.5 collective-permute-start.23
  197.3 1.3 copy.51
  198.6 2.2 collective-permute-start.16
  200.9 1.5 collective-permute-start.28
  203.8 5.5 %collective-permute-done.24 = bf16[4,16,2176]{2,1,0:T(8,128)(2,1)S(1)} collective-permute-done((bf16[4,16,2176]{2,1,0:T(8,128)(2,1)S(1)}, bf16[4,16,2176]{2,1,0:T(8,128)(2,1)S(1)}, u32[]{:S(2)}, u32[]{:S(2)}) %collective-permute-start.24) | collective-permute-done | bytes 278560 | tf_op jit(solution)/shard_map/ppermute | solution.py:480
  209.3 1.3 collective-permute-done.23
  210.8 1.7 collective-permute-start.25
  212.5 2.7 %collective-permute-start.27 = (bf16[16,2176]{1,0:T(8,128)(2,1)S(1)}, bf16[16,2176]{1,0:T(8,128)(2,1)S(1)}, u32[]{:S(2)}, u32[]{:S(2)}) collective-permute-start(bf16[16,2176]{1,0:T(8,128)(2,1)S(1)} %get-tuple-element.177), channel_id=1, source_target_pairs={{0,3},{1,2},{2,1},{3,0},{4,7},{5,6},{6,5},{7,4},{8,11},{9,10},{10,... | collective-permute-start | bytes 208904 | tf_op jit(solution)/shard_map/ppermute | solution.py:480
  215.2 11.1 %collective-permute-start.26 = (bf16[16,2176]{1,0:T(8,128)(2,1)S(1)}, bf16[16,2176]{1,0:T(8,128)(2,1)S(1)}, u32[]{:S(2)}, u32[]{:S(2)}) collective-permute-start(bf16[16,2176]{1,0:T(8,128)(2,1)S(1)} %get-tuple-element.178), channel_id=1, source_target_pairs={{0,2},{1,3},{2,0},{3,1},{4,6},{5,7},{6,4},{7,5},{8,10},{9,11},{10,... | collective-permute-start | bytes 208904 | tf_op jit(solution)/shard_map/ppermute | solution.py:480
  226.2 3.0 %combine_output.1 = bf16[4,197,512]{2,1,0:T(8,128)(2,1)S(1)} custom-call(f32[4,197,512]{2,1,0:T(8,128)S(1)} %copy-done.20, f32[4,197,8]{2,1,0:T(8,128)S(1)} %copy-done.26, f32[4,197,8]{2,1,0:T(8,128)S(1)} %copy-done.28, bf16[2,248,512]{2,1,0:T(8,128)(2,1)S(1)} %copy-done.22, bf16[2,248,512]{2,1,0:T(8,128)(2,1)S(1)} %collective-permute-done.14.rest_1_, ...), custom_call_target="tpu_custom_call" | custom-call | flops 5000000000 | bytes 4096 | tf_op jit(solution)/shard_map/combine_output/pallas_call | solution.py:467
  229.2 1.3 copy.50
  231.6 2.1 collective-permute-start.32
  235.1 3.0 %expert_gradient_result.4.refs_3_ = f32[2,512,2048]{2,1,0:T(8,128)} custom-call(s32[2]{0:T(128)S(1)} %pad_add_fusion.2.place_ref, bf16[1,512,512]{2,1,0:T(8,128)(2,1)S(1)} %slice_add_fusion.3.refs_0_, bf16[1,512,512]{2,1,0:T(8,128)(2,1)S(1)} %collective-permute-done.21.refs_1_, bf16[2,512,512]{2,1,0:T(8,128)(2,1)S(1)} %collective-permute-done.29.refs_2_), custom_call_target="tpu_custom_call" | custom-call | flops 4000000000 | bytes 4096 | tf_op jit(solution)/shard_map/expert_gradient_result/pallas_call | solution.py:519
  239.2 3.0 %expert_gradient_result.6.refs_3_ = f32[2,2048,512]{2,1,0:T(8,128)} custom-call(s32[2]{0:T(128)S(1)} %pad_add_fusion.5.place_ref, bf16[1,512,512]{2,1,0:T(8,128)(2,1)S(1)} %slice_add_fusion.4.refs_0_, bf16[1,512,512]{2,1,0:T(8,128)(2,1)S(1)} %collective-permute-done.20.refs_1_, bf16[2,512,512]{2,1,0:T(8,128)(2,1)S(1)} %collective-permute-done.28.refs_2_), custom_call_target="tpu_custom_call" | custom-call | flops 4000000000 | bytes 4096 | tf_op jit(solution)/shard_map/expert_gradient_result/pallas_call | solution.py:519
  244.8 3.0 %expert_gradient_result.5 = f32[2,512,2048]{2,1,0:T(8,128)} custom-call(s32[2]{0:T(128)S(1)} %get-tuple-element.184.place_ref, bf16[1,512,512]{2,1,0:T(8,128)(2,1)S(1)} %collective-permute-done.37.refs_0_, bf16[1,512,512]{2,1,0:T(8,128)(2,1)S(1)} %collective-permute-done.38.refs_1_, ...), custom_call_target="tpu_custom_call", output_to_operand_aliasing={{}: (4, {})} | custom-call | flops 4000000000 | bytes 4096 | tf_op jit(solution)/shard_map/expert_gradient_result/pallas_call | solution.py:519
  247.8 3.0 %expert_gradient_result.7 = f32[2,2048,512]{2,1,0:T(8,128)} custom-call(s32[2]{0:T(128)S(1)} %get-tuple-element.185.place_ref, bf16[1,512,512]{2,1,0:T(8,128)(2,1)S(1)} %collective-permute-done.40.refs_0_, bf16[1,512,512]{2,1,0:T(8,128)(2,1)S(1)} %collective-permute-done.41.refs_1_, ...), custom_call_target="tpu_custom_call", output_to_operand_aliasing={{}: (4, {})} | custom-call | flops 4000000000 | bytes 4096 | tf_op jit(solution)/shard_map/expert_gradient_result/pallas_call | solution.py:519
  (172 shorter events, 29.0 us)
Async XLA Ops:
  0.6 50.5 %collective-permute-start.4 = (bf16[4,197,512]{2,0,1:T(4,128)(2,1)}, bf16[4,197,512]{2,0,1:T(4,128)(2,1)}, u32[]{:S(2)}, u32[]{:S(2)}) collective-permute-start(bf16[4,197,512]{2,0,1:T(4,128)(2,1)} %param.29), channel_id=1, source_target_pairs={{0,2},{1,3},{2,0},{3,1},{4,6},{5,7},{6,4},{7,5},{8,10},{9,11},{10,... | collective-permute-start | bytes 2420744 | tf_op jit(solution)/shard_map/ppermute | solution.py:480
  10.5 40.6 %collective-permute-start.3 = (f32[2,4,8,197]{3,2,1,0:T(8,128)S(1)}, f32[2,4,8,197]{3,2,1,0:T(8,128)S(1)}, u32[]{:S(2)}, u32[]{:S(2)}) collective-permute-start(f32[2,4,8,197]{3,2,1,0:T(8,128)S(1)} %get-tuple-element.80.info_ref), channel_id=1, source_target_pairs={{0,2},{1,3},{2,0},{3,1},{4,6},{5,7},{6,4},{7,5},{8,10},{9,11},{10,... | collective-permute-start | bytes 151304 | tf_op jit(solution)/shard_map/ppermute | solution.py:480
  10.5 25.2 %collective-permute-start = (bf16[2,248,512]{2,1,0:T(8,128)(2,1)}, bf16[2,248,512]{2,1,0:T(8,128)(2,1)}, u32[]{:S(2)}, u32[]{:S(2)}) collective-permute-start(bf16[2,248,512]{2,1,0:T(8,128)(2,1)} %get-tuple-element.85), channel_id=1, source_target_pairs={{0,1},{1,0},{2,3},{3,2},{4,5},{5,4},{6,7},{7,6},{8,9},{9,8},{10,11... | collective-permute-start | bytes 1523720 | tf_op jit(solution)/shard_map/ppermute | solution.py:480
  27.8 31.6 %collective-permute-start.1 = (bf16[2,248,512]{2,1,0:T(8,128)(2,1)}, bf16[2,248,512]{2,1,0:T(8,128)(2,1)}, u32[]{:S(2)}, u32[]{:S(2)}) collective-permute-start(bf16[2,248,512]{2,1,0:T(8,128)(2,1)} %get-tuple-element.89), channel_id=1, source_target_pairs={{0,1},{1,0},{2,3},{3,2},{4,5},{5,4},{6,7},{7,6},{8,9},{9,8},{10,11... | collective-permute-start | bytes 1523720 | tf_op jit(solution)/shard_map/ppermute | solution.py:480
  28.2 36.9 %collective-permute-start.2 = (bf16[2,248,512]{2,1,0:T(8,128)(2,1)}, bf16[2,248,512]{2,1,0:T(8,128)(2,1)}, u32[]{:S(2)}, u32[]{:S(2)}) collective-permute-start(bf16[2,248,512]{2,1,0:T(8,128)(2,1)} %get-tuple-element.90), channel_id=1, source_target_pairs={{0,2},{1,3},{2,0},{3,1},{4,6},{5,7},{6,4},{7,5},{8,10},{9,11},{10,... | collective-permute-start | bytes 1523720 | tf_op jit(solution)/shard_map/ppermute | solution.py:480
  53.9 33.0 %collective-permute-start.6 = (bf16[2,248,512]{2,1,0:T(8,128)(2,1)S(1)}, bf16[2,248,512]{2,1,0:T(8,128)(2,1)S(1)}, u32[]{:S(2)}, u32[]{:S(2)}) collective-permute-start(bf16[2,248,512]{2,1,0:T(8,128)(2,1)S(1)} %get-tuple-element.99), channel_id=1, source_target_pairs={{0,1},{1,0},{2,3},{3,2},{4,5},{5,4},{6,7},{7,6},{8,9},{9,8},{10,11... | collective-permute-start | bytes 1523720 | tf_op jit(solution)/shard_map/ppermute | solution.py:480
  65.1 21.8 %collective-permute-start.5 = (bf16[2,248,512]{2,1,0:T(8,128)(2,1)S(1)}, bf16[2,248,512]{2,1,0:T(8,128)(2,1)S(1)}, u32[]{:S(2)}, u32[]{:S(2)}) collective-permute-start(bf16[2,248,512]{2,1,0:T(8,128)(2,1)S(1)} %copy-done.14), channel_id=1, source_target_pairs={{0,3},{1,2},{2,1},{3,0},{4,7},{5,6},{6,5},{7,4},{8,11},{9,10},{10,... | collective-permute-start | bytes 1523720 | tf_op jit(solution)/shard_map/ppermute | solution.py:480
  95.7 4.2 %collective-permute-start.7 = (bf16[4,512,512]{2,1,0:T(8,128)(2,1)S(1)}, bf16[4,512,512]{2,1,0:T(8,128)(2,1)S(1)}, u32[]{:S(2)}, u32[]{:S(2)}) collective-permute-start(bf16[4,512,512]{2,1,0:T(8,128)(2,1)S(1)} %get-tuple-element.106), channel_id=1, source_target_pairs={{0,4},{4,0},{8,12},{12,8},{16,20},{20,16},{24,28},{28,24},{1,5},{5... | collective-permute-start | bytes 6291464 | tf_op jit(solution)/shard_map/ppermute | solution.py:480
  95.8 11.3 %collective-permute-start.9 = (bf16[4,512,512]{2,1,0:T(8,128)(2,1)S(1)}, bf16[4,512,512]{2,1,0:T(8,128)(2,1)S(1)}, u32[]{:S(2)}, u32[]{:S(2)}) collective-permute-start(bf16[4,512,512]{2,1,0:T(8,128)(2,1)S(1)} %get-tuple-element.108), channel_id=1, source_target_pairs={{0,4},{4,0},{8,12},{12,8},{16,20},{20,16},{24,28},{28,24},{1,5},{5... | collective-permute-start | bytes 6291464 | tf_op jit(solution)/shard_map/ppermute | solution.py:480
  101.7 25.5 %collective-permute-start.8 = (bf16[2,512,512]{2,1,0:T(8,128)(2,1)}, bf16[2,512,512]{2,1,0:T(8,128)(2,1)}, u32[]{:S(2)}, u32[]{:S(2)}) collective-permute-start(bf16[2,512,512]{2,1,0:T(8,128)(2,1)} %slice.93), channel_id=1, source_target_pairs={{0,8},{4,12},{8,0},{12,4},{16,24},{20,28},{24,16},{28,20},{1,9},{5... | collective-permute-start | bytes 3145736 | tf_op jit(solution)/shard_map/ppermute | solution.py:480
  103.3 34.0 %collective-permute-start.11 = (bf16[2,248,512]{2,1,0:T(8,128)(2,1)}, bf16[2,248,512]{2,1,0:T(8,128)(2,1)}, u32[]{:S(2)}, u32[]{:S(2)}) collective-permute-start(bf16[2,248,512]{2,1,0:T(8,128)(2,1)} %get-tuple-element.110), channel_id=1, source_target_pairs={{0,1},{1,0},{2,3},{3,2},{4,5},{5,4},{6,7},{7,6},{8,9},{9,8},{10,11... | collective-permute-start | bytes 1523720 | tf_op jit(solution)/shard_map/ppermute | solution.py:480
  106.5 37.5 %collective-permute-start.12 = (bf16[2,248,512]{2,1,0:T(8,128)(2,1)}, bf16[2,248,512]{2,1,0:T(8,128)(2,1)}, u32[]{:S(2)}, u32[]{:S(2)}) collective-permute-start(bf16[2,248,512]{2,1,0:T(8,128)(2,1)} %get-tuple-element.112), channel_id=1, source_target_pairs={{0,2},{1,3},{2,0},{3,1},{4,6},{5,7},{6,4},{7,5},{8,10},{9,11},{10,... | collective-permute-start | bytes 1523720 | tf_op jit(solution)/shard_map/ppermute | solution.py:480
  109.5 26.4 %collective-permute-start.10 = (bf16[2,512,512]{2,1,0:T(8,128)(2,1)}, bf16[2,512,512]{2,1,0:T(8,128)(2,1)}, u32[]{:S(2)}, u32[]{:S(2)}) collective-permute-start(bf16[2,512,512]{2,1,0:T(8,128)(2,1)} %slice.95), channel_id=1, source_target_pairs={{0,16},{4,20},{8,24},{12,28},{16,0},{20,4},{24,8},{28,12},{1,17},{... | collective-permute-start | bytes 3145736 | tf_op jit(solution)/shard_map/ppermute | solution.py:480
  111.1 33.0 %collective-permute-start.13 = (bf16[2,248,512]{2,1,0:T(8,128)(2,1)}, bf16[2,248,512]{2,1,0:T(8,128)(2,1)S(1)}, u32[]{:S(2)}, u32[]{:S(2)}) collective-permute-start(bf16[2,248,512]{2,1,0:T(8,128)(2,1)} %copy-done.15), channel_id=1, source_target_pairs={{0,3},{1,2},{2,1},{3,0},{4,7},{5,6},{6,5},{7,4},{8,11},{9,10},{10,... | collective-permute-start | bytes 1523720 | tf_op jit(solution)/shard_map/ppermute | solution.py:480
  129.0 25.5 %copy-start.6 = (bf16[512,512]{1,0:T(8,128)(2,1)S(1)}, bf16[512,512]{1,0:T(8,128)(2,1)}, u32[]{:S(2)}) copy-start(bf16[512,512]{1,0:T(8,128)(2,1)} %w_out_ref.3) | copy-start | bytes 1572868
  129.0 25.5 %copy-start.26 = (f32[4,197,8]{2,1,0:T(8,128)S(1)}, f32[4,197,8]{2,1,0:T(8,128)}, u32[]{:S(2)}) copy-start(f32[4,197,8]{2,1,0:T(8,128)} %copy-done.25) | copy-start | bytes 75652
  129.0 25.5 %copy-start.30 = (bf16[2,248,512]{2,1,0:T(8,128)(2,1)S(1)}, bf16[2,248,512]{2,1,0:T(8,128)(2,1)}, u32[]{:S(2)}) copy-start(bf16[2,248,512]{2,1,0:T(8,128)(2,1)} %copy-done.29) | copy-start | bytes 1523716
  129.0 48.3 %collective-permute-start.17 = (bf16[1,512,512]{2,1,0:T(8,128)(2,1)S(1)}, bf16[1,512,512]{2,1,0:T(8,128)(2,1)S(1)}, u32[]{:S(2)}, u32[]{:S(2)}) collective-permute-start(bf16[1,512,512]{2,1,0:T(8,128)(2,1)S(1)} %slice.97), channel_id=1, source_target_pairs={{0,16},{4,20},{8,24},{12,28},{16,0},{20,4},{24,8},{28,12},{1,17},{... | collective-permute-start | bytes 1572872 | tf_op jit(solution)/shard_map/ppermute | solution.py:480
  144.0 33.4 %collective-permute-start.14 = (bf16[2,248,512]{2,1,0:T(8,128)(2,1)S(1)}, bf16[2,248,512]{2,1,0:T(8,128)(2,1)S(1)}, u32[]{:S(2)}, u32[]{:S(2)}) collective-permute-start(bf16[2,248,512]{2,1,0:T(8,128)(2,1)S(1)} %copy-done.12), channel_id=1, source_target_pairs={{0,1},{1,0},{2,3},{3,2},{4,5},{5,4},{6,7},{7,6},{8,9},{9,8},{10,11... | collective-permute-start | bytes 1523720 | tf_op jit(solution)/shard_map/ppermute | solution.py:480
  154.0 23.7 %collective-permute-start.15 = (bf16[2,248,512]{2,1,0:T(8,128)(2,1)S(1)}, bf16[2,248,512]{2,1,0:T(8,128)(2,1)S(1)}, u32[]{:S(2)}, u32[]{:S(2)}) collective-permute-start(bf16[2,248,512]{2,1,0:T(8,128)(2,1)S(1)} %copy-done.10), channel_id=1, source_target_pairs={{0,2},{1,3},{2,0},{3,1},{4,6},{5,7},{6,4},{7,5},{8,10},{9,11},{10,... | collective-permute-start | bytes 1523720 | tf_op jit(solution)/shard_map/ppermute | solution.py:480
  154.0 23.4 %collective-permute-start.18 = (bf16[1,512,512]{2,1,0:T(8,128)(2,1)S(1)}, bf16[1,512,512]{2,1,0:T(8,128)(2,1)S(1)}, u32[]{:S(2)}, u32[]{:S(2)}) collective-permute-start(bf16[1,512,512]{2,1,0:T(8,128)(2,1)S(1)} %slice.99), channel_id=1, source_target_pairs={{0,8},{4,12},{8,0},{12,4},{16,24},{20,28},{24,16},{28,20},{1,9},{5... | collective-permute-start | bytes 1572872 | tf_op jit(solution)/shard_map/ppermute | solution.py:480
  177.8 3.0 %collective-permute-start.19 = (bf16[4,4,16,2176]{3,2,1,0:T(8,128)(2,1)S(1)}, bf16[4,4,16,2176]{3,2,1,0:T(8,128)(2,1)S(1)}, u32[]{:S(2)}, u32[]{:S(2)}) collective-permute-start(bf16[4,4,16,2176]{3,2,1,0:T(8,128)(2,1)S(1)} %slice.78), channel_id=1, source_target_pairs={{0,4},{4,0},{8,12},{12,8},{16,20},{20,16},{24,28},{28,24},{1,5},{5... | collective-permute-start | bytes 3342344 | tf_op jit(solution)/shard_map/ppermute | solution.py:480
  178.0 14.3 %collective-permute-start.20 = (bf16[1,512,512]{2,1,0:T(8,128)(2,1)S(1)}, bf16[1,512,512]{2,1,0:T(8,128)(2,1)S(1)}, u32[]{:S(2)}, u32[]{:S(2)}) collective-permute-start(bf16[1,512,512]{2,1,0:T(8,128)(2,1)S(1)} %slice_add_fusion.4.refs_0_), channel_id=1, source_target_pairs={{0,16},{4,20},{8,24},{12,28},{16,0},{20,4},{24,8},{28,12},{1,17},{... | collective-permute-start | bytes 1572872 | tf_op jit(solution)/shard_map/ppermute | solution.py:480
  179.6 14.0 %collective-permute-start.21 = (bf16[1,512,512]{2,1,0:T(8,128)(2,1)S(1)}, bf16[1,512,512]{2,1,0:T(8,128)(2,1)S(1)}, u32[]{:S(2)}, u32[]{:S(2)}) collective-permute-start(bf16[1,512,512]{2,1,0:T(8,128)(2,1)S(1)} %slice_add_fusion.3.refs_0_), channel_id=1, source_target_pairs={{0,8},{4,12},{8,0},{12,4},{16,24},{20,28},{24,16},{28,20},{1,9},{5... | collective-permute-start | bytes 1572872 | tf_op jit(solution)/shard_map/ppermute | solution.py:480
  193.7 9.7 %collective-permute-start.22 = (bf16[4,16,2176]{2,1,0:T(8,128)(2,1)S(1)}, bf16[4,16,2176]{2,1,0:T(8,128)(2,1)S(1)}, u32[]{:S(2)}, u32[]{:S(2)}) collective-permute-start(bf16[4,16,2176]{2,1,0:T(8,128)(2,1)S(1)} %get-tuple-element.173), channel_id=1, source_target_pairs={{0,8},{4,12},{8,0},{12,4},{16,24},{20,28},{24,16},{28,20},{1,9},{5... | collective-permute-start | bytes 835592 | tf_op jit(solution)/shard_map/ppermute | solution.py:480
  194.9 14.3 %collective-permute-start.24 = (bf16[4,16,2176]{2,1,0:T(8,128)(2,1)S(1)}, bf16[4,16,2176]{2,1,0:T(8,128)(2,1)S(1)}, u32[]{:S(2)}, u32[]{:S(2)}) collective-permute-start(bf16[4,16,2176]{2,1,0:T(8,128)(2,1)S(1)} %get-tuple-element.174), channel_id=1, source_target_pairs={{0,24},{4,28},{8,16},{12,20},{16,8},{20,12},{24,0},{28,4},{1,25},{... | collective-permute-start | bytes 835592 | tf_op jit(solution)/shard_map/ppermute | solution.py:480
  195.7 14.9 %collective-permute-start.23 = (bf16[4,16,2176]{2,1,0:T(8,128)(2,1)S(1)}, bf16[4,16,2176]{2,1,0:T(8,128)(2,1)S(1)}, u32[]{:S(2)}, u32[]{:S(2)}) collective-permute-start(bf16[4,16,2176]{2,1,0:T(8,128)(2,1)S(1)} %get-tuple-element.175), channel_id=1, source_target_pairs={{0,16},{4,20},{8,24},{12,28},{16,0},{20,4},{24,8},{28,12},{1,17},{... | collective-permute-start | bytes 835592 | tf_op jit(solution)/shard_map/ppermute | solution.py:480
  198.6 16.6 %collective-permute-start.16 = (bf16[2,248,512]{2,1,0:T(8,128)(2,1)S(1)}, bf16[2,248,512]{2,1,0:T(8,128)(2,1)S(1)}, u32[]{:S(2)}, u32[]{:S(2)}) collective-permute-start(bf16[2,248,512]{2,1,0:T(8,128)(2,1)S(1)} %copy-done.8), channel_id=1, source_target_pairs={{0,3},{1,2},{2,1},{3,0},{4,7},{5,6},{6,5},{7,4},{8,11},{9,10},{10,... | collective-permute-start | bytes 1523720 | tf_op jit(solution)/shard_map/ppermute | solution.py:480
  200.9 25.4 %copy-start.20 = (f32[4,197,512]{2,1,0:T(8,128)S(1)}, f32[4,197,512]{2,1,0:T(8,128)}, u32[]{:S(2)}) copy-start(f32[4,197,512]{2,1,0:T(8,128)} %get-tuple-element.126.resid_ref) | copy-start | bytes 4841476
  200.9 25.4 %copy-start.22 = (bf16[2,248,512]{2,1,0:T(8,128)(2,1)S(1)}, bf16[2,248,512]{2,1,0:T(8,128)(2,1)}, u32[]{:S(2)}) copy-start(bf16[2,248,512]{2,1,0:T(8,128)(2,1)} %copy-done.21) | copy-start | bytes 1523716
  200.9 29.7 %collective-permute-start.28 = (bf16[2,512,512]{2,1,0:T(8,128)(2,1)S(1)}, bf16[2,512,512]{2,1,0:T(8,128)(2,1)S(1)}, u32[]{:S(2)}, u32[]{:S(2)}) collective-permute-start(bf16[2,512,512]{2,1,0:T(8,128)(2,1)S(1)} %pad_maximum_fusion), channel_id=1, source_target_pairs={{0,8},{4,12},{8,0},{12,4},{16,24},{20,28},{24,16},{28,20},{1,9},{5... | collective-permute-start | bytes 3145736 | tf_op jit(solution)/shard_map/ppermute | solution.py:480
  203.3 28.3 %collective-permute-start.29 = (bf16[2,512,512]{2,1,0:T(8,128)(2,1)S(1)}, bf16[2,512,512]{2,1,0:T(8,128)(2,1)S(1)}, u32[]{:S(2)}, u32[]{:S(2)}) collective-permute-start(bf16[2,512,512]{2,1,0:T(8,128)(2,1)S(1)} %pad_maximum_fusion.1), channel_id=1, source_target_pairs={{0,16},{4,20},{8,24},{12,28},{16,0},{20,4},{24,8},{28,12},{1,17},{... | collective-permute-start | bytes 3145736 | tf_op jit(solution)/shard_map/ppermute | solution.py:480
  210.8 19.7 %collective-permute-start.25 = (bf16[16,2176]{1,0:T(8,128)(2,1)S(1)}, bf16[16,2176]{1,0:T(8,128)(2,1)S(1)}, u32[]{:S(2)}, u32[]{:S(2)}) collective-permute-start(bf16[16,2176]{1,0:T(8,128)(2,1)S(1)} %get-tuple-element.176), channel_id=1, source_target_pairs={{0,1},{1,0},{2,3},{3,2},{4,5},{5,4},{6,7},{7,6},{8,9},{9,8},{10,11... | collective-permute-start | bytes 208904 | tf_op jit(solution)/shard_map/ppermute | solution.py:480
  212.5 18.0 %collective-permute-start.27 = (bf16[16,2176]{1,0:T(8,128)(2,1)S(1)}, bf16[16,2176]{1,0:T(8,128)(2,1)S(1)}, u32[]{:S(2)}, u32[]{:S(2)}) collective-permute-start(bf16[16,2176]{1,0:T(8,128)(2,1)S(1)} %get-tuple-element.177), channel_id=1, source_target_pairs={{0,3},{1,2},{2,1},{3,0},{4,7},{5,6},{6,5},{7,4},{8,11},{9,10},{10,... | collective-permute-start | bytes 208904 | tf_op jit(solution)/shard_map/ppermute | solution.py:480
  215.2 15.3 %collective-permute-start.26 = (bf16[16,2176]{1,0:T(8,128)(2,1)S(1)}, bf16[16,2176]{1,0:T(8,128)(2,1)S(1)}, u32[]{:S(2)}, u32[]{:S(2)}) collective-permute-start(bf16[16,2176]{1,0:T(8,128)(2,1)S(1)} %get-tuple-element.178), channel_id=1, source_target_pairs={{0,2},{1,3},{2,0},{3,1},{4,6},{5,7},{6,4},{7,5},{8,10},{9,11},{10,... | collective-permute-start | bytes 208904 | tf_op jit(solution)/shard_map/ppermute | solution.py:480
  231.6 6.5 %collective-permute-start.33 = (bf16[16,2176]{1,0:T(8,128)(2,1)S(1)}, bf16[16,2176]{1,0:T(8,128)(2,1)S(1)}, u32[]{:S(2)}, u32[]{:S(2)}) collective-permute-start(bf16[16,2176]{1,0:T(8,128)(2,1)S(1)} %fusion.5.refs_0_), channel_id=1, source_target_pairs={{0,4},{4,0},{8,12},{12,8},{16,20},{20,16},{24,28},{28,24},{1,5},{5... | collective-permute-start | bytes 208904 | tf_op jit(solution)/shard_map/ppermute | solution.py:480
  231.6 7.0 %collective-permute-start.32 = (bf16[16,2176]{1,0:T(8,128)(2,1)S(1)}, bf16[16,2176]{1,0:T(8,128)(2,1)S(1)}, u32[]{:S(2)}, u32[]{:S(2)}) collective-permute-start(bf16[16,2176]{1,0:T(8,128)(2,1)S(1)} %fusion.5.refs_0_), channel_id=1, source_target_pairs={{0,24},{4,28},{8,16},{12,20},{16,8},{20,12},{24,0},{28,4},{1,25},{... | collective-permute-start | bytes 208904 | tf_op jit(solution)/shard_map/ppermute | solution.py:480
  233.7 5.0 %collective-permute-start.31 = (bf16[16,2176]{1,0:T(8,128)(2,1)S(1)}, bf16[16,2176]{1,0:T(8,128)(2,1)S(1)}, u32[]{:S(2)}, u32[]{:S(2)}) collective-permute-start(bf16[16,2176]{1,0:T(8,128)(2,1)S(1)} %fusion.5.refs_0_), channel_id=1, source_target_pairs={{0,16},{4,20},{8,24},{12,28},{16,0},{20,4},{24,8},{28,12},{1,17},{... | collective-permute-start | bytes 208904 | tf_op jit(solution)/shard_map/ppermute | solution.py:480
  234.3 4.9 %collective-permute-start.30 = (bf16[16,2176]{1,0:T(8,128)(2,1)S(1)}, bf16[16,2176]{1,0:T(8,128)(2,1)S(1)}, u32[]{:S(2)}, u32[]{:S(2)}) collective-permute-start(bf16[16,2176]{1,0:T(8,128)(2,1)S(1)} %fusion.5.refs_0_), channel_id=1, source_target_pairs={{0,8},{4,12},{8,0},{12,4},{16,24},{20,28},{24,16},{28,20},{1,9},{5... | collective-permute-start | bytes 208904 | tf_op jit(solution)/shard_map/ppermute | solution.py:480
  235.1 9.1 %collective-permute-start.37 = (bf16[1,512,512]{2,1,0:T(8,128)(2,1)S(1)}, bf16[1,512,512]{2,1,0:T(8,128)(2,1)S(1)}, u32[]{:S(2)}, u32[]{:S(2)}) collective-permute-start(bf16[1,512,512]{2,1,0:T(8,128)(2,1)S(1)} %slice_add_fusion.3.refs_0_), channel_id=1, source_target_pairs={{0,4},{4,0},{8,12},{12,8},{16,20},{20,16},{24,28},{28,24},{1,5},{5... | collective-permute-start | bytes 1572872 | tf_op jit(solution)/shard_map/ppermute | solution.py:480
  238.1 6.7 %collective-permute-start.39 = (bf16[2,512,512]{2,1,0:T(8,128)(2,1)S(1)}, bf16[2,512,512]{2,1,0:T(8,128)(2,1)S(1)}, u32[]{:S(2)}, u32[]{:S(2)}) collective-permute-start(bf16[2,512,512]{2,1,0:T(8,128)(2,1)S(1)} %collective-permute-done.29.refs_2_), channel_id=1, source_target_pairs={{0,4},{4,0},{8,12},{12,8},{16,20},{20,16},{24,28},{28,24},{1,5},{5... | collective-permute-start | bytes 3145736 | tf_op jit(solution)/shard_map/ppermute | solution.py:480
  238.7 3.6 %collective-permute-start.36 = (bf16[16,2176]{1,0:T(8,128)(2,1)S(1)}, bf16[16,2176]{1,0:T(8,128)(2,1)S(1)}, u32[]{:S(2)}, u32[]{:S(2)}) collective-permute-start(bf16[16,2176]{1,0:T(8,128)(2,1)S(1)} %collective-permute-done.32.refs_3_), channel_id=1, source_target_pairs={{0,4},{4,0},{8,12},{12,8},{16,20},{20,16},{24,28},{28,24},{1,5},{5... | collective-permute-start | bytes 208904 | tf_op jit(solution)/shard_map/ppermute | solution.py:480
  238.7 4.0 %collective-permute-start.35 = (bf16[16,2176]{1,0:T(8,128)(2,1)S(1)}, bf16[16,2176]{1,0:T(8,128)(2,1)S(1)}, u32[]{:S(2)}, u32[]{:S(2)}) collective-permute-start(bf16[16,2176]{1,0:T(8,128)(2,1)S(1)} %collective-permute-done.31.refs_2_), channel_id=1, source_target_pairs={{0,4},{4,0},{8,12},{12,8},{16,20},{20,16},{24,28},{28,24},{1,5},{5... | collective-permute-start | bytes 208904 | tf_op jit(solution)/shard_map/ppermute | solution.py:480
  239.2 3.6 %collective-permute-start.34 = (bf16[16,2176]{1,0:T(8,128)(2,1)S(1)}, bf16[16,2176]{1,0:T(8,128)(2,1)S(1)}, u32[]{:S(2)}, u32[]{:S(2)}) collective-permute-start(bf16[16,2176]{1,0:T(8,128)(2,1)S(1)} %collective-permute-done.30.refs_1_), channel_id=1, source_target_pairs={{0,4},{4,0},{8,12},{12,8},{16,20},{20,16},{24,28},{28,24},{1,5},{5... | collective-permute-start | bytes 208904 | tf_op jit(solution)/shard_map/ppermute | solution.py:480
  242.3 2.6 %collective-permute-start.38 = (bf16[1,512,512]{2,1,0:T(8,128)(2,1)S(1)}, bf16[1,512,512]{2,1,0:T(8,128)(2,1)S(1)}, u32[]{:S(2)}, u32[]{:S(2)}) collective-permute-start(bf16[1,512,512]{2,1,0:T(8,128)(2,1)S(1)} %collective-permute-done.21.refs_1_), channel_id=1, source_target_pairs={{0,4},{4,0},{8,12},{12,8},{16,20},{20,16},{24,28},{28,24},{1,5},{5... | collective-permute-start | bytes 1572872 | tf_op jit(solution)/shard_map/ppermute | solution.py:480
  242.7 5.1 %collective-permute-start.40 = (bf16[1,512,512]{2,1,0:T(8,128)(2,1)S(1)}, bf16[1,512,512]{2,1,0:T(8,128)(2,1)S(1)}, u32[]{:S(2)}, u32[]{:S(2)}) collective-permute-start(bf16[1,512,512]{2,1,0:T(8,128)(2,1)S(1)} %slice_add_fusion.4.refs_0_), channel_id=1, source_target_pairs={{0,4},{4,0},{8,12},{12,8},{16,20},{20,16},{24,28},{28,24},{1,5},{5... | collective-permute-start | bytes 1572872 | tf_op jit(solution)/shard_map/ppermute | solution.py:480
  242.8 5.1 %collective-permute-start.42 = (bf16[2,512,512]{2,1,0:T(8,128)(2,1)S(1)}, bf16[2,512,512]{2,1,0:T(8,128)(2,1)S(1)}, u32[]{:S(2)}, u32[]{:S(2)}) collective-permute-start(bf16[2,512,512]{2,1,0:T(8,128)(2,1)S(1)} %collective-permute-done.28.refs_2_), channel_id=1, source_target_pairs={{0,4},{4,0},{8,12},{12,8},{16,20},{20,16},{24,28},{28,24},{1,5},{5... | collective-permute-start | bytes 3145736 | tf_op jit(solution)/shard_map/ppermute | solution.py:480
  244.2 3.6 %collective-permute-start.41 = (bf16[1,512,512]{2,1,0:T(8,128)(2,1)S(1)}, bf16[1,512,512]{2,1,0:T(8,128)(2,1)S(1)}, u32[]{:S(2)}, u32[]{:S(2)}) collective-permute-start(bf16[1,512,512]{2,1,0:T(8,128)(2,1)S(1)} %collective-permute-done.20.refs_1_), channel_id=1, source_target_pairs={{0,4},{4,0},{8,12},{12,8},{16,20},{20,16},{24,28},{28,24},{1,5},{5... | collective-permute-start | bytes 1572872 | tf_op jit(solution)/shard_map/ppermute | solution.py:480
  (37 other events, 285.9 us)
